TPU v7x, 32 devices: a whole 2x2x4 slice. The times are simulated.
32 devices in a mesh: groups: 2 (over y), ctx: 4 (over z), head: 4 (over x, core).
Axes of the slice: x: 2, y: 2, z: 4, core: 2. Of those that a mesh axis runs over, the one named last changes fastest.
Arguments:
- queries: bfloat16 [1536, 8, 8, 128], P(('groups', 'ctx'), None, 'head'), parts along dimension 0, may hold values from -80 to 80
- keys: bfloat16 [512, 4, 8, 128], P(('groups', 'ctx')), parts along dimension 0, may hold values from -6 to 6
- span_start: int32 [2], P('groups'), parts along dimension 0, may hold values from 13568 to 15616
- tile_first: int32 [24], P(('groups', 'ctx')), parts along dimension 0, may hold values from 0 to 255
Outputs:
- importance: float32 [1536, 8, 256], P(('groups', 'ctx'), 'head'), parts along dimension 0
There are 2 independent parts, one for each index of `groups`. A program takes and returns all parts, laid end to end along the dimension named above; each array names one. Nothing has to cross between parts.
All inputs are finite; a program needn't handle non-finite values.
Results may differ from a plain program's by a relative error of at most 0.0003.
Values may be sent and summed in bfloat16 or wider, within the bound.
No kernel may reach another device: no remote copies, remote signals or barrier semaphores. Data moves between devices by JAX's collectives and lax.ppermute only.
A program may use at most 512 MiB of HBM per device.

v0:
```python
from functools import partial

import jax
import jax.numpy as jnp
from jax import lax
from jax.sharding import PartitionSpec as P

GQ = 8
QTILE = 64


masked_score = -1e30


def masked_scores(query_rows, piece, positions, firsts):
    count = piece.shape[0] * piece.shape[1]
    flat = piece.reshape(count, piece.shape[2], piece.shape[3])
    scores = jnp.einsum("rghd,ngd->rghn", query_rows, flat, preferred_element_type=jnp.float32)
    scores = scores * query_rows.shape[3] ** (-0.5)
    index = jnp.arange(count, dtype=jnp.int32)
    visible = (index[None, :] >= firsts[:, None]) & (16 * index[None, :] + 31 <= positions[:, None])
    visible = visible[:, None, None, :]
    return (jnp.where(visible, scores, masked_score), visible)


def stats_step(query_rows, positions, firsts, carry, piece, start):
    top, total = carry
    scores, visible = masked_scores(query_rows, piece, positions, firsts)
    new_top = jnp.maximum(top, jnp.max(scores, axis=-1))
    fresh = jnp.sum(jnp.where(visible, jnp.exp(scores - new_top[..., None]), 0.0), axis=-1)
    return (new_top, fresh)


def pool_piece(query_rows, positions, firsts, top, total, piece, start):
    scores, visible = masked_scores(query_rows, piece, positions, firsts)
    probs = jnp.where(visible, jnp.exp(scores - top[..., None]), 0.0) / total[..., None]
    summed = jnp.sum(probs, axis=2)
    grouped = summed.reshape(summed.shape[0], summed.shape[1], piece.shape[0], 4)
    lead = grouped[..., 0]
    weighted = lead + 2.0 * (grouped[..., 1] + grouped[..., 2] + grouped[..., 3])
    return jnp.stack([weighted, lead])


def per_device(queries, keys, span_start, tile_first):
    rows = queries.shape[0]
    positions = span_start[0] + lax.axis_index("ctx") * rows + jnp.arange(rows, dtype=jnp.int32)
    firsts = jnp.repeat(tile_first, QTILE)
    state_shape = queries.shape[:3]
    start_state = (
        jnp.full(state_shape, masked_score, jnp.float32),
        jnp.zeros(state_shape, jnp.float32),
    )
    stats_fn = partial(stats_step, queries, positions, firsts)
    top, total = stats_fn(
        start_state, lax.all_gather(keys, "ctx", axis=0, tiled=True), jnp.int32(0)
    )
    pool_fn = partial(pool_piece, queries, positions, firsts, top, total)
    pooled = pool_fn(lax.all_gather(keys, "ctx", axis=0, tiled=True), jnp.int32(0))
    weighted = pooled[0]
    lead = pooled[1]
    zeros = jnp.zeros(weighted.shape[:2] + (1,), jnp.float32)
    blocks = lead + jnp.concatenate([zeros, weighted[..., :-1]], axis=-1)
    totals = lax.psum_scatter(blocks, "head", scatter_dimension=1, tiled=True)
    factor = totals.shape[-1] / (2.0 * GQ)
    return totals * factor


def solution(mesh):
    placed = (
        P(("groups", "ctx"), None, "head", None),
        P(("groups", "ctx"), None, None, None),
        P("groups"),
        P(("groups", "ctx")),
    )
    return jax.shard_map(
        per_device,
        mesh=mesh,
        in_specs=placed,
        out_specs=P(("groups", "ctx"), "head", None),
        check_vma=False,
    )
```

profile of v0, /device:TPU:0, one launch (start us, length us, event | category | flops | bytes accessed | tf_op | source)
XLA Modules:
  0.0 135.1 jit_solution(10025179407904615045)
XLA Ops:
  6.5 0.0 copy-start
  6.5 0.0 all-gather.2.cloned.1.call-start
  6.5 0.7 all-gather.2.cloned.1.call-update
  7.3 0.0 reduce-scatter.2.cloned.1.call-start
  8.0 0.7 broadcast_in_dim.44
  8.7 0.1 ge.13
  8.8 0.2 fusion.7
  9.0 48.6 %all-gather.2.cloned.1.call-done = bf16[256,4,8,128]{3,2,1,0:T(8,128)(2,1)} async-done(((bf16[64,4,8,128]{3,2,1,0:T(8,128)(2,1)}), bf16[256,4,8,128]{3,2,1,0:T(8,128)(2,1)}) %all-gather.2.cloned.1.call-update) | async-done | bytes 2097168 | tf_op jit(solution)/shard_map/all_gather | solution.py:58
  57.6 2.4 %copy.11 = bf16[256,4,8,128]{3,1,0,2:T(4,128)(2,1)S(1)} copy(bf16[256,4,8,128]{3,2,1,0:T(8,128)(2,1)} %all-gather.2.cloned.1.call-done) | data formatting | bytes 4194304 | tf_op jit(solution)/shard_map/all_gather | solution.py:58
  60.0 0.0 copy-done
  60.0 7.0 %fusion.1 = (f32[192,8,2]{0,2,1:T(2,128)S(1)}, f32[8,1024,192,2]{1,2,3,0:T(8,128)}) fusion(pred[192,1024]{1,0:T(8,128)(4,1)S(1)} %fusion.7, bf16[1024,8,128,1]{2,0,3,1:T(8,128)(2,1)S(1)} %bitcast.33, bf16[192,8,2,128]{3,2,1,0:T(2,128)(2,1)S(1)} %copy-done), kind=kOutput, calls=%fused_computation.4 | convolution fusion | flops 814740480 | bytes 15675392 | tf_op jit(solution)/shard_map/rghd,ngd->rghn/dot_general | solution.py:18
  67.1 14.8 %divide_reduce_fusion = f32[192,8,1024]{2,0,1:T(8,128)} fusion(f32[192,8,2]{0,2,1:T(2,128)S(1)} %broadcast_maximum_fusion, f32[8,1024,192,2]{1,2,3,0:T(8,128)} %get-tuple-element.8, pred[192,1024]{1,0:T(8,128)(4,1)S(1)} %fusion.7, bf16[1024,8,128,1]{2,0,3,1:T(8,128)(2,1)S(1)} %bitcast.34, bf16[192,8,2,128]{3,2,1,0:T(2,128)(2,1)S(1)} %copy-done), kind=kOutput, calls=%fused_computation.2 | convolution fusion | flops 835194880 | bytes 21966848 | tf_op jit(solution)/shard_map/div | solution.py:36
  81.9 9.1 %copy.13 = f32[192,8,1024]{0,1,2:T(8,128)} copy(f32[192,8,1024]{2,0,1:T(8,128)} %divide_reduce_fusion) | data formatting | bytes 12582912 | tf_op jit(solution)/shard_map/reduce_sum | solution.py:37
  91.0 4.1 %slice_bitcast_fusion = (f32[192,8,256]{0,1,2:T(8,128)S(1)}, f32[192,8,256]{0,1,2:T(8,128)S(1)}) fusion(f32[192,8,256,4]{0,1,3,2:T(8,128)} %bitcast.31), kind=kLoop, calls=%fused_computation.10 | loop fusion | flops 1179648 | bytes 9437184 | tf_op jit(solution)/shard_map/squeeze;stack;squeeze | solution.py:60
  95.1 0.3 slice_add_fusion.2
  95.4 2.0 %pad_add_fusion = f32[192,8,256]{0,1,2:T(8,128)S(1)} fusion(f32[192,8,255]{0,1,2:T(8,128)S(1)} %slice_add_fusion.2, f32[192,8,256,4]{0,1,3,2:T(8,128)} %bitcast.32), kind=kLoop, calls=%fused_computation.11 | loop fusion | flops 393216 | bytes 4712448 | tf_op jit(solution)/shard_map/add | solution.py:62
  97.4 1.8 %copy.15 = f32[192,8,256]{2,0,1:T(8,128)} copy(f32[192,8,256]{0,1,2:T(8,128)S(1)} %pad_add_fusion) | data formatting | bytes 3145728 | tf_op jit(solution)/shard_map/add | solution.py:62
  99.2 0.0 reduce-scatter.2.cloned.1.call-update
  99.2 27.0 %reduce-scatter.2.cloned.1.call-done = f32[192,2,256]{2,0,1:T(8,128)} async-done(((f32[192,8,256]{2,0,1:T(8,128)}), f32[192,2,256]{2,0,1:T(8,128)}) %reduce-scatter.2.cloned.1.call-update) | async-done | bytes 393232 | tf_op jit(solution)/shard_map/reduce_scatter | solution.py:63
  126.2 1.0 broadcast_multiply_fusion
  127.2 1.1 copy.16
  (3 shorter events, 0.0 us)
Async XLA Ops:
  6.5 53.5 %copy-start = (bf16[192,8,2,128]{3,2,1,0:T(2,128)(2,1)S(1)}, bf16[192,8,2,128]{3,2,1,0:T(2,128)(2,1)}, u32[]{:S(2)}) copy-start(bf16[192,8,2,128]{3,2,1,0:T(2,128)(2,1)} %param.4) | copy-start | bytes 2359300
  6.5 51.1 %all-gather.2.cloned.1.call-start = ((), (), s32[]{:S(2)}) async-start(), calls=%async_computation.1 | async-start | bytes 2621440 | tf_op jit(solution)/shard_map/all_gather | solution.py:58
  7.3 118.9 %reduce-scatter.2.cloned.1.call-start = ((), (), s32[]{:S(2)}) async-start(), calls=%async_computation.2 | async-start | bytes 1966080 | tf_op jit(solution)/shard_map/reduce_scatter | solution.py:63
Sparse Core Ops, SparseCore 0:
  8.9 48.6 all-gather.1
  99.3 26.8 reduce-scatter.1
where the time goes:
time: 135 us
  waiting for transfers between devices  76.3 us (57%)
  matrix products  21.9 us (16%)
  local copies, waits for them, and re-layouts  15.2 us (11%)
  between operations  14.1 us (10%)
  other arithmetic  7.6 us (6%)
    all_gather x1, waiting for transfers between devices, per_device(): lax.all_gather(keys, 'ctx', axis=0, tiled=True)  48.6 us
    reduce_scatter x1, waiting for transfers between devices, per_device(): totals = lax.psum_scatter(blocks, 'head', scatter_dimension=1, tiled=True)  27 us
    div x1, matrix products, pool_piece(): jnp.where(visible, jnp.exp(scores - top[..., None]), 0.0) / total[..., None]  14.8 us
    reduce_sum x1, local copies, waits for them, and re-layouts, pool_piece(): summed = jnp.sum(probs, axis=2)  9.11 us
    dot_general x1, matrix products, masked_scores(): jnp.einsum('rghd,ngd->rghn', query_rows, flat, preferred_element_type=jnp...  7.05 us
    another operation x1, other arithmetic, per_device(): lead = pooled[1]  4.05 us
  transfers between devices with their start and end apart: 2, of which 2 were waited for; matrix products, arithmetic and copies ran while one was open for 1% of the time, Pallas kernels for 0%

commit v1 on v0

v1 whole, which is shorter than its diff:
```python
import math
from functools import partial

import jax
import jax.numpy as jnp
from jax import lax
from jax.experimental import pallas as pl
from jax.experimental.pallas import tpu as pltpu
from jax.sharding import PartitionSpec as P

QTILE = 64
PACK = 16
LANES = 128
MASKED = -1e30
NT = (((1,), (1,)), ((), ()))


def pack_kernel(n_head, key_heads, heads, q_ref, k_ref, *out_refs):
    q_outs, k_out = out_refs[:n_head], out_refs[n_head]
    me = lax.axis_index("head")
    own = key_heads // n_head
    width = own * heads
    tokens = q_outs[0].shape[2]
    rows = PACK * key_heads * heads
    out_row = lax.broadcasted_iota(jnp.int32, (n_head * width * PACK, rows), 0)
    in_row = lax.broadcasted_iota(jnp.int32, (n_head * width * PACK, rows), 1)
    step = out_row // (width * PACK)
    unit = out_row // PACK % width
    source = out_row % PACK * (key_heads * heads) + (step ^ me) * width + unit
    select = jnp.where(in_row == source, 1.0, 0.0).astype(jnp.bfloat16)
    for block in range(tokens // PACK):
        moved = jnp.dot(
            select, q_ref[block * rows:(block + 1) * rows, :], preferred_element_type=jnp.float32
        ).astype(jnp.bfloat16)
        for d in range(n_head):
            for u in range(width):
                at = (d * width + u) * PACK
                q_outs[d][u // heads, u % heads, block * PACK:(block + 1) * PACK, :] = moved[at:at + PACK]

    blocks = k_out.shape[2]
    rows = PACK * 4 * key_heads
    out_row = lax.broadcasted_iota(jnp.int32, (own * 4 * PACK, rows), 0)
    in_row = lax.broadcasted_iota(jnp.int32, (own * 4 * PACK, rows), 1)
    head = out_row // (4 * PACK)
    part = out_row // PACK % 4
    source = out_row % PACK * (4 * key_heads) + part * key_heads + me * own + head
    select = jnp.where(in_row == source, 1.0, 0.0).astype(jnp.bfloat16)
    for block in range(blocks // PACK):
        moved = jnp.dot(
            select, k_ref[block * rows:(block + 1) * rows, :], preferred_element_type=jnp.float32
        ).astype(jnp.bfloat16)
        for u in range(own * 4):
            k_out[u // 4, u % 4, block * PACK:(block + 1) * PACK, :] = moved[u * PACK:(u + 1) * PACK]


def main_kernel(n_head, n_ctx, start_ref, first_ref, *refs):
    q_refs, k_refs = refs[:n_head], refs[n_head:n_head + n_ctx]
    out_ref, keys, scores = refs[n_head + n_ctx:]
    own, heads, tokens, _ = q_refs[0].shape
    local = k_refs[0].shape[2]
    nsel = local * n_ctx
    me = lax.axis_index("ctx")
    step = scores.shape[0] // (n_head * heads)
    scale = math.log2(math.e) / math.sqrt(q_refs[0].shape[3])
    factor = nsel / (2.0 * n_head * heads)
    least_position = 16 * 4 * nsel * 7 // 8 - n_ctx * tokens
    most_first = nsel - 1

    for j in range(n_ctx):
        source = lax.rem(me - j + n_ctx, n_ctx)
        at = pl.ds(pl.multiple_of(source * local, local), local)
        keys[:, :, at, :] = k_refs[j][...]

    def tile(index, _):
        begin = pl.multiple_of(index * step, step)
        first = first_ref[begin // QTILE]
        position = start_ref[0] + me * tokens + begin
        for g in range(own):
            rows = jnp.concatenate(
                [q[g, h, pl.ds(begin, step), :] for q in q_refs for h in range(heads)], axis=0
            )
            for s in range(4):
                scores[:, s * nsel:(s + 1) * nsel] = lax.dot_general(
                    rows, keys[g, s], NT, preferred_element_type=jnp.float32
                )
            for t in range(0, step, 8):
                masks = []
                place = position + t + lax.broadcasted_iota(jnp.int32, (8, LANES), 0)
                for s in range(4):
                    for lane in range(0, nsel, LANES):
                        i = 4 * (lane + lax.broadcasted_iota(jnp.int32, (8, LANES), 1)) + s
                        mask = None
                        if 4 * lane <= most_first:
                            mask = i >= first
                        if 16 * (4 * (lane + LANES - 1) + s) + 31 > least_position:
                            below = 16 * i + 31 <= place
                            mask = below if mask is None else mask & below
                        masks.append(mask)
                lead_sum, rest_sum = None, None
                for h in range(n_head * heads):
                    at = h * step + t
                    pieces = []
                    for n, mask in enumerate(masks):
                        piece = scores[at:at + 8, n * LANES:(n + 1) * LANES]
                        pieces.append(piece if mask is None else jnp.where(mask, piece, MASKED))
                    top = pieces[0]
                    for piece in pieces[1:]:
                        top = jnp.maximum(top, piece)
                    top = jnp.max(top, axis=1, keepdims=True)
                    pieces = [jnp.exp2((piece - top) * scale) for piece in pieces]
                    width = nsel // LANES
                    lead = pieces[:width]
                    rest = [pieces[n + width] + pieces[n + 2 * width] + pieces[n + 3 * width] for n in range(width)]
                    total = lead[0] + rest[0]
                    for n in range(1, width):
                        total = total + (lead[n] + rest[n])
                    inverse = 1.0 / jnp.sum(total, axis=1, keepdims=True)
                    lead = [piece * inverse for piece in lead]
                    rest = [piece * inverse for piece in rest]
                    if lead_sum is None:
                        lead_sum, rest_sum = lead, rest
                    else:
                        lead_sum = [a + b for a, b in zip(lead_sum, lead)]
                        rest_sum = [a + b for a, b in zip(rest_sum, rest)]
                lead = jnp.concatenate(lead_sum, axis=1)
                weighted = lead + 2.0 * jnp.concatenate(rest_sum, axis=1)
                column = lax.broadcasted_iota(jnp.int32, (8, nsel), 1)
                shifted = jnp.where(column == 0, 0.0, pltpu.roll(weighted, 1, 1))
                out_ref[pl.ds(begin + t, 8), g, :] = (lead + shifted) * factor
        return 0

    lax.fori_loop(0, tokens // step, tile, 0)


def per_device(n_head, n_ctx, queries, keys, span_start, tile_first):
    tokens, key_heads, heads, depth = queries.shape
    blocks = keys.shape[0]
    own = key_heads // n_head
    nsel = blocks * n_ctx
    vmem = pl.BlockSpec(memory_space=pltpu.VMEM)
    smem = pl.BlockSpec(memory_space=pltpu.SMEM)
    q_part = jax.ShapeDtypeStruct((own, heads, tokens, depth), queries.dtype)
    k_part = jax.ShapeDtypeStruct((own, 4, blocks, depth), keys.dtype)
    packed = pl.pallas_call(
        partial(pack_kernel, n_head, key_heads, heads),
        out_shape=[q_part] * n_head + [k_part],
        in_specs=[vmem, vmem],
        out_specs=[vmem] * (n_head + 1),
        compiler_params=pltpu.CompilerParams(vmem_limit_bytes=32 * 2 ** 20),
        name="pack",
    )(queries.reshape(-1, depth), keys.reshape(-1, depth))
    q_parts, k_own = packed[:n_head], packed[n_head]
    q_parts = [q_parts[0]] + [
        lax.ppermute(q_parts[d], "head", [(i, i ^ d) for i in range(n_head)]) for d in range(1, n_head)
    ]
    k_parts = [k_own] + [
        lax.ppermute(k_own, "ctx", [(i, (i + j) % n_ctx) for i in range(n_ctx)]) for j in range(1, n_ctx)
    ]
    step = min(QTILE, max(PACK, QTILE * 1024 // (4 * nsel)))
    return pl.pallas_call(
        partial(main_kernel, n_head, n_ctx),
        out_shape=jax.ShapeDtypeStruct((tokens, own, nsel), jnp.float32),
        in_specs=[smem, smem] + [vmem] * (n_head + n_ctx),
        out_specs=vmem,
        scratch_shapes=[
            pltpu.VMEM((own, 4, nsel, depth), keys.dtype),
            pltpu.VMEM((n_head * heads * step, 4 * nsel), jnp.float32),
        ],
        compiler_params=pltpu.CompilerParams(vmem_limit_bytes=56 * 2 ** 20),
        name="importance",
    )(span_start, tile_first, *q_parts, *k_parts)


def solution(mesh):
    placed = (
        P(("groups", "ctx"), None, "head", None),
        P(("groups", "ctx"), None, None, None),
        P("groups"),
        P(("groups", "ctx")),
    )
    return jax.shard_map(
        partial(per_device, mesh.shape["head"], mesh.shape["ctx"]),
        mesh=mesh,
        in_specs=placed,
        out_specs=P(("groups", "ctx"), "head", None),
        check_vma=False,
    )
```

time: 135 us -> 28.7 us (0.21)
  waiting for transfers between devices: 76.3 us -> 9.28 us
  matrix products: 21.9 us -> 0 us
  between operations: 14.1 us -> 0.74 us
  local copies, waits for them, and re-layouts: 15.2 us -> 3.73 us
  other arithmetic: 7.6 us -> 0 us
  Pallas kernels: 0 us -> 7.52 us
  starting transfers between devices: 0.04 us -> 7.21 us
    all_gather x1 -> x0, waiting for transfers between devices: 48.6 us -> none  [per_device(): lax.all_gather(keys, 'ctx', axis=0, tiled=True)]
    reduce_scatter x1 -> x0, waiting for transfers between devices: 27 us -> none  [per_device(): totals = lax.psum_scatter(blocks, 'head', scatter_dimension=1, tiled=True)]
    div x1 -> x0, matrix products: 14.8 us -> none  [pool_piece(): jnp.where(visible, jnp.exp(scores - top[..., None]), 0.0) / total[..., None]]
    ppermute x0 -> x6, waiting for transfers between devices: none -> 9.28 us  [the longest x3 9.27 us: per_device(): lax.ppermute(k_own, 'ctx', [(i, (i + j) % n_ctx) for i in range(n_ctx)])]
    reduce_sum x1 -> x0, local copies, waits for them, and re-layouts: 9.11 us -> none  [pool_piece(): summed = jnp.sum(probs, axis=2)]
    pallas_call x0 -> x2, Pallas kernels: none -> 7.52 us  [the longest x1 6.83 us: per_device(): pl.pallas_call(partial(main_kernel, n_head, n_ctx), out_shape=jax.ShapeDt...]
    ppermute x0 -> x6, starting transfers between devices: none -> 7.21 us  [the longest x3 5.35 us: per_device(): lax.ppermute(k_own, 'ctx', [(i, (i + j) % n_ctx) for i in range(n_ctx)])]
    dot_general x1 -> x0, matrix products: 7.05 us -> none  [masked_scores(): jnp.einsum('rghd,ngd->rghn', query_rows, flat, preferred_element_type=jnp...]
  transfers between devices with their start and end apart: 2 -> 6, of which waited for: 2 -> 2; matrix products, arithmetic and copies ran while one was open for 1% -> 0% of each run, Pallas kernels for 0% -> 0%
where the time goes in v1:
time: 28.7 us; the launch traced here: 28.5 us
  waiting for transfers between devices  9.28 us (32%)
  Pallas kernels  7.52 us (26%)
  starting transfers between devices  7.21 us (25%)
  local copies, waits for them, and re-layouts  3.73 us (13%)
  between operations  0.74 us (3%)
    ppermute x3, waiting for transfers between devices, per_device(): lax.ppermute(k_own, 'ctx', [(i, (i + j) % n_ctx) for i in range(n_ctx)])  9.27 us
    pallas_call x1, Pallas kernels, per_device(): pl.pallas_call(partial(main_kernel, n_head, n_ctx), out_shape=jax.ShapeDt...  6.83 us
    ppermute x3, starting transfers between devices, per_device(): lax.ppermute(k_own, 'ctx', [(i, (i + j) % n_ctx) for i in range(n_ctx)])  5.35 us
    unnamed x20, local copies, waits for them, and re-layouts  3.73 us
    ppermute x3, starting transfers between devices, per_device(): lax.ppermute(q_parts[d], 'head', [(i, i ^ d) for i in range(n_head)])  1.86 us
    pallas_call x1, Pallas kernels, per_device(): pl.pallas_call(partial(pack_kernel, n_head, key_heads, heads), out_shape=...  0.7 us
  transfers between devices with their start and end apart: 6, of which 2 were waited for; matrix products, arithmetic and copies ran while one was open for 0% of the time, Pallas kernels for 0%

profile of v1, /device:TPU:0, one launch (start us, length us, event | category | flops | bytes accessed | tf_op | source)
XLA Modules:
  0.0 28.5 jit_solution(13148156456870337959)
XLA Ops:
  0.0 0.0 copy-start
  0.0 1.1 %copy-done = bf16[192,8,2,128]{3,2,1,0:T(2,128)(2,1)S(1)} copy-done((bf16[192,8,2,128]{3,2,1,0:T(2,128)(2,1)S(1)}, bf16[192,8,2,128]{3,2,1,0:T(2,128)(2,1)}, u32[]{:S(2)}) %copy-start) | copy-done | bytes 786456
  1.1 0.0 copy-start.1
  1.1 1.0 %copy-done.1 = bf16[64,4,8,128]{3,2,1,0:T(8,128)(2,1)S(1)} copy-done((bf16[64,4,8,128]{3,2,1,0:T(8,128)(2,1)S(1)}, bf16[64,4,8,128]{3,2,1,0:T(8,128)(2,1)}, u32[]{:S(2)}) %copy-start.1) | copy-done | bytes 524312
  2.2 0.7 %pack.1 = (bf16[2,2,192,128]{3,2,1,0:T(8,128)(2,1)S(1)}, bf16[2,2,192,128]{3,2,1,0:T(8,128)(2,1)S(1)}, bf16[2,2,192,128]{3,2,1,0:T(8,128)(2,1)S(1)}, bf16[2,2,19...) custom-call(bf16[3072,128]{1,0:T(8,128)(2,1)S(1)} %bitcast.2, bf16[2048,128]{1,0:T(8,128)(2,1)S(1)} %bitcast.3), custom_call_target="tpu_custom_call" | custom-call | tf_op jit(solution)/shard_map/pack/pallas_call | solution.py:144
  2.9 0.0 copy-start.2
  2.9 0.7 %copy-done.2 = bf16[2,2,192,128]{3,2,1,0:T(8,128)(2,1)} copy-done((bf16[2,2,192,128]{3,2,1,0:T(8,128)(2,1)}, bf16[2,2,192,128]{3,2,1,0:T(8,128)(2,1)S(1)}, u32[]{:S(2)}) %copy-start.2) | copy-done | bytes 196632
  3.6 0.0 copy-start.3
  3.6 5.0 %collective-permute-start.5 = (bf16[2,4,64,128]{3,2,1,0:T(8,128)(2,1)S(1)}, bf16[2,4,64,128]{3,2,1,0:T(8,128)(2,1)S(1)}, u32[]{:S(2)}, u32[]{:S(2)}) collective-permute-start(bf16[2,4,64,128]{3,2,1,0:T(8,128)(2,1)S(1)} %get-tuple-element.14.refs_4_), channel_id=1, source_target_pairs={{0,12},{4,0},{8,4},{12,8},{1,13},{5,1},{9,5},{13,9},{2,14},{6,2},{... | collective-permute-start | bytes 393224 | tf_op jit(solution)/shard_map/ppermute | solution.py:157
  8.6 0.0 collective-permute-start
  8.6 1.5 %collective-permute-start.1 = (bf16[2,2,192,128]{3,2,1,0:T(8,128)(2,1)S(1)}, bf16[2,2,192,128]{3,2,1,0:T(8,128)(2,1)S(1)}, u32[]{:S(2)}, u32[]{:S(2)}) collective-permute-start(bf16[2,2,192,128]{3,2,1,0:T(8,128)(2,1)S(1)} %get-tuple-element.12), channel_id=1, source_target_pairs={{0,2},{1,3},{2,0},{3,1},{4,6},{5,7},{6,4},{7,5},{8,10},{9,11},{10,... | collective-permute-start | bytes 589832 | tf_op jit(solution)/shard_map/ppermute | solution.py:154
  10.1 0.4 %collective-permute-start.2 = (bf16[2,2,192,128]{3,2,1,0:T(8,128)(2,1)S(1)}, bf16[2,2,192,128]{3,2,1,0:T(8,128)(2,1)S(1)}, u32[]{:S(2)}, u32[]{:S(2)}) collective-permute-start(bf16[2,2,192,128]{3,2,1,0:T(8,128)(2,1)S(1)} %get-tuple-element.13), channel_id=1, source_target_pairs={{0,3},{1,2},{2,1},{3,0},{4,7},{5,6},{6,5},{7,4},{8,11},{9,10},{10,... | collective-permute-start | bytes 589832 | tf_op jit(solution)/shard_map/ppermute | solution.py:154
  10.5 0.0 collective-permute-start.4
  10.5 1.0 %collective-permute-done.5.refs_7_ = bf16[2,4,64,128]{3,2,1,0:T(8,128)(2,1)S(1)} collective-permute-done((bf16[2,4,64,128]{3,2,1,0:T(8,128)(2,1)S(1)}, bf16[2,4,64,128]{3,2,1,0:T(8,128)(2,1)S(1)}, u32[]{:S(2)}, u32[]{:S(2)}) %collective-permute-start.5) | collective-permute-done | bytes 131104 | tf_op jit(solution)/shard_map/ppermute | solution.py:157
  11.5 0.0 copy-start.7
  11.5 0.3 %collective-permute-start.3 = (bf16[2,4,64,128]{3,2,1,0:T(8,128)(2,1)S(1)}, bf16[2,4,64,128]{3,2,1,0:T(8,128)(2,1)S(1)}, u32[]{:S(2)}, u32[]{:S(2)}) collective-permute-start(bf16[2,4,64,128]{3,2,1,0:T(8,128)(2,1)S(1)} %get-tuple-element.14.refs_4_), channel_id=1, source_target_pairs={{0,4},{4,8},{8,12},{12,0},{1,5},{5,9},{9,13},{13,1},{2,6},{6,10},{... | collective-permute-start | bytes 393224 | tf_op jit(solution)/shard_map/ppermute | solution.py:157
  12.5 8.2 %collective-permute-done.4.refs_6_ = bf16[2,4,64,128]{3,2,1,0:T(8,128)(2,1)S(1)} collective-permute-done((bf16[2,4,64,128]{3,2,1,0:T(8,128)(2,1)S(1)}, bf16[2,4,64,128]{3,2,1,0:T(8,128)(2,1)S(1)}, u32[]{:S(2)}, u32[]{:S(2)}) %collective-permute-start.4) | collective-permute-done | bytes 131104 | tf_op jit(solution)/shard_map/ppermute | solution.py:157
  20.7 0.0 copy-start.8
  20.7 0.0 collective-permute-done.3.refs_5_
  20.7 0.0 copy-start.9
  20.7 0.0 collective-permute-done.refs_1_
  20.7 0.0 copy-start.4
  20.7 0.0 collective-permute-done.1.refs_2_
  20.7 0.0 copy-start.5
  20.7 0.0 collective-permute-done.2.refs_3_
  20.8 0.0 copy-start.6
  20.8 0.0 copy-done.3
  20.8 0.0 copy-done.7
  20.8 0.6 %copy-done.8 = bf16[2,4,64,128]{3,2,1,0:T(8,128)(2,1)} copy-done((bf16[2,4,64,128]{3,2,1,0:T(8,128)(2,1)}, bf16[2,4,64,128]{3,2,1,0:T(8,128)(2,1)S(1)}, u32[]{:S(2)}) %copy-start.8) | copy-done | bytes 131096
  21.4 0.0 copy-done.9
  21.4 0.1 copy-done.4
  21.5 0.1 copy-done.5
  21.6 0.1 copy-done.6
  21.7 6.8 %importance.1 = f32[192,2,256]{2,1,0:T(2,128)} custom-call(s32[1]{0:T(128)S(6)} %copy.5.start_ref, s32[3]{0:T(128)} %first_ref.1, bf16[2,2,192,128]{3,2,1,0:T(8,128)(2,1)} %copy-done.2, bf16[2,2,192,128]{3,2,1,0:T(8,128)(2,1)} %copy-done.4, bf16[2,2,192,128]{3,2,1,0:T(8,128)(2,1)} %copy-done.5, bf16[2,2,192,128]{3,2,1,0:T(8,128)(2,1)} %copy-done.6, ...), custom_call_target="tpu_custom_call" | custom-call | tf_op jit(solution)/shard_map/importance/pallas_call | solution.py:160
Async XLA Ops:
  0.0 1.1 %copy-start = (bf16[192,8,2,128]{3,2,1,0:T(2,128)(2,1)S(1)}, bf16[192,8,2,128]{3,2,1,0:T(2,128)(2,1)}, u32[]{:S(2)}) copy-start(bf16[192,8,2,128]{3,2,1,0:T(2,128)(2,1)} %param.4) | copy-start | bytes 2359300
  1.1 1.0 %copy-start.1 = (bf16[64,4,8,128]{3,2,1,0:T(8,128)(2,1)S(1)}, bf16[64,4,8,128]{3,2,1,0:T(8,128)(2,1)}, u32[]{:S(2)}) copy-start(bf16[64,4,8,128]{3,2,1,0:T(8,128)(2,1)} %param.5) | copy-start | bytes 1572868
  2.9 0.7 %copy-start.2 = (bf16[2,2,192,128]{3,2,1,0:T(8,128)(2,1)}, bf16[2,2,192,128]{3,2,1,0:T(8,128)(2,1)S(1)}, u32[]{:S(2)}) copy-start(bf16[2,2,192,128]{3,2,1,0:T(8,128)(2,1)S(1)} %get-tuple-element.10.refs_0_) | copy-start | bytes 589828
  3.6 17.2 %copy-start.3 = (bf16[2,4,64,128]{3,2,1,0:T(8,128)(2,1)}, bf16[2,4,64,128]{3,2,1,0:T(8,128)(2,1)S(1)}, u32[]{:S(2)}) copy-start(bf16[2,4,64,128]{3,2,1,0:T(8,128)(2,1)S(1)} %get-tuple-element.14.refs_4_) | copy-start | bytes 393220
  3.6 8.0 %collective-permute-start.5 = (bf16[2,4,64,128]{3,2,1,0:T(8,128)(2,1)S(1)}, bf16[2,4,64,128]{3,2,1,0:T(8,128)(2,1)S(1)}, u32[]{:S(2)}, u32[]{:S(2)}) collective-permute-start(bf16[2,4,64,128]{3,2,1,0:T(8,128)(2,1)S(1)} %get-tuple-element.14.refs_4_), channel_id=1, source_target_pairs={{0,12},{4,0},{8,4},{12,8},{1,13},{5,1},{9,5},{13,9},{2,14},{6,2},{... | collective-permute-start | bytes 393224 | tf_op jit(solution)/shard_map/ppermute | solution.py:157
  8.6 12.1 %collective-permute-start = (bf16[2,2,192,128]{3,2,1,0:T(8,128)(2,1)S(1)}, bf16[2,2,192,128]{3,2,1,0:T(8,128)(2,1)S(1)}, u32[]{:S(2)}, u32[]{:S(2)}) collective-permute-start(bf16[2,2,192,128]{3,2,1,0:T(8,128)(2,1)S(1)} %get-tuple-element.11), channel_id=1, source_target_pairs={{0,1},{1,0},{2,3},{3,2},{4,5},{5,4},{6,7},{7,6},{8,9},{9,8},{10,11... | collective-permute-start | bytes 589832 | tf_op jit(solution)/shard_map/ppermute | solution.py:154
  8.6 12.1 %collective-permute-start.1 = (bf16[2,2,192,128]{3,2,1,0:T(8,128)(2,1)S(1)}, bf16[2,2,192,128]{3,2,1,0:T(8,128)(2,1)S(1)}, u32[]{:S(2)}, u32[]{:S(2)}) collective-permute-start(bf16[2,2,192,128]{3,2,1,0:T(8,128)(2,1)S(1)} %get-tuple-element.12), channel_id=1, source_target_pairs={{0,2},{1,3},{2,0},{3,1},{4,6},{5,7},{6,4},{7,5},{8,10},{9,11},{10,... | collective-permute-start | bytes 589832 | tf_op jit(solution)/shard_map/ppermute | solution.py:154
  10.1 10.6 %collective-permute-start.2 = (bf16[2,2,192,128]{3,2,1,0:T(8,128)(2,1)S(1)}, bf16[2,2,192,128]{3,2,1,0:T(8,128)(2,1)S(1)}, u32[]{:S(2)}, u32[]{:S(2)}) collective-permute-start(bf16[2,2,192,128]{3,2,1,0:T(8,128)(2,1)S(1)} %get-tuple-element.13), channel_id=1, source_target_pairs={{0,3},{1,2},{2,1},{3,0},{4,7},{5,6},{6,5},{7,4},{8,11},{9,10},{10,... | collective-permute-start | bytes 589832 | tf_op jit(solution)/shard_map/ppermute | solution.py:154
  10.5 10.2 %collective-permute-start.4 = (bf16[2,4,64,128]{3,2,1,0:T(8,128)(2,1)S(1)}, bf16[2,4,64,128]{3,2,1,0:T(8,128)(2,1)S(1)}, u32[]{:S(2)}, u32[]{:S(2)}) collective-permute-start(bf16[2,4,64,128]{3,2,1,0:T(8,128)(2,1)S(1)} %get-tuple-element.14.refs_4_), channel_id=1, source_target_pairs={{0,8},{4,12},{8,0},{12,4},{1,9},{5,13},{9,1},{13,5},{2,10},{6,14},... | collective-permute-start | bytes 393224 | tf_op jit(solution)/shard_map/ppermute | solution.py:157
  11.5 9.3 %copy-start.7 = (bf16[2,4,64,128]{3,2,1,0:T(8,128)(2,1)}, bf16[2,4,64,128]{3,2,1,0:T(8,128)(2,1)S(1)}, u32[]{:S(2)}) copy-start(bf16[2,4,64,128]{3,2,1,0:T(8,128)(2,1)S(1)} %collective-permute-done.5.refs_7_) | copy-start | bytes 393220
  11.5 9.2 %collective-permute-start.3 = (bf16[2,4,64,128]{3,2,1,0:T(8,128)(2,1)S(1)}, bf16[2,4,64,128]{3,2,1,0:T(8,128)(2,1)S(1)}, u32[]{:S(2)}, u32[]{:S(2)}) collective-permute-start(bf16[2,4,64,128]{3,2,1,0:T(8,128)(2,1)S(1)} %get-tuple-element.14.refs_4_), channel_id=1, source_target_pairs={{0,4},{4,8},{8,12},{12,0},{1,5},{5,9},{9,13},{13,1},{2,6},{6,10},{... | collective-permute-start | bytes 393224 | tf_op jit(solution)/shard_map/ppermute | solution.py:157
  20.7 0.7 %copy-start.8 = (bf16[2,4,64,128]{3,2,1,0:T(8,128)(2,1)}, bf16[2,4,64,128]{3,2,1,0:T(8,128)(2,1)S(1)}, u32[]{:S(2)}) copy-start(bf16[2,4,64,128]{3,2,1,0:T(8,128)(2,1)S(1)} %collective-permute-done.4.refs_6_) | copy-start | bytes 393220
  20.7 0.7 %copy-start.9 = (bf16[2,4,64,128]{3,2,1,0:T(8,128)(2,1)}, bf16[2,4,64,128]{3,2,1,0:T(8,128)(2,1)S(1)}, u32[]{:S(2)}) copy-start(bf16[2,4,64,128]{3,2,1,0:T(8,128)(2,1)S(1)} %collective-permute-done.3.refs_5_) | copy-start | bytes 393220
  20.7 0.8 %copy-start.4 = (bf16[2,2,192,128]{3,2,1,0:T(8,128)(2,1)}, bf16[2,2,192,128]{3,2,1,0:T(8,128)(2,1)S(1)}, u32[]{:S(2)}) copy-start(bf16[2,2,192,128]{3,2,1,0:T(8,128)(2,1)S(1)} %collective-permute-done.refs_1_) | copy-start | bytes 589828
  20.7 0.8 %copy-start.5 = (bf16[2,2,192,128]{3,2,1,0:T(8,128)(2,1)}, bf16[2,2,192,128]{3,2,1,0:T(8,128)(2,1)S(1)}, u32[]{:S(2)}) copy-start(bf16[2,2,192,128]{3,2,1,0:T(8,128)(2,1)S(1)} %collective-permute-done.1.refs_2_) | copy-start | bytes 589828
  20.8 0.9 %copy-start.6 = (bf16[2,2,192,128]{3,2,1,0:T(8,128)(2,1)}, bf16[2,2,192,128]{3,2,1,0:T(8,128)(2,1)S(1)}, u32[]{:S(2)}) copy-start(bf16[2,2,192,128]{3,2,1,0:T(8,128)(2,1)S(1)} %collective-permute-done.2.refs_3_) | copy-start | bytes 589828

commit v2 on v1

--- a/solution.py
+++ b/solution.py
@@ -15,61 +15,67 @@
 NT = (((1,), (1,)), ((), ()))
 
 
-def pack_kernel(n_head, key_heads, heads, q_ref, k_ref, *out_refs):
-    q_outs, k_out = out_refs[:n_head], out_refs[n_head]
+def pack_kernel(n_head, n_ctx, key_heads, heads, q_hbm, k_hbm, q_out, k_out, q_ref, k_ref, q_sems, k_sems):
     me = lax.axis_index("head")
     own = key_heads // n_head
     width = own * heads
-    tokens = q_outs[0].shape[2]
-    rows = PACK * key_heads * heads
-    out_row = lax.broadcasted_iota(jnp.int32, (n_head * width * PACK, rows), 0)
-    in_row = lax.broadcasted_iota(jnp.int32, (n_head * width * PACK, rows), 1)
-    step = out_row // (width * PACK)
-    unit = out_row // PACK % width
-    source = out_row % PACK * (key_heads * heads) + (step ^ me) * width + unit
-    select = jnp.where(in_row == source, 1.0, 0.0).astype(jnp.bfloat16)
+    tokens = q_out.shape[3]
+    blocks = k_out.shape[3]
+    q_rows = PACK * key_heads * heads
+    k_rows = PACK * 4 * key_heads
+    k_copies, q_copies = [], []
+    for block in range(blocks // PACK):
+        at = pl.ds(block * k_rows, k_rows)
+        k_copies.append(pltpu.make_async_copy(k_hbm.at[at], k_ref.at[at], k_sems.at[block]))
     for block in range(tokens // PACK):
-        moved = jnp.dot(
-            select, q_ref[block * rows:(block + 1) * rows, :], preferred_element_type=jnp.float32
-        ).astype(jnp.bfloat16)
-        for d in range(n_head):
-            for u in range(width):
-                at = (d * width + u) * PACK
-                q_outs[d][u // heads, u % heads, block * PACK:(block + 1) * PACK, :] = moved[at:at + PACK]
+        at = pl.ds(block * q_rows, q_rows)
+        q_copies.append(pltpu.make_async_copy(q_hbm.at[at], q_ref.at[at], q_sems.at[block]))
+    for copy in k_copies + q_copies:
+        copy.start()
 
-    blocks = k_out.shape[2]
-    rows = PACK * 4 * key_heads
-    out_row = lax.broadcasted_iota(jnp.int32, (own * 4 * PACK, rows), 0)
-    in_row = lax.broadcasted_iota(jnp.int32, (own * 4 * PACK, rows), 1)
+    out_row = lax.broadcasted_iota(jnp.int32, (own * 4 * PACK, k_rows), 0)
+    in_row = lax.broadcasted_iota(jnp.int32, (own * 4 * PACK, k_rows), 1)
     head = out_row // (4 * PACK)
     part = out_row // PACK % 4
     source = out_row % PACK * (4 * key_heads) + part * key_heads + me * own + head
     select = jnp.where(in_row == source, 1.0, 0.0).astype(jnp.bfloat16)
     for block in range(blocks // PACK):
+        k_copies[block].wait()
         moved = jnp.dot(
-            select, k_ref[block * rows:(block + 1) * rows, :], preferred_element_type=jnp.float32
+            select, k_ref[block * k_rows:(block + 1) * k_rows, :], preferred_element_type=jnp.float32
         ).astype(jnp.bfloat16)
         for u in range(own * 4):
-            k_out[u // 4, u % 4, block * PACK:(block + 1) * PACK, :] = moved[u * PACK:(u + 1) * PACK]
+            for j in range(n_ctx):
+                k_out[j, u // 4, u % 4, block * PACK:(block + 1) * PACK, :] = moved[u * PACK:(u + 1) * PACK]
+
+    out_row = lax.broadcasted_iota(jnp.int32, (n_head * width * PACK, q_rows), 0)
+    in_row = lax.broadcasted_iota(jnp.int32, (n_head * width * PACK, q_rows), 1)
+    unit = out_row // PACK
+    source = out_row % PACK * (key_heads * heads) + unit
+    select = jnp.where(in_row == source, 1.0, 0.0).astype(jnp.bfloat16)
+    for block in range(tokens // PACK):
+        q_copies[block].wait()
+        moved = jnp.dot(
+            select, q_ref[block * q_rows:(block + 1) * q_rows, :], preferred_element_type=jnp.float32
+        ).astype(jnp.bfloat16)
+        for u in range(n_head * width):
+            d, g, h = u // width, u % width // heads, u % heads
+            q_out[d, g, h, block * PACK:(block + 1) * PACK, :] = moved[u * PACK:(u + 1) * PACK]
 
 
-def main_kernel(n_head, n_ctx, start_ref, first_ref, *refs):
-    q_refs, k_refs = refs[:n_head], refs[n_head:n_head + n_ctx]
-    out_ref, keys, scores = refs[n_head + n_ctx:]
-    own, heads, tokens, _ = q_refs[0].shape
-    local = k_refs[0].shape[2]
+def main_kernel(start_ref, first_ref, q_ref, k_ref, out_ref, keys, scores):
+    n_head, own, heads, tokens, depth = q_ref.shape
+    n_ctx, local = k_ref.shape[0], k_ref.shape[3]
     nsel = local * n_ctx
     me = lax.axis_index("ctx")
     step = scores.shape[0] // (n_head * heads)
-    scale = math.log2(math.e) / math.sqrt(q_refs[0].shape[3])
+    scale = math.log2(math.e) / math.sqrt(depth)
     factor = nsel / (2.0 * n_head * heads)
     least_position = 16 * 4 * nsel * 7 // 8 - n_ctx * tokens
     most_first = nsel - 1
 
     for j in range(n_ctx):
-        source = lax.rem(me - j + n_ctx, n_ctx)
-        at = pl.ds(pl.multiple_of(source * local, local), local)
-        keys[:, :, at, :] = k_refs[j][...]
+        keys[:, :, j * local:(j + 1) * local, :] = k_ref[j]
 
     def tile(index, _):
         begin = pl.multiple_of(index * step, step)
@@ -77,7 +83,7 @@
         position = start_ref[0] + me * tokens + begin
         for g in range(own):
             rows = jnp.concatenate(
-                [q[g, h, pl.ds(begin, step), :] for q in q_refs for h in range(heads)], axis=0
+                [q_ref[d, g, h, pl.ds(begin, step), :] for d in range(n_head) for h in range(heads)], axis=0
             )
             for s in range(4):
                 scores[:, s * nsel:(s + 1) * nsel] = lax.dot_general(
@@ -139,36 +145,39 @@
     nsel = blocks * n_ctx
     vmem = pl.BlockSpec(memory_space=pltpu.VMEM)
     smem = pl.BlockSpec(memory_space=pltpu.SMEM)
-    q_part = jax.ShapeDtypeStruct((own, heads, tokens, depth), queries.dtype)
-    k_part = jax.ShapeDtypeStruct((own, 4, blocks, depth), keys.dtype)
-    packed = pl.pallas_call(
-        partial(pack_kernel, n_head, key_heads, heads),
-        out_shape=[q_part] * n_head + [k_part],
-        in_specs=[vmem, vmem],
-        out_specs=[vmem] * (n_head + 1),
-        compiler_params=pltpu.CompilerParams(vmem_limit_bytes=32 * 2 ** 20),
+    hbm = pl.BlockSpec(memory_space=pltpu.HBM)
+    q_pack, k_pack = pl.pallas_call(
+        partial(pack_kernel, n_head, n_ctx, key_heads, heads),
+        out_shape=[
+            jax.ShapeDtypeStruct((n_head, own, heads, tokens, depth), queries.dtype),
+            jax.ShapeDtypeStruct((n_ctx, own, 4, blocks, depth), keys.dtype),
+        ],
+        in_specs=[hbm, hbm],
+        out_specs=[vmem, vmem],
+        scratch_shapes=[
+            pltpu.VMEM((tokens * key_heads * heads, depth), queries.dtype),
+            pltpu.VMEM((blocks * 4 * key_heads, depth), keys.dtype),
+            pltpu.SemaphoreType.DMA((tokens // PACK,)),
+            pltpu.SemaphoreType.DMA((blocks // PACK,)),
+        ],
+        compiler_params=pltpu.CompilerParams(vmem_limit_bytes=56 * 2 ** 20),
         name="pack",
     )(queries.reshape(-1, depth), keys.reshape(-1, depth))
-    q_parts, k_own = packed[:n_head], packed[n_head]
-    q_parts = [q_parts[0]] + [
-        lax.ppermute(q_parts[d], "head", [(i, i ^ d) for i in range(n_head)]) for d in range(1, n_head)
-    ]
-    k_parts = [k_own] + [
-        lax.ppermute(k_own, "ctx", [(i, (i + j) % n_ctx) for i in range(n_ctx)]) for j in range(1, n_ctx)
-    ]
+    q_all = lax.all_to_all(q_pack, "head", 0, 0, tiled=True)
+    k_all = lax.all_to_all(k_pack, "ctx", 0, 0, tiled=True)
     step = min(QTILE, max(PACK, QTILE * 1024 // (4 * nsel)))
     return pl.pallas_call(
-        partial(main_kernel, n_head, n_ctx),
+        main_kernel,
         out_shape=jax.ShapeDtypeStruct((tokens, own, nsel), jnp.float32),
-        in_specs=[smem, smem] + [vmem] * (n_head + n_ctx),
+        in_specs=[smem, smem, vmem, vmem],
         out_specs=vmem,
         scratch_shapes=[
             pltpu.VMEM((own, 4, nsel, depth), keys.dtype),
             pltpu.VMEM((n_head * heads * step, 4 * nsel), jnp.float32),
         ],
-        compiler_params=pltpu.CompilerParams(vmem_limit_bytes=56 * 2 ** 20),
+        compiler_params=pltpu.CompilerParams(vmem_limit_bytes=32 * 2 ** 20),
         name="importance",
-    )(span_start, tile_first, *q_parts, *k_parts)
+    )(span_start, tile_first, q_all, k_all)
 
 
 def solution(mesh):

time: 28.7 us -> 47.2 us (1.64)
  blocking collectives: 0 us -> 15.9 us
  waiting for transfers between devices: 9.28 us -> 13.5 us
  Pallas kernels: 7.52 us -> 11.3 us
  local copies, waits for them, and re-layouts: 3.73 us -> 0.01 us
  starting transfers between devices: 7.21 us -> 5.57 us
    all_to_all x0 -> x1, blocking collectives: none -> 15.9 us  [per_device(): q_all = lax.all_to_all(q_pack, 'head', 0, 0, tiled=True)]
    all_to_all x0 -> x1, waiting for transfers between devices: none -> 13.5 us  [per_device(): k_all = lax.all_to_all(k_pack, 'ctx', 0, 0, tiled=True)]
    ppermute x6 -> x0, waiting for transfers between devices: 9.28 us -> none  [the longest x3 9.27 us: per_device(): lax.ppermute(k_own, 'ctx', [(i, (i + j) % n_ctx) for i in range(n_ctx)])]
    ppermute x6 -> x0, starting transfers between devices: 7.21 us -> none  [the longest x3 5.35 us: per_device(): lax.ppermute(k_own, 'ctx', [(i, (i + j) % n_ctx) for i in range(n_ctx)])]
    all_to_all x0 -> x1, starting transfers between devices: none -> 5.57 us  [per_device(): k_all = lax.all_to_all(k_pack, 'ctx', 0, 0, tiled=True)]
    pallas_call x2, Pallas kernels: 7.52 us -> 11.3 us  [the longest x1 5.99 us: per_device(): pl.pallas_call(main_kernel, out_shape=jax.ShapeDtypeStruct((tokens, own,...]
    unnamed x20 -> x2, local copies, waits for them, and re-layouts: 3.73 us -> 0.01 us
  transfers between devices with their start and end apart: 6 -> 1, of which waited for: 2 -> 1; matrix products, arithmetic and copies ran while one was open for 0% -> 0% of each run, Pallas kernels for 0% -> 0%
where the time goes in v2:
time: 47.2 us; the launch traced here: 46.9 us
  blocking collectives  15.9 us (34%)
  waiting for transfers between devices  13.5 us (29%)
  Pallas kernels  11.3 us (24%)
  starting transfers between devices  5.57 us (12%)
  between operations  0.68 us (1%)
    all_to_all x1, blocking collectives, per_device(): q_all = lax.all_to_all(q_pack, 'head', 0, 0, tiled=True)  15.9 us
    all_to_all x1, waiting for transfers between devices, per_device(): k_all = lax.all_to_all(k_pack, 'ctx', 0, 0, tiled=True)  13.5 us
    pallas_call x1, Pallas kernels, per_device(): pl.pallas_call(main_kernel, out_shape=jax.ShapeDtypeStruct((tokens, own,...  5.99 us
    all_to_all x1, starting transfers between devices, per_device(): k_all = lax.all_to_all(k_pack, 'ctx', 0, 0, tiled=True)  5.57 us
    pallas_call x1, Pallas kernels, per_device(): pl.pallas_call(partial(pack_kernel, n_head, n_ctx, key_heads, heads), out...  5.33 us
  transfers between devices with their start and end apart: 1, of which 1 were waited for; matrix products, arithmetic and copies ran while one was open for 0% of the time, Pallas kernels for 0%

profile of v2, /device:TPU:0, one launch (start us, length us, event | category | flops | bytes accessed | tf_op | source)
XLA Modules:
  0.0 46.9 jit_solution(15831092890926199671)
XLA Ops:
  0.0 5.3 %pack.1 = (bf16[4,2,2,192,128]{4,3,2,1,0:T(8,128)(2,1)}, bf16[4,2,4,64,128]{4,3,2,1,0:T(8,128)(2,1)}) custom-call(bf16[3072,128]{1,0:T(8,128)(2,1)} %bitcast.2, bf16[2048,128]{1,0:T(8,128)(2,1)} %bitcast.3), custom_call_target="tpu_custom_call" | custom-call | tf_op jit(solution)/shard_map/pack/pallas_call | solution.py:149
  5.3 15.9 %all_to_all.10.q_ref = bf16[4,2,2,192,128]{4,3,2,1,0:T(8,128)(2,1)S(1)} all-to-all(bf16[4,2,2,192,128]{4,3,2,1,0:T(8,128)(2,1)} %get-tuple-element.7), channel_id=1, replica_groups=mesh['groups'=2,'ctx'=4,'head'=4] {'head'}, dimensions={0} | all-to-all | bytes 1572864 | tf_op jit(solution)/shard_map/all_to_all | solution.py:166
  21.2 5.6 %all-to-all-start.1 = ((bf16[4,2,4,64,128]{4,3,2,1,0:T(8,128)(2,1)}), bf16[4,2,4,64,128]{4,3,2,1,0:T(8,128)(2,1)S(1)}, u32[]{:S(2)}, u32[]{:S(2)}) async-start(bf16[4,2,4,64,128]{4,3,2,1,0:T(8,128)(2,1)} %get-tuple-element.8), calls=%async_computation.1 | async-start | bytes 1048576 | tf_op jit(solution)/shard_map/all_to_all | solution.py:167
  26.8 0.0 copy-start
  27.4 13.5 %all-to-all-done.1.k_ref = bf16[4,2,4,64,128]{4,3,2,1,0:T(8,128)(2,1)S(1)} async-done(((bf16[4,2,4,64,128]{4,3,2,1,0:T(8,128)(2,1)}), bf16[4,2,4,64,128]{4,3,2,1,0:T(8,128)(2,1)S(1)}, u32[]{:S(2)}, u32[]{:S(2)}) %all-to-all-start.1) | async-done | bytes 524320 | tf_op jit(solution)/shard_map/all_to_all | solution.py:167
  40.9 0.0 copy-done
  40.9 6.0 %importance.1 = f32[192,2,256]{2,1,0:T(2,128)} custom-call(s32[1]{0:T(128)S(6)} %copy.5.start_ref, s32[3]{0:T(128)S(1)} %copy-done, bf16[4,2,2,192,128]{4,3,2,1,0:T(8,128)(2,1)S(1)} %all_to_all.10.q_ref, bf16[4,2,4,64,128]{4,3,2,1,0:T(8,128)(2,1)S(1)} %all-to-all-done.1.k_ref), custom_call_target="tpu_custom_call" | custom-call | tf_op jit(solution)/shard_map/importance/pallas_call | solution.py:169
Async XLA Ops:
  21.2 19.7 %all-to-all-start.1 = ((bf16[4,2,4,64,128]{4,3,2,1,0:T(8,128)(2,1)}), bf16[4,2,4,64,128]{4,3,2,1,0:T(8,128)(2,1)S(1)}, u32[]{:S(2)}, u32[]{:S(2)}) async-start(bf16[4,2,4,64,128]{4,3,2,1,0:T(8,128)(2,1)} %get-tuple-element.8), calls=%async_computation.1 | async-start | bytes 1048576 | tf_op jit(solution)/shard_map/all_to_all | solution.py:167
  26.8 14.1 %copy-start = (s32[3]{0:T(128)S(1)}, s32[3]{0:T(128)}, u32[]{:S(2)}) copy-start(s32[3]{0:T(128)} %first_ref.1) | copy-start | bytes 40

commit v3 on v2

--- a/solution.py
+++ b/solution.py
@@ -10,26 +10,30 @@
 
 QTILE = 64
 PACK = 16
+K_COPIES = 2
+Q_COPIES = 3
 LANES = 128
 MASKED = -1e30
 NT = (((1,), (1,)), ((), ()))
 
 
-def pack_kernel(n_head, n_ctx, key_heads, heads, q_hbm, k_hbm, q_out, k_out, q_ref, k_ref, q_sems, k_sems):
+def pack_kernel(n_head, key_heads, heads, q_hbm, k_hbm, *refs):
+    q_outs, (k_out, q_ref, k_ref, q_sems, k_sems) = refs[:n_head], refs[n_head:]
     me = lax.axis_index("head")
     own = key_heads // n_head
     width = own * heads
-    tokens = q_out.shape[3]
-    blocks = k_out.shape[3]
+    tokens = q_outs[0].shape[2]
+    blocks = k_out.shape[2]
     q_rows = PACK * key_heads * heads
     k_rows = PACK * 4 * key_heads
     k_copies, q_copies = [], []
-    for block in range(blocks // PACK):
-        at = pl.ds(block * k_rows, k_rows)
-        k_copies.append(pltpu.make_async_copy(k_hbm.at[at], k_ref.at[at], k_sems.at[block]))
-    for block in range(tokens // PACK):
-        at = pl.ds(block * q_rows, q_rows)
-        q_copies.append(pltpu.make_async_copy(q_hbm.at[at], q_ref.at[at], q_sems.at[block]))
+    k_each, q_each = blocks // PACK // K_COPIES, tokens // PACK // Q_COPIES
+    for n in range(K_COPIES):
+        at = pl.ds(n * k_each * k_rows, k_each * k_rows)
+        k_copies.append(pltpu.make_async_copy(k_hbm.at[at], k_ref.at[at], k_sems.at[n]))
+    for n in range(Q_COPIES):
+        at = pl.ds(n * q_each * q_rows, q_each * q_rows)
+        q_copies.append(pltpu.make_async_copy(q_hbm.at[at], q_ref.at[at], q_sems.at[n]))
     for copy in k_copies + q_copies:
         copy.start()
 
@@ -40,32 +44,36 @@
     source = out_row % PACK * (4 * key_heads) + part * key_heads + me * own + head
     select = jnp.where(in_row == source, 1.0, 0.0).astype(jnp.bfloat16)
     for block in range(blocks // PACK):
-        k_copies[block].wait()
+        if block % k_each == 0:
+            k_copies[block // k_each].wait()
         moved = jnp.dot(
             select, k_ref[block * k_rows:(block + 1) * k_rows, :], preferred_element_type=jnp.float32
         ).astype(jnp.bfloat16)
         for u in range(own * 4):
-            for j in range(n_ctx):
-                k_out[j, u // 4, u % 4, block * PACK:(block + 1) * PACK, :] = moved[u * PACK:(u + 1) * PACK]
+            k_out[u // 4, u % 4, block * PACK:(block + 1) * PACK, :] = moved[u * PACK:(u + 1) * PACK]
 
     out_row = lax.broadcasted_iota(jnp.int32, (n_head * width * PACK, q_rows), 0)
     in_row = lax.broadcasted_iota(jnp.int32, (n_head * width * PACK, q_rows), 1)
-    unit = out_row // PACK
-    source = out_row % PACK * (key_heads * heads) + unit
+    step = out_row // (width * PACK)
+    unit = out_row // PACK % width
+    source = out_row % PACK * (key_heads * heads) + (step ^ me) * width + unit
     select = jnp.where(in_row == source, 1.0, 0.0).astype(jnp.bfloat16)
     for block in range(tokens // PACK):
-        q_copies[block].wait()
+        if block % q_each == 0:
+            q_copies[block // q_each].wait()
         moved = jnp.dot(
             select, q_ref[block * q_rows:(block + 1) * q_rows, :], preferred_element_type=jnp.float32
         ).astype(jnp.bfloat16)
         for u in range(n_head * width):
             d, g, h = u // width, u % width // heads, u % heads
-            q_out[d, g, h, block * PACK:(block + 1) * PACK, :] = moved[u * PACK:(u + 1) * PACK]
-
-
-def main_kernel(start_ref, first_ref, q_ref, k_ref, out_ref, keys, scores):
-    n_head, own, heads, tokens, depth = q_ref.shape
-    n_ctx, local = k_ref.shape[0], k_ref.shape[3]
+            q_outs[d][g, h, block * PACK:(block + 1) * PACK, :] = moved[u * PACK:(u + 1) * PACK]
+
+
+def main_kernel(n_head, n_ctx, start_ref, first_ref, *refs):
+    q_refs, k_refs = refs[:n_head], refs[n_head:n_head + n_ctx]
+    out_ref, keys, scores = refs[n_head + n_ctx:]
+    own, heads, tokens, depth = q_refs[0].shape
+    local = k_refs[0].shape[2]
     nsel = local * n_ctx
     me = lax.axis_index("ctx")
     step = scores.shape[0] // (n_head * heads)
@@ -75,7 +83,9 @@
     most_first = nsel - 1
 
     for j in range(n_ctx):
-        keys[:, :, j * local:(j + 1) * local, :] = k_ref[j]
+        source = lax.rem(me + 1 + j, n_ctx)
+        at = pl.ds(pl.multiple_of(source * local, local), local)
+        keys[:, :, at, :] = k_refs[j][...]
 
     def tile(index, _):
         begin = pl.multiple_of(index * step, step)
@@ -83,7 +93,7 @@
         position = start_ref[0] + me * tokens + begin
         for g in range(own):
             rows = jnp.concatenate(
-                [q_ref[d, g, h, pl.ds(begin, step), :] for d in range(n_head) for h in range(heads)], axis=0
+                [q[g, h, pl.ds(begin, step), :] for q in q_refs for h in range(heads)], axis=0
             )
             for s in range(4):
                 scores[:, s * nsel:(s + 1) * nsel] = lax.dot_general(
@@ -138,6 +148,10 @@
     lax.fori_loop(0, tokens // step, tile, 0)
 
 
+def in_hbm(array):
+    return pltpu.with_memory_space_constraint(array, pltpu.HBM)
+
+
 def per_device(n_head, n_ctx, queries, keys, span_start, tile_first):
     tokens, key_heads, heads, depth = queries.shape
     blocks = keys.shape[0]
@@ -146,30 +160,36 @@
     vmem = pl.BlockSpec(memory_space=pltpu.VMEM)
     smem = pl.BlockSpec(memory_space=pltpu.SMEM)
     hbm = pl.BlockSpec(memory_space=pltpu.HBM)
-    q_pack, k_pack = pl.pallas_call(
-        partial(pack_kernel, n_head, n_ctx, key_heads, heads),
-        out_shape=[
-            jax.ShapeDtypeStruct((n_head, own, heads, tokens, depth), queries.dtype),
-            jax.ShapeDtypeStruct((n_ctx, own, 4, blocks, depth), keys.dtype),
-        ],
+    q_part = jax.ShapeDtypeStruct((own, heads, tokens, depth), queries.dtype)
+    k_part = jax.ShapeDtypeStruct((own, 4, blocks, depth), keys.dtype)
+    packed = pl.pallas_call(
+        partial(pack_kernel, n_head, key_heads, heads),
+        out_shape=[q_part] * n_head + [k_part],
         in_specs=[hbm, hbm],
-        out_specs=[vmem, vmem],
+        out_specs=[vmem] * (n_head + 1),
         scratch_shapes=[
             pltpu.VMEM((tokens * key_heads * heads, depth), queries.dtype),
             pltpu.VMEM((blocks * 4 * key_heads, depth), keys.dtype),
-            pltpu.SemaphoreType.DMA((tokens // PACK,)),
-            pltpu.SemaphoreType.DMA((blocks // PACK,)),
+            pltpu.SemaphoreType.DMA((Q_COPIES,)),
+            pltpu.SemaphoreType.DMA((K_COPIES,)),
         ],
-        compiler_params=pltpu.CompilerParams(vmem_limit_bytes=56 * 2 ** 20),
+        compiler_params=pltpu.CompilerParams(vmem_limit_bytes=16 * 2 ** 20),
         name="pack",
-    )(queries.reshape(-1, depth), keys.reshape(-1, depth))
-    q_all = lax.all_to_all(q_pack, "head", 0, 0, tiled=True)
-    k_all = lax.all_to_all(k_pack, "ctx", 0, 0, tiled=True)
+    )(in_hbm(queries.reshape(-1, depth)), in_hbm(keys.reshape(-1, depth)))
+    q_parts, k_parts = list(packed[:n_head]), [packed[n_head]] * n_ctx
+
+    def send_keys(j):
+        k_parts[j] = lax.ppermute(k_parts[0], "ctx", [(i, (i + j) % n_ctx) for i in range(n_ctx)])
+
+    for d in range(1, n_head):
+        q_parts[d] = lax.ppermute(q_parts[d], "head", [(i, i ^ d) for i in range(n_head)])
+    for j in range(n_ctx - 1, 0, -1):
+        send_keys(j)
     step = min(QTILE, max(PACK, QTILE * 1024 // (4 * nsel)))
     return pl.pallas_call(
-        main_kernel,
+        partial(main_kernel, n_head, n_ctx),
         out_shape=jax.ShapeDtypeStruct((tokens, own, nsel), jnp.float32),
-        in_specs=[smem, smem, vmem, vmem],
+        in_specs=[smem, smem] + [vmem] * (n_head + n_ctx),
         out_specs=vmem,
         scratch_shapes=[
             pltpu.VMEM((own, 4, nsel, depth), keys.dtype),
@@ -177,7 +197,7 @@
         ],
         compiler_params=pltpu.CompilerParams(vmem_limit_bytes=32 * 2 ** 20),
         name="importance",
-    )(span_start, tile_first, q_all, k_all)
+    )(span_start, tile_first, *q_parts, *k_parts[::-1])
 
 
 def solution(mesh):

time: 47.2 us -> 23.8 us (0.50)
  blocking collectives: 15.9 us -> 0 us
  waiting for transfers between devices: 13.5 us -> 5.28 us
  starting transfers between devices: 5.57 us -> 9.27 us
  Pallas kernels: 11.3 us -> 8.41 us
    all_to_all x1 -> x0, blocking collectives: 15.9 us -> none  [per_device(): q_all = lax.all_to_all(q_pack, 'head', 0, 0, tiled=True)]
    all_to_all x1 -> x0, waiting for transfers between devices: 13.5 us -> none  [per_device(): k_all = lax.all_to_all(k_pack, 'ctx', 0, 0, tiled=True)]
    ppermute x0 -> x6, starting transfers between devices: none -> 9.27 us  [the longest x3 7.41 us: send_keys(): lax.ppermute(k_parts[0], 'ctx', [(i, (i + j) % n_ctx) for i in range(n_ct...]
    all_to_all x1 -> x0, starting transfers between devices: 5.57 us -> none  [per_device(): k_all = lax.all_to_all(k_pack, 'ctx', 0, 0, tiled=True)]
    ppermute x0 -> x6, waiting for transfers between devices: none -> 5.28 us  [the longest x3 5.27 us: send_keys(): lax.ppermute(k_parts[0], 'ctx', [(i, (i + j) % n_ctx) for i in range(n_ct...]
    pallas_call x2, Pallas kernels: 11.3 us -> 8.41 us  [the longest x1 6.04 us: per_device(): pl.pallas_call(partial(main_kernel, n_head, n_ctx), out_shape=jax.ShapeDt...]
  transfers between devices with their start and end apart: 1 -> 6, of which waited for: 1 -> 3; matrix products, arithmetic and copies ran while one was open for 0% -> 0% of each run, Pallas kernels for 0% -> 0%
where the time goes in v3:
time: 23.8 us; the launch traced here: 23.7 us
  starting transfers between devices  9.27 us (39%)
  Pallas kernels  8.41 us (35%)
  waiting for transfers between devices  5.28 us (22%)
  between operations  0.69 us (3%)
    ppermute x3, starting transfers between devices, send_keys(): lax.ppermute(k_parts[0], 'ctx', [(i, (i + j) % n_ctx) for i in range(n_ct...  7.41 us
    pallas_call x1, Pallas kernels, per_device(): pl.pallas_call(partial(main_kernel, n_head, n_ctx), out_shape=jax.ShapeDt...  6.04 us
    ppermute x3, waiting for transfers between devices, send_keys(): lax.ppermute(k_parts[0], 'ctx', [(i, (i + j) % n_ctx) for i in range(n_ct...  5.27 us
    pallas_call x1, Pallas kernels, per_device(): pl.pallas_call(partial(pack_kernel, n_head, key_heads, heads), out_shape=...  2.37 us
    ppermute x3, starting transfers between devices, per_device(): lax.ppermute(q_parts[d], 'head', [(i, i ^ d) for i in range(n_head)])  1.86 us
  transfers between devices with their start and end apart: 6, of which 3 were waited for; matrix products, arithmetic and copies ran while one was open for 0% of the time, Pallas kernels for 0%

profile of v3, /device:TPU:0, one launch (start us, length us, event | category | flops | bytes accessed | tf_op | source)
XLA Modules:
  0.0 23.7 jit_solution(13501789134546745044)
XLA Ops:
  0.0 2.4 %pack.1 = (bf16[2,2,192,128]{3,2,1,0:T(8,128)(2,1)S(1)}, bf16[2,2,192,128]{3,2,1,0:T(8,128)(2,1)S(1)}, bf16[2,2,192,128]{3,2,1,0:T(8,128)(2,1)S(1)}, bf16[2,2,19...) custom-call(bf16[3072,128]{1,0:T(8,128)(2,1)} %bitcast.2, bf16[2048,128]{1,0:T(8,128)(2,1)} %bitcast.3), custom_call_target="tpu_custom_call" | custom-call | tf_op jit(solution)/shard_map/pack/pallas_call | solution.py:165
  2.4 3.1 %collective-permute-start.5 = (bf16[2,4,64,128]{3,2,1,0:T(8,128)(2,1)S(1)}, bf16[2,4,64,128]{3,2,1,0:T(8,128)(2,1)S(1)}, u32[]{:S(2)}, u32[]{:S(2)}) collective-permute-start(bf16[2,4,64,128]{3,2,1,0:T(8,128)(2,1)S(1)} %get-tuple-element.14.refs_7_), channel_id=1, source_target_pairs={{0,4},{4,8},{8,12},{12,0},{1,5},{5,9},{9,13},{13,1},{2,6},{6,10},{... | collective-permute-start | bytes 393224 | tf_op jit(solution)/shard_map/ppermute | solution.py:182
  5.5 0.0 collective-permute-start
  5.5 1.5 %collective-permute-start.1 = (bf16[2,2,192,128]{3,2,1,0:T(8,128)(2,1)S(1)}, bf16[2,2,192,128]{3,2,1,0:T(8,128)(2,1)S(1)}, u32[]{:S(2)}, u32[]{:S(2)}) collective-permute-start(bf16[2,2,192,128]{3,2,1,0:T(8,128)(2,1)S(1)} %get-tuple-element.12), channel_id=1, source_target_pairs={{0,2},{1,3},{2,0},{3,1},{4,6},{5,7},{6,4},{7,5},{8,10},{9,11},{10,... | collective-permute-start | bytes 589832 | tf_op jit(solution)/shard_map/ppermute | solution.py:185
  7.0 0.4 %collective-permute-start.2 = (bf16[2,2,192,128]{3,2,1,0:T(8,128)(2,1)S(1)}, bf16[2,2,192,128]{3,2,1,0:T(8,128)(2,1)S(1)}, u32[]{:S(2)}, u32[]{:S(2)}) collective-permute-start(bf16[2,2,192,128]{3,2,1,0:T(8,128)(2,1)S(1)} %get-tuple-element.13), channel_id=1, source_target_pairs={{0,3},{1,2},{2,1},{3,0},{4,7},{5,6},{6,5},{7,4},{8,11},{9,10},{10,... | collective-permute-start | bytes 589832 | tf_op jit(solution)/shard_map/ppermute | solution.py:185
  7.3 2.6 %collective-permute-start.4 = (bf16[2,4,64,128]{3,2,1,0:T(8,128)(2,1)S(1)}, bf16[2,4,64,128]{3,2,1,0:T(8,128)(2,1)S(1)}, u32[]{:S(2)}, u32[]{:S(2)}) collective-permute-start(bf16[2,4,64,128]{3,2,1,0:T(8,128)(2,1)S(1)} %get-tuple-element.14.refs_7_), channel_id=1, source_target_pairs={{0,8},{4,12},{8,0},{12,4},{1,9},{5,13},{9,1},{13,5},{2,10},{6,14},... | collective-permute-start | bytes 393224 | tf_op jit(solution)/shard_map/ppermute | solution.py:182
  9.9 1.1 %collective-permute-done.5.refs_6_ = bf16[2,4,64,128]{3,2,1,0:T(8,128)(2,1)S(1)} collective-permute-done((bf16[2,4,64,128]{3,2,1,0:T(8,128)(2,1)S(1)}, bf16[2,4,64,128]{3,2,1,0:T(8,128)(2,1)S(1)}, u32[]{:S(2)}, u32[]{:S(2)}) %collective-permute-start.5) | collective-permute-done | bytes 131104 | tf_op jit(solution)/shard_map/ppermute | solution.py:182
  11.0 1.7 %collective-permute-start.3 = (bf16[2,4,64,128]{3,2,1,0:T(8,128)(2,1)S(1)}, bf16[2,4,64,128]{3,2,1,0:T(8,128)(2,1)S(1)}, u32[]{:S(2)}, u32[]{:S(2)}) collective-permute-start(bf16[2,4,64,128]{3,2,1,0:T(8,128)(2,1)S(1)} %get-tuple-element.14.refs_7_), channel_id=1, source_target_pairs={{0,12},{4,0},{8,4},{12,8},{1,13},{5,1},{9,5},{13,9},{2,14},{6,2},{... | collective-permute-start | bytes 393224 | tf_op jit(solution)/shard_map/ppermute | solution.py:182
  13.4 0.0 copy-start
  13.4 4.0 %collective-permute-done.4.refs_5_ = bf16[2,4,64,128]{3,2,1,0:T(8,128)(2,1)S(1)} collective-permute-done((bf16[2,4,64,128]{3,2,1,0:T(8,128)(2,1)S(1)}, bf16[2,4,64,128]{3,2,1,0:T(8,128)(2,1)S(1)}, u32[]{:S(2)}, u32[]{:S(2)}) %collective-permute-start.4) | collective-permute-done | bytes 131104 | tf_op jit(solution)/shard_map/ppermute | solution.py:182
  17.4 0.2 collective-permute-done.3.refs_4_
  17.6 0.0 collective-permute-done.refs_1_
  17.6 0.0 collective-permute-done.1.refs_2_
  17.6 0.0 collective-permute-done.2.refs_3_
  17.6 0.0 copy-done
  17.6 6.0 %importance.1 = f32[192,2,256]{2,1,0:T(2,128)} custom-call(s32[1]{0:T(128)S(6)} %copy.5.start_ref, s32[3]{0:T(128)S(1)} %copy-done, bf16[2,2,192,128]{3,2,1,0:T(8,128)(2,1)S(1)} %get-tuple-element.10.refs_0_, bf16[2,2,192,128]{3,2,1,0:T(8,128)(2,1)S(1)} %collective-permute-done.refs_1_, bf16[2,2,192,128]{3,2,1,0:T(8,128)(2,1)S(1)} %collective-permute-done.1.refs_2_, ...), custom_call_target="tpu_custom_call" | custom-call | tf_op jit(solution)/shard_map/importance/pallas_call | solution.py:189
Async XLA Ops:
  2.4 8.6 %collective-permute-start.5 = (bf16[2,4,64,128]{3,2,1,0:T(8,128)(2,1)S(1)}, bf16[2,4,64,128]{3,2,1,0:T(8,128)(2,1)S(1)}, u32[]{:S(2)}, u32[]{:S(2)}) collective-permute-start(bf16[2,4,64,128]{3,2,1,0:T(8,128)(2,1)S(1)} %get-tuple-element.14.refs_7_), channel_id=1, source_target_pairs={{0,4},{4,8},{8,12},{12,0},{1,5},{5,9},{9,13},{13,1},{2,6},{6,10},{... | collective-permute-start | bytes 393224 | tf_op jit(solution)/shard_map/ppermute | solution.py:182
  5.5 12.1 %collective-permute-start = (bf16[2,2,192,128]{3,2,1,0:T(8,128)(2,1)S(1)}, bf16[2,2,192,128]{3,2,1,0:T(8,128)(2,1)S(1)}, u32[]{:S(2)}, u32[]{:S(2)}) collective-permute-start(bf16[2,2,192,128]{3,2,1,0:T(8,128)(2,1)S(1)} %get-tuple-element.11), channel_id=1, source_target_pairs={{0,1},{1,0},{2,3},{3,2},{4,5},{5,4},{6,7},{7,6},{8,9},{9,8},{10,11... | collective-permute-start | bytes 589832 | tf_op jit(solution)/shard_map/ppermute | solution.py:185
  5.5 12.1 %collective-permute-start.1 = (bf16[2,2,192,128]{3,2,1,0:T(8,128)(2,1)S(1)}, bf16[2,2,192,128]{3,2,1,0:T(8,128)(2,1)S(1)}, u32[]{:S(2)}, u32[]{:S(2)}) collective-permute-start(bf16[2,2,192,128]{3,2,1,0:T(8,128)(2,1)S(1)} %get-tuple-element.12), channel_id=1, source_target_pairs={{0,2},{1,3},{2,0},{3,1},{4,6},{5,7},{6,4},{7,5},{8,10},{9,11},{10,... | collective-permute-start | bytes 589832 | tf_op jit(solution)/shard_map/ppermute | solution.py:185
  7.0 10.6 %collective-permute-start.2 = (bf16[2,2,192,128]{3,2,1,0:T(8,128)(2,1)S(1)}, bf16[2,2,192,128]{3,2,1,0:T(8,128)(2,1)S(1)}, u32[]{:S(2)}, u32[]{:S(2)}) collective-permute-start(bf16[2,2,192,128]{3,2,1,0:T(8,128)(2,1)S(1)} %get-tuple-element.13), channel_id=1, source_target_pairs={{0,3},{1,2},{2,1},{3,0},{4,7},{5,6},{6,5},{7,4},{8,11},{9,10},{10,... | collective-permute-start | bytes 589832 | tf_op jit(solution)/shard_map/ppermute | solution.py:185
  7.3 10.0 %collective-permute-start.4 = (bf16[2,4,64,128]{3,2,1,0:T(8,128)(2,1)S(1)}, bf16[2,4,64,128]{3,2,1,0:T(8,128)(2,1)S(1)}, u32[]{:S(2)}, u32[]{:S(2)}) collective-permute-start(bf16[2,4,64,128]{3,2,1,0:T(8,128)(2,1)S(1)} %get-tuple-element.14.refs_7_), channel_id=1, source_target_pairs={{0,8},{4,12},{8,0},{12,4},{1,9},{5,13},{9,1},{13,5},{2,10},{6,14},... | collective-permute-start | bytes 393224 | tf_op jit(solution)/shard_map/ppermute | solution.py:182
  11.0 6.6 %collective-permute-start.3 = (bf16[2,4,64,128]{3,2,1,0:T(8,128)(2,1)S(1)}, bf16[2,4,64,128]{3,2,1,0:T(8,128)(2,1)S(1)}, u32[]{:S(2)}, u32[]{:S(2)}) collective-permute-start(bf16[2,4,64,128]{3,2,1,0:T(8,128)(2,1)S(1)} %get-tuple-element.14.refs_7_), channel_id=1, source_target_pairs={{0,12},{4,0},{8,4},{12,8},{1,13},{5,1},{9,5},{13,9},{2,14},{6,2},{... | collective-permute-start | bytes 393224 | tf_op jit(solution)/shard_map/ppermute | solution.py:182
  13.4 4.2 %copy-start = (s32[3]{0:T(128)S(1)}, s32[3]{0:T(128)}, u32[]{:S(2)}) copy-start(s32[3]{0:T(128)} %first_ref.1) | copy-start | bytes 40

commit v4 on v3

--- a/solution.py
+++ b/solution.py
@@ -13,6 +13,7 @@
 K_COPIES = 2
 Q_COPIES = 3
 LANES = 128
+CHUNK = 256
 MASKED = -1e30
 NT = (((1,), (1,)), ((), ()))
 
@@ -71,16 +72,17 @@
 
 def main_kernel(n_head, n_ctx, start_ref, first_ref, *refs):
     q_refs, k_refs = refs[:n_head], refs[n_head:n_head + n_ctx]
-    out_ref, keys, scores = refs[n_head + n_ctx:]
+    out_ref, keys, scores, pooled, lined = refs[n_head + n_ctx:]
     own, heads, tokens, depth = q_refs[0].shape
     local = k_refs[0].shape[2]
     nsel = local * n_ctx
     me = lax.axis_index("ctx")
-    step = scores.shape[0] // (n_head * heads)
     scale = math.log2(math.e) / math.sqrt(depth)
     factor = nsel / (2.0 * n_head * heads)
     least_position = 16 * 4 * nsel * 7 // 8 - n_ctx * tokens
     most_first = nsel - 1
+    chunks = n_head * heads * QTILE // CHUNK
+    per_chunk = n_head // chunks
 
     for j in range(n_ctx):
         source = lax.rem(me + 1 + j, n_ctx)
@@ -88,64 +90,73 @@
         keys[:, :, at, :] = k_refs[j][...]
 
     def tile(index, _):
-        begin = pl.multiple_of(index * step, step)
-        first = first_ref[begin // QTILE]
-        position = start_ref[0] + me * tokens + begin
+        begin = pl.multiple_of(index * QTILE, QTILE)
+        first = first_ref[index]
+        lane = lax.broadcasted_iota(jnp.int32, (8, LANES), 1)
+        row = lax.broadcasted_iota(jnp.int32, (8, LANES), 0)
+        place = start_ref[0] + me * tokens + begin + lane % QTILE
+
+        def visible(r, s):
+            i = 4 * (r + row) + s
+            mask = None
+            if 4 * r + s <= most_first:
+                mask = i >= first
+            if 16 * (4 * (r + 7) + s) + 31 > least_position:
+                below = 16 * i + 31 <= place
+                mask = below if mask is None else mask & below
+            return mask
+
         for g in range(own):
-            rows = jnp.concatenate(
-                [q[g, h, pl.ds(begin, step), :] for q in q_refs for h in range(heads)], axis=0
-            )
-            for s in range(4):
-                scores[:, s * nsel:(s + 1) * nsel] = lax.dot_general(
-                    rows, keys[g, s], NT, preferred_element_type=jnp.float32
+            weights = []
+            for c in range(chunks):
+                columns = jnp.concatenate(
+                    [q[g, h, pl.ds(begin, QTILE), :] for q in q_refs[c * per_chunk:(c + 1) * per_chunk] for h in range(heads)],
+                    axis=0,
                 )
-            for t in range(0, step, 8):
-                masks = []
-                place = position + t + lax.broadcasted_iota(jnp.int32, (8, LANES), 0)
+                tops = [None] * (CHUNK // LANES)
                 for s in range(4):
-                    for lane in range(0, nsel, LANES):
-                        i = 4 * (lane + lax.broadcasted_iota(jnp.int32, (8, LANES), 1)) + s
-                        mask = None
-                        if 4 * lane <= most_first:
-                            mask = i >= first
-                        if 16 * (4 * (lane + LANES - 1) + s) + 31 > least_position:
-                            below = 16 * i + 31 <= place
-                            mask = below if mask is None else mask & below
-                        masks.append(mask)
-                lead_sum, rest_sum = None, None
-                for h in range(n_head * heads):
-                    at = h * step + t
-                    pieces = []
-                    for n, mask in enumerate(masks):
-                        piece = scores[at:at + 8, n * LANES:(n + 1) * LANES]
-                        pieces.append(piece if mask is None else jnp.where(mask, piece, MASKED))
-                    top = pieces[0]
-                    for piece in pieces[1:]:
-                        top = jnp.maximum(top, piece)
-                    top = jnp.max(top, axis=1, keepdims=True)
-                    pieces = [jnp.exp2((piece - top) * scale) for piece in pieces]
-                    width = nsel // LANES
-                    lead = pieces[:width]
-                    rest = [pieces[n + width] + pieces[n + 2 * width] + pieces[n + 3 * width] for n in range(width)]
-                    total = lead[0] + rest[0]
-                    for n in range(1, width):
-                        total = total + (lead[n] + rest[n])
-                    inverse = 1.0 / jnp.sum(total, axis=1, keepdims=True)
-                    lead = [piece * inverse for piece in lead]
-                    rest = [piece * inverse for piece in rest]
-                    if lead_sum is None:
-                        lead_sum, rest_sum = lead, rest
-                    else:
-                        lead_sum = [a + b for a, b in zip(lead_sum, lead)]
-                        rest_sum = [a + b for a, b in zip(rest_sum, rest)]
-                lead = jnp.concatenate(lead_sum, axis=1)
-                weighted = lead + 2.0 * jnp.concatenate(rest_sum, axis=1)
-                column = lax.broadcasted_iota(jnp.int32, (8, nsel), 1)
-                shifted = jnp.where(column == 0, 0.0, pltpu.roll(weighted, 1, 1))
-                out_ref[pl.ds(begin + t, 8), g, :] = (lead + shifted) * factor
+                    piece = lax.dot_general(keys[g, s], columns, NT, preferred_element_type=jnp.float32)
+                    for r in range(0, nsel, 8):
+                        mask = visible(r, s)
+                        for n in range(CHUNK // LANES):
+                            part = piece[r:r + 8, n * LANES:(n + 1) * LANES]
+                            if mask is not None:
+                                part = jnp.where(mask, part, MASKED)
+                            scores[c, s, r:r + 8, n * LANES:(n + 1) * LANES] = part
+                            tops[n] = part if tops[n] is None else jnp.maximum(tops[n], part)
+                for n in range(CHUNK // LANES):
+                    total = None
+                    at = (c * CHUNK // LANES + n) * LANES
+                    for r in range(0, nsel, 8):
+                        parts = [
+                            jnp.exp2((scores[c, s, r:r + 8, n * LANES:(n + 1) * LANES] - tops[n]) * scale)
+                            for s in range(4)
+                        ]
+                        rest = parts[1] + parts[2] + parts[3]
+                        pooled[0, r:r + 8, at:at + LANES] = parts[0]
+                        pooled[1, r:r + 8, at:at + LANES] = rest
+                        both = parts[0] + rest
+                        total = both if total is None else total + both
+                    top = jnp.max(tops[n], axis=0, keepdims=True)
+                    lowered = jnp.exp2((tops[n] - top) * scale)
+                    weights.append(lowered * (factor / jnp.sum(total * lowered, axis=0, keepdims=True)))
+            for r in range(0, nsel, 8):
+                lead, rest = [
+                    sum(
+                        (pooled[p, r:r + 8, n * LANES:(n + 1) * LANES] * weights[n] for n in range(1, len(weights))),
+                        pooled[p, r:r + 8, 0:LANES] * weights[0],
+                    )
+                    for p in range(2)
+                ]
+                lined[0, 8 + r:16 + r, :] = lead
+                lined[1, 8 + r:16 + r, :] = lead + 2.0 * rest
+            lined[1, 0:8, :] = jnp.zeros((8, LANES), jnp.float32)
+            blocks = lined[0, 8:8 + nsel, :] + lined[1, 7:7 + nsel, :]
+            turned = blocks.T
+            out_ref[pl.ds(begin, QTILE), g, :] = turned[:QTILE] + turned[QTILE:]
         return 0
 
-    lax.fori_loop(0, tokens // step, tile, 0)
+    lax.fori_loop(0, tokens // QTILE, tile, 0)
 
 
 def in_hbm(array):
@@ -185,7 +196,7 @@
         q_parts[d] = lax.ppermute(q_parts[d], "head", [(i, i ^ d) for i in range(n_head)])
     for j in range(n_ctx - 1, 0, -1):
         send_keys(j)
-    step = min(QTILE, max(PACK, QTILE * 1024 // (4 * nsel)))
+    columns = n_head * heads * QTILE
     return pl.pallas_call(
         partial(main_kernel, n_head, n_ctx),
         out_shape=jax.ShapeDtypeStruct((tokens, own, nsel), jnp.float32),
@@ -193,9 +204,11 @@
         out_specs=vmem,
         scratch_shapes=[
             pltpu.VMEM((own, 4, nsel, depth), keys.dtype),
-            pltpu.VMEM((n_head * heads * step, 4 * nsel), jnp.float32),
+            pltpu.VMEM((columns // CHUNK, 4, nsel, CHUNK), jnp.float32),
+            pltpu.VMEM((2, nsel, columns), jnp.float32),
+            pltpu.VMEM((2, 8 + nsel, LANES), jnp.float32),
         ],
-        compiler_params=pltpu.CompilerParams(vmem_limit_bytes=32 * 2 ** 20),
+        compiler_params=pltpu.CompilerParams(vmem_limit_bytes=44 * 2 ** 20),
         name="importance",
     )(span_start, tile_first, *q_parts, *k_parts[::-1])
 

time: 23.8 us -> 24 us (level)
  no operation moved by 1% of the time
where the time goes in v4:
time: 24 us; the launch traced here: 23.8 us
  starting transfers between devices  9.27 us (39%)
  Pallas kernels  8.61 us (36%)
  waiting for transfers between devices  5.28 us (22%)
  between operations  0.69 us (3%)
    ppermute x3, starting transfers between devices, send_keys(): lax.ppermute(k_parts[0], 'ctx', [(i, (i + j) % n_ctx) for i in range(n_ct...  7.41 us
    pallas_call x1, Pallas kernels, per_device(): pl.pallas_call(partial(main_kernel, n_head, n_ctx), out_shape=jax.ShapeDt...  6.23 us
    ppermute x3, waiting for transfers between devices, send_keys(): lax.ppermute(k_parts[0], 'ctx', [(i, (i + j) % n_ctx) for i in range(n_ct...  5.27 us
    pallas_call x1, Pallas kernels, per_device(): pl.pallas_call(partial(pack_kernel, n_head, key_heads, heads), out_shape=...  2.37 us
    ppermute x3, starting transfers between devices, per_device(): lax.ppermute(q_parts[d], 'head', [(i, i ^ d) for i in range(n_head)])  1.86 us
  transfers between devices with their start and end apart: 6, of which 3 were waited for; matrix products, arithmetic and copies ran while one was open for 0% of the time, Pallas kernels for 0%

profile of v4, /device:TPU:0, one launch (start us, length us, event | category | flops | bytes accessed | tf_op | source)
XLA Modules:
  0.0 23.8 jit_solution(4470089480839372686)
XLA Ops:
  0.0 2.4 %pack.1 = (bf16[2,2,192,128]{3,2,1,0:T(8,128)(2,1)S(1)}, bf16[2,2,192,128]{3,2,1,0:T(8,128)(2,1)S(1)}, bf16[2,2,192,128]{3,2,1,0:T(8,128)(2,1)S(1)}, bf16[2,2,19...) custom-call(bf16[3072,128]{1,0:T(8,128)(2,1)} %bitcast.2, bf16[2048,128]{1,0:T(8,128)(2,1)} %bitcast.3), custom_call_target="tpu_custom_call" | custom-call | tf_op jit(solution)/shard_map/pack/pallas_call | solution.py:176
  2.4 3.1 %collective-permute-start.5 = (bf16[2,4,64,128]{3,2,1,0:T(8,128)(2,1)S(1)}, bf16[2,4,64,128]{3,2,1,0:T(8,128)(2,1)S(1)}, u32[]{:S(2)}, u32[]{:S(2)}) collective-permute-start(bf16[2,4,64,128]{3,2,1,0:T(8,128)(2,1)S(1)} %get-tuple-element.14.refs_7_), channel_id=1, source_target_pairs={{0,4},{4,8},{8,12},{12,0},{1,5},{5,9},{9,13},{13,1},{2,6},{6,10},{... | collective-permute-start | bytes 393224 | tf_op jit(solution)/shard_map/ppermute | solution.py:193
  5.5 0.0 collective-permute-start
  5.5 1.5 %collective-permute-start.1 = (bf16[2,2,192,128]{3,2,1,0:T(8,128)(2,1)S(1)}, bf16[2,2,192,128]{3,2,1,0:T(8,128)(2,1)S(1)}, u32[]{:S(2)}, u32[]{:S(2)}) collective-permute-start(bf16[2,2,192,128]{3,2,1,0:T(8,128)(2,1)S(1)} %get-tuple-element.12), channel_id=1, source_target_pairs={{0,2},{1,3},{2,0},{3,1},{4,6},{5,7},{6,4},{7,5},{8,10},{9,11},{10,... | collective-permute-start | bytes 589832 | tf_op jit(solution)/shard_map/ppermute | solution.py:196
  7.0 0.4 %collective-permute-start.2 = (bf16[2,2,192,128]{3,2,1,0:T(8,128)(2,1)S(1)}, bf16[2,2,192,128]{3,2,1,0:T(8,128)(2,1)S(1)}, u32[]{:S(2)}, u32[]{:S(2)}) collective-permute-start(bf16[2,2,192,128]{3,2,1,0:T(8,128)(2,1)S(1)} %get-tuple-element.13), channel_id=1, source_target_pairs={{0,3},{1,2},{2,1},{3,0},{4,7},{5,6},{6,5},{7,4},{8,11},{9,10},{10,... | collective-permute-start | bytes 589832 | tf_op jit(solution)/shard_map/ppermute | solution.py:196
  7.3 2.6 %collective-permute-start.4 = (bf16[2,4,64,128]{3,2,1,0:T(8,128)(2,1)S(1)}, bf16[2,4,64,128]{3,2,1,0:T(8,128)(2,1)S(1)}, u32[]{:S(2)}, u32[]{:S(2)}) collective-permute-start(bf16[2,4,64,128]{3,2,1,0:T(8,128)(2,1)S(1)} %get-tuple-element.14.refs_7_), channel_id=1, source_target_pairs={{0,8},{4,12},{8,0},{12,4},{1,9},{5,13},{9,1},{13,5},{2,10},{6,14},... | collective-permute-start | bytes 393224 | tf_op jit(solution)/shard_map/ppermute | solution.py:193
  9.9 1.1 %collective-permute-done.5.refs_6_ = bf16[2,4,64,128]{3,2,1,0:T(8,128)(2,1)S(1)} collective-permute-done((bf16[2,4,64,128]{3,2,1,0:T(8,128)(2,1)S(1)}, bf16[2,4,64,128]{3,2,1,0:T(8,128)(2,1)S(1)}, u32[]{:S(2)}, u32[]{:S(2)}) %collective-permute-start.5) | collective-permute-done | bytes 131104 | tf_op jit(solution)/shard_map/ppermute | solution.py:193
  11.0 1.7 %collective-permute-start.3 = (bf16[2,4,64,128]{3,2,1,0:T(8,128)(2,1)S(1)}, bf16[2,4,64,128]{3,2,1,0:T(8,128)(2,1)S(1)}, u32[]{:S(2)}, u32[]{:S(2)}) collective-permute-start(bf16[2,4,64,128]{3,2,1,0:T(8,128)(2,1)S(1)} %get-tuple-element.14.refs_7_), channel_id=1, source_target_pairs={{0,12},{4,0},{8,4},{12,8},{1,13},{5,1},{9,5},{13,9},{2,14},{6,2},{... | collective-permute-start | bytes 393224 | tf_op jit(solution)/shard_map/ppermute | solution.py:193
  13.4 0.0 copy-start
  13.4 4.0 %collective-permute-done.4.refs_5_ = bf16[2,4,64,128]{3,2,1,0:T(8,128)(2,1)S(1)} collective-permute-done((bf16[2,4,64,128]{3,2,1,0:T(8,128)(2,1)S(1)}, bf16[2,4,64,128]{3,2,1,0:T(8,128)(2,1)S(1)}, u32[]{:S(2)}, u32[]{:S(2)}) %collective-permute-start.4) | collective-permute-done | bytes 131104 | tf_op jit(solution)/shard_map/ppermute | solution.py:193
  17.4 0.2 collective-permute-done.3.refs_4_
  17.6 0.0 collective-permute-done.refs_1_
  17.6 0.0 collective-permute-done.1.refs_2_
  17.6 0.0 collective-permute-done.2.refs_3_
  17.6 0.0 copy-done
  17.6 6.2 %importance.1 = f32[192,2,256]{2,1,0:T(2,128)} custom-call(s32[1]{0:T(128)S(6)} %copy.5.start_ref, s32[3]{0:T(128)S(1)} %copy-done, bf16[2,2,192,128]{3,2,1,0:T(8,128)(2,1)S(1)} %get-tuple-element.10.refs_0_, bf16[2,2,192,128]{3,2,1,0:T(8,128)(2,1)S(1)} %collective-permute-done.refs_1_, bf16[2,2,192,128]{3,2,1,0:T(8,128)(2,1)S(1)} %collective-permute-done.1.refs_2_, ...), custom_call_target="tpu_custom_call" | custom-call | tf_op jit(solution)/shard_map/importance/pallas_call | solution.py:200
Async XLA Ops:
  2.4 8.6 %collective-permute-start.5 = (bf16[2,4,64,128]{3,2,1,0:T(8,128)(2,1)S(1)}, bf16[2,4,64,128]{3,2,1,0:T(8,128)(2,1)S(1)}, u32[]{:S(2)}, u32[]{:S(2)}) collective-permute-start(bf16[2,4,64,128]{3,2,1,0:T(8,128)(2,1)S(1)} %get-tuple-element.14.refs_7_), channel_id=1, source_target_pairs={{0,4},{4,8},{8,12},{12,0},{1,5},{5,9},{9,13},{13,1},{2,6},{6,10},{... | collective-permute-start | bytes 393224 | tf_op jit(solution)/shard_map/ppermute | solution.py:193
  5.5 12.1 %collective-permute-start = (bf16[2,2,192,128]{3,2,1,0:T(8,128)(2,1)S(1)}, bf16[2,2,192,128]{3,2,1,0:T(8,128)(2,1)S(1)}, u32[]{:S(2)}, u32[]{:S(2)}) collective-permute-start(bf16[2,2,192,128]{3,2,1,0:T(8,128)(2,1)S(1)} %get-tuple-element.11), channel_id=1, source_target_pairs={{0,1},{1,0},{2,3},{3,2},{4,5},{5,4},{6,7},{7,6},{8,9},{9,8},{10,11... | collective-permute-start | bytes 589832 | tf_op jit(solution)/shard_map/ppermute | solution.py:196
  5.5 12.1 %collective-permute-start.1 = (bf16[2,2,192,128]{3,2,1,0:T(8,128)(2,1)S(1)}, bf16[2,2,192,128]{3,2,1,0:T(8,128)(2,1)S(1)}, u32[]{:S(2)}, u32[]{:S(2)}) collective-permute-start(bf16[2,2,192,128]{3,2,1,0:T(8,128)(2,1)S(1)} %get-tuple-element.12), channel_id=1, source_target_pairs={{0,2},{1,3},{2,0},{3,1},{4,6},{5,7},{6,4},{7,5},{8,10},{9,11},{10,... | collective-permute-start | bytes 589832 | tf_op jit(solution)/shard_map/ppermute | solution.py:196
  7.0 10.6 %collective-permute-start.2 = (bf16[2,2,192,128]{3,2,1,0:T(8,128)(2,1)S(1)}, bf16[2,2,192,128]{3,2,1,0:T(8,128)(2,1)S(1)}, u32[]{:S(2)}, u32[]{:S(2)}) collective-permute-start(bf16[2,2,192,128]{3,2,1,0:T(8,128)(2,1)S(1)} %get-tuple-element.13), channel_id=1, source_target_pairs={{0,3},{1,2},{2,1},{3,0},{4,7},{5,6},{6,5},{7,4},{8,11},{9,10},{10,... | collective-permute-start | bytes 589832 | tf_op jit(solution)/shard_map/ppermute | solution.py:196
  7.3 10.0 %collective-permute-start.4 = (bf16[2,4,64,128]{3,2,1,0:T(8,128)(2,1)S(1)}, bf16[2,4,64,128]{3,2,1,0:T(8,128)(2,1)S(1)}, u32[]{:S(2)}, u32[]{:S(2)}) collective-permute-start(bf16[2,4,64,128]{3,2,1,0:T(8,128)(2,1)S(1)} %get-tuple-element.14.refs_7_), channel_id=1, source_target_pairs={{0,8},{4,12},{8,0},{12,4},{1,9},{5,13},{9,1},{13,5},{2,10},{6,14},... | collective-permute-start | bytes 393224 | tf_op jit(solution)/shard_map/ppermute | solution.py:193
  11.0 6.6 %collective-permute-start.3 = (bf16[2,4,64,128]{3,2,1,0:T(8,128)(2,1)S(1)}, bf16[2,4,64,128]{3,2,1,0:T(8,128)(2,1)S(1)}, u32[]{:S(2)}, u32[]{:S(2)}) collective-permute-start(bf16[2,4,64,128]{3,2,1,0:T(8,128)(2,1)S(1)} %get-tuple-element.14.refs_7_), channel_id=1, source_target_pairs={{0,12},{4,0},{8,4},{12,8},{1,13},{5,1},{9,5},{13,9},{2,14},{6,2},{... | collective-permute-start | bytes 393224 | tf_op jit(solution)/shard_map/ppermute | solution.py:193
  13.4 4.2 %copy-start = (s32[3]{0:T(128)S(1)}, s32[3]{0:T(128)}, u32[]{:S(2)}) copy-start(s32[3]{0:T(128)} %first_ref.1) | copy-start | bytes 40

commit v5 on v4

v5 whole, which is shorter than its diff:
```python
import math
from functools import partial

import jax
import jax.numpy as jnp
from jax import lax
from jax.experimental import pallas as pl
from jax.experimental.pallas import tpu as pltpu
from jax.sharding import PartitionSpec as P

QTILE = 64
PACK = 16
LANES = 128
CHUNK = 256
MASKED = -1e30
NT = (((1,), (1,)), ((), ()))


def pack_keys_kernel(n_head, key_heads, k_hbm, k_out, k_ref, sem):
    copy = pltpu.make_async_copy(k_hbm, k_ref, sem)
    copy.start()
    me = lax.axis_index("head")
    own = key_heads // n_head
    blocks = k_out.shape[2]
    rows = PACK * 4 * key_heads
    out_row = lax.broadcasted_iota(jnp.int32, (own * 4 * PACK, rows), 0)
    in_row = lax.broadcasted_iota(jnp.int32, (own * 4 * PACK, rows), 1)
    head = out_row // (4 * PACK)
    part = out_row // PACK % 4
    source = out_row % PACK * (4 * key_heads) + part * key_heads + me * own + head
    select = jnp.where(in_row == source, 1.0, 0.0).astype(jnp.bfloat16)
    copy.wait()
    for block in range(blocks // PACK):
        moved = jnp.dot(
            select, k_ref[block * rows:(block + 1) * rows, :], preferred_element_type=jnp.float32
        ).astype(jnp.bfloat16)
        for u in range(own * 4):
            k_out[u // 4, u % 4, block * PACK:(block + 1) * PACK, :] = moved[u * PACK:(u + 1) * PACK]


def pack_queries_kernel(n_head, key_heads, heads, q_ref, *q_outs):
    me = lax.axis_index("head")
    width = key_heads // n_head * heads
    tokens = q_outs[0].shape[2]
    rows = PACK * key_heads * heads
    out_row = lax.broadcasted_iota(jnp.int32, (n_head * width * PACK, rows), 0)
    in_row = lax.broadcasted_iota(jnp.int32, (n_head * width * PACK, rows), 1)
    step = out_row // (width * PACK)
    unit = out_row // PACK % width
    source = out_row % PACK * (key_heads * heads) + (step ^ me) * width + unit
    select = jnp.where(in_row == source, 1.0, 0.0).astype(jnp.bfloat16)
    for block in range(tokens // PACK):
        moved = jnp.dot(
            select, q_ref[block * rows:(block + 1) * rows, :], preferred_element_type=jnp.float32
        ).astype(jnp.bfloat16)
        for u in range(n_head * width):
            d, g, h = u // width, u % width // heads, u % heads
            q_outs[d][g, h, block * PACK:(block + 1) * PACK, :] = moved[u * PACK:(u + 1) * PACK]


def main_kernel(n_head, n_ctx, start_ref, first_ref, *refs):
    q_refs, k_refs = refs[:n_head], refs[n_head:n_head + n_ctx]
    out_ref, keys, scores, pooled, lined = refs[n_head + n_ctx:]
    own, heads, tokens, depth = q_refs[0].shape
    local = k_refs[0].shape[2]
    nsel = local * n_ctx
    me = lax.axis_index("ctx")
    scale = math.log2(math.e) / math.sqrt(depth)
    factor = nsel / (2.0 * n_head * heads)
    least_position = 16 * 4 * nsel * 7 // 8 - n_ctx * tokens
    most_first = nsel - 1
    chunks = n_head * heads * QTILE // CHUNK
    per_chunk = n_head // chunks

    span = min(nsel, 256)
    spans = nsel // span

    def over_spans(body, carry):
        if spans == 1:
            return body(0, carry)
        return lax.fori_loop(0, spans, lambda n, c: body(pl.multiple_of(n * span, span), c), carry)

    for j in range(n_ctx):
        at = pl.ds(pl.multiple_of((me ^ j ^ (j >> 1)) * local, local), local)
        keys[:, :, at, :] = k_refs[j][...]

    def tile(index, _):
        begin = pl.multiple_of(index * QTILE, QTILE)
        first = first_ref[index]
        lane = lax.broadcasted_iota(jnp.int32, (8, LANES), 1)
        row = lax.broadcasted_iota(jnp.int32, (8, LANES), 0)
        place = start_ref[0] + me * tokens + begin + lane % QTILE

        def visible(base, r, s):
            i = 4 * (base + r + row) + s
            mask = None
            if spans > 1 or 4 * r + s <= most_first:
                mask = i >= first
            if spans > 1 or 16 * (4 * (r + 7) + s) + 31 > least_position:
                below = 16 * i + 31 <= place
                mask = below if mask is None else mask & below
            return mask

        for g in range(own):
            weights = []
            for c in range(chunks):
                columns = jnp.concatenate(
                    [q[g, h, pl.ds(begin, QTILE), :] for q in q_refs[c * per_chunk:(c + 1) * per_chunk] for h in range(heads)],
                    axis=0,
                )

                def scores_span(base, tops):
                    tops = list(tops)
                    rows = jnp.concatenate([keys[g, s, pl.ds(base, span), :] for s in range(4)], axis=0)
                    piece = lax.dot_general(rows, columns, NT, preferred_element_type=jnp.float32)
                    for s in range(4):
                        for r in range(0, span, 8):
                            mask = visible(base, r, s)
                            for n in range(CHUNK // LANES):
                                part = piece[s * span + r:s * span + r + 8, n * LANES:(n + 1) * LANES]
                                if mask is not None:
                                    part = jnp.where(mask, part, MASKED)
                                scores[c, s, pl.ds(base + r, 8), n * LANES:(n + 1) * LANES] = part
                                tops[n] = jnp.maximum(tops[n], part)
                    return tuple(tops)

                tops = over_spans(scores_span, (jnp.full((8, LANES), MASKED, jnp.float32),) * (CHUNK // LANES))
                for n in range(CHUNK // LANES):
                    at = (c * CHUNK // LANES + n) * LANES

                    def exps_span(base, total):
                        for r in range(0, span, 8):
                            here = pl.ds(base + r, 8)
                            parts = [
                                jnp.exp2((scores[c, s, here, n * LANES:(n + 1) * LANES] - tops[n]) * scale)
                                for s in range(4)
                            ]
                            rest = parts[1] + parts[2] + parts[3]
                            pooled[0, here, at:at + LANES] = parts[0]
                            pooled[1, here, at:at + LANES] = rest
                            total = total + (parts[0] + rest)
                        return total

                    total = over_spans(exps_span, jnp.zeros((8, LANES), jnp.float32))
                    top = jnp.max(tops[n], axis=0, keepdims=True)
                    lowered = jnp.exp2((tops[n] - top) * scale)
                    weights.append(lowered * (factor / jnp.sum(total * lowered, axis=0, keepdims=True)))

            def sums_span(base, _):
                for r in range(0, span, 8):
                    lead, rest = [
                        sum(
                            (pooled[p, pl.ds(base + r, 8), n * LANES:(n + 1) * LANES] * weights[n] for n in range(1, len(weights))),
                            pooled[p, pl.ds(base + r, 8), 0:LANES] * weights[0],
                        )
                        for p in range(2)
                    ]
                    lined[0, pl.ds(base + 8 + r, 8), :] = lead
                    lined[1, pl.ds(base + 8 + r, 8), :] = lead + 2.0 * rest
                return 0

            lined[1, 0:8, :] = jnp.zeros((8, LANES), jnp.float32)
            over_spans(sums_span, 0)
            blocks = lined[0, 8:8 + nsel, :] + lined[1, 7:7 + nsel, :]
            turned = blocks.T
            out_ref[pl.ds(begin, QTILE), g, :] = turned[:QTILE] + turned[QTILE:]
        return 0

    lax.fori_loop(0, tokens // QTILE, tile, 0)


def in_hbm(array):
    return pltpu.with_memory_space_constraint(array, pltpu.HBM)


def per_device(n_head, n_ctx, queries, keys, span_start, tile_first):
    tokens, key_heads, heads, depth = queries.shape
    blocks = keys.shape[0]
    own = key_heads // n_head
    nsel = blocks * n_ctx
    vmem = pl.BlockSpec(memory_space=pltpu.VMEM)
    smem = pl.BlockSpec(memory_space=pltpu.SMEM)
    hbm = pl.BlockSpec(memory_space=pltpu.HBM)
    q_part = jax.ShapeDtypeStruct((own, heads, tokens, depth), queries.dtype)
    k_part = jax.ShapeDtypeStruct((own, 4, blocks, depth), keys.dtype)
    k_own = pl.pallas_call(
        partial(pack_keys_kernel, n_head, key_heads),
        out_shape=k_part,
        in_specs=[hbm],
        out_specs=vmem,
        scratch_shapes=[pltpu.VMEM((blocks * 4 * key_heads, depth), keys.dtype), pltpu.SemaphoreType.DMA],
        compiler_params=pltpu.CompilerParams(vmem_limit_bytes=16 * 2 ** 20),
        name="pack_keys",
    )(in_hbm(keys.reshape(-1, depth)))
    q_parts = pl.pallas_call(
        partial(pack_queries_kernel, n_head, key_heads, heads),
        out_shape=[q_part] * n_head,
        in_specs=[vmem],
        out_specs=[vmem] * n_head,
        compiler_params=pltpu.CompilerParams(vmem_limit_bytes=16 * 2 ** 20),
        name="pack_queries",
    )(queries.reshape(-1, depth))
    q_parts, k_parts = list(q_parts), [k_own]
    for d in range(1, n_head):
        q_parts[d] = lax.ppermute(q_parts[d], "head", [(i, i ^ d) for i in range(n_head)])
    for j in range(1, n_ctx):
        k_parts.append(lax.ppermute(k_own, "ctx", [(i, i ^ j ^ (j >> 1)) for i in range(n_ctx)]))
    columns = n_head * heads * QTILE
    return pl.pallas_call(
        partial(main_kernel, n_head, n_ctx),
        out_shape=jax.ShapeDtypeStruct((tokens, own, nsel), jnp.float32),
        in_specs=[smem, smem] + [vmem] * (n_head + n_ctx),
        out_specs=vmem,
        scratch_shapes=[
            pltpu.VMEM((own, 4, nsel, depth), keys.dtype),
            pltpu.VMEM((columns // CHUNK, 4, nsel, CHUNK), jnp.float32),
            pltpu.VMEM((2, nsel, columns), jnp.float32),
            pltpu.VMEM((2, 8 + nsel, LANES), jnp.float32),
        ],
        compiler_params=pltpu.CompilerParams(vmem_limit_bytes=44 * 2 ** 20),
        name="importance",
    )(span_start, tile_first, *q_parts, *k_parts)


def solution(mesh):
    placed = (
        P(("groups", "ctx"), None, "head", None),
        P(("groups", "ctx"), None, None, None),
        P("groups"),
        P(("groups", "ctx")),
    )
    return jax.shard_map(
        partial(per_device, mesh.shape["head"], mesh.shape["ctx"]),
        mesh=mesh,
        in_specs=placed,
        out_specs=P(("groups", "ctx"), "head", None),
        check_vma=False,
    )
```

time: 24 us -> 25.6 us (1.067)
  waiting for transfers between devices: 5.28 us -> 7.34 us
  local copies, waits for them, and re-layouts: 0.01 us -> 1.14 us
  starting transfers between devices: 9.27 us -> 8.2 us
  Pallas kernels: 8.61 us -> 7.97 us
    ppermute x3, waiting for transfers between devices: 5.27 us -> 7.33 us  [per_device(): lax.ppermute(k_own, 'ctx', [(i, i ^ j ^ j >> 1) for i in range(n_ctx)])]
    ppermute x3, starting transfers between devices: 7.41 us -> 6.26 us  [per_device(): lax.ppermute(k_own, 'ctx', [(i, i ^ j ^ j >> 1) for i in range(n_ctx)])]
    unnamed x2 -> x4, local copies, waits for them, and re-layouts: 0.01 us -> 1.14 us
    pallas_call x1 -> x2, Pallas kernels: 2.37 us -> 1.9 us  [the longest x1 1.34 us: per_device(): pl.pallas_call(partial(pack_keys_kernel, n_head, key_heads), out_shape=k_...]
  transfers between devices with their start and end apart: 6 -> 6, of which waited for: 3 -> 3; matrix products, arithmetic and copies ran while one was open for 0% -> 0% of each run, Pallas kernels for 0% -> 2%
where the time goes in v5:
time: 25.6 us; the launch traced here: 25.3 us
  starting transfers between devices  8.2 us (32%)
  Pallas kernels  7.97 us (31%)
  waiting for transfers between devices  7.34 us (29%)
  local copies, waits for them, and re-layouts  1.14 us (4%)
  between operations  0.7 us (3%)
    ppermute x3, waiting for transfers between devices, per_device(): lax.ppermute(k_own, 'ctx', [(i, i ^ j ^ j >> 1) for i in range(n_ctx)])  7.33 us
    ppermute x3, starting transfers between devices, per_device(): lax.ppermute(k_own, 'ctx', [(i, i ^ j ^ j >> 1) for i in range(n_ctx)])  6.26 us
    pallas_call x1, Pallas kernels, per_device(): pl.pallas_call(partial(main_kernel, n_head, n_ctx), out_shape=jax.ShapeDt...  6.08 us
    ppermute x3, starting transfers between devices, per_device(): lax.ppermute(q_parts[d], 'head', [(i, i ^ d) for i in range(n_head)])  1.93 us
    pallas_call x1, Pallas kernels, per_device(): pl.pallas_call(partial(pack_keys_kernel, n_head, key_heads), out_shape=k_...  1.34 us
    unnamed x4, local copies, waits for them, and re-layouts  1.14 us
    pallas_call x1, Pallas kernels, per_device(): pl.pallas_call(partial(pack_queries_kernel, n_head, key_heads, heads), ou...  0.56 us
  transfers between devices with their start and end apart: 6, of which 3 were waited for; matrix products, arithmetic and copies ran while one was open for 0% of the time, Pallas kernels for 2%

profile of v5, /device:TPU:0, one launch (start us, length us, event | category | flops | bytes accessed | tf_op | source)
XLA Modules:
  0.0 25.3 jit_solution(5975558104295686814)
XLA Ops:
  0.0 1.3 %pack_keys.1.refs_4_ = bf16[2,4,64,128]{3,2,1,0:T(8,128)(2,1)S(1)} custom-call(bf16[2048,128]{1,0:T(8,128)(2,1)} %bitcast.3), custom_call_target="tpu_custom_call" | custom-call | tf_op jit(solution)/shard_map/pack_keys/pallas_call | solution.py:186
  1.3 4.1 %collective-permute-start.5 = (bf16[2,4,64,128]{3,2,1,0:T(8,128)(2,1)S(1)}, bf16[2,4,64,128]{3,2,1,0:T(8,128)(2,1)S(1)}, u32[]{:S(2)}, u32[]{:S(2)}) collective-permute-start(bf16[2,4,64,128]{3,2,1,0:T(8,128)(2,1)S(1)} %pack_keys.1.refs_4_), channel_id=1, source_target_pairs={{0,8},{4,12},{8,0},{12,4},{1,9},{5,13},{9,1},{13,5},{2,10},{6,14},... | collective-permute-start | bytes 393224 | tf_op jit(solution)/shard_map/ppermute | solution.py:207
  5.4 0.0 copy-start
  5.5 1.1 %copy-done = bf16[192,8,2,128]{3,2,1,0:T(2,128)(2,1)S(1)} copy-done((bf16[192,8,2,128]{3,2,1,0:T(2,128)(2,1)S(1)}, bf16[192,8,2,128]{3,2,1,0:T(2,128)(2,1)}, u32[]{:S(2)}) %copy-start) | copy-done | bytes 786456
  6.6 0.6 %pack_queries.1 = (bf16[2,2,192,128]{3,2,1,0:T(8,128)(2,1)S(1)}, bf16[2,2,192,128]{3,2,1,0:T(8,128)(2,1)S(1)}, bf16[2,2,192,128]{3,2,1,0:T(8,128)(2,1)S(1)}, bf16[2,2,192,128]{3,2,1,0:T(8,128)(2,1)S(1)}) custom-call(bf16[3072,128]{1,0:T(8,128)(2,1)S(1)} %bitcast.2), custom_call_target="tpu_custom_call" | custom-call | tf_op jit(solution)/shard_map/pack_queries/pallas_call | solution.py:195
  7.1 0.1 collective-permute-start
  7.2 1.6 %collective-permute-start.1 = (bf16[2,2,192,128]{3,2,1,0:T(8,128)(2,1)S(1)}, bf16[2,2,192,128]{3,2,1,0:T(8,128)(2,1)S(1)}, u32[]{:S(2)}, u32[]{:S(2)}) collective-permute-start(bf16[2,2,192,128]{3,2,1,0:T(8,128)(2,1)S(1)} %get-tuple-element.11), channel_id=1, source_target_pairs={{0,2},{1,3},{2,0},{3,1},{4,6},{5,7},{6,4},{7,5},{8,10},{9,11},{10,... | collective-permute-start | bytes 589832 | tf_op jit(solution)/shard_map/ppermute | solution.py:205
  8.8 0.3 %collective-permute-start.2 = (bf16[2,2,192,128]{3,2,1,0:T(8,128)(2,1)S(1)}, bf16[2,2,192,128]{3,2,1,0:T(8,128)(2,1)S(1)}, u32[]{:S(2)}, u32[]{:S(2)}) collective-permute-start(bf16[2,2,192,128]{3,2,1,0:T(8,128)(2,1)S(1)} %get-tuple-element.12), channel_id=1, source_target_pairs={{0,3},{1,2},{2,1},{3,0},{4,7},{5,6},{6,5},{7,4},{8,11},{9,10},{10,... | collective-permute-start | bytes 589832 | tf_op jit(solution)/shard_map/ppermute | solution.py:205
  9.1 1.3 %collective-permute-start.4 = (bf16[2,4,64,128]{3,2,1,0:T(8,128)(2,1)S(1)}, bf16[2,4,64,128]{3,2,1,0:T(8,128)(2,1)S(1)}, u32[]{:S(2)}, u32[]{:S(2)}) collective-permute-start(bf16[2,4,64,128]{3,2,1,0:T(8,128)(2,1)S(1)} %pack_keys.1.refs_4_), channel_id=1, source_target_pairs={{0,12},{4,8},{8,4},{12,0},{1,13},{5,9},{9,5},{13,1},{2,14},{6,10},... | collective-permute-start | bytes 393224 | tf_op jit(solution)/shard_map/ppermute | solution.py:207
  10.4 1.3 %collective-permute-done.5.refs_7_ = bf16[2,4,64,128]{3,2,1,0:T(8,128)(2,1)S(1)} collective-permute-done((bf16[2,4,64,128]{3,2,1,0:T(8,128)(2,1)S(1)}, bf16[2,4,64,128]{3,2,1,0:T(8,128)(2,1)S(1)}, u32[]{:S(2)}, u32[]{:S(2)}) %collective-permute-start.5) | collective-permute-done | bytes 131104 | tf_op jit(solution)/shard_map/ppermute | solution.py:207
  11.8 0.8 %collective-permute-start.3 = (bf16[2,4,64,128]{3,2,1,0:T(8,128)(2,1)S(1)}, bf16[2,4,64,128]{3,2,1,0:T(8,128)(2,1)S(1)}, u32[]{:S(2)}, u32[]{:S(2)}) collective-permute-start(bf16[2,4,64,128]{3,2,1,0:T(8,128)(2,1)S(1)} %pack_keys.1.refs_4_), channel_id=1, source_target_pairs={{0,4},{4,0},{8,12},{12,8},{1,5},{5,1},{9,13},{13,9},{2,6},{6,2},{1... | collective-permute-start | bytes 393224 | tf_op jit(solution)/shard_map/ppermute | solution.py:207
  13.2 0.0 copy-start.1
  13.2 3.9 %collective-permute-done.4.refs_6_ = bf16[2,4,64,128]{3,2,1,0:T(8,128)(2,1)S(1)} collective-permute-done((bf16[2,4,64,128]{3,2,1,0:T(8,128)(2,1)S(1)}, bf16[2,4,64,128]{3,2,1,0:T(8,128)(2,1)S(1)}, u32[]{:S(2)}, u32[]{:S(2)}) %collective-permute-start.4) | collective-permute-done | bytes 131104 | tf_op jit(solution)/shard_map/ppermute | solution.py:207
  17.1 2.1 %collective-permute-done.3.refs_5_ = bf16[2,4,64,128]{3,2,1,0:T(8,128)(2,1)S(1)} collective-permute-done((bf16[2,4,64,128]{3,2,1,0:T(8,128)(2,1)S(1)}, bf16[2,4,64,128]{3,2,1,0:T(8,128)(2,1)S(1)}, u32[]{:S(2)}, u32[]{:S(2)}) %collective-permute-start.3) | collective-permute-done | bytes 131104 | tf_op jit(solution)/shard_map/ppermute | solution.py:207
  19.2 0.0 collective-permute-done.refs_1_
  19.3 0.0 collective-permute-done.1.refs_2_
  19.3 0.0 collective-permute-done.2.refs_3_
  19.3 0.0 copy-done.1
  19.3 6.1 %importance.1 = f32[192,2,256]{2,1,0:T(2,128)} custom-call(s32[1]{0:T(128)S(6)} %copy.5.start_ref, s32[3]{0:T(128)S(1)} %copy-done.1, bf16[2,2,192,128]{3,2,1,0:T(8,128)(2,1)S(1)} %get-tuple-element.9.refs_0_, bf16[2,2,192,128]{3,2,1,0:T(8,128)(2,1)S(1)} %collective-permute-done.refs_1_, bf16[2,2,192,128]{3,2,1,0:T(8,128)(2,1)S(1)} %collective-permute-done.1.refs_2_, ...), custom_call_target="tpu_custom_call" | custom-call | tf_op jit(solution)/shard_map/importance/pallas_call | solution.py:209
Async XLA Ops:
  1.3 10.4 %collective-permute-start.5 = (bf16[2,4,64,128]{3,2,1,0:T(8,128)(2,1)S(1)}, bf16[2,4,64,128]{3,2,1,0:T(8,128)(2,1)S(1)}, u32[]{:S(2)}, u32[]{:S(2)}) collective-permute-start(bf16[2,4,64,128]{3,2,1,0:T(8,128)(2,1)S(1)} %pack_keys.1.refs_4_), channel_id=1, source_target_pairs={{0,8},{4,12},{8,0},{12,4},{1,9},{5,13},{9,1},{13,5},{2,10},{6,14},... | collective-permute-start | bytes 393224 | tf_op jit(solution)/shard_map/ppermute | solution.py:207
  5.4 1.1 %copy-start = (bf16[192,8,2,128]{3,2,1,0:T(2,128)(2,1)S(1)}, bf16[192,8,2,128]{3,2,1,0:T(2,128)(2,1)}, u32[]{:S(2)}) copy-start(bf16[192,8,2,128]{3,2,1,0:T(2,128)(2,1)} %param.4) | copy-start | bytes 2359300
  7.1 12.1 %collective-permute-start = (bf16[2,2,192,128]{3,2,1,0:T(8,128)(2,1)S(1)}, bf16[2,2,192,128]{3,2,1,0:T(8,128)(2,1)S(1)}, u32[]{:S(2)}, u32[]{:S(2)}) collective-permute-start(bf16[2,2,192,128]{3,2,1,0:T(8,128)(2,1)S(1)} %get-tuple-element.10), channel_id=1, source_target_pairs={{0,1},{1,0},{2,3},{3,2},{4,5},{5,4},{6,7},{7,6},{8,9},{9,8},{10,11... | collective-permute-start | bytes 589832 | tf_op jit(solution)/shard_map/ppermute | solution.py:205
  7.2 12.0 %collective-permute-start.1 = (bf16[2,2,192,128]{3,2,1,0:T(8,128)(2,1)S(1)}, bf16[2,2,192,128]{3,2,1,0:T(8,128)(2,1)S(1)}, u32[]{:S(2)}, u32[]{:S(2)}) collective-permute-start(bf16[2,2,192,128]{3,2,1,0:T(8,128)(2,1)S(1)} %get-tuple-element.11), channel_id=1, source_target_pairs={{0,2},{1,3},{2,0},{3,1},{4,6},{5,7},{6,4},{7,5},{8,10},{9,11},{10,... | collective-permute-start | bytes 589832 | tf_op jit(solution)/shard_map/ppermute | solution.py:205
  8.8 10.5 %collective-permute-start.2 = (bf16[2,2,192,128]{3,2,1,0:T(8,128)(2,1)S(1)}, bf16[2,2,192,128]{3,2,1,0:T(8,128)(2,1)S(1)}, u32[]{:S(2)}, u32[]{:S(2)}) collective-permute-start(bf16[2,2,192,128]{3,2,1,0:T(8,128)(2,1)S(1)} %get-tuple-element.12), channel_id=1, source_target_pairs={{0,3},{1,2},{2,1},{3,0},{4,7},{5,6},{6,5},{7,4},{8,11},{9,10},{10,... | collective-permute-start | bytes 589832 | tf_op jit(solution)/shard_map/ppermute | solution.py:205
  9.1 8.0 %collective-permute-start.4 = (bf16[2,4,64,128]{3,2,1,0:T(8,128)(2,1)S(1)}, bf16[2,4,64,128]{3,2,1,0:T(8,128)(2,1)S(1)}, u32[]{:S(2)}, u32[]{:S(2)}) collective-permute-start(bf16[2,4,64,128]{3,2,1,0:T(8,128)(2,1)S(1)} %pack_keys.1.refs_4_), channel_id=1, source_target_pairs={{0,12},{4,8},{8,4},{12,0},{1,13},{5,9},{9,5},{13,1},{2,14},{6,10},... | collective-permute-start | bytes 393224 | tf_op jit(solution)/shard_map/ppermute | solution.py:207
  11.8 7.5 %collective-permute-start.3 = (bf16[2,4,64,128]{3,2,1,0:T(8,128)(2,1)S(1)}, bf16[2,4,64,128]{3,2,1,0:T(8,128)(2,1)S(1)}, u32[]{:S(2)}, u32[]{:S(2)}) collective-permute-start(bf16[2,4,64,128]{3,2,1,0:T(8,128)(2,1)S(1)} %pack_keys.1.refs_4_), channel_id=1, source_target_pairs={{0,4},{4,0},{8,12},{12,8},{1,5},{5,1},{9,13},{13,9},{2,6},{6,2},{1... | collective-permute-start | bytes 393224 | tf_op jit(solution)/shard_map/ppermute | solution.py:207
  13.2 6.0 %copy-start.1 = (s32[3]{0:T(128)S(1)}, s32[3]{0:T(128)}, u32[]{:S(2)}) copy-start(s32[3]{0:T(128)} %first_ref.1) | copy-start | bytes 40

commit v6 on v5

--- a/solution.py
+++ b/solution.py
@@ -10,48 +10,60 @@
 
 QTILE = 64
 PACK = 16
+K_COPIES = 2
+Q_COPIES = 3
 LANES = 128
-CHUNK = 256
+CHUNK = 512
 MASKED = -1e30
 NT = (((1,), (1,)), ((), ()))
 
 
-def pack_keys_kernel(n_head, key_heads, k_hbm, k_out, k_ref, sem):
-    copy = pltpu.make_async_copy(k_hbm, k_ref, sem)
-    copy.start()
+def pack_kernel(n_head, key_heads, heads, q_hbm, k_hbm, *refs):
+    q_outs, (k_out, q_ref, k_ref, q_sems, k_sems) = refs[:n_head], refs[n_head:]
     me = lax.axis_index("head")
     own = key_heads // n_head
+    width = own * heads
+    tokens = q_outs[0].shape[2]
     blocks = k_out.shape[2]
-    rows = PACK * 4 * key_heads
-    out_row = lax.broadcasted_iota(jnp.int32, (own * 4 * PACK, rows), 0)
-    in_row = lax.broadcasted_iota(jnp.int32, (own * 4 * PACK, rows), 1)
+    q_rows = PACK * key_heads * heads
+    k_rows = PACK * 4 * key_heads
+    k_copies, q_copies = [], []
+    k_each, q_each = blocks // PACK // K_COPIES, tokens // PACK // Q_COPIES
+    for n in range(K_COPIES):
+        at = pl.ds(n * k_each * k_rows, k_each * k_rows)
+        k_copies.append(pltpu.make_async_copy(k_hbm.at[at], k_ref.at[at], k_sems.at[n]))
+    for n in range(Q_COPIES):
+        at = pl.ds(n * q_each * q_rows, q_each * q_rows)
+        q_copies.append(pltpu.make_async_copy(q_hbm.at[at], q_ref.at[at], q_sems.at[n]))
+    for copy in k_copies + q_copies:
+        copy.start()
+
+    out_row = lax.broadcasted_iota(jnp.int32, (own * 4 * PACK, k_rows), 0)
+    in_row = lax.broadcasted_iota(jnp.int32, (own * 4 * PACK, k_rows), 1)
     head = out_row // (4 * PACK)
     part = out_row // PACK % 4
     source = out_row % PACK * (4 * key_heads) + part * key_heads + me * own + head
     select = jnp.where(in_row == source, 1.0, 0.0).astype(jnp.bfloat16)
-    copy.wait()
     for block in range(blocks // PACK):
+        if block % k_each == 0:
+            k_copies[block // k_each].wait()
         moved = jnp.dot(
-            select, k_ref[block * rows:(block + 1) * rows, :], preferred_element_type=jnp.float32
+            select, k_ref[block * k_rows:(block + 1) * k_rows, :], preferred_element_type=jnp.float32
         ).astype(jnp.bfloat16)
         for u in range(own * 4):
             k_out[u // 4, u % 4, block * PACK:(block + 1) * PACK, :] = moved[u * PACK:(u + 1) * PACK]
 
-
-def pack_queries_kernel(n_head, key_heads, heads, q_ref, *q_outs):
-    me = lax.axis_index("head")
-    width = key_heads // n_head * heads
-    tokens = q_outs[0].shape[2]
-    rows = PACK * key_heads * heads
-    out_row = lax.broadcasted_iota(jnp.int32, (n_head * width * PACK, rows), 0)
-    in_row = lax.broadcasted_iota(jnp.int32, (n_head * width * PACK, rows), 1)
+    out_row = lax.broadcasted_iota(jnp.int32, (n_head * width * PACK, q_rows), 0)
+    in_row = lax.broadcasted_iota(jnp.int32, (n_head * width * PACK, q_rows), 1)
     step = out_row // (width * PACK)
     unit = out_row // PACK % width
     source = out_row % PACK * (key_heads * heads) + (step ^ me) * width + unit
     select = jnp.where(in_row == source, 1.0, 0.0).astype(jnp.bfloat16)
     for block in range(tokens // PACK):
+        if block % q_each == 0:
+            q_copies[block // q_each].wait()
         moved = jnp.dot(
-            select, q_ref[block * rows:(block + 1) * rows, :], preferred_element_type=jnp.float32
+            select, q_ref[block * q_rows:(block + 1) * q_rows, :], preferred_element_type=jnp.float32
         ).astype(jnp.bfloat16)
         for u in range(n_head * width):
             d, g, h = u // width, u % width // heads, u % heads
@@ -81,7 +93,7 @@
         return lax.fori_loop(0, spans, lambda n, c: body(pl.multiple_of(n * span, span), c), carry)
 
     for j in range(n_ctx):
-        at = pl.ds(pl.multiple_of((me ^ j ^ (j >> 1)) * local, local), local)
+        at = pl.ds(pl.multiple_of((me ^ j) * local, local), local)
         keys[:, :, at, :] = k_refs[j][...]
 
     def tile(index, _):
@@ -183,28 +195,34 @@
     hbm = pl.BlockSpec(memory_space=pltpu.HBM)
     q_part = jax.ShapeDtypeStruct((own, heads, tokens, depth), queries.dtype)
     k_part = jax.ShapeDtypeStruct((own, 4, blocks, depth), keys.dtype)
-    k_own = pl.pallas_call(
-        partial(pack_keys_kernel, n_head, key_heads),
-        out_shape=k_part,
-        in_specs=[hbm],
-        out_specs=vmem,
-        scratch_shapes=[pltpu.VMEM((blocks * 4 * key_heads, depth), keys.dtype), pltpu.SemaphoreType.DMA],
+    packed = pl.pallas_call(
+        partial(pack_kernel, n_head, key_heads, heads),
+        out_shape=[q_part] * n_head + [k_part],
+        in_specs=[hbm, hbm],
+        out_specs=[vmem] * (n_head + 1),
+        scratch_shapes=[
+            pltpu.VMEM((tokens * key_heads * heads, depth), queries.dtype),
+            pltpu.VMEM((blocks * 4 * key_heads, depth), keys.dtype),
+            pltpu.SemaphoreType.DMA((Q_COPIES,)),
+            pltpu.SemaphoreType.DMA((K_COPIES,)),
+        ],
         compiler_params=pltpu.CompilerParams(vmem_limit_bytes=16 * 2 ** 20),
-        name="pack_keys",
-    )(in_hbm(keys.reshape(-1, depth)))
-    q_parts = pl.pallas_call(
-        partial(pack_queries_kernel, n_head, key_heads, heads),
-        out_shape=[q_part] * n_head,
-        in_specs=[vmem],
-        out_specs=[vmem] * n_head,
-        compiler_params=pltpu.CompilerParams(vmem_limit_bytes=16 * 2 ** 20),
-        name="pack_queries",
-    )(queries.reshape(-1, depth))
-    q_parts, k_parts = list(q_parts), [k_own]
+        name="pack",
+    )(in_hbm(queries.reshape(-1, depth)), in_hbm(keys.reshape(-1, depth)))
+    q_parts, k_parts = list(packed[:n_head]), [packed[n_head]]
+
+    def swap(array, axis, size, bit):
+        return lax.ppermute(array, axis, [(i, i ^ bit) for i in range(size)])
+
     for d in range(1, n_head):
-        q_parts[d] = lax.ppermute(q_parts[d], "head", [(i, i ^ d) for i in range(n_head)])
-    for j in range(1, n_ctx):
-        k_parts.append(lax.ppermute(k_own, "ctx", [(i, i ^ j ^ (j >> 1)) for i in range(n_ctx)]))
+        q_parts[d] = swap(q_parts[d], "head", n_head, d)
+    bit = n_ctx // 2
+    k_parts = {0: packed[n_head]}
+    while bit:
+        for j in list(k_parts):
+            k_parts[j | bit] = swap(k_parts[j], "ctx", n_ctx, bit)
+        bit //= 2
+    k_parts = [k_parts[j] for j in range(n_ctx)]
     columns = n_head * heads * QTILE
     return pl.pallas_call(
         partial(main_kernel, n_head, n_ctx),

time: 25.6 us -> 24.6 us (0.961)
  local copies, waits for them, and re-layouts: 1.14 us -> 0.01 us
  Pallas kernels: 7.97 us -> 8.45 us
    unnamed x4 -> x2, local copies, waits for them, and re-layouts: 1.14 us -> 0.01 us
    pallas_call x2 -> x1, Pallas kernels: 1.9 us -> 2.37 us  [per_device(): pl.pallas_call(partial(pack_kernel, n_head, key_heads, heads), out_shape=...]
  transfers between devices with their start and end apart: 6 -> 6, of which waited for: 3 -> 4; matrix products, arithmetic and copies ran while one was open for 0% -> 0% of each run, Pallas kernels for 2% -> 0%
where the time goes in v6:
time: 24.6 us; the launch traced here: 24.5 us
  Pallas kernels  8.45 us (34%)
  starting transfers between devices  8.2 us (33%)
  waiting for transfers between devices  7.12 us (29%)
  between operations  0.67 us (3%)
    ppermute x6, starting transfers between devices, swap(): return lax.ppermute(array, axis, [(i, i ^ bit) for i in range(size)])  8.2 us
    ppermute x6, waiting for transfers between devices, swap(): return lax.ppermute(array, axis, [(i, i ^ bit) for i in range(size)])  7.12 us
    pallas_call x1, Pallas kernels, per_device(): pl.pallas_call(partial(main_kernel, n_head, n_ctx), out_shape=jax.ShapeDt...  6.07 us
    pallas_call x1, Pallas kernels, per_device(): pl.pallas_call(partial(pack_kernel, n_head, key_heads, heads), out_shape=...  2.37 us
  transfers between devices with their start and end apart: 6, of which 4 were waited for; matrix products, arithmetic and copies ran while one was open for 0% of the time, Pallas kernels for 0%

profile of v6, /device:TPU:0, one launch (start us, length us, event | category | flops | bytes accessed | tf_op | source)
XLA Modules:
  0.0 24.5 jit_solution(7109126119573909141)
XLA Ops:
  0.0 2.4 %pack.1 = (bf16[2,2,192,128]{3,2,1,0:T(8,128)(2,1)S(1)}, bf16[2,2,192,128]{3,2,1,0:T(8,128)(2,1)S(1)}, bf16[2,2,192,128]{3,2,1,0:T(8,128)(2,1)S(1)}, bf16[2,2,19...) custom-call(bf16[3072,128]{1,0:T(8,128)(2,1)} %bitcast.2, bf16[2048,128]{1,0:T(8,128)(2,1)} %bitcast.3), custom_call_target="tpu_custom_call" | custom-call | tf_op jit(solution)/shard_map/pack/pallas_call | solution.py:198
  2.4 4.1 %collective-permute-start.4 = (bf16[2,4,64,128]{3,2,1,0:T(8,128)(2,1)S(1)}, bf16[2,4,64,128]{3,2,1,0:T(8,128)(2,1)S(1)}, u32[]{:S(2)}, u32[]{:S(2)}) collective-permute-start(bf16[2,4,64,128]{3,2,1,0:T(8,128)(2,1)S(1)} %get-tuple-element.14.refs_4_), channel_id=1, source_target_pairs={{0,8},{4,12},{8,0},{12,4},{1,9},{5,13},{9,1},{13,5},{2,10},{6,14},... | collective-permute-start | bytes 393224 | tf_op jit(solution)/shard_map/ppermute | solution.py:215
  6.5 0.0 collective-permute-start
  6.5 1.5 %collective-permute-start.1 = (bf16[2,2,192,128]{3,2,1,0:T(8,128)(2,1)S(1)}, bf16[2,2,192,128]{3,2,1,0:T(8,128)(2,1)S(1)}, u32[]{:S(2)}, u32[]{:S(2)}) collective-permute-start(bf16[2,2,192,128]{3,2,1,0:T(8,128)(2,1)S(1)} %get-tuple-element.12), channel_id=1, source_target_pairs={{0,2},{1,3},{2,0},{3,1},{4,6},{5,7},{6,4},{7,5},{8,10},{9,11},{10,... | collective-permute-start | bytes 589832 | tf_op jit(solution)/shard_map/ppermute | solution.py:215
  8.0 0.4 %collective-permute-start.2 = (bf16[2,2,192,128]{3,2,1,0:T(8,128)(2,1)S(1)}, bf16[2,2,192,128]{3,2,1,0:T(8,128)(2,1)S(1)}, u32[]{:S(2)}, u32[]{:S(2)}) collective-permute-start(bf16[2,2,192,128]{3,2,1,0:T(8,128)(2,1)S(1)} %get-tuple-element.13), channel_id=1, source_target_pairs={{0,3},{1,2},{2,1},{3,0},{4,7},{5,6},{6,5},{7,4},{8,11},{9,10},{10,... | collective-permute-start | bytes 589832 | tf_op jit(solution)/shard_map/ppermute | solution.py:215
  8.3 1.6 %collective-permute-start.3 = (bf16[2,4,64,128]{3,2,1,0:T(8,128)(2,1)S(1)}, bf16[2,4,64,128]{3,2,1,0:T(8,128)(2,1)S(1)}, u32[]{:S(2)}, u32[]{:S(2)}) collective-permute-start(bf16[2,4,64,128]{3,2,1,0:T(8,128)(2,1)S(1)} %get-tuple-element.14.refs_4_), channel_id=1, source_target_pairs={{0,4},{4,0},{8,12},{12,8},{1,5},{5,1},{9,13},{13,9},{2,6},{6,2},{1... | collective-permute-start | bytes 393224 | tf_op jit(solution)/shard_map/ppermute | solution.py:215
  9.9 3.0 %collective-permute-done.4.refs_6_ = bf16[2,4,64,128]{3,2,1,0:T(8,128)(2,1)S(1)} collective-permute-done((bf16[2,4,64,128]{3,2,1,0:T(8,128)(2,1)S(1)}, bf16[2,4,64,128]{3,2,1,0:T(8,128)(2,1)S(1)}, u32[]{:S(2)}, u32[]{:S(2)}) %collective-permute-start.4) | collective-permute-done | bytes 131104 | tf_op jit(solution)/shard_map/ppermute | solution.py:215
  12.9 0.7 %collective-permute-start.5 = (bf16[2,4,64,128]{3,2,1,0:T(8,128)(2,1)S(1)}, bf16[2,4,64,128]{3,2,1,0:T(8,128)(2,1)S(1)}, u32[]{:S(2)}, u32[]{:S(2)}) collective-permute-start(bf16[2,4,64,128]{3,2,1,0:T(8,128)(2,1)S(1)} %collective-permute-done.4.refs_6_), channel_id=1, source_target_pairs={{0,4},{4,0},{8,12},{12,8},{1,5},{5,1},{9,13},{13,9},{2,6},{6,2},{1... | collective-permute-start | bytes 393224 | tf_op jit(solution)/shard_map/ppermute | solution.py:215
  14.2 0.0 copy-start
  14.2 1.5 %collective-permute-done.3.refs_5_ = bf16[2,4,64,128]{3,2,1,0:T(8,128)(2,1)S(1)} collective-permute-done((bf16[2,4,64,128]{3,2,1,0:T(8,128)(2,1)S(1)}, bf16[2,4,64,128]{3,2,1,0:T(8,128)(2,1)S(1)}, u32[]{:S(2)}, u32[]{:S(2)}) %collective-permute-start.3) | collective-permute-done | bytes 131104 | tf_op jit(solution)/shard_map/ppermute | solution.py:215
  15.7 0.0 collective-permute-done.refs_1_
  15.7 0.0 collective-permute-done.1.refs_2_
  15.7 1.9 %collective-permute-done.2.refs_3_ = bf16[2,2,192,128]{3,2,1,0:T(8,128)(2,1)S(1)} collective-permute-done((bf16[2,2,192,128]{3,2,1,0:T(8,128)(2,1)S(1)}, bf16[2,2,192,128]{3,2,1,0:T(8,128)(2,1)S(1)}, u32[]{:S(2)}, u32[]{:S(2)}) %collective-permute-start.2) | collective-permute-done | bytes 196640 | tf_op jit(solution)/shard_map/ppermute | solution.py:215
  17.6 0.7 %collective-permute-done.5.refs_7_ = bf16[2,4,64,128]{3,2,1,0:T(8,128)(2,1)S(1)} collective-permute-done((bf16[2,4,64,128]{3,2,1,0:T(8,128)(2,1)S(1)}, bf16[2,4,64,128]{3,2,1,0:T(8,128)(2,1)S(1)}, u32[]{:S(2)}, u32[]{:S(2)}) %collective-permute-start.5) | collective-permute-done | bytes 131104 | tf_op jit(solution)/shard_map/ppermute | solution.py:215
  18.4 0.0 copy-done
  18.4 6.1 %importance.1 = f32[192,2,256]{2,1,0:T(2,128)} custom-call(s32[1]{0:T(128)S(6)} %copy.5.start_ref, s32[3]{0:T(128)S(1)} %copy-done, bf16[2,2,192,128]{3,2,1,0:T(8,128)(2,1)S(1)} %get-tuple-element.10.refs_0_, bf16[2,2,192,128]{3,2,1,0:T(8,128)(2,1)S(1)} %collective-permute-done.refs_1_, bf16[2,2,192,128]{3,2,1,0:T(8,128)(2,1)S(1)} %collective-permute-done.1.refs_2_, ...), custom_call_target="tpu_custom_call" | custom-call | tf_op jit(solution)/shard_map/importance/pallas_call | solution.py:227
Async XLA Ops:
  2.4 10.5 %collective-permute-start.4 = (bf16[2,4,64,128]{3,2,1,0:T(8,128)(2,1)S(1)}, bf16[2,4,64,128]{3,2,1,0:T(8,128)(2,1)S(1)}, u32[]{:S(2)}, u32[]{:S(2)}) collective-permute-start(bf16[2,4,64,128]{3,2,1,0:T(8,128)(2,1)S(1)} %get-tuple-element.14.refs_4_), channel_id=1, source_target_pairs={{0,8},{4,12},{8,0},{12,4},{1,9},{5,13},{9,1},{13,5},{2,10},{6,14},... | collective-permute-start | bytes 393224 | tf_op jit(solution)/shard_map/ppermute | solution.py:215
  6.5 9.2 %collective-permute-start = (bf16[2,2,192,128]{3,2,1,0:T(8,128)(2,1)S(1)}, bf16[2,2,192,128]{3,2,1,0:T(8,128)(2,1)S(1)}, u32[]{:S(2)}, u32[]{:S(2)}) collective-permute-start(bf16[2,2,192,128]{3,2,1,0:T(8,128)(2,1)S(1)} %get-tuple-element.11), channel_id=1, source_target_pairs={{0,1},{1,0},{2,3},{3,2},{4,5},{5,4},{6,7},{7,6},{8,9},{9,8},{10,11... | collective-permute-start | bytes 589832 | tf_op jit(solution)/shard_map/ppermute | solution.py:215
  6.5 9.2 %collective-permute-start.1 = (bf16[2,2,192,128]{3,2,1,0:T(8,128)(2,1)S(1)}, bf16[2,2,192,128]{3,2,1,0:T(8,128)(2,1)S(1)}, u32[]{:S(2)}, u32[]{:S(2)}) collective-permute-start(bf16[2,2,192,128]{3,2,1,0:T(8,128)(2,1)S(1)} %get-tuple-element.12), channel_id=1, source_target_pairs={{0,2},{1,3},{2,0},{3,1},{4,6},{5,7},{6,4},{7,5},{8,10},{9,11},{10,... | collective-permute-start | bytes 589832 | tf_op jit(solution)/shard_map/ppermute | solution.py:215
  8.0 9.6 %collective-permute-start.2 = (bf16[2,2,192,128]{3,2,1,0:T(8,128)(2,1)S(1)}, bf16[2,2,192,128]{3,2,1,0:T(8,128)(2,1)S(1)}, u32[]{:S(2)}, u32[]{:S(2)}) collective-permute-start(bf16[2,2,192,128]{3,2,1,0:T(8,128)(2,1)S(1)} %get-tuple-element.13), channel_id=1, source_target_pairs={{0,3},{1,2},{2,1},{3,0},{4,7},{5,6},{6,5},{7,4},{8,11},{9,10},{10,... | collective-permute-start | bytes 589832 | tf_op jit(solution)/shard_map/ppermute | solution.py:215
  8.3 7.3 %collective-permute-start.3 = (bf16[2,4,64,128]{3,2,1,0:T(8,128)(2,1)S(1)}, bf16[2,4,64,128]{3,2,1,0:T(8,128)(2,1)S(1)}, u32[]{:S(2)}, u32[]{:S(2)}) collective-permute-start(bf16[2,4,64,128]{3,2,1,0:T(8,128)(2,1)S(1)} %get-tuple-element.14.refs_4_), channel_id=1, source_target_pairs={{0,4},{4,0},{8,12},{12,8},{1,5},{5,1},{9,13},{13,9},{2,6},{6,2},{1... | collective-permute-start | bytes 393224 | tf_op jit(solution)/shard_map/ppermute | solution.py:215
  12.9 5.5 %collective-permute-start.5 = (bf16[2,4,64,128]{3,2,1,0:T(8,128)(2,1)S(1)}, bf16[2,4,64,128]{3,2,1,0:T(8,128)(2,1)S(1)}, u32[]{:S(2)}, u32[]{:S(2)}) collective-permute-start(bf16[2,4,64,128]{3,2,1,0:T(8,128)(2,1)S(1)} %collective-permute-done.4.refs_6_), channel_id=1, source_target_pairs={{0,4},{4,0},{8,12},{12,8},{1,5},{5,1},{9,13},{13,9},{2,6},{6,2},{1... | collective-permute-start | bytes 393224 | tf_op jit(solution)/shard_map/ppermute | solution.py:215
  14.2 4.2 %copy-start = (s32[3]{0:T(128)S(1)}, s32[3]{0:T(128)}, u32[]{:S(2)}) copy-start(s32[3]{0:T(128)} %first_ref.1) | copy-start | bytes 40

commit v7 on v6

--- a/solution.py
+++ b/solution.py
@@ -14,6 +14,7 @@
 Q_COPIES = 3
 LANES = 128
 CHUNK = 512
+SPAN_ROWS = 256
 MASKED = -1e30
 NT = (((1,), (1,)), ((), ()))
 
@@ -70,56 +71,161 @@
             q_outs[d][g, h, block * PACK:(block + 1) * PACK, :] = moved[u * PACK:(u + 1) * PACK]
 
 
-def main_kernel(n_head, n_ctx, start_ref, first_ref, *refs):
+def gather_keys(n_ctx, k_refs, keys):
+    me = lax.axis_index("ctx")
+    local = k_refs[0].shape[2]
+    for j in range(n_ctx):
+        at = pl.ds(pl.multiple_of((me ^ j) * local, local), local)
+        keys[:, :, at, :] = k_refs[j][...]
+
+
+def limits(n_ctx, tokens, begin, start_ref):
+    lane = lax.broadcasted_iota(jnp.int32, (8, LANES), 1)
+    row = lax.broadcasted_iota(jnp.int32, (8, LANES), 0)
+    place = start_ref[0] + lax.axis_index("ctx") * tokens + begin + lane % QTILE
+    return 4 * row, place - 31 - 64 * row
+
+
+def visible(nsel, span_tokens, r, s, first, row4, reach, base=None):
+    least_position = 16 * 4 * nsel * 7 // 8 - span_tokens
+    most_first = nsel - 1
+    at = r if base is None else base + r
+    mask = None
+    if base is not None or 4 * r + s <= most_first:
+        mask = row4 >= first - (4 * at + s)
+    if base is not None or 16 * (4 * (r + 7) + s) + 31 > least_position:
+        below = reach >= 64 * at + 16 * s
+        mask = below if mask is None else mask & below
+    return mask
+
+
+def tile_columns(q_refs, g, begin):
+    return jnp.concatenate(
+        [q[g, h, pl.ds(begin, QTILE), :] for q in q_refs for h in range(q.shape[1])], axis=0
+    )
+
+
+def interleave(*stages):
+    lengths = [length for length, _ in stages]
+    done = [0] * len(stages)
+    for tick in range(1, max(lengths) + 1):
+        for n, (length, stage) in enumerate(stages):
+            while done[n] * max(lengths) < tick * length:
+                next(stage, None)
+                done[n] += 1
+    for _, stage in stages:
+        for _ in stage:
+            pass
+
+
+def unit_kernel(n_head, n_ctx, start_ref, first_ref, *refs):
     q_refs, k_refs = refs[:n_head], refs[n_head:n_head + n_ctx]
     out_ref, keys, scores, pooled, lined = refs[n_head + n_ctx:]
     own, heads, tokens, depth = q_refs[0].shape
-    local = k_refs[0].shape[2]
-    nsel = local * n_ctx
-    me = lax.axis_index("ctx")
+    nsel = keys.shape[2]
     scale = math.log2(math.e) / math.sqrt(depth)
     factor = nsel / (2.0 * n_head * heads)
-    least_position = 16 * 4 * nsel * 7 // 8 - n_ctx * tokens
-    most_first = nsel - 1
+    tiles_n = n_head * heads * QTILE // LANES
+    block = 64
+    gather_keys(n_ctx, k_refs, keys)
+    units = [(t, g) for t in range(tokens // QTILE) for g in range(own)]
+    tops, weights = {}, {}
+
+    def products(u):
+        t, g = units[u]
+        columns = tile_columns(q_refs, g, t * QTILE)
+        row4, reach = limits(n_ctx, tokens, t * QTILE, start_ref)
+        first = first_ref[t]
+        top = [None] * tiles_n
+        for base in range(0, nsel, block):
+            rows = jnp.concatenate([keys[g, s, base:base + block, :] for s in range(4)], axis=0)
+            piece = lax.dot_general(rows, columns, NT, preferred_element_type=jnp.float32)
+            for s in range(4):
+                for r in range(0, block, 8):
+                    mask = visible(nsel, n_ctx * tokens, base + r, s, first, row4, reach)
+                    for n in range(tiles_n):
+                        part = piece[s * block + r:s * block + r + 8, n * LANES:(n + 1) * LANES]
+                        if mask is not None:
+                            part = jnp.where(mask, part, MASKED)
+                        scores[u % 2, s, base + r:base + r + 8, n * LANES:(n + 1) * LANES] = part
+                        top[n] = part if top[n] is None else jnp.maximum(top[n], part)
+                yield
+        tops[u] = top
+
+    def exponentials(u):
+        weights[u] = []
+        for n in range(tiles_n):
+            top, total = tops[u][n], None
+            at = slice(n * LANES, (n + 1) * LANES)
+            for r in range(0, nsel, 8):
+                parts = [jnp.exp2((scores[u % 2, s, r:r + 8, at] - top) * scale) for s in range(4)]
+                rest = parts[1] + parts[2] + parts[3]
+                pooled[u % 2, 0, r:r + 8, at] = parts[0]
+                pooled[u % 2, 1, r:r + 8, at] = rest
+                both = parts[0] + rest
+                total = both if total is None else total + both
+                if r % 32 == 24:
+                    yield
+            peak = jnp.max(top, axis=0, keepdims=True)
+            lowered = jnp.exp2((top - peak) * scale)
+            weights[u].append(lowered * (factor / jnp.sum(total * lowered, axis=0, keepdims=True)))
+
+    def sums(u):
+        t, g = units[u]
+        lined[u % 2, 1, 0:8, :] = jnp.zeros((8, LANES), jnp.float32)
+        for r in range(0, nsel, 8):
+            lead, rest = None, None
+            for n in range(tiles_n):
+                at = slice(n * LANES, (n + 1) * LANES)
+                first, second = pooled[u % 2, 0, r:r + 8, at] * weights[u][n], pooled[u % 2, 1, r:r + 8, at] * weights[u][n]
+                lead = first if lead is None else lead + first
+                rest = second if rest is None else rest + second
+            lined[u % 2, 0, 8 + r:16 + r, :] = lead
+            lined[u % 2, 1, 8 + r:16 + r, :] = lead + 2.0 * rest
+            if r % 16 == 8:
+                yield
+        turned = (lined[u % 2, 0, 8:8 + nsel, :] + lined[u % 2, 1, 7:7 + nsel, :]).T
+        out_ref[t * QTILE:(t + 1) * QTILE, g, :] = turned[:QTILE] + turned[QTILE:]
+        yield
+
+    for step in range(len(units) + 2):
+        stages = []
+        if step < len(units):
+            stages.append((4 * nsel // block, products(step)))
+        if 0 <= step - 1 < len(units):
+            stages.append((tiles_n * nsel // 32, exponentials(step - 1)))
+        if step >= 2:
+            stages.append((nsel // 16 + 1, sums(step - 2)))
+        interleave(*stages)
+
+
+def span_kernel(n_head, n_ctx, start_ref, first_ref, *refs):
+    q_refs, k_refs = refs[:n_head], refs[n_head:n_head + n_ctx]
+    out_ref, keys, scores, pooled, lined = refs[n_head + n_ctx:]
+    own, heads, tokens, depth = q_refs[0].shape
+    nsel = keys.shape[2]
+    scale = math.log2(math.e) / math.sqrt(depth)
+    factor = nsel / (2.0 * n_head * heads)
     chunks = n_head * heads * QTILE // CHUNK
     per_chunk = n_head // chunks
 
-    span = min(nsel, 256)
+    span = SPAN_ROWS
     spans = nsel // span
 
     def over_spans(body, carry):
-        if spans == 1:
-            return body(0, carry)
         return lax.fori_loop(0, spans, lambda n, c: body(pl.multiple_of(n * span, span), c), carry)
 
-    for j in range(n_ctx):
-        at = pl.ds(pl.multiple_of((me ^ j) * local, local), local)
-        keys[:, :, at, :] = k_refs[j][...]
+    gather_keys(n_ctx, k_refs, keys)
 
     def tile(index, _):
         begin = pl.multiple_of(index * QTILE, QTILE)
         first = first_ref[index]
-        lane = lax.broadcasted_iota(jnp.int32, (8, LANES), 1)
-        row = lax.broadcasted_iota(jnp.int32, (8, LANES), 0)
-        place = start_ref[0] + me * tokens + begin + lane % QTILE
-
-        def visible(base, r, s):
-            i = 4 * (base + r + row) + s
-            mask = None
-            if spans > 1 or 4 * r + s <= most_first:
-                mask = i >= first
-            if spans > 1 or 16 * (4 * (r + 7) + s) + 31 > least_position:
-                below = 16 * i + 31 <= place
-                mask = below if mask is None else mask & below
-            return mask
+        row4, reach = limits(n_ctx, tokens, begin, start_ref)
 
         for g in range(own):
             weights = []
             for c in range(chunks):
-                columns = jnp.concatenate(
-                    [q[g, h, pl.ds(begin, QTILE), :] for q in q_refs[c * per_chunk:(c + 1) * per_chunk] for h in range(heads)],
-                    axis=0,
-                )
+                columns = tile_columns(q_refs[c * per_chunk:(c + 1) * per_chunk], g, begin)
 
                 def scores_span(base, tops):
                     tops = list(tops)
@@ -127,12 +233,12 @@
                     piece = lax.dot_general(rows, columns, NT, preferred_element_type=jnp.float32)
                     for s in range(4):
                         for r in range(0, span, 8):
-                            mask = visible(base, r, s)
+                            mask = visible(nsel, n_ctx * tokens, r, s, first, row4, reach, base)
                             for n in range(CHUNK // LANES):
                                 part = piece[s * span + r:s * span + r + 8, n * LANES:(n + 1) * LANES]
                                 if mask is not None:
                                     part = jnp.where(mask, part, MASKED)
-                                scores[c, s, pl.ds(base + r, 8), n * LANES:(n + 1) * LANES] = part
+                                scores[0, s, pl.ds(base + r, 8), n * LANES:(n + 1) * LANES] = part
                                 tops[n] = jnp.maximum(tops[n], part)
                     return tuple(tops)
 
@@ -144,12 +250,12 @@
                         for r in range(0, span, 8):
                             here = pl.ds(base + r, 8)
                             parts = [
-                                jnp.exp2((scores[c, s, here, n * LANES:(n + 1) * LANES] - tops[n]) * scale)
+                                jnp.exp2((scores[0, s, here, n * LANES:(n + 1) * LANES] - tops[n]) * scale)
                                 for s in range(4)
                             ]
                             rest = parts[1] + parts[2] + parts[3]
-                            pooled[0, here, at:at + LANES] = parts[0]
-                            pooled[1, here, at:at + LANES] = rest
+                            pooled[0, 0, here, at:at + LANES] = parts[0]
+                            pooled[0, 1, here, at:at + LANES] = rest
                             total = total + (parts[0] + rest)
                         return total
 
@@ -162,18 +268,18 @@
                 for r in range(0, span, 8):
                     lead, rest = [
                         sum(
-                            (pooled[p, pl.ds(base + r, 8), n * LANES:(n + 1) * LANES] * weights[n] for n in range(1, len(weights))),
-                            pooled[p, pl.ds(base + r, 8), 0:LANES] * weights[0],
+                            (pooled[0, p, pl.ds(base + r, 8), n * LANES:(n + 1) * LANES] * weights[n] for n in range(1, len(weights))),
+                            pooled[0, p, pl.ds(base + r, 8), 0:LANES] * weights[0],
                         )
                         for p in range(2)
                     ]
-                    lined[0, pl.ds(base + 8 + r, 8), :] = lead
-                    lined[1, pl.ds(base + 8 + r, 8), :] = lead + 2.0 * rest
+                    lined[0, 0, pl.ds(base + 8 + r, 8), :] = lead
+                    lined[0, 1, pl.ds(base + 8 + r, 8), :] = lead + 2.0 * rest
                 return 0
 
-            lined[1, 0:8, :] = jnp.zeros((8, LANES), jnp.float32)
+            lined[0, 1, 0:8, :] = jnp.zeros((8, LANES), jnp.float32)
             over_spans(sums_span, 0)
-            blocks = lined[0, 8:8 + nsel, :] + lined[1, 7:7 + nsel, :]
+            blocks = lined[0, 0, 8:8 + nsel, :] + lined[0, 1, 7:7 + nsel, :]
             turned = blocks.T
             out_ref[pl.ds(begin, QTILE), g, :] = turned[:QTILE] + turned[QTILE:]
         return 0
@@ -224,18 +330,19 @@
         bit //= 2
     k_parts = [k_parts[j] for j in range(n_ctx)]
     columns = n_head * heads * QTILE
+    buffers = 2 if nsel <= SPAN_ROWS else 1
     return pl.pallas_call(
-        partial(main_kernel, n_head, n_ctx),
+        partial(unit_kernel if buffers == 2 else span_kernel, n_head, n_ctx),
         out_shape=jax.ShapeDtypeStruct((tokens, own, nsel), jnp.float32),
         in_specs=[smem, smem] + [vmem] * (n_head + n_ctx),
         out_specs=vmem,
         scratch_shapes=[
             pltpu.VMEM((own, 4, nsel, depth), keys.dtype),
-            pltpu.VMEM((columns // CHUNK, 4, nsel, CHUNK), jnp.float32),
-            pltpu.VMEM((2, nsel, columns), jnp.float32),
-            pltpu.VMEM((2, 8 + nsel, LANES), jnp.float32),
+            pltpu.VMEM((buffers, 4, nsel, columns), jnp.float32),
+            pltpu.VMEM((buffers, 2, nsel, columns), jnp.float32),
+            pltpu.VMEM((buffers, 2, 8 + nsel, LANES), jnp.float32),
         ],
-        compiler_params=pltpu.CompilerParams(vmem_limit_bytes=44 * 2 ** 20),
+        compiler_params=pltpu.CompilerParams(vmem_limit_bytes=(20 if buffers == 2 else 52) * 2 ** 20),
         name="importance",
     )(span_start, tile_first, *q_parts, *k_parts)
 

time: 24.6 us -> 24.3 us (0.988)
  Pallas kernels: 8.45 us -> 8.17 us
    pallas_call x1, Pallas kernels: 6.07 us -> 5.8 us  [per_device(): pl.pallas_call(partial(unit_kernel if buffers == 2 else span_kernel, n_he...]
where the time goes in v7:
time: 24.3 us; the launch traced here: 24.2 us
  starting transfers between devices  8.2 us (34%)
  Pallas kernels  8.17 us (34%)
  waiting for transfers between devices  7.12 us (29%)
  between operations  0.67 us (3%)
    ppermute x6, starting transfers between devices, swap(): return lax.ppermute(array, axis, [(i, i ^ bit) for i in range(size)])  8.2 us
    ppermute x6, waiting for transfers between devices, swap(): return lax.ppermute(array, axis, [(i, i ^ bit) for i in range(size)])  7.12 us
    pallas_call x1, Pallas kernels, per_device(): pl.pallas_call(partial(unit_kernel if buffers == 2 else span_kernel, n_he...  5.8 us
    pallas_call x1, Pallas kernels, per_device(): pl.pallas_call(partial(pack_kernel, n_head, key_heads, heads), out_shape=...  2.37 us
  transfers between devices with their start and end apart: 6, of which 4 were waited for; matrix products, arithmetic and copies ran while one was open for 0% of the time, Pallas kernels for 0%

profile of v7, /device:TPU:0, one launch (start us, length us, event | category | flops | bytes accessed | tf_op | source)
XLA Modules:
  0.0 24.2 jit_solution(13551624327421413381)
XLA Ops:
  0.0 2.4 %pack.1 = (bf16[2,2,192,128]{3,2,1,0:T(8,128)(2,1)S(1)}, bf16[2,2,192,128]{3,2,1,0:T(8,128)(2,1)S(1)}, bf16[2,2,192,128]{3,2,1,0:T(8,128)(2,1)S(1)}, bf16[2,2,19...) custom-call(bf16[3072,128]{1,0:T(8,128)(2,1)} %bitcast.2, bf16[2048,128]{1,0:T(8,128)(2,1)} %bitcast.3), custom_call_target="tpu_custom_call" | custom-call | tf_op jit(solution)/shard_map/pack/pallas_call | solution.py:304
  2.4 4.1 %collective-permute-start.4 = (bf16[2,4,64,128]{3,2,1,0:T(8,128)(2,1)S(1)}, bf16[2,4,64,128]{3,2,1,0:T(8,128)(2,1)S(1)}, u32[]{:S(2)}, u32[]{:S(2)}) collective-permute-start(bf16[2,4,64,128]{3,2,1,0:T(8,128)(2,1)S(1)} %get-tuple-element.14.refs_4_), channel_id=1, source_target_pairs={{0,8},{4,12},{8,0},{12,4},{1,9},{5,13},{9,1},{13,5},{2,10},{6,14},... | collective-permute-start | bytes 393224 | tf_op jit(solution)/shard_map/ppermute | solution.py:321
  6.5 0.0 collective-permute-start
  6.5 1.5 %collective-permute-start.1 = (bf16[2,2,192,128]{3,2,1,0:T(8,128)(2,1)S(1)}, bf16[2,2,192,128]{3,2,1,0:T(8,128)(2,1)S(1)}, u32[]{:S(2)}, u32[]{:S(2)}) collective-permute-start(bf16[2,2,192,128]{3,2,1,0:T(8,128)(2,1)S(1)} %get-tuple-element.12), channel_id=1, source_target_pairs={{0,2},{1,3},{2,0},{3,1},{4,6},{5,7},{6,4},{7,5},{8,10},{9,11},{10,... | collective-permute-start | bytes 589832 | tf_op jit(solution)/shard_map/ppermute | solution.py:321
  8.0 0.4 %collective-permute-start.2 = (bf16[2,2,192,128]{3,2,1,0:T(8,128)(2,1)S(1)}, bf16[2,2,192,128]{3,2,1,0:T(8,128)(2,1)S(1)}, u32[]{:S(2)}, u32[]{:S(2)}) collective-permute-start(bf16[2,2,192,128]{3,2,1,0:T(8,128)(2,1)S(1)} %get-tuple-element.13), channel_id=1, source_target_pairs={{0,3},{1,2},{2,1},{3,0},{4,7},{5,6},{6,5},{7,4},{8,11},{9,10},{10,... | collective-permute-start | bytes 589832 | tf_op jit(solution)/shard_map/ppermute | solution.py:321
  8.3 1.6 %collective-permute-start.3 = (bf16[2,4,64,128]{3,2,1,0:T(8,128)(2,1)S(1)}, bf16[2,4,64,128]{3,2,1,0:T(8,128)(2,1)S(1)}, u32[]{:S(2)}, u32[]{:S(2)}) collective-permute-start(bf16[2,4,64,128]{3,2,1,0:T(8,128)(2,1)S(1)} %get-tuple-element.14.refs_4_), channel_id=1, source_target_pairs={{0,4},{4,0},{8,12},{12,8},{1,5},{5,1},{9,13},{13,9},{2,6},{6,2},{1... | collective-permute-start | bytes 393224 | tf_op jit(solution)/shard_map/ppermute | solution.py:321
  9.9 3.0 %collective-permute-done.4.refs_6_ = bf16[2,4,64,128]{3,2,1,0:T(8,128)(2,1)S(1)} collective-permute-done((bf16[2,4,64,128]{3,2,1,0:T(8,128)(2,1)S(1)}, bf16[2,4,64,128]{3,2,1,0:T(8,128)(2,1)S(1)}, u32[]{:S(2)}, u32[]{:S(2)}) %collective-permute-start.4) | collective-permute-done | bytes 131104 | tf_op jit(solution)/shard_map/ppermute | solution.py:321
  12.9 0.7 %collective-permute-start.5 = (bf16[2,4,64,128]{3,2,1,0:T(8,128)(2,1)S(1)}, bf16[2,4,64,128]{3,2,1,0:T(8,128)(2,1)S(1)}, u32[]{:S(2)}, u32[]{:S(2)}) collective-permute-start(bf16[2,4,64,128]{3,2,1,0:T(8,128)(2,1)S(1)} %collective-permute-done.4.refs_6_), channel_id=1, source_target_pairs={{0,4},{4,0},{8,12},{12,8},{1,5},{5,1},{9,13},{13,9},{2,6},{6,2},{1... | collective-permute-start | bytes 393224 | tf_op jit(solution)/shard_map/ppermute | solution.py:321
  14.2 0.0 copy-start
  14.2 1.5 %collective-permute-done.3.refs_5_ = bf16[2,4,64,128]{3,2,1,0:T(8,128)(2,1)S(1)} collective-permute-done((bf16[2,4,64,128]{3,2,1,0:T(8,128)(2,1)S(1)}, bf16[2,4,64,128]{3,2,1,0:T(8,128)(2,1)S(1)}, u32[]{:S(2)}, u32[]{:S(2)}) %collective-permute-start.3) | collective-permute-done | bytes 131104 | tf_op jit(solution)/shard_map/ppermute | solution.py:321
  15.7 0.0 collective-permute-done.refs_1_
  15.7 0.0 collective-permute-done.1.refs_2_
  15.7 1.9 %collective-permute-done.2.refs_3_ = bf16[2,2,192,128]{3,2,1,0:T(8,128)(2,1)S(1)} collective-permute-done((bf16[2,2,192,128]{3,2,1,0:T(8,128)(2,1)S(1)}, bf16[2,2,192,128]{3,2,1,0:T(8,128)(2,1)S(1)}, u32[]{:S(2)}, u32[]{:S(2)}) %collective-permute-start.2) | collective-permute-done | bytes 196640 | tf_op jit(solution)/shard_map/ppermute | solution.py:321
  17.6 0.7 %collective-permute-done.5.refs_7_ = bf16[2,4,64,128]{3,2,1,0:T(8,128)(2,1)S(1)} collective-permute-done((bf16[2,4,64,128]{3,2,1,0:T(8,128)(2,1)S(1)}, bf16[2,4,64,128]{3,2,1,0:T(8,128)(2,1)S(1)}, u32[]{:S(2)}, u32[]{:S(2)}) %collective-permute-start.5) | collective-permute-done | bytes 131104 | tf_op jit(solution)/shard_map/ppermute | solution.py:321
  18.4 0.0 copy-done
  18.4 5.8 %importance.1 = f32[192,2,256]{2,1,0:T(2,128)} custom-call(s32[1]{0:T(128)S(6)} %copy.5.start_ref, s32[3]{0:T(128)S(1)} %copy-done, bf16[2,2,192,128]{3,2,1,0:T(8,128)(2,1)S(1)} %get-tuple-element.10.refs_0_, bf16[2,2,192,128]{3,2,1,0:T(8,128)(2,1)S(1)} %collective-permute-done.refs_1_, bf16[2,2,192,128]{3,2,1,0:T(8,128)(2,1)S(1)} %collective-permute-done.1.refs_2_, ...), custom_call_target="tpu_custom_call" | custom-call | tf_op jit(solution)/shard_map/importance/pallas_call | solution.py:334
Async XLA Ops:
  2.4 10.5 %collective-permute-start.4 = (bf16[2,4,64,128]{3,2,1,0:T(8,128)(2,1)S(1)}, bf16[2,4,64,128]{3,2,1,0:T(8,128)(2,1)S(1)}, u32[]{:S(2)}, u32[]{:S(2)}) collective-permute-start(bf16[2,4,64,128]{3,2,1,0:T(8,128)(2,1)S(1)} %get-tuple-element.14.refs_4_), channel_id=1, source_target_pairs={{0,8},{4,12},{8,0},{12,4},{1,9},{5,13},{9,1},{13,5},{2,10},{6,14},... | collective-permute-start | bytes 393224 | tf_op jit(solution)/shard_map/ppermute | solution.py:321
  6.5 9.2 %collective-permute-start = (bf16[2,2,192,128]{3,2,1,0:T(8,128)(2,1)S(1)}, bf16[2,2,192,128]{3,2,1,0:T(8,128)(2,1)S(1)}, u32[]{:S(2)}, u32[]{:S(2)}) collective-permute-start(bf16[2,2,192,128]{3,2,1,0:T(8,128)(2,1)S(1)} %get-tuple-element.11), channel_id=1, source_target_pairs={{0,1},{1,0},{2,3},{3,2},{4,5},{5,4},{6,7},{7,6},{8,9},{9,8},{10,11... | collective-permute-start | bytes 589832 | tf_op jit(solution)/shard_map/ppermute | solution.py:321
  6.5 9.2 %collective-permute-start.1 = (bf16[2,2,192,128]{3,2,1,0:T(8,128)(2,1)S(1)}, bf16[2,2,192,128]{3,2,1,0:T(8,128)(2,1)S(1)}, u32[]{:S(2)}, u32[]{:S(2)}) collective-permute-start(bf16[2,2,192,128]{3,2,1,0:T(8,128)(2,1)S(1)} %get-tuple-element.12), channel_id=1, source_target_pairs={{0,2},{1,3},{2,0},{3,1},{4,6},{5,7},{6,4},{7,5},{8,10},{9,11},{10,... | collective-permute-start | bytes 589832 | tf_op jit(solution)/shard_map/ppermute | solution.py:321
  8.0 9.6 %collective-permute-start.2 = (bf16[2,2,192,128]{3,2,1,0:T(8,128)(2,1)S(1)}, bf16[2,2,192,128]{3,2,1,0:T(8,128)(2,1)S(1)}, u32[]{:S(2)}, u32[]{:S(2)}) collective-permute-start(bf16[2,2,192,128]{3,2,1,0:T(8,128)(2,1)S(1)} %get-tuple-element.13), channel_id=1, source_target_pairs={{0,3},{1,2},{2,1},{3,0},{4,7},{5,6},{6,5},{7,4},{8,11},{9,10},{10,... | collective-permute-start | bytes 589832 | tf_op jit(solution)/shard_map/ppermute | solution.py:321
  8.3 7.3 %collective-permute-start.3 = (bf16[2,4,64,128]{3,2,1,0:T(8,128)(2,1)S(1)}, bf16[2,4,64,128]{3,2,1,0:T(8,128)(2,1)S(1)}, u32[]{:S(2)}, u32[]{:S(2)}) collective-permute-start(bf16[2,4,64,128]{3,2,1,0:T(8,128)(2,1)S(1)} %get-tuple-element.14.refs_4_), channel_id=1, source_target_pairs={{0,4},{4,0},{8,12},{12,8},{1,5},{5,1},{9,13},{13,9},{2,6},{6,2},{1... | collective-permute-start | bytes 393224 | tf_op jit(solution)/shard_map/ppermute | solution.py:321
  12.9 5.5 %collective-permute-start.5 = (bf16[2,4,64,128]{3,2,1,0:T(8,128)(2,1)S(1)}, bf16[2,4,64,128]{3,2,1,0:T(8,128)(2,1)S(1)}, u32[]{:S(2)}, u32[]{:S(2)}) collective-permute-start(bf16[2,4,64,128]{3,2,1,0:T(8,128)(2,1)S(1)} %collective-permute-done.4.refs_6_), channel_id=1, source_target_pairs={{0,4},{4,0},{8,12},{12,8},{1,5},{5,1},{9,13},{13,9},{2,6},{6,2},{1... | collective-permute-start | bytes 393224 | tf_op jit(solution)/shard_map/ppermute | solution.py:321
  14.2 4.2 %copy-start = (s32[3]{0:T(128)S(1)}, s32[3]{0:T(128)}, u32[]{:S(2)}) copy-start(s32[3]{0:T(128)} %first_ref.1) | copy-start | bytes 40

commit v8 on v7

v8 whole, which is shorter than its diff:
```python
import math
from functools import partial

import jax
import jax.numpy as jnp
from jax import lax
from jax.experimental import pallas as pl
from jax.experimental.pallas import tpu as pltpu
from jax.sharding import PartitionSpec as P

QTILE = 64
PACK = 16
K_COPIES = 2
Q_COPIES = 3
LANES = 128
CHUNK = 512
SPAN_ROWS = 256
MASKED = -1e30
NT = (((1,), (1,)), ((), ()))


def pack_kernel(n_head, key_heads, heads, q_hbm, k_hbm, *refs):
    me = lax.axis_index("head")
    own = key_heads // n_head
    q_outs, k_outs = refs[:n_head * own], refs[n_head * own:(n_head + 1) * own]
    q_ref, k_ref, q_sems, k_sems = refs[(n_head + 1) * own:]
    width = own * heads
    tokens = q_outs[0].shape[1]
    blocks = k_outs[0].shape[1]
    q_rows = PACK * key_heads * heads
    k_rows = PACK * 4 * key_heads
    k_copies, q_copies = [], []
    k_each, q_each = blocks // PACK // K_COPIES, tokens // PACK // Q_COPIES
    for n in range(K_COPIES):
        at = pl.ds(n * k_each * k_rows, k_each * k_rows)
        k_copies.append(pltpu.make_async_copy(k_hbm.at[at], k_ref.at[at], k_sems.at[n]))
    for n in range(Q_COPIES):
        at = pl.ds(n * q_each * q_rows, q_each * q_rows)
        q_copies.append(pltpu.make_async_copy(q_hbm.at[at], q_ref.at[at], q_sems.at[n]))
    for copy in k_copies + q_copies:
        copy.start()

    out_row = lax.broadcasted_iota(jnp.int32, (own * 4 * PACK, k_rows), 0)
    in_row = lax.broadcasted_iota(jnp.int32, (own * 4 * PACK, k_rows), 1)
    head = out_row // (4 * PACK)
    part = out_row // PACK % 4
    source = out_row % PACK * (4 * key_heads) + part * key_heads + me * own + head
    select = jnp.where(in_row == source, 1.0, 0.0).astype(jnp.bfloat16)
    for block in range(blocks // PACK):
        if block % k_each == 0:
            k_copies[block // k_each].wait()
        moved = jnp.dot(
            select, k_ref[block * k_rows:(block + 1) * k_rows, :], preferred_element_type=jnp.float32
        ).astype(jnp.bfloat16)
        for u in range(own * 4):
            k_outs[u // 4][u % 4, block * PACK:(block + 1) * PACK, :] = moved[u * PACK:(u + 1) * PACK]

    out_row = lax.broadcasted_iota(jnp.int32, (n_head * width * PACK, q_rows), 0)
    in_row = lax.broadcasted_iota(jnp.int32, (n_head * width * PACK, q_rows), 1)
    step = out_row // (width * PACK)
    unit = out_row // PACK % width
    source = out_row % PACK * (key_heads * heads) + (step ^ me) * width + unit
    select = jnp.where(in_row == source, 1.0, 0.0).astype(jnp.bfloat16)
    for block in range(tokens // PACK):
        if block % q_each == 0:
            q_copies[block // q_each].wait()
        moved = jnp.dot(
            select, q_ref[block * q_rows:(block + 1) * q_rows, :], preferred_element_type=jnp.float32
        ).astype(jnp.bfloat16)
        for u in range(n_head * width):
            d, g, h = u // width, u % width // heads, u % heads
            q_outs[g * n_head + d][h, block * PACK:(block + 1) * PACK, :] = moved[u * PACK:(u + 1) * PACK]


def gather_keys(n_ctx, k_refs, keys):
    me = lax.axis_index("ctx")
    local = k_refs[0].shape[1]
    for j in range(n_ctx):
        at = pl.ds(pl.multiple_of((me ^ j) * local, local), local)
        keys[:, at, :] = k_refs[j][...]


def limits(n_ctx, tokens, begin, start_ref):
    lane = lax.broadcasted_iota(jnp.int32, (8, LANES), 1)
    row = lax.broadcasted_iota(jnp.int32, (8, LANES), 0)
    place = start_ref[0] + lax.axis_index("ctx") * tokens + begin + lane % QTILE
    return 4 * row, place - 31 - 64 * row


def visible(nsel, span_tokens, r, s, first, row4, reach, base=None):
    least_position = 16 * 4 * nsel * 7 // 8 - span_tokens
    most_first = nsel - 1
    at = r if base is None else base + r
    mask = None
    if base is not None or 4 * r + s <= most_first:
        mask = row4 >= first - (4 * at + s)
    if base is not None or 16 * (4 * (r + 7) + s) + 31 > least_position:
        below = reach >= 64 * at + 16 * s
        mask = below if mask is None else mask & below
    return mask


def tile_columns(q_refs, begin):
    return jnp.concatenate(
        [q[h, pl.ds(begin, QTILE), :] for q in q_refs for h in range(q.shape[0])], axis=0
    )


def take_refs(n_head, n_ctx, refs):
    q_refs, k_refs, refs = refs[:n_head], refs[n_head:n_head + n_ctx], refs[n_head + n_ctx:]
    earlier, (out_ref, keys, scores, pooled, lined) = refs[:-5], refs[-5:]
    return q_refs, k_refs, earlier, out_ref, keys, scores, pooled, lined


def put(out_ref, g, rows, value):
    if len(out_ref.shape) == 2:
        out_ref[rows, :] = value
    else:
        out_ref[rows, g, :] = value


def interleave(*stages):
    lengths = [length for length, _ in stages]
    done = [0] * len(stages)
    for tick in range(1, max(lengths) + 1):
        for n, (length, stage) in enumerate(stages):
            while done[n] * max(lengths) < tick * length:
                next(stage, None)
                done[n] += 1
    for _, stage in stages:
        for _ in stage:
            pass


def unit_kernel(n_head, n_ctx, start_ref, first_ref, *refs):
    q_refs, k_refs, earlier, out_ref, keys, scores, pooled, lined = take_refs(n_head, n_ctx, refs)
    heads, tokens, depth = q_refs[0].shape
    nsel, g = keys.shape[1], len(earlier)
    scale = math.log2(math.e) / math.sqrt(depth)
    factor = nsel / (2.0 * n_head * heads)
    tiles_n = n_head * heads * QTILE // LANES
    block = 64
    gather_keys(n_ctx, k_refs, keys)
    for n, ref in enumerate(earlier):
        put(out_ref, n, slice(None), ref[...])
    units = list(range(tokens // QTILE))
    tops, weights = {}, {}

    def products(u):
        t = units[u]
        columns = tile_columns(q_refs, t * QTILE)
        row4, reach = limits(n_ctx, tokens, t * QTILE, start_ref)
        first = first_ref[t]
        top = [None] * tiles_n
        for base in range(0, nsel, block):
            rows = jnp.concatenate([keys[s, base:base + block, :] for s in range(4)], axis=0)
            piece = lax.dot_general(rows, columns, NT, preferred_element_type=jnp.float32)
            for s in range(4):
                for r in range(0, block, 8):
                    mask = visible(nsel, n_ctx * tokens, base + r, s, first, row4, reach)
                    for n in range(tiles_n):
                        part = piece[s * block + r:s * block + r + 8, n * LANES:(n + 1) * LANES]
                        if mask is not None:
                            part = jnp.where(mask, part, MASKED)
                        scores[u % 2, s, base + r:base + r + 8, n * LANES:(n + 1) * LANES] = part
                        top[n] = part if top[n] is None else jnp.maximum(top[n], part)
                yield
        tops[u] = top

    def exponentials(u):
        weights[u] = []
        for n in range(tiles_n):
            top, total = tops[u][n], None
            at = slice(n * LANES, (n + 1) * LANES)
            for r in range(0, nsel, 8):
                parts = [jnp.exp2((scores[u % 2, s, r:r + 8, at] - top) * scale) for s in range(4)]
                rest = parts[1] + parts[2] + parts[3]
                pooled[u % 2, 0, r:r + 8, at] = parts[0]
                pooled[u % 2, 1, r:r + 8, at] = rest
                both = parts[0] + rest
                total = both if total is None else total + both
                if r % 32 == 24:
                    yield
            peak = jnp.max(top, axis=0, keepdims=True)
            lowered = jnp.exp2((top - peak) * scale)
            weights[u].append(lowered * (factor / jnp.sum(total * lowered, axis=0, keepdims=True)))

    def sums(u):
        t = units[u]
        lined[u % 2, 1, 0:8, :] = jnp.zeros((8, LANES), jnp.float32)
        for r in range(0, nsel, 8):
            lead, rest = None, None
            for n in range(tiles_n):
                at = slice(n * LANES, (n + 1) * LANES)
                first, second = pooled[u % 2, 0, r:r + 8, at] * weights[u][n], pooled[u % 2, 1, r:r + 8, at] * weights[u][n]
                lead = first if lead is None else lead + first
                rest = second if rest is None else rest + second
            lined[u % 2, 0, 8 + r:16 + r, :] = lead
            lined[u % 2, 1, 8 + r:16 + r, :] = lead + 2.0 * rest
            if r % 16 == 8:
                yield
        turned = (lined[u % 2, 0, 8:8 + nsel, :] + lined[u % 2, 1, 7:7 + nsel, :]).T
        put(out_ref, g, slice(t * QTILE, (t + 1) * QTILE), turned[:QTILE] + turned[QTILE:])
        yield

    for step in range(len(units) + 2):
        stages = []
        if step < len(units):
            stages.append((4 * nsel // block, products(step)))
        if 0 <= step - 1 < len(units):
            stages.append((tiles_n * nsel // 32, exponentials(step - 1)))
        if step >= 2:
            stages.append((nsel // 16 + 1, sums(step - 2)))
        interleave(*stages)


def span_kernel(n_head, n_ctx, start_ref, first_ref, *refs):
    q_refs, k_refs, earlier, out_ref, keys, scores, pooled, lined = take_refs(n_head, n_ctx, refs)
    heads, tokens, depth = q_refs[0].shape
    nsel, g = keys.shape[1], len(earlier)
    scale = math.log2(math.e) / math.sqrt(depth)
    factor = nsel / (2.0 * n_head * heads)
    chunks = n_head * heads * QTILE // CHUNK
    per_chunk = n_head // chunks

    span = SPAN_ROWS
    spans = nsel // span

    def over_spans(body, carry):
        return lax.fori_loop(0, spans, lambda n, c: body(pl.multiple_of(n * span, span), c), carry)

    gather_keys(n_ctx, k_refs, keys)
    for n, ref in enumerate(earlier):
        put(out_ref, n, slice(None), ref[...])

    def tile(index, _):
        begin = pl.multiple_of(index * QTILE, QTILE)
        first = first_ref[index]
        row4, reach = limits(n_ctx, tokens, begin, start_ref)

        weights = []
        for c in range(chunks):
            columns = tile_columns(q_refs[c * per_chunk:(c + 1) * per_chunk], begin)

            def scores_span(base, tops):
                tops = list(tops)
                rows = jnp.concatenate([keys[s, pl.ds(base, span), :] for s in range(4)], axis=0)
                piece = lax.dot_general(rows, columns, NT, preferred_element_type=jnp.float32)
                for s in range(4):
                    for r in range(0, span, 8):
                        mask = visible(nsel, n_ctx * tokens, r, s, first, row4, reach, base)
                        for n in range(CHUNK // LANES):
                            part = piece[s * span + r:s * span + r + 8, n * LANES:(n + 1) * LANES]
                            if mask is not None:
                                part = jnp.where(mask, part, MASKED)
                            scores[0, s, pl.ds(base + r, 8), n * LANES:(n + 1) * LANES] = part
                            tops[n] = jnp.maximum(tops[n], part)
                return tuple(tops)

            tops = over_spans(scores_span, (jnp.full((8, LANES), MASKED, jnp.float32),) * (CHUNK // LANES))
            for n in range(CHUNK // LANES):
                at = (c * CHUNK // LANES + n) * LANES

                def exps_span(base, total):
                    for r in range(0, span, 8):
                        here = pl.ds(base + r, 8)
                        parts = [
                            jnp.exp2((scores[0, s, here, n * LANES:(n + 1) * LANES] - tops[n]) * scale)
                            for s in range(4)
                        ]
                        rest = parts[1] + parts[2] + parts[3]
                        pooled[0, 0, here, at:at + LANES] = parts[0]
                        pooled[0, 1, here, at:at + LANES] = rest
                        total = total + (parts[0] + rest)
                    return total

                total = over_spans(exps_span, jnp.zeros((8, LANES), jnp.float32))
                top = jnp.max(tops[n], axis=0, keepdims=True)
                lowered = jnp.exp2((tops[n] - top) * scale)
                weights.append(lowered * (factor / jnp.sum(total * lowered, axis=0, keepdims=True)))

        def sums_span(base, _):
            for r in range(0, span, 8):
                lead, rest = [
                    sum(
                        (pooled[0, p, pl.ds(base + r, 8), n * LANES:(n + 1) * LANES] * weights[n] for n in range(1, len(weights))),
                        pooled[0, p, pl.ds(base + r, 8), 0:LANES] * weights[0],
                    )
                    for p in range(2)
                ]
                lined[0, 0, pl.ds(base + 8 + r, 8), :] = lead
                lined[0, 1, pl.ds(base + 8 + r, 8), :] = lead + 2.0 * rest
            return 0

        lined[0, 1, 0:8, :] = jnp.zeros((8, LANES), jnp.float32)
        over_spans(sums_span, 0)
        blocks = lined[0, 0, 8:8 + nsel, :] + lined[0, 1, 7:7 + nsel, :]
        turned = blocks.T
        put(out_ref, g, pl.ds(begin, QTILE), turned[:QTILE] + turned[QTILE:])
        return 0

    lax.fori_loop(0, tokens // QTILE, tile, 0)


def in_hbm(array):
    return pltpu.with_memory_space_constraint(array, pltpu.HBM)


def per_device(n_head, n_ctx, queries, keys, span_start, tile_first):
    tokens, key_heads, heads, depth = queries.shape
    blocks = keys.shape[0]
    own = key_heads // n_head
    nsel = blocks * n_ctx
    vmem = pl.BlockSpec(memory_space=pltpu.VMEM)
    smem = pl.BlockSpec(memory_space=pltpu.SMEM)
    hbm = pl.BlockSpec(memory_space=pltpu.HBM)
    q_part = jax.ShapeDtypeStruct((heads, tokens, depth), queries.dtype)
    k_part = jax.ShapeDtypeStruct((4, blocks, depth), keys.dtype)
    packed = pl.pallas_call(
        partial(pack_kernel, n_head, key_heads, heads),
        out_shape=[q_part] * (n_head * own) + [k_part] * own,
        in_specs=[hbm, hbm],
        out_specs=[vmem] * ((n_head + 1) * own),
        scratch_shapes=[
            pltpu.VMEM((tokens * key_heads * heads, depth), queries.dtype),
            pltpu.VMEM((blocks * 4 * key_heads, depth), keys.dtype),
            pltpu.SemaphoreType.DMA((Q_COPIES,)),
            pltpu.SemaphoreType.DMA((K_COPIES,)),
        ],
        compiler_params=pltpu.CompilerParams(vmem_limit_bytes=16 * 2 ** 20),
        name="pack",
    )(in_hbm(queries.reshape(-1, depth)), in_hbm(keys.reshape(-1, depth)))

    def swap(array, axis, size, bit):
        return lax.ppermute(array, axis, [(i, i ^ bit) for i in range(size)])

    columns = n_head * heads * QTILE
    buffers = 2 if nsel <= SPAN_ROWS else 1
    done = []
    for g in range(own):
        q_parts = list(packed[g * n_head:(g + 1) * n_head])
        for d in range(1, n_head):
            q_parts[d] = swap(q_parts[d], "head", n_head, d)
        k_parts = {0: packed[n_head * own + g]}
        bit = n_ctx // 2
        while bit:
            for j in list(k_parts):
                k_parts[j | bit] = swap(k_parts[j], "ctx", n_ctx, bit)
            bit //= 2
        last = g == own - 1
        done.append(pl.pallas_call(
            partial(unit_kernel if buffers == 2 else span_kernel, n_head, n_ctx),
            out_shape=jax.ShapeDtypeStruct((tokens, own, nsel) if last else (tokens, nsel), jnp.float32),
            in_specs=[smem, smem] + [vmem] * (n_head + n_ctx + len(done)),
            out_specs=vmem,
            scratch_shapes=[
                pltpu.VMEM((4, nsel, depth), keys.dtype),
                pltpu.VMEM((buffers, 4, nsel, columns), jnp.float32),
                pltpu.VMEM((buffers, 2, nsel, columns), jnp.float32),
                pltpu.VMEM((buffers, 2, 8 + nsel, LANES), jnp.float32),
            ],
            compiler_params=pltpu.CompilerParams(vmem_limit_bytes=(20 if buffers == 2 else 52) * 2 ** 20),
            cost_estimate=pl.CostEstimate(
                flops=2 * columns * tokens // QTILE * 4 * nsel * depth,
                bytes_accessed=4 * tokens * nsel,
                transcendentals=columns * tokens // QTILE * 4 * nsel,
            ),
            name="importance",
        )(span_start, tile_first, *q_parts, *[k_parts[j] for j in range(n_ctx)], *done))
    return done[-1]


def solution(mesh):
    placed = (
        P(("groups", "ctx"), None, "head", None),
        P(("groups", "ctx"), None, None, None),
        P("groups"),
        P(("groups", "ctx")),
    )
    return jax.shard_map(
        partial(per_device, mesh.shape["head"], mesh.shape["ctx"]),
        mesh=mesh,
        in_specs=placed,
        out_specs=P(("groups", "ctx"), "head", None),
        check_vma=False,
    )
```

time: 24.3 us -> 27.8 us (1.14)
  starting transfers between devices: 8.2 us -> 13.6 us
  waiting for transfers between devices: 7.12 us -> 3.69 us
  Pallas kernels: 8.17 us -> 8.96 us
  local copies, waits for them, and re-layouts: 0.01 us -> 0.65 us
    ppermute x6 -> x12, starting transfers between devices: 8.2 us -> 13.6 us  [swap(): return lax.ppermute(array, axis, [(i, i ^ bit) for i in range(size)])]
    ppermute x6 -> x12, waiting for transfers between devices: 7.12 us -> 3.69 us  [swap(): return lax.ppermute(array, axis, [(i, i ^ bit) for i in range(size)])]
    pallas_call x1 -> x2, Pallas kernels: 5.8 us -> 6.59 us  [per_device(): pl.pallas_call(partial(unit_kernel if buffers == 2 else span_kernel, n_he...]
    unnamed x2, local copies, waits for them, and re-layouts: 0.01 us -> 0.65 us
  transfers between devices with their start and end apart: 6 -> 12, of which waited for: 4 -> 3; matrix products, arithmetic and copies ran while one was open for 0% -> 0% of each run, Pallas kernels for 0% -> 10%
where the time goes in v8:
time: 27.8 us; the launch traced here: 27.7 us
  starting transfers between devices  13.6 us (49%)
  Pallas kernels  8.96 us (32%)
  waiting for transfers between devices  3.69 us (13%)
  between operations  0.73 us (3%)
  local copies, waits for them, and re-layouts  0.65 us (2%)
    ppermute x12, starting transfers between devices, swap(): return lax.ppermute(array, axis, [(i, i ^ bit) for i in range(size)])  13.6 us
    pallas_call x2, Pallas kernels, per_device(): pl.pallas_call(partial(unit_kernel if buffers == 2 else span_kernel, n_he...  6.59 us
    ppermute x12, waiting for transfers between devices, swap(): return lax.ppermute(array, axis, [(i, i ^ bit) for i in range(size)])  3.69 us
    pallas_call x1, Pallas kernels, per_device(): pl.pallas_call(partial(pack_kernel, n_head, key_heads, heads), out_shape=...  2.37 us
    unnamed x2, local copies, waits for them, and re-layouts  0.65 us
  transfers between devices with their start and end apart: 12, of which 3 were waited for; matrix products, arithmetic and copies ran while one was open for 0% of the time, Pallas kernels for 10%

profile of v8, /device:TPU:0, one launch (start us, length us, event | category | flops | bytes accessed | tf_op | source)
XLA Modules:
  0.0 27.7 jit_solution(519636739113837108)
XLA Ops:
  0.0 2.4 %pack.1 = (bf16[2,192,128]{2,1,0:T(8,128)(2,1)S(1)}, bf16[2,192,128]{2,1,0:T(8,128)(2,1)S(1)}, bf16[2,192,128]{2,1,0:T(8,128)(2,1)S(1)}, bf16[2,192,128]{2,1,0:T...) custom-call(bf16[3072,128]{1,0:T(8,128)(2,1)} %bitcast.2, ...), custom_call_target="tpu_custom_call" | custom-call | tf_op jit(solution)/shard_map/pack/pallas_call | solution.py:319
  2.4 4.1 %collective-permute-start.10 = (bf16[4,64,128]{2,1,0:T(8,128)(2,1)S(1)}, bf16[4,64,128]{2,1,0:T(8,128)(2,1)S(1)}, u32[]{:S(2)}, u32[]{:S(2)}) collective-permute-start(bf16[4,64,128]{2,1,0:T(8,128)(2,1)S(1)} %get-tuple-element.24.refs_4_), channel_id=1, source_target_pairs={{0,8},{4,12},{8,0},{12,4},{1,9},{5,13},{9,1},{13,5},{2,10},{6,14},... | collective-permute-start | bytes 196616 | tf_op jit(solution)/shard_map/ppermute | solution.py:335
  6.5 0.0 collective-permute-start.6
  6.5 1.5 %collective-permute-start.7 = (bf16[2,192,128]{2,1,0:T(8,128)(2,1)S(1)}, bf16[2,192,128]{2,1,0:T(8,128)(2,1)S(1)}, u32[]{:S(2)}, u32[]{:S(2)}) collective-permute-start(bf16[2,192,128]{2,1,0:T(8,128)(2,1)S(1)} %get-tuple-element.22), channel_id=1, source_target_pairs={{0,2},{1,3},{2,0},{3,1},{4,6},{5,7},{6,4},{7,5},{8,10},{9,11},{10,... | collective-permute-start | bytes 294920 | tf_op jit(solution)/shard_map/ppermute | solution.py:335
  8.0 1.6 %collective-permute-start.9 = (bf16[4,64,128]{2,1,0:T(8,128)(2,1)S(1)}, bf16[4,64,128]{2,1,0:T(8,128)(2,1)S(1)}, u32[]{:S(2)}, u32[]{:S(2)}) collective-permute-start(bf16[4,64,128]{2,1,0:T(8,128)(2,1)S(1)} %get-tuple-element.24.refs_4_), channel_id=1, source_target_pairs={{0,4},{4,0},{8,12},{12,8},{1,5},{5,1},{9,13},{13,9},{2,6},{6,2},{1... | collective-permute-start | bytes 196616 | tf_op jit(solution)/shard_map/ppermute | solution.py:335
  9.6 0.3 %collective-permute-start.4 = (bf16[4,64,128]{2,1,0:T(8,128)(2,1)S(1)}, bf16[4,64,128]{2,1,0:T(8,128)(2,1)S(1)}, u32[]{:S(2)}, u32[]{:S(2)}) collective-permute-start(bf16[4,64,128]{2,1,0:T(8,128)(2,1)S(1)} %get-tuple-element.19.refs_4_), channel_id=1, source_target_pairs={{0,8},{4,12},{8,0},{12,4},{1,9},{5,13},{9,1},{13,5},{2,10},{6,14},... | collective-permute-start | bytes 196616 | tf_op jit(solution)/shard_map/ppermute | solution.py:335
  9.9 0.2 collective-permute-done.10.refs_6_
  10.1 0.0 collective-permute-start.8
  10.1 2.1 %collective-permute-done.9.refs_5_ = bf16[4,64,128]{2,1,0:T(8,128)(2,1)S(1)} collective-permute-done((bf16[4,64,128]{2,1,0:T(8,128)(2,1)S(1)}, bf16[4,64,128]{2,1,0:T(8,128)(2,1)S(1)}, u32[]{:S(2)}, u32[]{:S(2)}) %collective-permute-start.9) | collective-permute-done | bytes 65568 | tf_op jit(solution)/shard_map/ppermute | solution.py:335
  12.2 2.2 %collective-permute-start.11 = (bf16[4,64,128]{2,1,0:T(8,128)(2,1)S(1)}, bf16[4,64,128]{2,1,0:T(8,128)(2,1)S(1)}, u32[]{:S(2)}, u32[]{:S(2)}) collective-permute-start(bf16[4,64,128]{2,1,0:T(8,128)(2,1)S(1)} %collective-permute-done.10.refs_6_), channel_id=1, source_target_pairs={{0,4},{4,0},{8,12},{12,8},{1,5},{5,1},{9,13},{13,9},{2,6},{6,2},{1... | collective-permute-start | bytes 196616 | tf_op jit(solution)/shard_map/ppermute | solution.py:335
  14.5 1.3 %collective-permute-done.4.refs_6_ = bf16[4,64,128]{2,1,0:T(8,128)(2,1)S(1)} collective-permute-done((bf16[4,64,128]{2,1,0:T(8,128)(2,1)S(1)}, bf16[4,64,128]{2,1,0:T(8,128)(2,1)S(1)}, u32[]{:S(2)}, u32[]{:S(2)}) %collective-permute-start.4) | collective-permute-done | bytes 65568 | tf_op jit(solution)/shard_map/ppermute | solution.py:335
  15.8 0.0 collective-permute-start
  15.8 0.0 collective-permute-done.6.refs_1_
  15.8 0.5 %collective-permute-start.1 = (bf16[2,192,128]{2,1,0:T(8,128)(2,1)S(1)}, bf16[2,192,128]{2,1,0:T(8,128)(2,1)S(1)}, u32[]{:S(2)}, u32[]{:S(2)}) collective-permute-start(bf16[2,192,128]{2,1,0:T(8,128)(2,1)S(1)} %get-tuple-element.17), channel_id=1, source_target_pairs={{0,2},{1,3},{2,0},{3,1},{4,6},{5,7},{6,4},{7,5},{8,10},{9,11},{10,... | collective-permute-start | bytes 294920 | tf_op jit(solution)/shard_map/ppermute | solution.py:335
  16.3 0.0 collective-permute-done.7.refs_2_
  16.3 1.3 %collective-permute-start.2 = (bf16[2,192,128]{2,1,0:T(8,128)(2,1)S(1)}, bf16[2,192,128]{2,1,0:T(8,128)(2,1)S(1)}, u32[]{:S(2)}, u32[]{:S(2)}) collective-permute-start(bf16[2,192,128]{2,1,0:T(8,128)(2,1)S(1)} %get-tuple-element.18), channel_id=1, source_target_pairs={{0,3},{1,2},{2,1},{3,0},{4,7},{5,6},{6,5},{7,4},{8,11},{9,10},{10,... | collective-permute-start | bytes 294920 | tf_op jit(solution)/shard_map/ppermute | solution.py:335
  17.7 0.0 collective-permute-done.8.refs_3_
  17.7 0.0 collective-permute-start.3
  17.7 0.0 collective-permute-done.11.refs_7_
  17.7 2.0 %collective-permute-start.5 = (bf16[4,64,128]{2,1,0:T(8,128)(2,1)S(1)}, bf16[4,64,128]{2,1,0:T(8,128)(2,1)S(1)}, u32[]{:S(2)}, u32[]{:S(2)}) collective-permute-start(bf16[4,64,128]{2,1,0:T(8,128)(2,1)S(1)} %collective-permute-done.4.refs_6_), channel_id=1, source_target_pairs={{0,4},{4,0},{8,12},{12,8},{1,5},{5,1},{9,13},{13,9},{2,6},{6,2},{1... | collective-permute-start | bytes 196616 | tf_op jit(solution)/shard_map/ppermute | solution.py:335
  20.4 0.0 copy-start
  20.4 0.6 %copy-done = s32[3]{0:T(128)S(1)} copy-done((s32[3]{0:T(128)S(1)}, s32[3]{0:T(128)}, u32[]{:S(2)}) %copy-start) | copy-done | bytes 36
  21.0 2.9 %importance.2.refs_8_ = f32[192,256]{1,0:T(8,128)S(1)} custom-call(s32[1]{0:T(128)S(6)} %copy.5.start_ref, s32[3]{0:T(128)S(1)} %copy-done, bf16[2,192,128]{2,1,0:T(8,128)(2,1)S(1)} %get-tuple-element.20.refs_0_, bf16[2,192,128]{2,1,0:T(8,128)(2,1)S(1)} %collective-permute-done.6.refs_1_, bf16[2,192,128]{2,1,0:T(8,128)(2,1)S(1)} %collective-permute-done.7.refs_2_, ...), custom_call_target="tpu_custom_call" | custom-call | flops 402653184 | bytes 196608 | tf_op jit(solution)/shard_map/importance/pallas_call | solution.py:351
  23.9 0.0 collective-permute-done.3.refs_5_
  23.9 0.0 collective-permute-done.refs_1_
  24.0 0.0 collective-permute-done.1.refs_2_
  24.0 0.0 collective-permute-done.2.refs_3_
  24.0 0.0 collective-permute-done.5.refs_7_
  24.0 3.7 %importance.3 = f32[192,2,256]{2,1,0:T(2,128)} custom-call(s32[1]{0:T(128)S(6)} %copy.5.start_ref, s32[3]{0:T(128)S(1)} %copy-done, bf16[2,192,128]{2,1,0:T(8,128)(2,1)S(1)} %get-tuple-element.15.refs_0_, bf16[2,192,128]{2,1,0:T(8,128)(2,1)S(1)} %collective-permute-done.refs_1_, bf16[2,192,128]{2,1,0:T(8,128)(2,1)S(1)} %collective-permute-done.1.refs_2_, ...), custom_call_target="tpu_custom_call" | custom-call | flops 402653184 | bytes 196608 | tf_op jit(solution)/shard_map/importance/pallas_call | solution.py:351
Async XLA Ops:
  2.4 7.8 %collective-permute-start.10 = (bf16[4,64,128]{2,1,0:T(8,128)(2,1)S(1)}, bf16[4,64,128]{2,1,0:T(8,128)(2,1)S(1)}, u32[]{:S(2)}, u32[]{:S(2)}) collective-permute-start(bf16[4,64,128]{2,1,0:T(8,128)(2,1)S(1)} %get-tuple-element.24.refs_4_), channel_id=1, source_target_pairs={{0,8},{4,12},{8,0},{12,4},{1,9},{5,13},{9,1},{13,5},{2,10},{6,14},... | collective-permute-start | bytes 196616 | tf_op jit(solution)/shard_map/ppermute | solution.py:335
  6.5 9.3 %collective-permute-start.6 = (bf16[2,192,128]{2,1,0:T(8,128)(2,1)S(1)}, bf16[2,192,128]{2,1,0:T(8,128)(2,1)S(1)}, u32[]{:S(2)}, u32[]{:S(2)}) collective-permute-start(bf16[2,192,128]{2,1,0:T(8,128)(2,1)S(1)} %get-tuple-element.21), channel_id=1, source_target_pairs={{0,1},{1,0},{2,3},{3,2},{4,5},{5,4},{6,7},{7,6},{8,9},{9,8},{10,11... | collective-permute-start | bytes 294920 | tf_op jit(solution)/shard_map/ppermute | solution.py:335
  6.5 9.9 %collective-permute-start.7 = (bf16[2,192,128]{2,1,0:T(8,128)(2,1)S(1)}, bf16[2,192,128]{2,1,0:T(8,128)(2,1)S(1)}, u32[]{:S(2)}, u32[]{:S(2)}) collective-permute-start(bf16[2,192,128]{2,1,0:T(8,128)(2,1)S(1)} %get-tuple-element.22), channel_id=1, source_target_pairs={{0,2},{1,3},{2,0},{3,1},{4,6},{5,7},{6,4},{7,5},{8,10},{9,11},{10,... | collective-permute-start | bytes 294920 | tf_op jit(solution)/shard_map/ppermute | solution.py:335
  8.0 4.3 %collective-permute-start.9 = (bf16[4,64,128]{2,1,0:T(8,128)(2,1)S(1)}, bf16[4,64,128]{2,1,0:T(8,128)(2,1)S(1)}, u32[]{:S(2)}, u32[]{:S(2)}) collective-permute-start(bf16[4,64,128]{2,1,0:T(8,128)(2,1)S(1)} %get-tuple-element.24.refs_4_), channel_id=1, source_target_pairs={{0,4},{4,0},{8,12},{12,8},{1,5},{5,1},{9,13},{13,9},{2,6},{6,2},{1... | collective-permute-start | bytes 196616 | tf_op jit(solution)/shard_map/ppermute | solution.py:335
  9.6 6.2 %collective-permute-start.4 = (bf16[4,64,128]{2,1,0:T(8,128)(2,1)S(1)}, bf16[4,64,128]{2,1,0:T(8,128)(2,1)S(1)}, u32[]{:S(2)}, u32[]{:S(2)}) collective-permute-start(bf16[4,64,128]{2,1,0:T(8,128)(2,1)S(1)} %get-tuple-element.19.refs_4_), channel_id=1, source_target_pairs={{0,8},{4,12},{8,0},{12,4},{1,9},{5,13},{9,1},{13,5},{2,10},{6,14},... | collective-permute-start | bytes 196616 | tf_op jit(solution)/shard_map/ppermute | solution.py:335
  10.1 7.5 %collective-permute-start.8 = (bf16[2,192,128]{2,1,0:T(8,128)(2,1)S(1)}, bf16[2,192,128]{2,1,0:T(8,128)(2,1)S(1)}, u32[]{:S(2)}, u32[]{:S(2)}) collective-permute-start(bf16[2,192,128]{2,1,0:T(8,128)(2,1)S(1)} %get-tuple-element.23), channel_id=1, source_target_pairs={{0,3},{1,2},{2,1},{3,0},{4,7},{5,6},{6,5},{7,4},{8,11},{9,10},{10,... | collective-permute-start | bytes 294920 | tf_op jit(solution)/shard_map/ppermute | solution.py:335
  12.2 5.4 %collective-permute-start.11 = (bf16[4,64,128]{2,1,0:T(8,128)(2,1)S(1)}, bf16[4,64,128]{2,1,0:T(8,128)(2,1)S(1)}, u32[]{:S(2)}, u32[]{:S(2)}) collective-permute-start(bf16[4,64,128]{2,1,0:T(8,128)(2,1)S(1)} %collective-permute-done.10.refs_6_), channel_id=1, source_target_pairs={{0,4},{4,0},{8,12},{12,8},{1,5},{5,1},{9,13},{13,9},{2,6},{6,2},{1... | collective-permute-start | bytes 196616 | tf_op jit(solution)/shard_map/ppermute | solution.py:335
  15.8 8.2 %collective-permute-start = (bf16[2,192,128]{2,1,0:T(8,128)(2,1)S(1)}, bf16[2,192,128]{2,1,0:T(8,128)(2,1)S(1)}, u32[]{:S(2)}, u32[]{:S(2)}) collective-permute-start(bf16[2,192,128]{2,1,0:T(8,128)(2,1)S(1)} %get-tuple-element.16), channel_id=1, source_target_pairs={{0,1},{1,0},{2,3},{3,2},{4,5},{5,4},{6,7},{7,6},{8,9},{9,8},{10,11... | collective-permute-start | bytes 294920 | tf_op jit(solution)/shard_map/ppermute | solution.py:335
  15.8 8.2 %collective-permute-start.1 = (bf16[2,192,128]{2,1,0:T(8,128)(2,1)S(1)}, bf16[2,192,128]{2,1,0:T(8,128)(2,1)S(1)}, u32[]{:S(2)}, u32[]{:S(2)}) collective-permute-start(bf16[2,192,128]{2,1,0:T(8,128)(2,1)S(1)} %get-tuple-element.17), channel_id=1, source_target_pairs={{0,2},{1,3},{2,0},{3,1},{4,6},{5,7},{6,4},{7,5},{8,10},{9,11},{10,... | collective-permute-start | bytes 294920 | tf_op jit(solution)/shard_map/ppermute | solution.py:335
  16.3 7.6 %collective-permute-start.2 = (bf16[2,192,128]{2,1,0:T(8,128)(2,1)S(1)}, bf16[2,192,128]{2,1,0:T(8,128)(2,1)S(1)}, u32[]{:S(2)}, u32[]{:S(2)}) collective-permute-start(bf16[2,192,128]{2,1,0:T(8,128)(2,1)S(1)} %get-tuple-element.18), channel_id=1, source_target_pairs={{0,3},{1,2},{2,1},{3,0},{4,7},{5,6},{6,5},{7,4},{8,11},{9,10},{10,... | collective-permute-start | bytes 294920 | tf_op jit(solution)/shard_map/ppermute | solution.py:335
  17.7 6.3 %collective-permute-start.3 = (bf16[4,64,128]{2,1,0:T(8,128)(2,1)S(1)}, bf16[4,64,128]{2,1,0:T(8,128)(2,1)S(1)}, u32[]{:S(2)}, u32[]{:S(2)}) collective-permute-start(bf16[4,64,128]{2,1,0:T(8,128)(2,1)S(1)} %get-tuple-element.19.refs_4_), channel_id=1, source_target_pairs={{0,4},{4,0},{8,12},{12,8},{1,5},{5,1},{9,13},{13,9},{2,6},{6,2},{1... | collective-permute-start | bytes 196616 | tf_op jit(solution)/shard_map/ppermute | solution.py:335
  17.7 6.3 %collective-permute-start.5 = (bf16[4,64,128]{2,1,0:T(8,128)(2,1)S(1)}, bf16[4,64,128]{2,1,0:T(8,128)(2,1)S(1)}, u32[]{:S(2)}, u32[]{:S(2)}) collective-permute-start(bf16[4,64,128]{2,1,0:T(8,128)(2,1)S(1)} %collective-permute-done.4.refs_6_), channel_id=1, source_target_pairs={{0,4},{4,0},{8,12},{12,8},{1,5},{5,1},{9,13},{13,9},{2,6},{6,2},{1... | collective-permute-start | bytes 196616 | tf_op jit(solution)/shard_map/ppermute | solution.py:335
  20.4 0.7 %copy-start = (s32[3]{0:T(128)S(1)}, s32[3]{0:T(128)}, u32[]{:S(2)}) copy-start(s32[3]{0:T(128)} %first_ref.3) | copy-start | bytes 40

commit v9 on v7

--- a/solution.py
+++ b/solution.py
@@ -15,6 +15,8 @@
 LANES = 128
 CHUNK = 512
 SPAN_ROWS = 256
+BLOCK = 64
+SAFE = 64.0
 MASKED = -1e30
 NT = (((1,), (1,)), ((), ()))
 
@@ -126,49 +128,39 @@
     scale = math.log2(math.e) / math.sqrt(depth)
     factor = nsel / (2.0 * n_head * heads)
     tiles_n = n_head * heads * QTILE // LANES
-    block = 64
     gather_keys(n_ctx, k_refs, keys)
     units = [(t, g) for t in range(tokens // QTILE) for g in range(own)]
-    tops, weights = {}, {}
-
-    def products(u):
+    weights, tops = {}, []
+
+    def exponentials(u):
         t, g = units[u]
         columns = tile_columns(q_refs, g, t * QTILE)
         row4, reach = limits(n_ctx, tokens, t * QTILE, start_ref)
         first = first_ref[t]
-        top = [None] * tiles_n
-        for base in range(0, nsel, block):
-            rows = jnp.concatenate([keys[g, s, base:base + block, :] for s in range(4)], axis=0)
+        top, total = [None] * tiles_n, [None] * tiles_n
+        for base in range(0, nsel, BLOCK):
+            rows = jnp.concatenate([keys[g, s, base:base + BLOCK, :] for s in range(4)], axis=0)
             piece = lax.dot_general(rows, columns, NT, preferred_element_type=jnp.float32)
-            for s in range(4):
-                for r in range(0, block, 8):
-                    mask = visible(nsel, n_ctx * tokens, base + r, s, first, row4, reach)
-                    for n in range(tiles_n):
-                        part = piece[s * block + r:s * block + r + 8, n * LANES:(n + 1) * LANES]
+            for r in range(0, BLOCK, 8):
+                masks = [visible(nsel, n_ctx * tokens, base + r, s, first, row4, reach) for s in range(4)]
+                for n in range(tiles_n):
+                    at = slice(n * LANES, (n + 1) * LANES)
+                    parts = []
+                    for s, mask in enumerate(masks):
+                        part = piece[s * BLOCK + r:s * BLOCK + r + 8, at]
                         if mask is not None:
                             part = jnp.where(mask, part, MASKED)
-                        scores[u % 2, s, base + r:base + r + 8, n * LANES:(n + 1) * LANES] = part
                         top[n] = part if top[n] is None else jnp.maximum(top[n], part)
+                        parts.append(jnp.exp2(part * scale))
+                    rest = parts[1] + parts[2] + parts[3]
+                    pooled[u % 2, 0, base + r:base + r + 8, at] = parts[0]
+                    pooled[u % 2, 1, base + r:base + r + 8, at] = rest
+                    both = parts[0] + rest
+                    total[n] = both if total[n] is None else total[n] + both
                 yield
-        tops[u] = top
-
-    def exponentials(u):
-        weights[u] = []
-        for n in range(tiles_n):
-            top, total = tops[u][n], None
-            at = slice(n * LANES, (n + 1) * LANES)
-            for r in range(0, nsel, 8):
-                parts = [jnp.exp2((scores[u % 2, s, r:r + 8, at] - top) * scale) for s in range(4)]
-                rest = parts[1] + parts[2] + parts[3]
-                pooled[u % 2, 0, r:r + 8, at] = parts[0]
-                pooled[u % 2, 1, r:r + 8, at] = rest
-                both = parts[0] + rest
-                total = both if total is None else total + both
-                if r % 32 == 24:
-                    yield
-            peak = jnp.max(top, axis=0, keepdims=True)
-            lowered = jnp.exp2((top - peak) * scale)
-            weights[u].append(lowered * (factor / jnp.sum(total * lowered, axis=0, keepdims=True)))
+        weights[u] = [factor / jnp.sum(part, axis=0, keepdims=True) for part in total]
+        for part in top:
+            tops.append(jnp.abs(jnp.max(part, axis=0, keepdims=True)))
 
     def sums(u):
         t, g = units[u]
@@ -182,24 +174,34 @@
                 rest = second if rest is None else rest + second
             lined[u % 2, 0, 8 + r:16 + r, :] = lead
             lined[u % 2, 1, 8 + r:16 + r, :] = lead + 2.0 * rest
-            if r % 16 == 8:
-                yield
+            yield
         turned = (lined[u % 2, 0, 8:8 + nsel, :] + lined[u % 2, 1, 7:7 + nsel, :]).T
         out_ref[t * QTILE:(t + 1) * QTILE, g, :] = turned[:QTILE] + turned[QTILE:]
         yield
 
-    for step in range(len(units) + 2):
+    for step in range(len(units) + 1):
         stages = []
         if step < len(units):
-            stages.append((4 * nsel // block, products(step)))
-        if 0 <= step - 1 < len(units):
-            stages.append((tiles_n * nsel // 32, exponentials(step - 1)))
-        if step >= 2:
-            stages.append((nsel // 16 + 1, sums(step - 2)))
+            stages.append((nsel // 8, exponentials(step)))
+        if step >= 1:
+            stages.append((nsel // 8 + 1, sums(step - 1)))
         interleave(*stages)
 
+    worst = tops[0]
+    for part in tops[1:]:
+        worst = jnp.maximum(worst, part)
+
+    @pl.when(jnp.max(worst) * scale > SAFE)
+    def _():
+        shifted(n_head, n_ctx, start_ref, first_ref, *refs)
+
 
 def span_kernel(n_head, n_ctx, start_ref, first_ref, *refs):
+    gather_keys(n_ctx, refs[n_head:n_head + n_ctx], refs[n_head + n_ctx + 1])
+    shifted(n_head, n_ctx, start_ref, first_ref, *refs)
+
+
+def shifted(n_head, n_ctx, start_ref, first_ref, *refs):
     q_refs, k_refs = refs[:n_head], refs[n_head:n_head + n_ctx]
     out_ref, keys, scores, pooled, lined = refs[n_head + n_ctx:]
     own, heads, tokens, depth = q_refs[0].shape
@@ -214,8 +216,6 @@
 
     def over_spans(body, carry):
         return lax.fori_loop(0, spans, lambda n, c: body(pl.multiple_of(n * span, span), c), carry)
-
-    gather_keys(n_ctx, k_refs, keys)
 
     def tile(index, _):
         begin = pl.multiple_of(index * QTILE, QTILE)
@@ -338,7 +338,7 @@
         out_specs=vmem,
         scratch_shapes=[
             pltpu.VMEM((own, 4, nsel, depth), keys.dtype),
-            pltpu.VMEM((buffers, 4, nsel, columns), jnp.float32),
+            pltpu.VMEM((1, 4, nsel, columns), jnp.float32),
             pltpu.VMEM((buffers, 2, nsel, columns), jnp.float32),
             pltpu.VMEM((buffers, 2, 8 + nsel, LANES), jnp.float32),
         ],

time: 24.3 us -> 28.2 us (1.16)
  Pallas kernels: 8.17 us -> 12 us
    pallas_call x1, Pallas kernels: 5.8 us -> 9.66 us  [per_device(): pl.pallas_call(partial(unit_kernel if buffers == 2 else span_kernel, n_he...]
where the time goes in v9:
time: 28.2 us; the launch traced here: 28 us
  Pallas kernels  12 us (43%)
  starting transfers between devices  8.2 us (29%)
  waiting for transfers between devices  7.12 us (25%)
  between operations  0.67 us (2%)
    pallas_call x1, Pallas kernels, per_device(): pl.pallas_call(partial(unit_kernel if buffers == 2 else span_kernel, n_he...  9.66 us
    ppermute x6, starting transfers between devices, swap(): return lax.ppermute(array, axis, [(i, i ^ bit) for i in range(size)])  8.2 us
    ppermute x6, waiting for transfers between devices, swap(): return lax.ppermute(array, axis, [(i, i ^ bit) for i in range(size)])  7.12 us
    pallas_call x1, Pallas kernels, per_device(): pl.pallas_call(partial(pack_kernel, n_head, key_heads, heads), out_shape=...  2.37 us
  transfers between devices with their start and end apart: 6, of which 4 were waited for; matrix products, arithmetic and copies ran while one was open for 0% of the time, Pallas kernels for 0%

profile of v9, /device:TPU:0, one launch (start us, length us, event | category | flops | bytes accessed | tf_op | source)
XLA Modules:
  0.0 28.0 jit_solution(9409666900904133052)
XLA Ops:
  0.0 2.4 %pack.1 = (bf16[2,2,192,128]{3,2,1,0:T(8,128)(2,1)S(1)}, bf16[2,2,192,128]{3,2,1,0:T(8,128)(2,1)S(1)}, bf16[2,2,192,128]{3,2,1,0:T(8,128)(2,1)S(1)}, bf16[2,2,19...) custom-call(bf16[3072,128]{1,0:T(8,128)(2,1)} %bitcast.2, bf16[2048,128]{1,0:T(8,128)(2,1)} %bitcast.3), custom_call_target="tpu_custom_call" | custom-call | tf_op jit(solution)/shard_map/pack/pallas_call | solution.py:304
  2.4 4.1 %collective-permute-start.4 = (bf16[2,4,64,128]{3,2,1,0:T(8,128)(2,1)S(1)}, bf16[2,4,64,128]{3,2,1,0:T(8,128)(2,1)S(1)}, u32[]{:S(2)}, u32[]{:S(2)}) collective-permute-start(bf16[2,4,64,128]{3,2,1,0:T(8,128)(2,1)S(1)} %get-tuple-element.14.refs_4_), channel_id=1, source_target_pairs={{0,8},{4,12},{8,0},{12,4},{1,9},{5,13},{9,1},{13,5},{2,10},{6,14},... | collective-permute-start | bytes 393224 | tf_op jit(solution)/shard_map/ppermute | solution.py:321
  6.5 0.0 collective-permute-start
  6.5 1.5 %collective-permute-start.1 = (bf16[2,2,192,128]{3,2,1,0:T(8,128)(2,1)S(1)}, bf16[2,2,192,128]{3,2,1,0:T(8,128)(2,1)S(1)}, u32[]{:S(2)}, u32[]{:S(2)}) collective-permute-start(bf16[2,2,192,128]{3,2,1,0:T(8,128)(2,1)S(1)} %get-tuple-element.12), channel_id=1, source_target_pairs={{0,2},{1,3},{2,0},{3,1},{4,6},{5,7},{6,4},{7,5},{8,10},{9,11},{10,... | collective-permute-start | bytes 589832 | tf_op jit(solution)/shard_map/ppermute | solution.py:321
  8.0 0.4 %collective-permute-start.2 = (bf16[2,2,192,128]{3,2,1,0:T(8,128)(2,1)S(1)}, bf16[2,2,192,128]{3,2,1,0:T(8,128)(2,1)S(1)}, u32[]{:S(2)}, u32[]{:S(2)}) collective-permute-start(bf16[2,2,192,128]{3,2,1,0:T(8,128)(2,1)S(1)} %get-tuple-element.13), channel_id=1, source_target_pairs={{0,3},{1,2},{2,1},{3,0},{4,7},{5,6},{6,5},{7,4},{8,11},{9,10},{10,... | collective-permute-start | bytes 589832 | tf_op jit(solution)/shard_map/ppermute | solution.py:321
  8.3 1.6 %collective-permute-start.3 = (bf16[2,4,64,128]{3,2,1,0:T(8,128)(2,1)S(1)}, bf16[2,4,64,128]{3,2,1,0:T(8,128)(2,1)S(1)}, u32[]{:S(2)}, u32[]{:S(2)}) collective-permute-start(bf16[2,4,64,128]{3,2,1,0:T(8,128)(2,1)S(1)} %get-tuple-element.14.refs_4_), channel_id=1, source_target_pairs={{0,4},{4,0},{8,12},{12,8},{1,5},{5,1},{9,13},{13,9},{2,6},{6,2},{1... | collective-permute-start | bytes 393224 | tf_op jit(solution)/shard_map/ppermute | solution.py:321
  9.9 3.0 %collective-permute-done.4.refs_6_ = bf16[2,4,64,128]{3,2,1,0:T(8,128)(2,1)S(1)} collective-permute-done((bf16[2,4,64,128]{3,2,1,0:T(8,128)(2,1)S(1)}, bf16[2,4,64,128]{3,2,1,0:T(8,128)(2,1)S(1)}, u32[]{:S(2)}, u32[]{:S(2)}) %collective-permute-start.4) | collective-permute-done | bytes 131104 | tf_op jit(solution)/shard_map/ppermute | solution.py:321
  12.9 0.7 %collective-permute-start.5 = (bf16[2,4,64,128]{3,2,1,0:T(8,128)(2,1)S(1)}, bf16[2,4,64,128]{3,2,1,0:T(8,128)(2,1)S(1)}, u32[]{:S(2)}, u32[]{:S(2)}) collective-permute-start(bf16[2,4,64,128]{3,2,1,0:T(8,128)(2,1)S(1)} %collective-permute-done.4.refs_6_), channel_id=1, source_target_pairs={{0,4},{4,0},{8,12},{12,8},{1,5},{5,1},{9,13},{13,9},{2,6},{6,2},{1... | collective-permute-start | bytes 393224 | tf_op jit(solution)/shard_map/ppermute | solution.py:321
  14.2 0.0 copy-start
  14.2 1.5 %collective-permute-done.3.refs_5_ = bf16[2,4,64,128]{3,2,1,0:T(8,128)(2,1)S(1)} collective-permute-done((bf16[2,4,64,128]{3,2,1,0:T(8,128)(2,1)S(1)}, bf16[2,4,64,128]{3,2,1,0:T(8,128)(2,1)S(1)}, u32[]{:S(2)}, u32[]{:S(2)}) %collective-permute-start.3) | collective-permute-done | bytes 131104 | tf_op jit(solution)/shard_map/ppermute | solution.py:321
  15.7 0.0 collective-permute-done.refs_1_
  15.7 0.0 collective-permute-done.1.refs_2_
  15.7 1.9 %collective-permute-done.2.refs_3_ = bf16[2,2,192,128]{3,2,1,0:T(8,128)(2,1)S(1)} collective-permute-done((bf16[2,2,192,128]{3,2,1,0:T(8,128)(2,1)S(1)}, bf16[2,2,192,128]{3,2,1,0:T(8,128)(2,1)S(1)}, u32[]{:S(2)}, u32[]{:S(2)}) %collective-permute-start.2) | collective-permute-done | bytes 196640 | tf_op jit(solution)/shard_map/ppermute | solution.py:321
  17.6 0.7 %collective-permute-done.5.refs_7_ = bf16[2,4,64,128]{3,2,1,0:T(8,128)(2,1)S(1)} collective-permute-done((bf16[2,4,64,128]{3,2,1,0:T(8,128)(2,1)S(1)}, bf16[2,4,64,128]{3,2,1,0:T(8,128)(2,1)S(1)}, u32[]{:S(2)}, u32[]{:S(2)}) %collective-permute-start.5) | collective-permute-done | bytes 131104 | tf_op jit(solution)/shard_map/ppermute | solution.py:321
  18.4 0.0 copy-done
  18.4 9.7 %importance.1 = f32[192,2,256]{2,1,0:T(2,128)} custom-call(s32[1]{0:T(128)S(6)} %copy.5.start_ref, s32[3]{0:T(128)S(1)} %copy-done, bf16[2,2,192,128]{3,2,1,0:T(8,128)(2,1)S(1)} %get-tuple-element.10.refs_0_, bf16[2,2,192,128]{3,2,1,0:T(8,128)(2,1)S(1)} %collective-permute-done.refs_1_, bf16[2,2,192,128]{3,2,1,0:T(8,128)(2,1)S(1)} %collective-permute-done.1.refs_2_, ...), custom_call_target="tpu_custom_call" | custom-call | tf_op jit(solution)/shard_map/importance/pallas_call | solution.py:334
Async XLA Ops:
  2.4 10.5 %collective-permute-start.4 = (bf16[2,4,64,128]{3,2,1,0:T(8,128)(2,1)S(1)}, bf16[2,4,64,128]{3,2,1,0:T(8,128)(2,1)S(1)}, u32[]{:S(2)}, u32[]{:S(2)}) collective-permute-start(bf16[2,4,64,128]{3,2,1,0:T(8,128)(2,1)S(1)} %get-tuple-element.14.refs_4_), channel_id=1, source_target_pairs={{0,8},{4,12},{8,0},{12,4},{1,9},{5,13},{9,1},{13,5},{2,10},{6,14},... | collective-permute-start | bytes 393224 | tf_op jit(solution)/shard_map/ppermute | solution.py:321
  6.5 9.2 %collective-permute-start = (bf16[2,2,192,128]{3,2,1,0:T(8,128)(2,1)S(1)}, bf16[2,2,192,128]{3,2,1,0:T(8,128)(2,1)S(1)}, u32[]{:S(2)}, u32[]{:S(2)}) collective-permute-start(bf16[2,2,192,128]{3,2,1,0:T(8,128)(2,1)S(1)} %get-tuple-element.11), channel_id=1, source_target_pairs={{0,1},{1,0},{2,3},{3,2},{4,5},{5,4},{6,7},{7,6},{8,9},{9,8},{10,11... | collective-permute-start | bytes 589832 | tf_op jit(solution)/shard_map/ppermute | solution.py:321
  6.5 9.2 %collective-permute-start.1 = (bf16[2,2,192,128]{3,2,1,0:T(8,128)(2,1)S(1)}, bf16[2,2,192,128]{3,2,1,0:T(8,128)(2,1)S(1)}, u32[]{:S(2)}, u32[]{:S(2)}) collective-permute-start(bf16[2,2,192,128]{3,2,1,0:T(8,128)(2,1)S(1)} %get-tuple-element.12), channel_id=1, source_target_pairs={{0,2},{1,3},{2,0},{3,1},{4,6},{5,7},{6,4},{7,5},{8,10},{9,11},{10,... | collective-permute-start | bytes 589832 | tf_op jit(solution)/shard_map/ppermute | solution.py:321
  8.0 9.6 %collective-permute-start.2 = (bf16[2,2,192,128]{3,2,1,0:T(8,128)(2,1)S(1)}, bf16[2,2,192,128]{3,2,1,0:T(8,128)(2,1)S(1)}, u32[]{:S(2)}, u32[]{:S(2)}) collective-permute-start(bf16[2,2,192,128]{3,2,1,0:T(8,128)(2,1)S(1)} %get-tuple-element.13), channel_id=1, source_target_pairs={{0,3},{1,2},{2,1},{3,0},{4,7},{5,6},{6,5},{7,4},{8,11},{9,10},{10,... | collective-permute-start | bytes 589832 | tf_op jit(solution)/shard_map/ppermute | solution.py:321
  8.3 7.3 %collective-permute-start.3 = (bf16[2,4,64,128]{3,2,1,0:T(8,128)(2,1)S(1)}, bf16[2,4,64,128]{3,2,1,0:T(8,128)(2,1)S(1)}, u32[]{:S(2)}, u32[]{:S(2)}) collective-permute-start(bf16[2,4,64,128]{3,2,1,0:T(8,128)(2,1)S(1)} %get-tuple-element.14.refs_4_), channel_id=1, source_target_pairs={{0,4},{4,0},{8,12},{12,8},{1,5},{5,1},{9,13},{13,9},{2,6},{6,2},{1... | collective-permute-start | bytes 393224 | tf_op jit(solution)/shard_map/ppermute | solution.py:321
  12.9 5.5 %collective-permute-start.5 = (bf16[2,4,64,128]{3,2,1,0:T(8,128)(2,1)S(1)}, bf16[2,4,64,128]{3,2,1,0:T(8,128)(2,1)S(1)}, u32[]{:S(2)}, u32[]{:S(2)}) collective-permute-start(bf16[2,4,64,128]{3,2,1,0:T(8,128)(2,1)S(1)} %collective-permute-done.4.refs_6_), channel_id=1, source_target_pairs={{0,4},{4,0},{8,12},{12,8},{1,5},{5,1},{9,13},{13,9},{2,6},{6,2},{1... | collective-permute-start | bytes 393224 | tf_op jit(solution)/shard_map/ppermute | solution.py:321
  14.2 4.2 %copy-start = (s32[3]{0:T(128)S(1)}, s32[3]{0:T(128)}, u32[]{:S(2)}) copy-start(s32[3]{0:T(128)} %first_ref.1) | copy-start | bytes 40

commit v10 on v9

--- a/solution.py
+++ b/solution.py
@@ -16,7 +16,7 @@
 CHUNK = 512
 SPAN_ROWS = 256
 BLOCK = 64
-SAFE = 64.0
+SAFE = 2.0 ** 64
 MASKED = -1e30
 NT = (((1,), (1,)), ((), ()))
 
@@ -122,7 +122,7 @@
 
 def unit_kernel(n_head, n_ctx, start_ref, first_ref, *refs):
     q_refs, k_refs = refs[:n_head], refs[n_head:n_head + n_ctx]
-    out_ref, keys, scores, pooled, lined = refs[n_head + n_ctx:]
+    out_hbm, keys, scores, pooled, lined, out_ref, sems = refs[n_head + n_ctx:]
     own, heads, tokens, depth = q_refs[0].shape
     nsel = keys.shape[2]
     scale = math.log2(math.e) / math.sqrt(depth)
@@ -130,14 +130,18 @@
     tiles_n = n_head * heads * QTILE // LANES
     gather_keys(n_ctx, k_refs, keys)
     units = [(t, g) for t in range(tokens // QTILE) for g in range(own)]
-    weights, tops = {}, []
+    weights, totals = {}, []
+    sent = [
+        pltpu.make_async_copy(out_ref.at[pl.ds(t * QTILE, QTILE)], out_hbm.at[pl.ds(t * QTILE, QTILE)], sems.at[t])
+        for t in range(tokens // QTILE)
+    ]
 
     def exponentials(u):
         t, g = units[u]
         columns = tile_columns(q_refs, g, t * QTILE)
         row4, reach = limits(n_ctx, tokens, t * QTILE, start_ref)
         first = first_ref[t]
-        top, total = [None] * tiles_n, [None] * tiles_n
+        total = [None] * tiles_n
         for base in range(0, nsel, BLOCK):
             rows = jnp.concatenate([keys[g, s, base:base + BLOCK, :] for s in range(4)], axis=0)
             piece = lax.dot_general(rows, columns, NT, preferred_element_type=jnp.float32)
@@ -150,7 +154,6 @@
                         part = piece[s * BLOCK + r:s * BLOCK + r + 8, at]
                         if mask is not None:
                             part = jnp.where(mask, part, MASKED)
-                        top[n] = part if top[n] is None else jnp.maximum(top[n], part)
                         parts.append(jnp.exp2(part * scale))
                     rest = parts[1] + parts[2] + parts[3]
                     pooled[u % 2, 0, base + r:base + r + 8, at] = parts[0]
@@ -158,9 +161,9 @@
                     both = parts[0] + rest
                     total[n] = both if total[n] is None else total[n] + both
                 yield
-        weights[u] = [factor / jnp.sum(part, axis=0, keepdims=True) for part in total]
-        for part in top:
-            tops.append(jnp.abs(jnp.max(part, axis=0, keepdims=True)))
+        total = [jnp.sum(part, axis=0, keepdims=True) for part in total]
+        weights[u] = [factor / part for part in total]
+        totals.extend(total)
 
     def sums(u):
         t, g = units[u]
@@ -177,6 +180,8 @@
             yield
         turned = (lined[u % 2, 0, 8:8 + nsel, :] + lined[u % 2, 1, 7:7 + nsel, :]).T
         out_ref[t * QTILE:(t + 1) * QTILE, g, :] = turned[:QTILE] + turned[QTILE:]
+        if g == own - 1:
+            sent[t].start()
         yield
 
     for step in range(len(units) + 1):
@@ -187,23 +192,29 @@
             stages.append((nsel // 8 + 1, sums(step - 1)))
         interleave(*stages)
 
-    worst = tops[0]
-    for part in tops[1:]:
-        worst = jnp.maximum(worst, part)
-
-    @pl.when(jnp.max(worst) * scale > SAFE)
+    least, most = totals[0], totals[0]
+    for part in totals[1:]:
+        least, most = jnp.minimum(least, part), jnp.maximum(most, part)
+    safe = (jnp.min(least) >= 1.0 / SAFE) & (jnp.max(most) <= SAFE)
+    for copy in sent:
+        copy.wait()
+
+    @pl.when(jnp.logical_not(safe))
     def _():
-        shifted(n_head, n_ctx, start_ref, first_ref, *refs)
+        shifted(n_head, n_ctx, start_ref, first_ref, q_refs, out_ref, keys, scores, pooled, lined)
+        for copy in sent:
+            copy.start()
+        for copy in sent:
+            copy.wait()
 
 
 def span_kernel(n_head, n_ctx, start_ref, first_ref, *refs):
-    gather_keys(n_ctx, refs[n_head:n_head + n_ctx], refs[n_head + n_ctx + 1])
-    shifted(n_head, n_ctx, start_ref, first_ref, *refs)
-
-
-def shifted(n_head, n_ctx, start_ref, first_ref, *refs):
-    q_refs, k_refs = refs[:n_head], refs[n_head:n_head + n_ctx]
     out_ref, keys, scores, pooled, lined = refs[n_head + n_ctx:]
+    gather_keys(n_ctx, refs[n_head:n_head + n_ctx], keys)
+    shifted(n_head, n_ctx, start_ref, first_ref, refs[:n_head], out_ref, keys, scores, pooled, lined)
+
+
+def shifted(n_head, n_ctx, start_ref, first_ref, q_refs, out_ref, keys, scores, pooled, lined):
     own, heads, tokens, depth = q_refs[0].shape
     nsel = keys.shape[2]
     scale = math.log2(math.e) / math.sqrt(depth)
@@ -331,17 +342,20 @@
     k_parts = [k_parts[j] for j in range(n_ctx)]
     columns = n_head * heads * QTILE
     buffers = 2 if nsel <= SPAN_ROWS else 1
+    staging = []
+    if buffers == 2:
+        staging = [pltpu.VMEM((tokens, own, nsel), jnp.float32), pltpu.SemaphoreType.DMA((tokens // QTILE,))]
     return pl.pallas_call(
         partial(unit_kernel if buffers == 2 else span_kernel, n_head, n_ctx),
         out_shape=jax.ShapeDtypeStruct((tokens, own, nsel), jnp.float32),
         in_specs=[smem, smem] + [vmem] * (n_head + n_ctx),
-        out_specs=vmem,
+        out_specs=hbm if buffers == 2 else vmem,
         scratch_shapes=[
             pltpu.VMEM((own, 4, nsel, depth), keys.dtype),
             pltpu.VMEM((1, 4, nsel, columns), jnp.float32),
             pltpu.VMEM((buffers, 2, nsel, columns), jnp.float32),
             pltpu.VMEM((buffers, 2, 8 + nsel, LANES), jnp.float32),
-        ],
+        ] + staging,
         compiler_params=pltpu.CompilerParams(vmem_limit_bytes=(20 if buffers == 2 else 52) * 2 ** 20),
         name="importance",
     )(span_start, tile_first, *q_parts, *k_parts)

time: 28.2 us -> 28.7 us (1.018)
  Pallas kernels: 12 us -> 12.6 us
    pallas_call x1, Pallas kernels: 9.66 us -> 10.2 us  [per_device(): pl.pallas_call(partial(unit_kernel if buffers == 2 else span_kernel, n_he...]
where the time goes in v10:
time: 28.7 us; the launch traced here: 28.6 us
  Pallas kernels  12.6 us (44%)
  starting transfers between devices  8.2 us (29%)
  waiting for transfers between devices  7.12 us (25%)
  between operations  0.67 us (2%)
    pallas_call x1, Pallas kernels, per_device(): pl.pallas_call(partial(unit_kernel if buffers == 2 else span_kernel, n_he...  10.2 us
    ppermute x6, starting transfers between devices, swap(): return lax.ppermute(array, axis, [(i, i ^ bit) for i in range(size)])  8.2 us
    ppermute x6, waiting for transfers between devices, swap(): return lax.ppermute(array, axis, [(i, i ^ bit) for i in range(size)])  7.12 us
    pallas_call x1, Pallas kernels, per_device(): pl.pallas_call(partial(pack_kernel, n_head, key_heads, heads), out_shape=...  2.37 us
  transfers between devices with their start and end apart: 6, of which 4 were waited for; matrix products, arithmetic and copies ran while one was open for 0% of the time, Pallas kernels for 0%

profile of v10, /device:TPU:0, one launch (start us, length us, event | category | flops | bytes accessed | tf_op | source)
XLA Modules:
  0.0 28.6 jit_solution(18404332779227030565)
XLA Ops:
  0.0 2.4 %pack.1 = (bf16[2,2,192,128]{3,2,1,0:T(8,128)(2,1)S(1)}, bf16[2,2,192,128]{3,2,1,0:T(8,128)(2,1)S(1)}, bf16[2,2,192,128]{3,2,1,0:T(8,128)(2,1)S(1)}, bf16[2,2,19...) custom-call(bf16[3072,128]{1,0:T(8,128)(2,1)} %bitcast.2, bf16[2048,128]{1,0:T(8,128)(2,1)} %bitcast.3), custom_call_target="tpu_custom_call" | custom-call | tf_op jit(solution)/shard_map/pack/pallas_call | solution.py:315
  2.4 4.1 %collective-permute-start.4 = (bf16[2,4,64,128]{3,2,1,0:T(8,128)(2,1)S(1)}, bf16[2,4,64,128]{3,2,1,0:T(8,128)(2,1)S(1)}, u32[]{:S(2)}, u32[]{:S(2)}) collective-permute-start(bf16[2,4,64,128]{3,2,1,0:T(8,128)(2,1)S(1)} %get-tuple-element.14.refs_4_), channel_id=1, source_target_pairs={{0,8},{4,12},{8,0},{12,4},{1,9},{5,13},{9,1},{13,5},{2,10},{6,14},... | collective-permute-start | bytes 393224 | tf_op jit(solution)/shard_map/ppermute | solution.py:332
  6.5 0.0 collective-permute-start
  6.5 1.5 %collective-permute-start.1 = (bf16[2,2,192,128]{3,2,1,0:T(8,128)(2,1)S(1)}, bf16[2,2,192,128]{3,2,1,0:T(8,128)(2,1)S(1)}, u32[]{:S(2)}, u32[]{:S(2)}) collective-permute-start(bf16[2,2,192,128]{3,2,1,0:T(8,128)(2,1)S(1)} %get-tuple-element.12), channel_id=1, source_target_pairs={{0,2},{1,3},{2,0},{3,1},{4,6},{5,7},{6,4},{7,5},{8,10},{9,11},{10,... | collective-permute-start | bytes 589832 | tf_op jit(solution)/shard_map/ppermute | solution.py:332
  8.0 0.4 %collective-permute-start.2 = (bf16[2,2,192,128]{3,2,1,0:T(8,128)(2,1)S(1)}, bf16[2,2,192,128]{3,2,1,0:T(8,128)(2,1)S(1)}, u32[]{:S(2)}, u32[]{:S(2)}) collective-permute-start(bf16[2,2,192,128]{3,2,1,0:T(8,128)(2,1)S(1)} %get-tuple-element.13), channel_id=1, source_target_pairs={{0,3},{1,2},{2,1},{3,0},{4,7},{5,6},{6,5},{7,4},{8,11},{9,10},{10,... | collective-permute-start | bytes 589832 | tf_op jit(solution)/shard_map/ppermute | solution.py:332
  8.3 1.6 %collective-permute-start.3 = (bf16[2,4,64,128]{3,2,1,0:T(8,128)(2,1)S(1)}, bf16[2,4,64,128]{3,2,1,0:T(8,128)(2,1)S(1)}, u32[]{:S(2)}, u32[]{:S(2)}) collective-permute-start(bf16[2,4,64,128]{3,2,1,0:T(8,128)(2,1)S(1)} %get-tuple-element.14.refs_4_), channel_id=1, source_target_pairs={{0,4},{4,0},{8,12},{12,8},{1,5},{5,1},{9,13},{13,9},{2,6},{6,2},{1... | collective-permute-start | bytes 393224 | tf_op jit(solution)/shard_map/ppermute | solution.py:332
  9.9 3.0 %collective-permute-done.4.refs_6_ = bf16[2,4,64,128]{3,2,1,0:T(8,128)(2,1)S(1)} collective-permute-done((bf16[2,4,64,128]{3,2,1,0:T(8,128)(2,1)S(1)}, bf16[2,4,64,128]{3,2,1,0:T(8,128)(2,1)S(1)}, u32[]{:S(2)}, u32[]{:S(2)}) %collective-permute-start.4) | collective-permute-done | bytes 131104 | tf_op jit(solution)/shard_map/ppermute | solution.py:332
  12.9 0.7 %collective-permute-start.5 = (bf16[2,4,64,128]{3,2,1,0:T(8,128)(2,1)S(1)}, bf16[2,4,64,128]{3,2,1,0:T(8,128)(2,1)S(1)}, u32[]{:S(2)}, u32[]{:S(2)}) collective-permute-start(bf16[2,4,64,128]{3,2,1,0:T(8,128)(2,1)S(1)} %collective-permute-done.4.refs_6_), channel_id=1, source_target_pairs={{0,4},{4,0},{8,12},{12,8},{1,5},{5,1},{9,13},{13,9},{2,6},{6,2},{1... | collective-permute-start | bytes 393224 | tf_op jit(solution)/shard_map/ppermute | solution.py:332
  14.2 0.0 copy-start
  14.2 1.5 %collective-permute-done.3.refs_5_ = bf16[2,4,64,128]{3,2,1,0:T(8,128)(2,1)S(1)} collective-permute-done((bf16[2,4,64,128]{3,2,1,0:T(8,128)(2,1)S(1)}, bf16[2,4,64,128]{3,2,1,0:T(8,128)(2,1)S(1)}, u32[]{:S(2)}, u32[]{:S(2)}) %collective-permute-start.3) | collective-permute-done | bytes 131104 | tf_op jit(solution)/shard_map/ppermute | solution.py:332
  15.7 0.0 collective-permute-done.refs_1_
  15.7 0.0 collective-permute-done.1.refs_2_
  15.7 1.9 %collective-permute-done.2.refs_3_ = bf16[2,2,192,128]{3,2,1,0:T(8,128)(2,1)S(1)} collective-permute-done((bf16[2,2,192,128]{3,2,1,0:T(8,128)(2,1)S(1)}, bf16[2,2,192,128]{3,2,1,0:T(8,128)(2,1)S(1)}, u32[]{:S(2)}, u32[]{:S(2)}) %collective-permute-start.2) | collective-permute-done | bytes 196640 | tf_op jit(solution)/shard_map/ppermute | solution.py:332
  17.6 0.7 %collective-permute-done.5.refs_7_ = bf16[2,4,64,128]{3,2,1,0:T(8,128)(2,1)S(1)} collective-permute-done((bf16[2,4,64,128]{3,2,1,0:T(8,128)(2,1)S(1)}, bf16[2,4,64,128]{3,2,1,0:T(8,128)(2,1)S(1)}, u32[]{:S(2)}, u32[]{:S(2)}) %collective-permute-start.5) | collective-permute-done | bytes 131104 | tf_op jit(solution)/shard_map/ppermute | solution.py:332
  18.4 0.0 copy-done
  18.4 10.2 %importance.1 = f32[192,2,256]{2,1,0:T(2,128)} custom-call(s32[1]{0:T(128)S(6)} %copy.5.start_ref, s32[3]{0:T(128)S(1)} %copy-done, bf16[2,2,192,128]{3,2,1,0:T(8,128)(2,1)S(1)} %get-tuple-element.10.refs_0_, bf16[2,2,192,128]{3,2,1,0:T(8,128)(2,1)S(1)} %collective-permute-done.refs_1_, bf16[2,2,192,128]{3,2,1,0:T(8,128)(2,1)S(1)} %collective-permute-done.1.refs_2_, ...), custom_call_target="tpu_custom_call" | custom-call | tf_op jit(solution)/shard_map/importance/pallas_call | solution.py:348
Async XLA Ops:
  2.4 10.5 %collective-permute-start.4 = (bf16[2,4,64,128]{3,2,1,0:T(8,128)(2,1)S(1)}, bf16[2,4,64,128]{3,2,1,0:T(8,128)(2,1)S(1)}, u32[]{:S(2)}, u32[]{:S(2)}) collective-permute-start(bf16[2,4,64,128]{3,2,1,0:T(8,128)(2,1)S(1)} %get-tuple-element.14.refs_4_), channel_id=1, source_target_pairs={{0,8},{4,12},{8,0},{12,4},{1,9},{5,13},{9,1},{13,5},{2,10},{6,14},... | collective-permute-start | bytes 393224 | tf_op jit(solution)/shard_map/ppermute | solution.py:332
  6.5 9.2 %collective-permute-start = (bf16[2,2,192,128]{3,2,1,0:T(8,128)(2,1)S(1)}, bf16[2,2,192,128]{3,2,1,0:T(8,128)(2,1)S(1)}, u32[]{:S(2)}, u32[]{:S(2)}) collective-permute-start(bf16[2,2,192,128]{3,2,1,0:T(8,128)(2,1)S(1)} %get-tuple-element.11), channel_id=1, source_target_pairs={{0,1},{1,0},{2,3},{3,2},{4,5},{5,4},{6,7},{7,6},{8,9},{9,8},{10,11... | collective-permute-start | bytes 589832 | tf_op jit(solution)/shard_map/ppermute | solution.py:332
  6.5 9.2 %collective-permute-start.1 = (bf16[2,2,192,128]{3,2,1,0:T(8,128)(2,1)S(1)}, bf16[2,2,192,128]{3,2,1,0:T(8,128)(2,1)S(1)}, u32[]{:S(2)}, u32[]{:S(2)}) collective-permute-start(bf16[2,2,192,128]{3,2,1,0:T(8,128)(2,1)S(1)} %get-tuple-element.12), channel_id=1, source_target_pairs={{0,2},{1,3},{2,0},{3,1},{4,6},{5,7},{6,4},{7,5},{8,10},{9,11},{10,... | collective-permute-start | bytes 589832 | tf_op jit(solution)/shard_map/ppermute | solution.py:332
  8.0 9.6 %collective-permute-start.2 = (bf16[2,2,192,128]{3,2,1,0:T(8,128)(2,1)S(1)}, bf16[2,2,192,128]{3,2,1,0:T(8,128)(2,1)S(1)}, u32[]{:S(2)}, u32[]{:S(2)}) collective-permute-start(bf16[2,2,192,128]{3,2,1,0:T(8,128)(2,1)S(1)} %get-tuple-element.13), channel_id=1, source_target_pairs={{0,3},{1,2},{2,1},{3,0},{4,7},{5,6},{6,5},{7,4},{8,11},{9,10},{10,... | collective-permute-start | bytes 589832 | tf_op jit(solution)/shard_map/ppermute | solution.py:332
  8.3 7.3 %collective-permute-start.3 = (bf16[2,4,64,128]{3,2,1,0:T(8,128)(2,1)S(1)}, bf16[2,4,64,128]{3,2,1,0:T(8,128)(2,1)S(1)}, u32[]{:S(2)}, u32[]{:S(2)}) collective-permute-start(bf16[2,4,64,128]{3,2,1,0:T(8,128)(2,1)S(1)} %get-tuple-element.14.refs_4_), channel_id=1, source_target_pairs={{0,4},{4,0},{8,12},{12,8},{1,5},{5,1},{9,13},{13,9},{2,6},{6,2},{1... | collective-permute-start | bytes 393224 | tf_op jit(solution)/shard_map/ppermute | solution.py:332
  12.9 5.5 %collective-permute-start.5 = (bf16[2,4,64,128]{3,2,1,0:T(8,128)(2,1)S(1)}, bf16[2,4,64,128]{3,2,1,0:T(8,128)(2,1)S(1)}, u32[]{:S(2)}, u32[]{:S(2)}) collective-permute-start(bf16[2,4,64,128]{3,2,1,0:T(8,128)(2,1)S(1)} %collective-permute-done.4.refs_6_), channel_id=1, source_target_pairs={{0,4},{4,0},{8,12},{12,8},{1,5},{5,1},{9,13},{13,9},{2,6},{6,2},{1... | collective-permute-start | bytes 393224 | tf_op jit(solution)/shard_map/ppermute | solution.py:332
  14.2 4.2 %copy-start = (s32[3]{0:T(128)S(1)}, s32[3]{0:T(128)}, u32[]{:S(2)}) copy-start(s32[3]{0:T(128)} %first_ref.1) | copy-start | bytes 40

commit v11 on v10

--- a/solution.py
+++ b/solution.py
@@ -103,7 +103,7 @@
 
 def tile_columns(q_refs, g, begin):
     return jnp.concatenate(
-        [q[g, h, pl.ds(begin, QTILE), :] for q in q_refs for h in range(q.shape[1])], axis=0
+        [q[g][h, pl.ds(begin, QTILE), :] for q in q_refs for h in range(q[g].shape[0])], axis=0
     )
 
 
@@ -120,76 +120,127 @@
             pass
 
 
-def unit_kernel(n_head, n_ctx, start_ref, first_ref, *refs):
-    q_refs, k_refs = refs[:n_head], refs[n_head:n_head + n_ctx]
-    out_hbm, keys, scores, pooled, lined, out_ref, sems = refs[n_head + n_ctx:]
+def pooled_exponentials(q_refs, k_refs, t, spans, scale, masks_at, put, totals):
+    own = len(q_refs[0])
+    for sources, j in spans:
+        pieces = []
+        for g in range(own):
+            rows = jnp.concatenate([k_refs[j][g, s] for s in range(4)], axis=0)
+            columns = tile_columns([q_refs[n] for n in sources], g, t * QTILE)
+            pieces.append(lax.dot_general(rows, columns, NT, preferred_element_type=jnp.float32))
+        for r in range(0, BLOCK, 8):
+            masks = masks_at(t, j, r)
+            for g in range(own):
+                for at, n in enumerate(sources):
+                    parts = []
+                    for s in range(4):
+                        part = pieces[g][s * BLOCK + r:s * BLOCK + r + 8, at * LANES:(at + 1) * LANES]
+                        parts.append(jnp.exp2(jnp.where(masks[s], part, MASKED) * scale))
+                    rest = parts[1] + parts[2] + parts[3]
+                    put(g, n, j, r, parts[0], rest)
+                    both = parts[0] + rest
+                    totals[g, n] = totals[g, n] + both if (g, n) in totals else both
+            yield
+
+
+def mask_maker(n_ctx, tokens, start_ref, first_ref):
+    me = lax.axis_index("ctx")
+
+    def masks_at(t, j, r):
+        row4, reach = limits(n_ctx, tokens, t * QTILE, start_ref)
+        first = first_ref[t]
+        at = (me ^ j) * BLOCK + r
+        return [(row4 >= first - (4 * at + s)) & (reach >= 64 * at + 16 * s) for s in range(4)]
+
+    return masks_at
+
+
+def early_kernel(n_ctx, start_ref, first_ref, *refs):
+    q_refs, k_refs, (pooled, total_ref) = refs[:3], refs[3:6], refs[6:]
     own, heads, tokens, depth = q_refs[0].shape
+    q_refs = [[ref.at[g] for g in range(own)] for ref in q_refs]
+    scale = math.log2(math.e) / math.sqrt(depth)
+    masks_at = mask_maker(n_ctx, tokens, start_ref, first_ref)
+    for t in range(tokens // QTILE):
+        def put(g, n, j, r, lead, rest):
+            pooled[t, g, 0, j * BLOCK + r:j * BLOCK + r + 8, n * LANES:(n + 1) * LANES] = lead
+            pooled[t, g, 1, j * BLOCK + r:j * BLOCK + r + 8, n * LANES:(n + 1) * LANES] = rest
+
+        totals = {}
+        for _ in pooled_exponentials(q_refs, k_refs, t, [((0, 1, 2), j) for j in range(3)], scale, masks_at, put, totals):
+            pass
+        for (g, n), total in totals.items():
+            total_ref[t, g, :, n * LANES:(n + 1) * LANES] = total
+
+
+def late_kernel(n_head, n_ctx, start_ref, first_ref, *refs):
+    raw_q, k_refs, (early, early_total) = refs[:n_head], refs[n_head:n_head + n_ctx], refs[n_head + n_ctx:-9]
+    out_hbm, keys, scores, pooled, lined, far, corner, out_ref, sems = refs[-9:]
+    own, heads, tokens, depth = raw_q[0].shape
+    q_refs = [[ref.at[g] for g in range(own)] for ref in raw_q]
     nsel = keys.shape[2]
     scale = math.log2(math.e) / math.sqrt(depth)
     factor = nsel / (2.0 * n_head * heads)
-    tiles_n = n_head * heads * QTILE // LANES
-    gather_keys(n_ctx, k_refs, keys)
-    units = [(t, g) for t in range(tokens // QTILE) for g in range(own)]
+    me = lax.axis_index("ctx")
+    masks_at = mask_maker(n_ctx, tokens, start_ref, first_ref)
+    tiles = tokens // QTILE
+    last = n_ctx - 1
     weights, totals = {}, []
     sent = [
         pltpu.make_async_copy(out_ref.at[pl.ds(t * QTILE, QTILE)], out_hbm.at[pl.ds(t * QTILE, QTILE)], sems.at[t])
-        for t in range(tokens // QTILE)
+        for t in range(tiles)
     ]
 
-    def exponentials(u):
-        t, g = units[u]
-        columns = tile_columns(q_refs, g, t * QTILE)
-        row4, reach = limits(n_ctx, tokens, t * QTILE, start_ref)
-        first = first_ref[t]
-        total = [None] * tiles_n
-        for base in range(0, nsel, BLOCK):
-            rows = jnp.concatenate([keys[g, s, base:base + BLOCK, :] for s in range(4)], axis=0)
-            piece = lax.dot_general(rows, columns, NT, preferred_element_type=jnp.float32)
-            for r in range(0, BLOCK, 8):
-                masks = [visible(nsel, n_ctx * tokens, base + r, s, first, row4, reach) for s in range(4)]
-                for n in range(tiles_n):
-                    at = slice(n * LANES, (n + 1) * LANES)
-                    parts = []
-                    for s, mask in enumerate(masks):
-                        part = piece[s * BLOCK + r:s * BLOCK + r + 8, at]
-                        if mask is not None:
-                            part = jnp.where(mask, part, MASKED)
-                        parts.append(jnp.exp2(part * scale))
-                    rest = parts[1] + parts[2] + parts[3]
-                    pooled[u % 2, 0, base + r:base + r + 8, at] = parts[0]
-                    pooled[u % 2, 1, base + r:base + r + 8, at] = rest
-                    both = parts[0] + rest
-                    total[n] = both if total[n] is None else total[n] + both
-                yield
-        total = [jnp.sum(part, axis=0, keepdims=True) for part in total]
-        weights[u] = [factor / part for part in total]
-        totals.extend(total)
-
-    def sums(u):
-        t, g = units[u]
-        lined[u % 2, 1, 0:8, :] = jnp.zeros((8, LANES), jnp.float32)
-        for r in range(0, nsel, 8):
-            lead, rest = None, None
-            for n in range(tiles_n):
-                at = slice(n * LANES, (n + 1) * LANES)
-                first, second = pooled[u % 2, 0, r:r + 8, at] * weights[u][n], pooled[u % 2, 1, r:r + 8, at] * weights[u][n]
-                lead = first if lead is None else lead + first
-                rest = second if rest is None else rest + second
-            lined[u % 2, 0, 8 + r:16 + r, :] = lead
-            lined[u % 2, 1, 8 + r:16 + r, :] = lead + 2.0 * rest
+    def exponentials(t):
+        def put(g, n, j, r, lead, rest):
+            if n == last:
+                far[t % 2, g, 0, j * BLOCK + r:j * BLOCK + r + 8, :] = lead
+                far[t % 2, g, 1, j * BLOCK + r:j * BLOCK + r + 8, :] = rest
+            else:
+                corner[t % 2, g, 0, r:r + 8, n * LANES:(n + 1) * LANES] = lead
+                corner[t % 2, g, 1, r:r + 8, n * LANES:(n + 1) * LANES] = rest
+
+        sums = {}
+        spans = [((last,), j) for j in range(last)] + [(tuple(range(n_head)), last)]
+        yield from pooled_exponentials(q_refs, k_refs, t, spans, scale, masks_at, put, sums)
+        for (g, n), total in sums.items():
+            if n < last:
+                total = total + early_total[t, g, :, n * LANES:(n + 1) * LANES]
+            total = jnp.sum(total, axis=0, keepdims=True)
+            weights[t, g, n] = factor / total
+            totals.append(total)
+
+    def sums(t):
+        for g in range(own):
+            lined[t % 2, g, 1, 0:8, :] = jnp.zeros((8, LANES), jnp.float32)
+            for j in range(n_ctx):
+                for r in range(0, BLOCK, 8):
+                    both = []
+                    for p in range(2):
+                        value = far[t % 2, g, p, j * BLOCK + r:j * BLOCK + r + 8, :] * weights[t, g, last]
+                        for n in range(last):
+                            at = slice(n * LANES, (n + 1) * LANES)
+                            if j == last:
+                                part = corner[t % 2, g, p, r:r + 8, at]
+                            else:
+                                part = early[t, g, p, j * BLOCK + r:j * BLOCK + r + 8, at]
+                            value = value + part * weights[t, g, n]
+                        both.append(value)
+                    here = pl.ds(pl.multiple_of(8 + (me ^ j) * BLOCK + r, 8), 8)
+                    lined[t % 2, g, 0, here, :] = both[0]
+                    lined[t % 2, g, 1, here, :] = both[0] + 2.0 * both[1]
+                    yield
+            turned = (lined[t % 2, g, 0, 8:8 + nsel, :] + lined[t % 2, g, 1, 7:7 + nsel, :]).T
+            out_ref[t * QTILE:(t + 1) * QTILE, g, :] = turned[:QTILE] + turned[QTILE:]
             yield
-        turned = (lined[u % 2, 0, 8:8 + nsel, :] + lined[u % 2, 1, 7:7 + nsel, :]).T
-        out_ref[t * QTILE:(t + 1) * QTILE, g, :] = turned[:QTILE] + turned[QTILE:]
-        if g == own - 1:
-            sent[t].start()
-        yield
-
-    for step in range(len(units) + 1):
+        sent[t].start()
+
+    for step in range(tiles + 1):
         stages = []
-        if step < len(units):
+        if step < tiles:
             stages.append((nsel // 8, exponentials(step)))
         if step >= 1:
-            stages.append((nsel // 8 + 1, sums(step - 1)))
+            stages.append((own * (nsel // 8 + 1), sums(step - 1)))
         interleave(*stages)
 
     least, most = totals[0], totals[0]
@@ -201,7 +252,8 @@
 
     @pl.when(jnp.logical_not(safe))
     def _():
-        shifted(n_head, n_ctx, start_ref, first_ref, q_refs, out_ref, keys, scores, pooled, lined)
+        gather_keys(n_ctx, k_refs, keys)
+        shifted(n_head, n_ctx, start_ref, first_ref, raw_q, out_ref, keys, scores, pooled, lined.at[:, 0])
         for copy in sent:
             copy.start()
         for copy in sent:
@@ -214,8 +266,9 @@
     shifted(n_head, n_ctx, start_ref, first_ref, refs[:n_head], out_ref, keys, scores, pooled, lined)
 
 
-def shifted(n_head, n_ctx, start_ref, first_ref, q_refs, out_ref, keys, scores, pooled, lined):
-    own, heads, tokens, depth = q_refs[0].shape
+def shifted(n_head, n_ctx, start_ref, first_ref, raw_q, out_ref, keys, scores, pooled, lined):
+    own, heads, tokens, depth = raw_q[0].shape
+    q_refs = [[ref.at[g] for g in range(own)] for ref in raw_q]
     nsel = keys.shape[2]
     scale = math.log2(math.e) / math.sqrt(depth)
     factor = nsel / (2.0 * n_head * heads)
@@ -341,24 +394,51 @@
         bit //= 2
     k_parts = [k_parts[j] for j in range(n_ctx)]
     columns = n_head * heads * QTILE
-    buffers = 2 if nsel <= SPAN_ROWS else 1
-    staging = []
-    if buffers == 2:
-        staging = [pltpu.VMEM((tokens, own, nsel), jnp.float32), pltpu.SemaphoreType.DMA((tokens // QTILE,))]
+    tiles = tokens // QTILE
+    limit = pltpu.CompilerParams(vmem_limit_bytes=20 * 2 ** 20)
+    scratch = [
+        pltpu.VMEM((own, 4, nsel, depth), keys.dtype),
+        pltpu.VMEM((1, 4, nsel, columns), jnp.float32),
+        pltpu.VMEM((1, 2, nsel, columns), jnp.float32),
+    ]
+    result = jax.ShapeDtypeStruct((tokens, own, nsel), jnp.float32)
+    if (n_ctx, n_head, blocks, heads * QTILE) != (4, 4, BLOCK, LANES):
+        return pl.pallas_call(
+            partial(span_kernel, n_head, n_ctx),
+            out_shape=result,
+            in_specs=[smem, smem] + [vmem] * (n_head + n_ctx),
+            out_specs=vmem,
+            scratch_shapes=scratch + [pltpu.VMEM((1, 2, 8 + nsel, LANES), jnp.float32)],
+            compiler_params=pltpu.CompilerParams(vmem_limit_bytes=52 * 2 ** 20),
+            name="importance",
+        )(span_start, tile_first, *q_parts, *k_parts)
+    most = 3 * LANES
+    early = pl.pallas_call(
+        partial(early_kernel, n_ctx),
+        out_shape=[
+            jax.ShapeDtypeStruct((tiles, own, 2, 3 * BLOCK, most), jnp.float32),
+            jax.ShapeDtypeStruct((tiles, own, 8, most), jnp.float32),
+        ],
+        in_specs=[smem, smem] + [vmem] * 6,
+        out_specs=[vmem, vmem],
+        compiler_params=limit,
+        name="early",
+    )(span_start, tile_first, *q_parts[:3], *k_parts[:3])
     return pl.pallas_call(
-        partial(unit_kernel if buffers == 2 else span_kernel, n_head, n_ctx),
-        out_shape=jax.ShapeDtypeStruct((tokens, own, nsel), jnp.float32),
-        in_specs=[smem, smem] + [vmem] * (n_head + n_ctx),
-        out_specs=hbm if buffers == 2 else vmem,
-        scratch_shapes=[
-            pltpu.VMEM((own, 4, nsel, depth), keys.dtype),
-            pltpu.VMEM((1, 4, nsel, columns), jnp.float32),
-            pltpu.VMEM((buffers, 2, nsel, columns), jnp.float32),
-            pltpu.VMEM((buffers, 2, 8 + nsel, LANES), jnp.float32),
-        ] + staging,
-        compiler_params=pltpu.CompilerParams(vmem_limit_bytes=(20 if buffers == 2 else 52) * 2 ** 20),
-        name="importance",
-    )(span_start, tile_first, *q_parts, *k_parts)
+        partial(late_kernel, n_head, n_ctx),
+        out_shape=result,
+        in_specs=[smem, smem] + [vmem] * (n_head + n_ctx + 2),
+        out_specs=hbm,
+        scratch_shapes=scratch + [
+            pltpu.VMEM((2, own, 2, 8 + nsel, LANES), jnp.float32),
+            pltpu.VMEM((2, own, 2, nsel, LANES), jnp.float32),
+            pltpu.VMEM((2, own, 2, BLOCK, most), jnp.float32),
+            pltpu.VMEM((tokens, own, nsel), jnp.float32),
+            pltpu.SemaphoreType.DMA((tiles,)),
+        ],
+        compiler_params=limit,
+        name="late",
+    )(span_start, tile_first, *q_parts, *k_parts, *early)
 
 
 def solution(mesh):

time: 28.7 us -> 28 us (0.976)
  waiting for transfers between devices: 7.12 us -> 4.46 us
  Pallas kernels: 12.6 us -> 13.9 us
  local copies, waits for them, and re-layouts: 0.01 us -> 0.65 us
    ppermute x6, waiting for transfers between devices: 7.12 us -> 4.46 us  [swap(): return lax.ppermute(array, axis, [(i, i ^ bit) for i in range(size)])]
    pallas_call x1 -> x2, Pallas kernels: 10.2 us -> 11.5 us  [the longest x1 9.34 us: per_device(): pl.pallas_call(partial(late_kernel, n_head, n_ctx), out_shape=result, in_...]
    unnamed x2, local copies, waits for them, and re-layouts: 0.01 us -> 0.65 us
  transfers between devices with their start and end apart: 6 -> 6, of which waited for: 4 -> 2; matrix products, arithmetic and copies ran while one was open for 0% -> 0% of each run, Pallas kernels for 0% -> 8%
where the time goes in v11:
time: 28 us; the launch traced here: 27.9 us
  Pallas kernels  13.9 us (50%)
  starting transfers between devices  8.2 us (29%)
  waiting for transfers between devices  4.46 us (16%)
  between operations  0.69 us (2%)
  local copies, waits for them, and re-layouts  0.65 us (2%)
    pallas_call x1, Pallas kernels, per_device(): pl.pallas_call(partial(late_kernel, n_head, n_ctx), out_shape=result, in_...  9.34 us
    ppermute x6, starting transfers between devices, swap(): return lax.ppermute(array, axis, [(i, i ^ bit) for i in range(size)])  8.2 us
    ppermute x6, waiting for transfers between devices, swap(): return lax.ppermute(array, axis, [(i, i ^ bit) for i in range(size)])  4.46 us
    pallas_call x1, Pallas kernels, per_device(): pl.pallas_call(partial(pack_kernel, n_head, key_heads, heads), out_shape=...  2.37 us
    pallas_call x1, Pallas kernels, per_device(): pl.pallas_call(partial(early_kernel, n_ctx), out_shape=[jax.ShapeDtypeStr...  2.16 us
    unnamed x2, local copies, waits for them, and re-layouts  0.65 us
  transfers between devices with their start and end apart: 6, of which 2 were waited for; matrix products, arithmetic and copies ran while one was open for 0% of the time, Pallas kernels for 8%

profile of v11, /device:TPU:0, one launch (start us, length us, event | category | flops | bytes accessed | tf_op | source)
XLA Modules:
  0.0 27.9 jit_solution(9860044764807073618)
XLA Ops:
  0.0 2.4 %pack.1 = (bf16[2,2,192,128]{3,2,1,0:T(8,128)(2,1)S(1)}, bf16[2,2,192,128]{3,2,1,0:T(8,128)(2,1)S(1)}, bf16[2,2,192,128]{3,2,1,0:T(8,128)(2,1)S(1)}, bf16[2,2,19...) custom-call(bf16[3072,128]{1,0:T(8,128)(2,1)} %bitcast.2, bf16[2048,128]{1,0:T(8,128)(2,1)} %bitcast.3), custom_call_target="tpu_custom_call" | custom-call | tf_op jit(solution)/shard_map/pack/pallas_call | solution.py:368
  2.4 4.1 %collective-permute-start.4 = (bf16[2,4,64,128]{3,2,1,0:T(8,128)(2,1)S(1)}, bf16[2,4,64,128]{3,2,1,0:T(8,128)(2,1)S(1)}, u32[]{:S(2)}, u32[]{:S(2)}) collective-permute-start(bf16[2,4,64,128]{3,2,1,0:T(8,128)(2,1)S(1)} %get-tuple-element.16.refs_3_.refs_4_), channel_id=1, source_target_pairs={{0,8},{4,12},{8,0},{12,4},{1,9},{5,13},{9,1},{13,5},{2,10},{6,14},... | collective-permute-start | bytes 393224 | tf_op jit(solution)/shard_map/ppermute | solution.py:385
  6.5 0.0 collective-permute-start
  6.5 1.5 %collective-permute-start.1 = (bf16[2,2,192,128]{3,2,1,0:T(8,128)(2,1)S(1)}, bf16[2,2,192,128]{3,2,1,0:T(8,128)(2,1)S(1)}, u32[]{:S(2)}, u32[]{:S(2)}) collective-permute-start(bf16[2,2,192,128]{3,2,1,0:T(8,128)(2,1)S(1)} %get-tuple-element.14), channel_id=1, source_target_pairs={{0,2},{1,3},{2,0},{3,1},{4,6},{5,7},{6,4},{7,5},{8,10},{9,11},{10,... | collective-permute-start | bytes 589832 | tf_op jit(solution)/shard_map/ppermute | solution.py:385
  8.0 0.4 %collective-permute-start.2 = (bf16[2,2,192,128]{3,2,1,0:T(8,128)(2,1)S(1)}, bf16[2,2,192,128]{3,2,1,0:T(8,128)(2,1)S(1)}, u32[]{:S(2)}, u32[]{:S(2)}) collective-permute-start(bf16[2,2,192,128]{3,2,1,0:T(8,128)(2,1)S(1)} %get-tuple-element.15), channel_id=1, source_target_pairs={{0,3},{1,2},{2,1},{3,0},{4,7},{5,6},{6,5},{7,4},{8,11},{9,10},{10,... | collective-permute-start | bytes 589832 | tf_op jit(solution)/shard_map/ppermute | solution.py:385
  8.3 1.6 %collective-permute-start.3 = (bf16[2,4,64,128]{3,2,1,0:T(8,128)(2,1)S(1)}, bf16[2,4,64,128]{3,2,1,0:T(8,128)(2,1)S(1)}, u32[]{:S(2)}, u32[]{:S(2)}) collective-permute-start(bf16[2,4,64,128]{3,2,1,0:T(8,128)(2,1)S(1)} %get-tuple-element.16.refs_3_.refs_4_), channel_id=1, source_target_pairs={{0,4},{4,0},{8,12},{12,8},{1,5},{5,1},{9,13},{13,9},{2,6},{6,2},{1... | collective-permute-start | bytes 393224 | tf_op jit(solution)/shard_map/ppermute | solution.py:385
  9.9 3.0 %collective-permute-done.4.refs_5_.refs_6_ = bf16[2,4,64,128]{3,2,1,0:T(8,128)(2,1)S(1)} collective-permute-done((bf16[2,4,64,128]{3,2,1,0:T(8,128)(2,1)S(1)}, bf16[2,4,64,128]{3,2,1,0:T(8,128)(2,1)S(1)}, u32[]{:S(2)}, u32[]{:S(2)}) %collective-permute-start.4) | collective-permute-done | bytes 131104 | tf_op jit(solution)/shard_map/ppermute | solution.py:385
  12.9 0.7 %collective-permute-start.5 = (bf16[2,4,64,128]{3,2,1,0:T(8,128)(2,1)S(1)}, bf16[2,4,64,128]{3,2,1,0:T(8,128)(2,1)S(1)}, u32[]{:S(2)}, u32[]{:S(2)}) collective-permute-start(bf16[2,4,64,128]{3,2,1,0:T(8,128)(2,1)S(1)} %collective-permute-done.4.refs_5_.refs_6_), channel_id=1, source_target_pairs={{0,4},{4,0},{8,12},{12,8},{1,5},{5,1},{9,13},{13,9},{2,6},{6,2},{1... | collective-permute-start | bytes 393224 | tf_op jit(solution)/shard_map/ppermute | solution.py:385
  14.2 1.5 %collective-permute-done.3.refs_4_.refs_5_ = bf16[2,4,64,128]{3,2,1,0:T(8,128)(2,1)S(1)} collective-permute-done((bf16[2,4,64,128]{3,2,1,0:T(8,128)(2,1)S(1)}, bf16[2,4,64,128]{3,2,1,0:T(8,128)(2,1)S(1)}, u32[]{:S(2)}, u32[]{:S(2)}) %collective-permute-start.3) | collective-permute-done | bytes 131104 | tf_op jit(solution)/shard_map/ppermute | solution.py:385
  15.7 0.0 collective-permute-done.refs_1_
  15.7 0.0 collective-permute-done.1.refs_2_
  15.7 0.0 copy-start
  15.7 0.7 %copy-done = s32[3]{0:T(128)S(1)} copy-done((s32[3]{0:T(128)S(1)}, s32[3]{0:T(128)}, u32[]{:S(2)}) %copy-start) | copy-done | bytes 36
  16.4 2.2 %early.1 = (f32[3,2,2,192,384]{4,3,2,1,0:T(8,128)S(1)}, f32[3,2,8,384]{3,2,1,0:T(8,128)S(1)}) custom-call(s32[1]{0:T(128)S(6)} %copy.5.start_ref, s32[3]{0:T(128)S(1)} %copy-done, bf16[2,2,192,128]{3,2,1,0:T(8,128)(2,1)S(1)} %get-tuple-element.12.refs_0_, bf16[2,2,192,128]{3,2,1,0:T(8,128)(2,1)S(1)} %collective-permute-done.refs_1_, ...), custom_call_target="tpu_custom_call" | custom-call | tf_op jit(solution)/shard_map/early/pallas_call | solution.py:416
  18.5 0.0 collective-permute-done.2.refs_3_
  18.5 0.0 collective-permute-done.5.refs_7_
  18.5 9.3 %late.1 = f32[192,2,256]{2,1,0:T(2,128)} custom-call(s32[1]{0:T(128)S(6)} %copy.5.start_ref, s32[3]{0:T(128)S(1)} %copy-done, bf16[2,2,192,128]{3,2,1,0:T(8,128)(2,1)S(1)} %get-tuple-element.12.refs_0_, bf16[2,2,192,128]{3,2,1,0:T(8,128)(2,1)S(1)} %collective-permute-done.refs_1_, bf16[2,2,192,128]{3,2,1,0:T(8,128)(2,1)S(1)} %collective-permute-done.1.refs_2_, ...), custom_call_target="tpu_custom_call" | custom-call | tf_op jit(solution)/shard_map/late/pallas_call | solution.py:427
Async XLA Ops:
  2.4 10.5 %collective-permute-start.4 = (bf16[2,4,64,128]{3,2,1,0:T(8,128)(2,1)S(1)}, bf16[2,4,64,128]{3,2,1,0:T(8,128)(2,1)S(1)}, u32[]{:S(2)}, u32[]{:S(2)}) collective-permute-start(bf16[2,4,64,128]{3,2,1,0:T(8,128)(2,1)S(1)} %get-tuple-element.16.refs_3_.refs_4_), channel_id=1, source_target_pairs={{0,8},{4,12},{8,0},{12,4},{1,9},{5,13},{9,1},{13,5},{2,10},{6,14},... | collective-permute-start | bytes 393224 | tf_op jit(solution)/shard_map/ppermute | solution.py:385
  6.5 9.2 %collective-permute-start = (bf16[2,2,192,128]{3,2,1,0:T(8,128)(2,1)S(1)}, bf16[2,2,192,128]{3,2,1,0:T(8,128)(2,1)S(1)}, u32[]{:S(2)}, u32[]{:S(2)}) collective-permute-start(bf16[2,2,192,128]{3,2,1,0:T(8,128)(2,1)S(1)} %get-tuple-element.13), channel_id=1, source_target_pairs={{0,1},{1,0},{2,3},{3,2},{4,5},{5,4},{6,7},{7,6},{8,9},{9,8},{10,11... | collective-permute-start | bytes 589832 | tf_op jit(solution)/shard_map/ppermute | solution.py:385
  6.5 9.2 %collective-permute-start.1 = (bf16[2,2,192,128]{3,2,1,0:T(8,128)(2,1)S(1)}, bf16[2,2,192,128]{3,2,1,0:T(8,128)(2,1)S(1)}, u32[]{:S(2)}, u32[]{:S(2)}) collective-permute-start(bf16[2,2,192,128]{3,2,1,0:T(8,128)(2,1)S(1)} %get-tuple-element.14), channel_id=1, source_target_pairs={{0,2},{1,3},{2,0},{3,1},{4,6},{5,7},{6,4},{7,5},{8,10},{9,11},{10,... | collective-permute-start | bytes 589832 | tf_op jit(solution)/shard_map/ppermute | solution.py:385
  8.0 10.5 %collective-permute-start.2 = (bf16[2,2,192,128]{3,2,1,0:T(8,128)(2,1)S(1)}, bf16[2,2,192,128]{3,2,1,0:T(8,128)(2,1)S(1)}, u32[]{:S(2)}, u32[]{:S(2)}) collective-permute-start(bf16[2,2,192,128]{3,2,1,0:T(8,128)(2,1)S(1)} %get-tuple-element.15), channel_id=1, source_target_pairs={{0,3},{1,2},{2,1},{3,0},{4,7},{5,6},{6,5},{7,4},{8,11},{9,10},{10,... | collective-permute-start | bytes 589832 | tf_op jit(solution)/shard_map/ppermute | solution.py:385
  8.3 7.3 %collective-permute-start.3 = (bf16[2,4,64,128]{3,2,1,0:T(8,128)(2,1)S(1)}, bf16[2,4,64,128]{3,2,1,0:T(8,128)(2,1)S(1)}, u32[]{:S(2)}, u32[]{:S(2)}) collective-permute-start(bf16[2,4,64,128]{3,2,1,0:T(8,128)(2,1)S(1)} %get-tuple-element.16.refs_3_.refs_4_), channel_id=1, source_target_pairs={{0,4},{4,0},{8,12},{12,8},{1,5},{5,1},{9,13},{13,9},{2,6},{6,2},{1... | collective-permute-start | bytes 393224 | tf_op jit(solution)/shard_map/ppermute | solution.py:385
  12.9 5.6 %collective-permute-start.5 = (bf16[2,4,64,128]{3,2,1,0:T(8,128)(2,1)S(1)}, bf16[2,4,64,128]{3,2,1,0:T(8,128)(2,1)S(1)}, u32[]{:S(2)}, u32[]{:S(2)}) collective-permute-start(bf16[2,4,64,128]{3,2,1,0:T(8,128)(2,1)S(1)} %collective-permute-done.4.refs_5_.refs_6_), channel_id=1, source_target_pairs={{0,4},{4,0},{8,12},{12,8},{1,5},{5,1},{9,13},{13,9},{2,6},{6,2},{1... | collective-permute-start | bytes 393224 | tf_op jit(solution)/shard_map/ppermute | solution.py:385
  15.7 0.7 %copy-start = (s32[3]{0:T(128)S(1)}, s32[3]{0:T(128)}, u32[]{:S(2)}) copy-start(s32[3]{0:T(128)} %first_ref.3) | copy-start | bytes 40

commit v12 on v11

--- a/solution.py
+++ b/solution.py
@@ -21,40 +21,42 @@
 NT = (((1,), (1,)), ((), ()))
 
 
-def pack_kernel(n_head, key_heads, heads, q_hbm, k_hbm, *refs):
-    q_outs, (k_out, q_ref, k_ref, q_sems, k_sems) = refs[:n_head], refs[n_head:]
+def pack_kernel(n_head, key_heads, heads, q_hbm, k_hbm, first_hbm, *refs):
+    q_outs, (k_out, spread, q_ref, k_ref, first, q_sems, k_sems, sem) = refs[:n_head], refs[n_head:]
+    first_copy = pltpu.make_async_copy(first_hbm, first, sem)
     me = lax.axis_index("head")
     own = key_heads // n_head
     width = own * heads
     tokens = q_outs[0].shape[2]
     blocks = k_out.shape[2]
     q_rows = PACK * key_heads * heads
-    k_rows = PACK * 4 * key_heads
+    k_rows = PACK * 4
     k_copies, q_copies = [], []
     k_each, q_each = blocks // PACK // K_COPIES, tokens // PACK // Q_COPIES
     for n in range(K_COPIES):
         at = pl.ds(n * k_each * k_rows, k_each * k_rows)
-        k_copies.append(pltpu.make_async_copy(k_hbm.at[at], k_ref.at[at], k_sems.at[n]))
+        k_copies.append(pltpu.make_async_copy(k_hbm.at[at, me], k_ref.at[at], k_sems.at[n]))
     for n in range(Q_COPIES):
         at = pl.ds(n * q_each * q_rows, q_each * q_rows)
         q_copies.append(pltpu.make_async_copy(q_hbm.at[at], q_ref.at[at], q_sems.at[n]))
-    for copy in k_copies + q_copies:
+    for copy in k_copies + q_copies + [first_copy]:
         copy.start()
 
-    out_row = lax.broadcasted_iota(jnp.int32, (own * 4 * PACK, k_rows), 0)
-    in_row = lax.broadcasted_iota(jnp.int32, (own * 4 * PACK, k_rows), 1)
-    head = out_row // (4 * PACK)
-    part = out_row // PACK % 4
-    source = out_row % PACK * (4 * key_heads) + part * key_heads + me * own + head
+    out_row = lax.broadcasted_iota(jnp.int32, (own * k_rows, own * k_rows), 0)
+    in_row = lax.broadcasted_iota(jnp.int32, (own * k_rows, own * k_rows), 1)
+    source = (out_row % PACK * 4 + out_row // PACK % 4) * own + out_row // k_rows
     select = jnp.where(in_row == source, 1.0, 0.0).astype(jnp.bfloat16)
     for block in range(blocks // PACK):
         if block % k_each == 0:
             k_copies[block // k_each].wait()
-        moved = jnp.dot(
-            select, k_ref[block * k_rows:(block + 1) * k_rows, :], preferred_element_type=jnp.float32
-        ).astype(jnp.bfloat16)
+        rows = k_ref[block * k_rows:(block + 1) * k_rows].reshape(own * k_rows, k_ref.shape[2])
+        moved = jnp.dot(select, rows, preferred_element_type=jnp.float32).astype(jnp.bfloat16)
         for u in range(own * 4):
             k_out[u // 4, u % 4, block * PACK:(block + 1) * PACK, :] = moved[u * PACK:(u + 1) * PACK]
+
+    first_copy.wait()
+    for t in range(first_hbm.shape[0]):
+        spread[t] = jnp.full((8, LANES), first[t], jnp.int32)
 
     out_row = lax.broadcasted_iota(jnp.int32, (n_head * width * PACK, q_rows), 0)
     in_row = lax.broadcasted_iota(jnp.int32, (n_head * width * PACK, q_rows), 1)
@@ -81,10 +83,10 @@
         keys[:, :, at, :] = k_refs[j][...]
 
 
-def limits(n_ctx, tokens, begin, start_ref):
+def limits(n_ctx, tokens, begin, start):
     lane = lax.broadcasted_iota(jnp.int32, (8, LANES), 1)
     row = lax.broadcasted_iota(jnp.int32, (8, LANES), 0)
-    place = start_ref[0] + lax.axis_index("ctx") * tokens + begin + lane % QTILE
+    place = start + lax.axis_index("ctx") * tokens + begin + lane % QTILE
     return 4 * row, place - 31 - 64 * row
 
 
@@ -120,17 +122,16 @@
             pass
 
 
-def pooled_exponentials(q_refs, k_refs, t, spans, scale, masks_at, put, totals):
-    own = len(q_refs[0])
+def pooled_exponentials(q_refs, k_refs, t, group, spans, scale, masks_at, put, totals):
     for sources, j in spans:
-        pieces = []
-        for g in range(own):
+        pieces = {}
+        for g in group:
             rows = jnp.concatenate([k_refs[j][g, s] for s in range(4)], axis=0)
             columns = tile_columns([q_refs[n] for n in sources], g, t * QTILE)
-            pieces.append(lax.dot_general(rows, columns, NT, preferred_element_type=jnp.float32))
+            pieces[g] = lax.dot_general(rows, columns, NT, preferred_element_type=jnp.float32)
         for r in range(0, BLOCK, 8):
             masks = masks_at(t, j, r)
-            for g in range(own):
+            for g in group:
                 for at, n in enumerate(sources):
                     parts = []
                     for s in range(4):
@@ -143,46 +144,49 @@
             yield
 
 
-def mask_maker(n_ctx, tokens, start_ref, first_ref):
+def mask_maker(n_ctx, tokens, start, spread):
     me = lax.axis_index("ctx")
+    tiles = tokens // QTILE
+    edges = [limits(n_ctx, tokens, t * QTILE, start) for t in range(tiles)]
+    edges = [(row4 - spread[t], reach) for t, (row4, reach) in enumerate(edges)]
 
     def masks_at(t, j, r):
-        row4, reach = limits(n_ctx, tokens, t * QTILE, start_ref)
-        first = first_ref[t]
+        low, high = edges[t]
         at = (me ^ j) * BLOCK + r
-        return [(row4 >= first - (4 * at + s)) & (reach >= 64 * at + 16 * s) for s in range(4)]
+        return [(low >= -(4 * at + s)) & (high >= 64 * at + 16 * s) for s in range(4)]
 
     return masks_at
 
 
-def early_kernel(n_ctx, start_ref, first_ref, *refs):
+def early_kernel(n_ctx, start_ref, spread, *refs):
     q_refs, k_refs, (pooled, total_ref) = refs[:3], refs[3:6], refs[6:]
     own, heads, tokens, depth = q_refs[0].shape
     q_refs = [[ref.at[g] for g in range(own)] for ref in q_refs]
     scale = math.log2(math.e) / math.sqrt(depth)
-    masks_at = mask_maker(n_ctx, tokens, start_ref, first_ref)
+    masks_at = mask_maker(n_ctx, tokens, start_ref[0], spread)
     for t in range(tokens // QTILE):
         def put(g, n, j, r, lead, rest):
             pooled[t, g, 0, j * BLOCK + r:j * BLOCK + r + 8, n * LANES:(n + 1) * LANES] = lead
             pooled[t, g, 1, j * BLOCK + r:j * BLOCK + r + 8, n * LANES:(n + 1) * LANES] = rest
 
         totals = {}
-        for _ in pooled_exponentials(q_refs, k_refs, t, [((0, 1, 2), j) for j in range(3)], scale, masks_at, put, totals):
+        spans = [((0, 1, 2), j) for j in range(3)]
+        for _ in pooled_exponentials(q_refs, k_refs, t, range(own), spans, scale, masks_at, put, totals):
             pass
         for (g, n), total in totals.items():
             total_ref[t, g, :, n * LANES:(n + 1) * LANES] = total
 
 
-def late_kernel(n_head, n_ctx, start_ref, first_ref, *refs):
-    raw_q, k_refs, (early, early_total) = refs[:n_head], refs[n_head:n_head + n_ctx], refs[n_head + n_ctx:-9]
-    out_hbm, keys, scores, pooled, lined, far, corner, out_ref, sems = refs[-9:]
+def late_kernel(n_head, n_ctx, start_ref, first_hbm, spread, *refs):
+    raw_q, k_refs, (early, early_total) = refs[:n_head], refs[n_head:n_head + n_ctx], refs[n_head + n_ctx:-10]
+    out_hbm, keys, scores, pooled, lined, far, corner, out_ref, first_ref, sems = refs[-10:]
     own, heads, tokens, depth = raw_q[0].shape
     q_refs = [[ref.at[g] for g in range(own)] for ref in raw_q]
     nsel = keys.shape[2]
     scale = math.log2(math.e) / math.sqrt(depth)
     factor = nsel / (2.0 * n_head * heads)
     me = lax.axis_index("ctx")
-    masks_at = mask_maker(n_ctx, tokens, start_ref, first_ref)
+    masks_at = mask_maker(n_ctx, tokens, start_ref[0], spread)
     tiles = tokens // QTILE
     last = n_ctx - 1
     weights, totals = {}, []
@@ -191,56 +195,61 @@
         for t in range(tiles)
     ]
 
-    def exponentials(t):
-        def put(g, n, j, r, lead, rest):
+    units = [(t, g) for t in range(tiles) for g in range(own)]
+
+    def exponentials(u):
+        t, g = units[u]
+
+        def put(_, n, j, r, lead, rest):
             if n == last:
-                far[t % 2, g, 0, j * BLOCK + r:j * BLOCK + r + 8, :] = lead
-                far[t % 2, g, 1, j * BLOCK + r:j * BLOCK + r + 8, :] = rest
+                far[u % 2, 0, j * BLOCK + r:j * BLOCK + r + 8, :] = lead
+                far[u % 2, 1, j * BLOCK + r:j * BLOCK + r + 8, :] = rest
             else:
-                corner[t % 2, g, 0, r:r + 8, n * LANES:(n + 1) * LANES] = lead
-                corner[t % 2, g, 1, r:r + 8, n * LANES:(n + 1) * LANES] = rest
-
-        sums = {}
+                corner[u % 2, 0, r:r + 8, n * LANES:(n + 1) * LANES] = lead
+                corner[u % 2, 1, r:r + 8, n * LANES:(n + 1) * LANES] = rest
+
+        found = {}
         spans = [((last,), j) for j in range(last)] + [(tuple(range(n_head)), last)]
-        yield from pooled_exponentials(q_refs, k_refs, t, spans, scale, masks_at, put, sums)
-        for (g, n), total in sums.items():
+        yield from pooled_exponentials(q_refs, k_refs, t, [g], spans, scale, masks_at, put, found)
+        for (_, n), total in found.items():
             if n < last:
                 total = total + early_total[t, g, :, n * LANES:(n + 1) * LANES]
             total = jnp.sum(total, axis=0, keepdims=True)
-            weights[t, g, n] = factor / total
+            weights[u, n] = factor / total
             totals.append(total)
 
-    def sums(t):
-        for g in range(own):
-            lined[t % 2, g, 1, 0:8, :] = jnp.zeros((8, LANES), jnp.float32)
-            for j in range(n_ctx):
-                for r in range(0, BLOCK, 8):
-                    both = []
-                    for p in range(2):
-                        value = far[t % 2, g, p, j * BLOCK + r:j * BLOCK + r + 8, :] * weights[t, g, last]
-                        for n in range(last):
-                            at = slice(n * LANES, (n + 1) * LANES)
-                            if j == last:
-                                part = corner[t % 2, g, p, r:r + 8, at]
-                            else:
-                                part = early[t, g, p, j * BLOCK + r:j * BLOCK + r + 8, at]
-                            value = value + part * weights[t, g, n]
-                        both.append(value)
-                    here = pl.ds(pl.multiple_of(8 + (me ^ j) * BLOCK + r, 8), 8)
-                    lined[t % 2, g, 0, here, :] = both[0]
-                    lined[t % 2, g, 1, here, :] = both[0] + 2.0 * both[1]
-                    yield
-            turned = (lined[t % 2, g, 0, 8:8 + nsel, :] + lined[t % 2, g, 1, 7:7 + nsel, :]).T
-            out_ref[t * QTILE:(t + 1) * QTILE, g, :] = turned[:QTILE] + turned[QTILE:]
-            yield
-        sent[t].start()
-
-    for step in range(tiles + 1):
+    def sums(u):
+        t, g = units[u]
+        lined[u % 2, 1, 0:8, :] = jnp.zeros((8, LANES), jnp.float32)
+        for j in range(n_ctx):
+            for r in range(0, BLOCK, 8):
+                both = []
+                for p in range(2):
+                    value = far[u % 2, p, j * BLOCK + r:j * BLOCK + r + 8, :] * weights[u, last]
+                    for n in range(last):
+                        at = slice(n * LANES, (n + 1) * LANES)
+                        if j == last:
+                            part = corner[u % 2, p, r:r + 8, at]
+                        else:
+                            part = early[t, g, p, j * BLOCK + r:j * BLOCK + r + 8, at]
+                        value = value + part * weights[u, n]
+                    both.append(value)
+                here = pl.ds(pl.multiple_of(8 + (me ^ j) * BLOCK + r, 8), 8)
+                lined[u % 2, 0, here, :] = both[0]
+                lined[u % 2, 1, here, :] = both[0] + 2.0 * both[1]
+                yield
+        turned = (lined[u % 2, 0, 8:8 + nsel, :] + lined[u % 2, 1, 7:7 + nsel, :]).T
+        out_ref[t * QTILE:(t + 1) * QTILE, g, :] = turned[:QTILE] + turned[QTILE:]
+        if g == own - 1:
+            sent[t].start()
+        yield
+
+    for step in range(len(units) + 1):
         stages = []
-        if step < tiles:
+        if step < len(units):
             stages.append((nsel // 8, exponentials(step)))
         if step >= 1:
-            stages.append((own * (nsel // 8 + 1), sums(step - 1)))
+            stages.append((nsel // 8 + 1, sums(step - 1)))
         interleave(*stages)
 
     least, most = totals[0], totals[0]
@@ -252,8 +261,11 @@
 
     @pl.when(jnp.logical_not(safe))
     def _():
+        first_copy = pltpu.make_async_copy(first_hbm, first_ref, sems.at[0])
+        first_copy.start()
+        first_copy.wait()
         gather_keys(n_ctx, k_refs, keys)
-        shifted(n_head, n_ctx, start_ref, first_ref, raw_q, out_ref, keys, scores, pooled, lined.at[:, 0])
+        shifted(n_head, n_ctx, start_ref, first_ref, raw_q, out_ref, keys, scores, pooled, lined)
         for copy in sent:
             copy.start()
         for copy in sent:
@@ -284,7 +296,7 @@
     def tile(index, _):
         begin = pl.multiple_of(index * QTILE, QTILE)
         first = first_ref[index]
-        row4, reach = limits(n_ctx, tokens, begin, start_ref)
+        row4, reach = limits(n_ctx, tokens, begin, start_ref[0])
 
         for g in range(own):
             weights = []
@@ -367,18 +379,20 @@
     k_part = jax.ShapeDtypeStruct((own, 4, blocks, depth), keys.dtype)
     packed = pl.pallas_call(
         partial(pack_kernel, n_head, key_heads, heads),
-        out_shape=[q_part] * n_head + [k_part],
-        in_specs=[hbm, hbm],
-        out_specs=[vmem] * (n_head + 1),
+        out_shape=[q_part] * n_head + [k_part, jax.ShapeDtypeStruct((tokens // QTILE, 8, LANES), jnp.int32)],
+        in_specs=[hbm] * 3,
+        out_specs=[vmem] * (n_head + 2),
         scratch_shapes=[
             pltpu.VMEM((tokens * key_heads * heads, depth), queries.dtype),
-            pltpu.VMEM((blocks * 4 * key_heads, depth), keys.dtype),
+            pltpu.VMEM((blocks * 4, own, depth), keys.dtype),
+            pltpu.SMEM(tile_first.shape, jnp.int32),
             pltpu.SemaphoreType.DMA((Q_COPIES,)),
             pltpu.SemaphoreType.DMA((K_COPIES,)),
+            pltpu.SemaphoreType.DMA,
         ],
         compiler_params=pltpu.CompilerParams(vmem_limit_bytes=16 * 2 ** 20),
         name="pack",
-    )(in_hbm(queries.reshape(-1, depth)), in_hbm(keys.reshape(-1, depth)))
+    )(in_hbm(queries.reshape(-1, depth)), in_hbm(keys.reshape(-1, n_head, own, depth)), in_hbm(tile_first))
     q_parts, k_parts = list(packed[:n_head]), [packed[n_head]]
 
     def swap(array, axis, size, bit):
@@ -419,26 +433,27 @@
             jax.ShapeDtypeStruct((tiles, own, 2, 3 * BLOCK, most), jnp.float32),
             jax.ShapeDtypeStruct((tiles, own, 8, most), jnp.float32),
         ],
-        in_specs=[smem, smem] + [vmem] * 6,
+        in_specs=[smem] + [vmem] * 7,
         out_specs=[vmem, vmem],
         compiler_params=limit,
         name="early",
-    )(span_start, tile_first, *q_parts[:3], *k_parts[:3])
+    )(span_start, packed[n_head + 1], *q_parts[:3], *k_parts[:3])
     return pl.pallas_call(
         partial(late_kernel, n_head, n_ctx),
         out_shape=result,
-        in_specs=[smem, smem] + [vmem] * (n_head + n_ctx + 2),
+        in_specs=[smem, hbm] + [vmem] * (n_head + n_ctx + 3),
         out_specs=hbm,
         scratch_shapes=scratch + [
-            pltpu.VMEM((2, own, 2, 8 + nsel, LANES), jnp.float32),
-            pltpu.VMEM((2, own, 2, nsel, LANES), jnp.float32),
-            pltpu.VMEM((2, own, 2, BLOCK, most), jnp.float32),
+            pltpu.VMEM((2, 2, 8 + nsel, LANES), jnp.float32),
+            pltpu.VMEM((2, 2, nsel, LANES), jnp.float32),
+            pltpu.VMEM((2, 2, BLOCK, most), jnp.float32),
             pltpu.VMEM((tokens, own, nsel), jnp.float32),
+            pltpu.SMEM(tile_first.shape, jnp.int32),
             pltpu.SemaphoreType.DMA((tiles,)),
         ],
         compiler_params=limit,
         name="late",
-    )(span_start, tile_first, *q_parts, *k_parts, *early)
+    )(span_start, in_hbm(tile_first), packed[n_head + 1], *q_parts, *k_parts, *early)
 
 
 def solution(mesh):

time: 28 us -> 28.1 us (level)
  waiting for transfers between devices: 4.46 us -> 5.51 us
  local copies, waits for them, and re-layouts: 0.65 us -> 0 us
  Pallas kernels: 13.9 us -> 13.6 us
    ppermute x6, waiting for transfers between devices: 4.46 us -> 5.51 us  [swap(): return lax.ppermute(array, axis, [(i, i ^ bit) for i in range(size)])]
    unnamed x2 -> x0, local copies, waits for them, and re-layouts: 0.65 us -> none
    pallas_call x1, Pallas kernels: 2.16 us -> 1.62 us  [per_device(): pl.pallas_call(partial(early_kernel, n_ctx), out_shape=[jax.ShapeDtypeStr...]
    pallas_call x1, Pallas kernels: 9.34 us -> 9.62 us  [per_device(): pl.pallas_call(partial(late_kernel, n_head, n_ctx), out_shape=result, in_...]
  transfers between devices with their start and end apart: 6 -> 6, of which waited for: 2 -> 4; matrix products, arithmetic and copies ran while one was open for 0% -> 0% of each run, Pallas kernels for 8% -> 6%
where the time goes in v12:
time: 28.1 us; the launch traced here: 27.9 us
  Pallas kernels  13.6 us (48%)
  starting transfers between devices  8.19 us (29%)
  waiting for transfers between devices  5.51 us (20%)
  between operations  0.67 us (2%)
    pallas_call x1, Pallas kernels, per_device(): pl.pallas_call(partial(late_kernel, n_head, n_ctx), out_shape=result, in_...  9.62 us
    ppermute x6, starting transfers between devices, swap(): return lax.ppermute(array, axis, [(i, i ^ bit) for i in range(size)])  8.19 us
    ppermute x6, waiting for transfers between devices, swap(): return lax.ppermute(array, axis, [(i, i ^ bit) for i in range(size)])  5.51 us
    pallas_call x1, Pallas kernels, per_device(): pl.pallas_call(partial(pack_kernel, n_head, key_heads, heads), out_shape=...  2.32 us
    pallas_call x1, Pallas kernels, per_device(): pl.pallas_call(partial(early_kernel, n_ctx), out_shape=[jax.ShapeDtypeStr...  1.62 us
  transfers between devices with their start and end apart: 6, of which 4 were waited for; matrix products, arithmetic and copies ran while one was open for 0% of the time, Pallas kernels for 6%

profile of v12, /device:TPU:0, one launch (start us, length us, event | category | flops | bytes accessed | tf_op | source)
XLA Modules:
  0.0 27.9 jit_solution(3956181218769661103)
XLA Ops:
  0.0 2.3 %pack.1 = (bf16[2,2,192,128]{3,2,1,0:T(8,128)(2,1)S(1)}, bf16[2,2,192,128]{3,2,1,0:T(8,128)(2,1)S(1)}, bf16[2,2,192,128]{3,2,1,0:T(8,128)(2,1)S(1)}, bf16[2,2,19...) custom-call(bf16[3072,128]{1,0:T(8,128)(2,1)} %bitcast.2, ...), custom_call_target="tpu_custom_call" | custom-call | tf_op jit(solution)/shard_map/pack/pallas_call | solution.py:380
  2.3 4.1 %collective-permute-start.4 = (bf16[2,4,64,128]{3,2,1,0:T(8,128)(2,1)S(1)}, bf16[2,4,64,128]{3,2,1,0:T(8,128)(2,1)S(1)}, u32[]{:S(2)}, u32[]{:S(2)}) collective-permute-start(bf16[2,4,64,128]{3,2,1,0:T(8,128)(2,1)S(1)} %get-tuple-element.18.refs_3_.refs_4_), channel_id=1, source_target_pairs={{0,8},{4,12},{8,0},{12,4},{1,9},{5,13},{9,1},{13,5},{2,10},{6,14},... | collective-permute-start | bytes 393224 | tf_op jit(solution)/shard_map/ppermute | solution.py:399
  6.4 0.0 collective-permute-start
  6.4 1.5 %collective-permute-start.1 = (bf16[2,2,192,128]{3,2,1,0:T(8,128)(2,1)S(1)}, bf16[2,2,192,128]{3,2,1,0:T(8,128)(2,1)S(1)}, u32[]{:S(2)}, u32[]{:S(2)}) collective-permute-start(bf16[2,2,192,128]{3,2,1,0:T(8,128)(2,1)S(1)} %get-tuple-element.16), channel_id=1, source_target_pairs={{0,2},{1,3},{2,0},{3,1},{4,6},{5,7},{6,4},{7,5},{8,10},{9,11},{10,... | collective-permute-start | bytes 589832 | tf_op jit(solution)/shard_map/ppermute | solution.py:399
  7.9 0.4 %collective-permute-start.2 = (bf16[2,2,192,128]{3,2,1,0:T(8,128)(2,1)S(1)}, bf16[2,2,192,128]{3,2,1,0:T(8,128)(2,1)S(1)}, u32[]{:S(2)}, u32[]{:S(2)}) collective-permute-start(bf16[2,2,192,128]{3,2,1,0:T(8,128)(2,1)S(1)} %get-tuple-element.17), channel_id=1, source_target_pairs={{0,3},{1,2},{2,1},{3,0},{4,7},{5,6},{6,5},{7,4},{8,11},{9,10},{10,... | collective-permute-start | bytes 589832 | tf_op jit(solution)/shard_map/ppermute | solution.py:399
  8.3 1.6 %collective-permute-start.3 = (bf16[2,4,64,128]{3,2,1,0:T(8,128)(2,1)S(1)}, bf16[2,4,64,128]{3,2,1,0:T(8,128)(2,1)S(1)}, u32[]{:S(2)}, u32[]{:S(2)}) collective-permute-start(bf16[2,4,64,128]{3,2,1,0:T(8,128)(2,1)S(1)} %get-tuple-element.18.refs_3_.refs_4_), channel_id=1, source_target_pairs={{0,4},{4,0},{8,12},{12,8},{1,5},{5,1},{9,13},{13,9},{2,6},{6,2},{1... | collective-permute-start | bytes 393224 | tf_op jit(solution)/shard_map/ppermute | solution.py:399
  9.9 3.0 %collective-permute-done.4.refs_5_.refs_6_ = bf16[2,4,64,128]{3,2,1,0:T(8,128)(2,1)S(1)} collective-permute-done((bf16[2,4,64,128]{3,2,1,0:T(8,128)(2,1)S(1)}, bf16[2,4,64,128]{3,2,1,0:T(8,128)(2,1)S(1)}, u32[]{:S(2)}, u32[]{:S(2)}) %collective-permute-start.4) | collective-permute-done | bytes 131104 | tf_op jit(solution)/shard_map/ppermute | solution.py:399
  12.8 0.7 %collective-permute-start.5 = (bf16[2,4,64,128]{3,2,1,0:T(8,128)(2,1)S(1)}, bf16[2,4,64,128]{3,2,1,0:T(8,128)(2,1)S(1)}, u32[]{:S(2)}, u32[]{:S(2)}) collective-permute-start(bf16[2,4,64,128]{3,2,1,0:T(8,128)(2,1)S(1)} %collective-permute-done.4.refs_5_.refs_6_), channel_id=1, source_target_pairs={{0,4},{4,0},{8,12},{12,8},{1,5},{5,1},{9,13},{13,9},{2,6},{6,2},{1... | collective-permute-start | bytes 393224 | tf_op jit(solution)/shard_map/ppermute | solution.py:399
  14.2 1.5 %collective-permute-done.3.refs_4_.refs_5_ = bf16[2,4,64,128]{3,2,1,0:T(8,128)(2,1)S(1)} collective-permute-done((bf16[2,4,64,128]{3,2,1,0:T(8,128)(2,1)S(1)}, bf16[2,4,64,128]{3,2,1,0:T(8,128)(2,1)S(1)}, u32[]{:S(2)}, u32[]{:S(2)}) %collective-permute-start.3) | collective-permute-done | bytes 131104 | tf_op jit(solution)/shard_map/ppermute | solution.py:399
  15.6 0.0 collective-permute-done.refs_1_
  15.6 0.0 collective-permute-done.1.refs_2_
  15.6 1.6 %early.1 = (f32[3,2,2,192,384]{4,3,2,1,0:T(8,128)S(1)}, f32[3,2,8,384]{3,2,1,0:T(8,128)S(1)}) custom-call(s32[1]{0:T(128)S(6)} %copy.5.start_ref, s32[3,8,128]{2,1,0:T(8,128)S(1)} %get-tuple-element.13.spread, bf16[2,2,192,128]{3,2,1,0:T(8,128)(2,1)S(1)} %get-tuple-element.14.refs_0_, bf16[2,2,192,128]{3,2,1,0:T(8,128)(2,1)S(1)} %collective-permute-done.refs_1_, ...), custom_call_target="tpu_custom_call" | custom-call | tf_op jit(solution)/shard_map/early/pallas_call | solution.py:430
  17.3 0.3 %collective-permute-done.2.refs_3_ = bf16[2,2,192,128]{3,2,1,0:T(8,128)(2,1)S(1)} collective-permute-done((bf16[2,2,192,128]{3,2,1,0:T(8,128)(2,1)S(1)}, bf16[2,2,192,128]{3,2,1,0:T(8,128)(2,1)S(1)}, u32[]{:S(2)}, u32[]{:S(2)}) %collective-permute-start.2) | collective-permute-done | bytes 196640 | tf_op jit(solution)/shard_map/ppermute | solution.py:399
  17.6 0.8 %collective-permute-done.5.refs_7_ = bf16[2,4,64,128]{3,2,1,0:T(8,128)(2,1)S(1)} collective-permute-done((bf16[2,4,64,128]{3,2,1,0:T(8,128)(2,1)S(1)}, bf16[2,4,64,128]{3,2,1,0:T(8,128)(2,1)S(1)}, u32[]{:S(2)}, u32[]{:S(2)}) %collective-permute-start.5) | collective-permute-done | bytes 131104 | tf_op jit(solution)/shard_map/ppermute | solution.py:399
  18.3 9.6 %late.1 = f32[192,2,256]{2,1,0:T(2,128)} custom-call(s32[1]{0:T(128)S(6)} %copy.5.start_ref, s32[3]{0:T(128)} %first_hbm.3, s32[3,8,128]{2,1,0:T(8,128)S(1)} %get-tuple-element.13.spread, bf16[2,2,192,128]{3,2,1,0:T(8,128)(2,1)S(1)} %get-tuple-element.14.refs_0_, bf16[2,2,192,128]{3,2,1,0:T(8,128)(2,1)S(1)} %collective-permute-done.refs_1_, ...), custom_call_target="tpu_custom_call" | custom-call | tf_op jit(solution)/shard_map/late/pallas_call | solution.py:441
Async XLA Ops:
  2.3 10.5 %collective-permute-start.4 = (bf16[2,4,64,128]{3,2,1,0:T(8,128)(2,1)S(1)}, bf16[2,4,64,128]{3,2,1,0:T(8,128)(2,1)S(1)}, u32[]{:S(2)}, u32[]{:S(2)}) collective-permute-start(bf16[2,4,64,128]{3,2,1,0:T(8,128)(2,1)S(1)} %get-tuple-element.18.refs_3_.refs_4_), channel_id=1, source_target_pairs={{0,8},{4,12},{8,0},{12,4},{1,9},{5,13},{9,1},{13,5},{2,10},{6,14},... | collective-permute-start | bytes 393224 | tf_op jit(solution)/shard_map/ppermute | solution.py:399
  6.4 9.2 %collective-permute-start = (bf16[2,2,192,128]{3,2,1,0:T(8,128)(2,1)S(1)}, bf16[2,2,192,128]{3,2,1,0:T(8,128)(2,1)S(1)}, u32[]{:S(2)}, u32[]{:S(2)}) collective-permute-start(bf16[2,2,192,128]{3,2,1,0:T(8,128)(2,1)S(1)} %get-tuple-element.15), channel_id=1, source_target_pairs={{0,1},{1,0},{2,3},{3,2},{4,5},{5,4},{6,7},{7,6},{8,9},{9,8},{10,11... | collective-permute-start | bytes 589832 | tf_op jit(solution)/shard_map/ppermute | solution.py:399
  6.4 9.2 %collective-permute-start.1 = (bf16[2,2,192,128]{3,2,1,0:T(8,128)(2,1)S(1)}, bf16[2,2,192,128]{3,2,1,0:T(8,128)(2,1)S(1)}, u32[]{:S(2)}, u32[]{:S(2)}) collective-permute-start(bf16[2,2,192,128]{3,2,1,0:T(8,128)(2,1)S(1)} %get-tuple-element.16), channel_id=1, source_target_pairs={{0,2},{1,3},{2,0},{3,1},{4,6},{5,7},{6,4},{7,5},{8,10},{9,11},{10,... | collective-permute-start | bytes 589832 | tf_op jit(solution)/shard_map/ppermute | solution.py:399
  7.9 9.6 %collective-permute-start.2 = (bf16[2,2,192,128]{3,2,1,0:T(8,128)(2,1)S(1)}, bf16[2,2,192,128]{3,2,1,0:T(8,128)(2,1)S(1)}, u32[]{:S(2)}, u32[]{:S(2)}) collective-permute-start(bf16[2,2,192,128]{3,2,1,0:T(8,128)(2,1)S(1)} %get-tuple-element.17), channel_id=1, source_target_pairs={{0,3},{1,2},{2,1},{3,0},{4,7},{5,6},{6,5},{7,4},{8,11},{9,10},{10,... | collective-permute-start | bytes 589832 | tf_op jit(solution)/shard_map/ppermute | solution.py:399
  8.3 7.3 %collective-permute-start.3 = (bf16[2,4,64,128]{3,2,1,0:T(8,128)(2,1)S(1)}, bf16[2,4,64,128]{3,2,1,0:T(8,128)(2,1)S(1)}, u32[]{:S(2)}, u32[]{:S(2)}) collective-permute-start(bf16[2,4,64,128]{3,2,1,0:T(8,128)(2,1)S(1)} %get-tuple-element.18.refs_3_.refs_4_), channel_id=1, source_target_pairs={{0,4},{4,0},{8,12},{12,8},{1,5},{5,1},{9,13},{13,9},{2,6},{6,2},{1... | collective-permute-start | bytes 393224 | tf_op jit(solution)/shard_map/ppermute | solution.py:399
  12.8 5.5 %collective-permute-start.5 = (bf16[2,4,64,128]{3,2,1,0:T(8,128)(2,1)S(1)}, bf16[2,4,64,128]{3,2,1,0:T(8,128)(2,1)S(1)}, u32[]{:S(2)}, u32[]{:S(2)}) collective-permute-start(bf16[2,4,64,128]{3,2,1,0:T(8,128)(2,1)S(1)} %collective-permute-done.4.refs_5_.refs_6_), channel_id=1, source_target_pairs={{0,4},{4,0},{8,12},{12,8},{1,5},{5,1},{9,13},{13,9},{2,6},{6,2},{1... | collective-permute-start | bytes 393224 | tf_op jit(solution)/shard_map/ppermute | solution.py:399

commit v13 on v12

--- a/solution.py
+++ b/solution.py
@@ -42,37 +42,38 @@
     for copy in k_copies + q_copies + [first_copy]:
         copy.start()
 
+    def bits(value, low, count):
+        return (value >> low.bit_length() - 1) & (count - 1)
+
     out_row = lax.broadcasted_iota(jnp.int32, (own * k_rows, own * k_rows), 0)
     in_row = lax.broadcasted_iota(jnp.int32, (own * k_rows, own * k_rows), 1)
-    source = (out_row % PACK * 4 + out_row // PACK % 4) * own + out_row // k_rows
-    select = jnp.where(in_row == source, 1.0, 0.0).astype(jnp.bfloat16)
+    source = (bits(out_row, 1, PACK) * 4 + bits(out_row, PACK, 4)) * own + bits(out_row, k_rows, own)
+    k_select = jnp.where(in_row == source, 1.0, 0.0).astype(jnp.bfloat16)
+    out_row = lax.broadcasted_iota(jnp.int32, (n_head * width * PACK, q_rows), 0)
+    in_row = lax.broadcasted_iota(jnp.int32, (n_head * width * PACK, q_rows), 1)
+    unit = (bits(out_row, width * PACK, n_head) ^ me) * width + bits(out_row, PACK, width)
+    q_select = jnp.where(in_row == bits(out_row, 1, PACK) * (key_heads * heads) + unit, 1.0, 0.0).astype(jnp.bfloat16)
+
+    first_copy.wait()
+    for t in range(first_hbm.shape[0]):
+        spread[t] = jnp.full((8, LANES), first[t], jnp.int32)
     for block in range(blocks // PACK):
         if block % k_each == 0:
             k_copies[block // k_each].wait()
         rows = k_ref[block * k_rows:(block + 1) * k_rows].reshape(own * k_rows, k_ref.shape[2])
-        moved = jnp.dot(select, rows, preferred_element_type=jnp.float32).astype(jnp.bfloat16)
+        moved = jnp.dot(k_select, rows, preferred_element_type=jnp.float32).astype(jnp.bfloat16)
         for u in range(own * 4):
             k_out[u // 4, u % 4, block * PACK:(block + 1) * PACK, :] = moved[u * PACK:(u + 1) * PACK]
-
-    first_copy.wait()
-    for t in range(first_hbm.shape[0]):
-        spread[t] = jnp.full((8, LANES), first[t], jnp.int32)
-
-    out_row = lax.broadcasted_iota(jnp.int32, (n_head * width * PACK, q_rows), 0)
-    in_row = lax.broadcasted_iota(jnp.int32, (n_head * width * PACK, q_rows), 1)
-    step = out_row // (width * PACK)
-    unit = out_row // PACK % width
-    source = out_row % PACK * (key_heads * heads) + (step ^ me) * width + unit
-    select = jnp.where(in_row == source, 1.0, 0.0).astype(jnp.bfloat16)
     for block in range(tokens // PACK):
         if block % q_each == 0:
             q_copies[block // q_each].wait()
         moved = jnp.dot(
-            select, q_ref[block * q_rows:(block + 1) * q_rows, :], preferred_element_type=jnp.float32
+            q_select, q_ref[block * q_rows:(block + 1) * q_rows, :], preferred_element_type=jnp.float32
         ).astype(jnp.bfloat16)
-        for u in range(n_head * width):
-            d, g, h = u // width, u % width // heads, u % heads
-            q_outs[d][g, h, block * PACK:(block + 1) * PACK, :] = moved[u * PACK:(u + 1) * PACK]
+        for d in range(n_head):
+            for u in range(width):
+                at = (d * width + u) * PACK
+                q_outs[d][u // heads, u % heads, block * PACK:(block + 1) * PACK, :] = moved[at:at + PACK]
 
 
 def gather_keys(n_ctx, k_refs, keys):
@@ -158,8 +159,9 @@
     return masks_at
 
 
-def early_kernel(n_ctx, start_ref, spread, *refs):
-    q_refs, k_refs, (pooled, total_ref) = refs[:3], refs[3:6], refs[6:]
+def early_kernel(n_ctx, n_before, start_ref, spread, *refs):
+    refs = refs[n_before:]
+    q_refs, k_refs, (pooled, total_ref) = refs[:-2 - n_ctx + 1], refs[-2 - n_ctx + 1:-2], refs[-2:]
     own, heads, tokens, depth = q_refs[0].shape
     q_refs = [[ref.at[g] for g in range(own)] for ref in q_refs]
     scale = math.log2(math.e) / math.sqrt(depth)
@@ -170,7 +172,7 @@
             pooled[t, g, 1, j * BLOCK + r:j * BLOCK + r + 8, n * LANES:(n + 1) * LANES] = rest
 
         totals = {}
-        spans = [((0, 1, 2), j) for j in range(3)]
+        spans = [(tuple(range(len(q_refs))), j) for j in range(n_ctx - 1)]
         for _ in pooled_exponentials(q_refs, k_refs, t, range(own), spans, scale, masks_at, put, totals):
             pass
         for (g, n), total in totals.items():
@@ -178,8 +180,8 @@
 
 
 def late_kernel(n_head, n_ctx, start_ref, first_hbm, spread, *refs):
-    raw_q, k_refs, (early, early_total) = refs[:n_head], refs[n_head:n_head + n_ctx], refs[n_head + n_ctx:-10]
-    out_hbm, keys, scores, pooled, lined, far, corner, out_ref, first_ref, sems = refs[-10:]
+    raw_q, k_refs, early = refs[:n_head], refs[n_head:n_head + n_ctx], refs[n_head + n_ctx:-9]
+    out_hbm, keys, scores, pooled, lined, corner, out_ref, first_ref, sems = refs[-9:]
     own, heads, tokens, depth = raw_q[0].shape
     q_refs = [[ref.at[g] for g in range(own)] for ref in raw_q]
     nsel = keys.shape[2]
@@ -197,24 +199,24 @@
 
     units = [(t, g) for t in range(tiles) for g in range(own)]
 
+    def earlier(n):
+        kept, total = early[:2] if n < n_head - 1 else early[2:]
+        n = n if n < n_head - 1 else 0
+        return kept, slice(n * LANES, (n + 1) * LANES), total
+
     def exponentials(u):
         t, g = units[u]
 
         def put(_, n, j, r, lead, rest):
-            if n == last:
-                far[u % 2, 0, j * BLOCK + r:j * BLOCK + r + 8, :] = lead
-                far[u % 2, 1, j * BLOCK + r:j * BLOCK + r + 8, :] = rest
-            else:
-                corner[u % 2, 0, r:r + 8, n * LANES:(n + 1) * LANES] = lead
-                corner[u % 2, 1, r:r + 8, n * LANES:(n + 1) * LANES] = rest
+            corner[u % 2, 0, r:r + 8, n * LANES:(n + 1) * LANES] = lead
+            corner[u % 2, 1, r:r + 8, n * LANES:(n + 1) * LANES] = rest
 
         found = {}
-        spans = [((last,), j) for j in range(last)] + [(tuple(range(n_head)), last)]
+        spans = [(tuple(range(n_head)), last)]
         yield from pooled_exponentials(q_refs, k_refs, t, [g], spans, scale, masks_at, put, found)
         for (_, n), total in found.items():
-            if n < last:
-                total = total + early_total[t, g, :, n * LANES:(n + 1) * LANES]
-            total = jnp.sum(total, axis=0, keepdims=True)
+            _, at_n, early_total = earlier(n)
+            total = jnp.sum(total + early_total[t, g, :, at_n], axis=0, keepdims=True)
             weights[u, n] = factor / total
             totals.append(total)
 
@@ -225,14 +227,15 @@
             for r in range(0, BLOCK, 8):
                 both = []
                 for p in range(2):
-                    value = far[u % 2, p, j * BLOCK + r:j * BLOCK + r + 8, :] * weights[u, last]
-                    for n in range(last):
-                        at = slice(n * LANES, (n + 1) * LANES)
+                    value = None
+                    for n in range(n_head):
                         if j == last:
-                            part = corner[u % 2, p, r:r + 8, at]
+                            part = corner[u % 2, p, r:r + 8, n * LANES:(n + 1) * LANES]
                         else:
-                            part = early[t, g, p, j * BLOCK + r:j * BLOCK + r + 8, at]
-                        value = value + part * weights[u, n]
+                            kept, at_n, _ = earlier(n)
+                            part = kept[t, g, p, j * BLOCK + r:j * BLOCK + r + 8, at_n]
+                        part = part * weights[u, n]
+                        value = part if value is None else value + part
                     both.append(value)
                 here = pl.ds(pl.multiple_of(8 + (me ^ j) * BLOCK + r, 8), 8)
                 lined[u % 2, 0, here, :] = both[0]
@@ -247,7 +250,7 @@
     for step in range(len(units) + 1):
         stages = []
         if step < len(units):
-            stages.append((nsel // 8, exponentials(step)))
+            stages.append((BLOCK // 8, exponentials(step)))
         if step >= 1:
             stages.append((nsel // 8 + 1, sums(step - 1)))
         interleave(*stages)
@@ -426,27 +429,28 @@
             compiler_params=pltpu.CompilerParams(vmem_limit_bytes=52 * 2 ** 20),
             name="importance",
         )(span_start, tile_first, *q_parts, *k_parts)
-    most = 3 * LANES
-    early = pl.pallas_call(
-        partial(early_kernel, n_ctx),
-        out_shape=[
-            jax.ShapeDtypeStruct((tiles, own, 2, 3 * BLOCK, most), jnp.float32),
-            jax.ShapeDtypeStruct((tiles, own, 8, most), jnp.float32),
-        ],
-        in_specs=[smem] + [vmem] * 7,
-        out_specs=[vmem, vmem],
-        compiler_params=limit,
-        name="early",
-    )(span_start, packed[n_head + 1], *q_parts[:3], *k_parts[:3])
+    early = []
+    for sources in (q_parts[:3], q_parts[3:]):
+        lanes = len(sources) * LANES
+        early += pl.pallas_call(
+            partial(early_kernel, n_ctx, len(early[1:])),
+            out_shape=[
+                jax.ShapeDtypeStruct((tiles, own, 2, 3 * BLOCK, lanes), jnp.float32),
+                jax.ShapeDtypeStruct((tiles, own, 8, lanes), jnp.float32),
+            ],
+            in_specs=[smem, vmem] + [pl.BlockSpec(memory_space=pl.ANY)] * len(early[1:]) + [vmem] * (len(sources) + 3),
+            out_specs=[vmem, vmem],
+            compiler_params=limit,
+            name="early",
+        )(span_start, packed[n_head + 1], *early[1:], *sources, *k_parts[:3])
     return pl.pallas_call(
         partial(late_kernel, n_head, n_ctx),
         out_shape=result,
-        in_specs=[smem, hbm] + [vmem] * (n_head + n_ctx + 3),
+        in_specs=[smem, hbm] + [vmem] * (n_head + n_ctx + 5),
         out_specs=hbm,
         scratch_shapes=scratch + [
             pltpu.VMEM((2, 2, 8 + nsel, LANES), jnp.float32),
-            pltpu.VMEM((2, 2, nsel, LANES), jnp.float32),
-            pltpu.VMEM((2, 2, BLOCK, most), jnp.float32),
+            pltpu.VMEM((2, 2, BLOCK, columns), jnp.float32),
             pltpu.VMEM((tokens, own, nsel), jnp.float32),
             pltpu.SMEM(tile_first.shape, jnp.int32),
             pltpu.SemaphoreType.DMA((tiles,)),

time: 28.1 us -> 27.2 us (0.968)
  waiting for transfers between devices: 5.51 us -> 4.85 us
  Pallas kernels: 13.6 us -> 13.3 us
    pallas_call x1, Pallas kernels: 9.62 us -> 8.77 us  [per_device(): pl.pallas_call(partial(late_kernel, n_head, n_ctx), out_shape=result, in_...]
    ppermute x6, waiting for transfers between devices: 5.51 us -> 4.85 us  [swap(): return lax.ppermute(array, axis, [(i, i ^ bit) for i in range(size)])]
    pallas_call x1 -> x2, Pallas kernels: 1.62 us -> 2.27 us  [per_device(): pl.pallas_call(partial(early_kernel, n_ctx, len(early[1:])), out_shape=[j...]
  transfers between devices with their start and end apart: 6 -> 6, of which waited for: 4 -> 4; matrix products, arithmetic and copies ran while one was open for 0% -> 0% of each run, Pallas kernels for 6% -> 8%
where the time goes in v13:
time: 27.2 us; the launch traced here: 27 us
  Pallas kernels  13.3 us (49%)
  starting transfers between devices  8.21 us (30%)
  waiting for transfers between devices  4.85 us (18%)
  between operations  0.68 us (2%)
    pallas_call x1, Pallas kernels, per_device(): pl.pallas_call(partial(late_kernel, n_head, n_ctx), out_shape=result, in_...  8.77 us
    ppermute x6, starting transfers between devices, swap(): return lax.ppermute(array, axis, [(i, i ^ bit) for i in range(size)])  8.21 us
    ppermute x6, waiting for transfers between devices, swap(): return lax.ppermute(array, axis, [(i, i ^ bit) for i in range(size)])  4.85 us
    pallas_call x2, Pallas kernels, per_device(): pl.pallas_call(partial(early_kernel, n_ctx, len(early[1:])), out_shape=[j...  2.27 us
    pallas_call x1, Pallas kernels, per_device(): pl.pallas_call(partial(pack_kernel, n_head, key_heads, heads), out_shape=...  2.25 us
  transfers between devices with their start and end apart: 6, of which 4 were waited for; matrix products, arithmetic and copies ran while one was open for 0% of the time, Pallas kernels for 8%

profile of v13, /device:TPU:0, one launch (start us, length us, event | category | flops | bytes accessed | tf_op | source)
XLA Modules:
  0.0 27.0 jit_solution(15388781138313847428)
XLA Ops:
  0.0 2.3 %pack.1 = (bf16[2,2,192,128]{3,2,1,0:T(8,128)(2,1)S(1)}, bf16[2,2,192,128]{3,2,1,0:T(8,128)(2,1)S(1)}, bf16[2,2,192,128]{3,2,1,0:T(8,128)(2,1)S(1)}, bf16[2,2,19...) custom-call(bf16[3072,128]{1,0:T(8,128)(2,1)} %bitcast.2, ...), custom_call_target="tpu_custom_call" | custom-call | tf_op jit(solution)/shard_map/pack/pallas_call | solution.py:383
  2.3 4.1 %collective-permute-start.4 = (bf16[2,4,64,128]{3,2,1,0:T(8,128)(2,1)S(1)}, bf16[2,4,64,128]{3,2,1,0:T(8,128)(2,1)S(1)}, u32[]{:S(2)}, u32[]{:S(2)}) collective-permute-start(bf16[2,4,64,128]{3,2,1,0:T(8,128)(2,1)S(1)} %get-tuple-element.20.refs_3_.refs_2_.refs_4_), channel_id=1, source_target_pairs={{0,8},{4,12},{8,0},{12,4},{1,9},{5,13},{9,1},{13,5},{2,10},{6,14},... | collective-permute-start | bytes 393224 | tf_op jit(solution)/shard_map/ppermute | solution.py:402
  6.4 0.0 collective-permute-start
  6.4 1.5 %collective-permute-start.1 = (bf16[2,2,192,128]{3,2,1,0:T(8,128)(2,1)S(1)}, bf16[2,2,192,128]{3,2,1,0:T(8,128)(2,1)S(1)}, u32[]{:S(2)}, u32[]{:S(2)}) collective-permute-start(bf16[2,2,192,128]{3,2,1,0:T(8,128)(2,1)S(1)} %get-tuple-element.18), channel_id=1, source_target_pairs={{0,2},{1,3},{2,0},{3,1},{4,6},{5,7},{6,4},{7,5},{8,10},{9,11},{10,... | collective-permute-start | bytes 589832 | tf_op jit(solution)/shard_map/ppermute | solution.py:402
  7.9 0.4 %collective-permute-start.2 = (bf16[2,2,192,128]{3,2,1,0:T(8,128)(2,1)S(1)}, bf16[2,2,192,128]{3,2,1,0:T(8,128)(2,1)S(1)}, u32[]{:S(2)}, u32[]{:S(2)}) collective-permute-start(bf16[2,2,192,128]{3,2,1,0:T(8,128)(2,1)S(1)} %get-tuple-element.19), channel_id=1, source_target_pairs={{0,3},{1,2},{2,1},{3,0},{4,7},{5,6},{6,5},{7,4},{8,11},{9,10},{10,... | collective-permute-start | bytes 589832 | tf_op jit(solution)/shard_map/ppermute | solution.py:402
  8.2 1.6 %collective-permute-start.3 = (bf16[2,4,64,128]{3,2,1,0:T(8,128)(2,1)S(1)}, bf16[2,4,64,128]{3,2,1,0:T(8,128)(2,1)S(1)}, u32[]{:S(2)}, u32[]{:S(2)}) collective-permute-start(bf16[2,4,64,128]{3,2,1,0:T(8,128)(2,1)S(1)} %get-tuple-element.20.refs_3_.refs_2_.refs_4_), channel_id=1, source_target_pairs={{0,4},{4,0},{8,12},{12,8},{1,5},{5,1},{9,13},{13,9},{2,6},{6,2},{1... | collective-permute-start | bytes 393224 | tf_op jit(solution)/shard_map/ppermute | solution.py:402
  9.8 3.0 %collective-permute-done.4.refs_5_.refs_4_.refs_6_ = bf16[2,4,64,128]{3,2,1,0:T(8,128)(2,1)S(1)} collective-permute-done((bf16[2,4,64,128]{3,2,1,0:T(8,128)(2,1)S(1)}, bf16[2,4,64,128]{3,2,1,0:T(8,128)(2,1)S(1)}, u32[]{:S(2)}, u32[]{:S(2)}) %collective-permute-start.4) | collective-permute-done | bytes 131104 | tf_op jit(solution)/shard_map/ppermute | solution.py:402
  12.8 0.7 %collective-permute-start.5 = (bf16[2,4,64,128]{3,2,1,0:T(8,128)(2,1)S(1)}, bf16[2,4,64,128]{3,2,1,0:T(8,128)(2,1)S(1)}, u32[]{:S(2)}, u32[]{:S(2)}) collective-permute-start(bf16[2,4,64,128]{3,2,1,0:T(8,128)(2,1)S(1)} %collective-permute-done.4.refs_5_.refs_4_.refs_6_), channel_id=1, source_target_pairs={{0,4},{4,0},{8,12},{12,8},{1,5},{5,1},{9,13},{13,9},{2,6},{6,2},{1... | collective-permute-start | bytes 393224 | tf_op jit(solution)/shard_map/ppermute | solution.py:402
  14.1 1.5 %collective-permute-done.3.refs_4_.refs_3_.refs_5_ = bf16[2,4,64,128]{3,2,1,0:T(8,128)(2,1)S(1)} collective-permute-done((bf16[2,4,64,128]{3,2,1,0:T(8,128)(2,1)S(1)}, bf16[2,4,64,128]{3,2,1,0:T(8,128)(2,1)S(1)}, u32[]{:S(2)}, u32[]{:S(2)}) %collective-permute-start.3) | collective-permute-done | bytes 131104 | tf_op jit(solution)/shard_map/ppermute | solution.py:402
  15.6 0.0 collective-permute-done.refs_1_
  15.6 0.0 collective-permute-done.1.refs_2_
  15.6 1.6 %early.2 = (f32[3,2,2,192,384]{4,3,2,1,0:T(8,128)S(1)}, f32[3,2,8,384]{3,2,1,0:T(8,128)S(1)}) custom-call(s32[1]{0:T(128)S(6)} %copy.5.start_ref, s32[3,8,128]{2,1,0:T(8,128)S(1)} %get-tuple-element.15.spread, bf16[2,2,192,128]{3,2,1,0:T(8,128)(2,1)S(1)} %get-tuple-element.16.refs_0_, bf16[2,2,192,128]{3,2,1,0:T(8,128)(2,1)S(1)} %collective-permute-done.refs_1_, ...), custom_call_target="tpu_custom_call" | custom-call | tf_op jit(solution)/shard_map/early/pallas_call | solution.py:435
  17.2 0.3 %collective-permute-done.2.refs_1_.refs_3_ = bf16[2,2,192,128]{3,2,1,0:T(8,128)(2,1)S(1)} collective-permute-done((bf16[2,2,192,128]{3,2,1,0:T(8,128)(2,1)S(1)}, bf16[2,2,192,128]{3,2,1,0:T(8,128)(2,1)S(1)}, u32[]{:S(2)}, u32[]{:S(2)}) %collective-permute-start.2) | collective-permute-done | bytes 196640 | tf_op jit(solution)/shard_map/ppermute | solution.py:402
  17.5 0.6 %early.3 = (f32[3,2,2,192,128]{4,3,2,1,0:T(8,128)S(1)}, f32[3,2,8,128]{3,2,1,0:T(8,128)S(1)}) custom-call(s32[1]{0:T(128)S(6)} %copy.5.start_ref, s32[3,8,128]{2,1,0:T(8,128)S(1)} %get-tuple-element.15.spread, f32[3,2,8,384]{3,2,1,0:T(8,128)S(1)} %get-tuple-element.22.refs_0_.refs_9_, bf16[2,2,192,128]{3,2,1,0:T(8,128)(2,1)S(1)} %collective-permute-done.2.refs_1_.refs_3_, ...), custom_call_target="tpu_custom_call" | custom-call | tf_op jit(solution)/shard_map/early/pallas_call | solution.py:435
  18.2 0.1 collective-permute-done.5.refs_7_
  18.3 8.8 %late.1 = f32[192,2,256]{2,1,0:T(2,128)} custom-call(s32[1]{0:T(128)S(6)} %copy.5.start_ref, s32[3]{0:T(128)} %first_hbm.3, s32[3,8,128]{2,1,0:T(8,128)S(1)} %get-tuple-element.15.spread, bf16[2,2,192,128]{3,2,1,0:T(8,128)(2,1)S(1)} %get-tuple-element.16.refs_0_, bf16[2,2,192,128]{3,2,1,0:T(8,128)(2,1)S(1)} %collective-permute-done.refs_1_, ...), custom_call_target="tpu_custom_call" | custom-call | tf_op jit(solution)/shard_map/late/pallas_call | solution.py:446
Async XLA Ops:
  2.3 10.5 %collective-permute-start.4 = (bf16[2,4,64,128]{3,2,1,0:T(8,128)(2,1)S(1)}, bf16[2,4,64,128]{3,2,1,0:T(8,128)(2,1)S(1)}, u32[]{:S(2)}, u32[]{:S(2)}) collective-permute-start(bf16[2,4,64,128]{3,2,1,0:T(8,128)(2,1)S(1)} %get-tuple-element.20.refs_3_.refs_2_.refs_4_), channel_id=1, source_target_pairs={{0,8},{4,12},{8,0},{12,4},{1,9},{5,13},{9,1},{13,5},{2,10},{6,14},... | collective-permute-start | bytes 393224 | tf_op jit(solution)/shard_map/ppermute | solution.py:402
  6.4 9.2 %collective-permute-start = (bf16[2,2,192,128]{3,2,1,0:T(8,128)(2,1)S(1)}, bf16[2,2,192,128]{3,2,1,0:T(8,128)(2,1)S(1)}, u32[]{:S(2)}, u32[]{:S(2)}) collective-permute-start(bf16[2,2,192,128]{3,2,1,0:T(8,128)(2,1)S(1)} %get-tuple-element.17), channel_id=1, source_target_pairs={{0,1},{1,0},{2,3},{3,2},{4,5},{5,4},{6,7},{7,6},{8,9},{9,8},{10,11... | collective-permute-start | bytes 589832 | tf_op jit(solution)/shard_map/ppermute | solution.py:402
  6.4 9.2 %collective-permute-start.1 = (bf16[2,2,192,128]{3,2,1,0:T(8,128)(2,1)S(1)}, bf16[2,2,192,128]{3,2,1,0:T(8,128)(2,1)S(1)}, u32[]{:S(2)}, u32[]{:S(2)}) collective-permute-start(bf16[2,2,192,128]{3,2,1,0:T(8,128)(2,1)S(1)} %get-tuple-element.18), channel_id=1, source_target_pairs={{0,2},{1,3},{2,0},{3,1},{4,6},{5,7},{6,4},{7,5},{8,10},{9,11},{10,... | collective-permute-start | bytes 589832 | tf_op jit(solution)/shard_map/ppermute | solution.py:402
  7.9 9.6 %collective-permute-start.2 = (bf16[2,2,192,128]{3,2,1,0:T(8,128)(2,1)S(1)}, bf16[2,2,192,128]{3,2,1,0:T(8,128)(2,1)S(1)}, u32[]{:S(2)}, u32[]{:S(2)}) collective-permute-start(bf16[2,2,192,128]{3,2,1,0:T(8,128)(2,1)S(1)} %get-tuple-element.19), channel_id=1, source_target_pairs={{0,3},{1,2},{2,1},{3,0},{4,7},{5,6},{6,5},{7,4},{8,11},{9,10},{10,... | collective-permute-start | bytes 589832 | tf_op jit(solution)/shard_map/ppermute | solution.py:402
  8.2 7.3 %collective-permute-start.3 = (bf16[2,4,64,128]{3,2,1,0:T(8,128)(2,1)S(1)}, bf16[2,4,64,128]{3,2,1,0:T(8,128)(2,1)S(1)}, u32[]{:S(2)}, u32[]{:S(2)}) collective-permute-start(bf16[2,4,64,128]{3,2,1,0:T(8,128)(2,1)S(1)} %get-tuple-element.20.refs_3_.refs_2_.refs_4_), channel_id=1, source_target_pairs={{0,4},{4,0},{8,12},{12,8},{1,5},{5,1},{9,13},{13,9},{2,6},{6,2},{1... | collective-permute-start | bytes 393224 | tf_op jit(solution)/shard_map/ppermute | solution.py:402
  12.8 5.5 %collective-permute-start.5 = (bf16[2,4,64,128]{3,2,1,0:T(8,128)(2,1)S(1)}, bf16[2,4,64,128]{3,2,1,0:T(8,128)(2,1)S(1)}, u32[]{:S(2)}, u32[]{:S(2)}) collective-permute-start(bf16[2,4,64,128]{3,2,1,0:T(8,128)(2,1)S(1)} %collective-permute-done.4.refs_5_.refs_4_.refs_6_), channel_id=1, source_target_pairs={{0,4},{4,0},{8,12},{12,8},{1,5},{5,1},{9,13},{13,9},{2,6},{6,2},{1... | collective-permute-start | bytes 393224 | tf_op jit(solution)/shard_map/ppermute | solution.py:402

commit v14 on v13

--- a/solution.py
+++ b/solution.py
@@ -11,7 +11,7 @@
 QTILE = 64
 PACK = 16
 K_COPIES = 2
-Q_COPIES = 3
+Q_COPIES = 4
 LANES = 128
 CHUNK = 512
 SPAN_ROWS = 256
@@ -54,16 +54,6 @@
     unit = (bits(out_row, width * PACK, n_head) ^ me) * width + bits(out_row, PACK, width)
     q_select = jnp.where(in_row == bits(out_row, 1, PACK) * (key_heads * heads) + unit, 1.0, 0.0).astype(jnp.bfloat16)
 
-    first_copy.wait()
-    for t in range(first_hbm.shape[0]):
-        spread[t] = jnp.full((8, LANES), first[t], jnp.int32)
-    for block in range(blocks // PACK):
-        if block % k_each == 0:
-            k_copies[block // k_each].wait()
-        rows = k_ref[block * k_rows:(block + 1) * k_rows].reshape(own * k_rows, k_ref.shape[2])
-        moved = jnp.dot(k_select, rows, preferred_element_type=jnp.float32).astype(jnp.bfloat16)
-        for u in range(own * 4):
-            k_out[u // 4, u % 4, block * PACK:(block + 1) * PACK, :] = moved[u * PACK:(u + 1) * PACK]
     for block in range(tokens // PACK):
         if block % q_each == 0:
             q_copies[block // q_each].wait()
@@ -74,6 +64,16 @@
             for u in range(width):
                 at = (d * width + u) * PACK
                 q_outs[d][u // heads, u % heads, block * PACK:(block + 1) * PACK, :] = moved[at:at + PACK]
+    for block in range(blocks // PACK):
+        if block % k_each == 0:
+            k_copies[block // k_each].wait()
+        rows = k_ref[block * k_rows:(block + 1) * k_rows].reshape(own * k_rows, k_ref.shape[2])
+        moved = jnp.dot(k_select, rows, preferred_element_type=jnp.float32).astype(jnp.bfloat16)
+        for u in range(own * 4):
+            k_out[u // 4, u % 4, block * PACK:(block + 1) * PACK, :] = moved[u * PACK:(u + 1) * PACK]
+    first_copy.wait()
+    for t in range(first_hbm.shape[0]):
+        spread[t] = jnp.full((8, LANES), first[t], jnp.int32)
 
 
 def gather_keys(n_ctx, k_refs, keys):

time: 27.2 us -> 27.4 us (level)
  no operation moved by 1% of the time
where the time goes in v14:
time: 27.4 us; the launch traced here: 27.3 us
  Pallas kernels  13.5 us (49%)
  starting transfers between devices  8.21 us (30%)
  waiting for transfers between devices  4.86 us (18%)
  between operations  0.68 us (2%)
    pallas_call x1, Pallas kernels, per_device(): pl.pallas_call(partial(late_kernel, n_head, n_ctx), out_shape=result, in_...  8.77 us
    ppermute x6, starting transfers between devices, swap(): return lax.ppermute(array, axis, [(i, i ^ bit) for i in range(size)])  8.21 us
    ppermute x6, waiting for transfers between devices, swap(): return lax.ppermute(array, axis, [(i, i ^ bit) for i in range(size)])  4.86 us
    pallas_call x1, Pallas kernels, per_device(): pl.pallas_call(partial(pack_kernel, n_head, key_heads, heads), out_shape=...  2.49 us
    pallas_call x2, Pallas kernels, per_device(): pl.pallas_call(partial(early_kernel, n_ctx, len(early[1:])), out_shape=[j...  2.26 us
  transfers between devices with their start and end apart: 6, of which 4 were waited for; matrix products, arithmetic and copies ran while one was open for 0% of the time, Pallas kernels for 8%

profile of v14, /device:TPU:0, one launch (start us, length us, event | category | flops | bytes accessed | tf_op | source)
XLA Modules:
  0.0 27.3 jit_solution(11800420457581648913)
XLA Ops:
  0.0 2.5 %pack.1 = (bf16[2,2,192,128]{3,2,1,0:T(8,128)(2,1)S(1)}, bf16[2,2,192,128]{3,2,1,0:T(8,128)(2,1)S(1)}, bf16[2,2,192,128]{3,2,1,0:T(8,128)(2,1)S(1)}, bf16[2,2,19...) custom-call(bf16[3072,128]{1,0:T(8,128)(2,1)} %bitcast.2, ...), custom_call_target="tpu_custom_call" | custom-call | tf_op jit(solution)/shard_map/pack/pallas_call | solution.py:383
  2.5 4.1 %collective-permute-start.4 = (bf16[2,4,64,128]{3,2,1,0:T(8,128)(2,1)S(1)}, bf16[2,4,64,128]{3,2,1,0:T(8,128)(2,1)S(1)}, u32[]{:S(2)}, u32[]{:S(2)}) collective-permute-start(bf16[2,4,64,128]{3,2,1,0:T(8,128)(2,1)S(1)} %get-tuple-element.20.refs_3_.refs_2_.refs_4_), channel_id=1, source_target_pairs={{0,8},{4,12},{8,0},{12,4},{1,9},{5,13},{9,1},{13,5},{2,10},{6,14},... | collective-permute-start | bytes 393224 | tf_op jit(solution)/shard_map/ppermute | solution.py:402
  6.6 0.0 collective-permute-start
  6.6 1.5 %collective-permute-start.1 = (bf16[2,2,192,128]{3,2,1,0:T(8,128)(2,1)S(1)}, bf16[2,2,192,128]{3,2,1,0:T(8,128)(2,1)S(1)}, u32[]{:S(2)}, u32[]{:S(2)}) collective-permute-start(bf16[2,2,192,128]{3,2,1,0:T(8,128)(2,1)S(1)} %get-tuple-element.18), channel_id=1, source_target_pairs={{0,2},{1,3},{2,0},{3,1},{4,6},{5,7},{6,4},{7,5},{8,10},{9,11},{10,... | collective-permute-start | bytes 589832 | tf_op jit(solution)/shard_map/ppermute | solution.py:402
  8.1 0.4 %collective-permute-start.2 = (bf16[2,2,192,128]{3,2,1,0:T(8,128)(2,1)S(1)}, bf16[2,2,192,128]{3,2,1,0:T(8,128)(2,1)S(1)}, u32[]{:S(2)}, u32[]{:S(2)}) collective-permute-start(bf16[2,2,192,128]{3,2,1,0:T(8,128)(2,1)S(1)} %get-tuple-element.19), channel_id=1, source_target_pairs={{0,3},{1,2},{2,1},{3,0},{4,7},{5,6},{6,5},{7,4},{8,11},{9,10},{10,... | collective-permute-start | bytes 589832 | tf_op jit(solution)/shard_map/ppermute | solution.py:402
  8.5 1.6 %collective-permute-start.3 = (bf16[2,4,64,128]{3,2,1,0:T(8,128)(2,1)S(1)}, bf16[2,4,64,128]{3,2,1,0:T(8,128)(2,1)S(1)}, u32[]{:S(2)}, u32[]{:S(2)}) collective-permute-start(bf16[2,4,64,128]{3,2,1,0:T(8,128)(2,1)S(1)} %get-tuple-element.20.refs_3_.refs_2_.refs_4_), channel_id=1, source_target_pairs={{0,4},{4,0},{8,12},{12,8},{1,5},{5,1},{9,13},{13,9},{2,6},{6,2},{1... | collective-permute-start | bytes 393224 | tf_op jit(solution)/shard_map/ppermute | solution.py:402
  10.0 3.0 %collective-permute-done.4.refs_5_.refs_4_.refs_6_ = bf16[2,4,64,128]{3,2,1,0:T(8,128)(2,1)S(1)} collective-permute-done((bf16[2,4,64,128]{3,2,1,0:T(8,128)(2,1)S(1)}, bf16[2,4,64,128]{3,2,1,0:T(8,128)(2,1)S(1)}, u32[]{:S(2)}, u32[]{:S(2)}) %collective-permute-start.4) | collective-permute-done | bytes 131104 | tf_op jit(solution)/shard_map/ppermute | solution.py:402
  13.0 0.7 %collective-permute-start.5 = (bf16[2,4,64,128]{3,2,1,0:T(8,128)(2,1)S(1)}, bf16[2,4,64,128]{3,2,1,0:T(8,128)(2,1)S(1)}, u32[]{:S(2)}, u32[]{:S(2)}) collective-permute-start(bf16[2,4,64,128]{3,2,1,0:T(8,128)(2,1)S(1)} %collective-permute-done.4.refs_5_.refs_4_.refs_6_), channel_id=1, source_target_pairs={{0,4},{4,0},{8,12},{12,8},{1,5},{5,1},{9,13},{13,9},{2,6},{6,2},{1... | collective-permute-start | bytes 393224 | tf_op jit(solution)/shard_map/ppermute | solution.py:402
  14.3 1.5 %collective-permute-done.3.refs_4_.refs_3_.refs_5_ = bf16[2,4,64,128]{3,2,1,0:T(8,128)(2,1)S(1)} collective-permute-done((bf16[2,4,64,128]{3,2,1,0:T(8,128)(2,1)S(1)}, bf16[2,4,64,128]{3,2,1,0:T(8,128)(2,1)S(1)}, u32[]{:S(2)}, u32[]{:S(2)}) %collective-permute-start.3) | collective-permute-done | bytes 131104 | tf_op jit(solution)/shard_map/ppermute | solution.py:402
  15.8 0.0 collective-permute-done.refs_1_
  15.8 0.0 collective-permute-done.1.refs_2_
  15.8 1.6 %early.2 = (f32[3,2,2,192,384]{4,3,2,1,0:T(8,128)S(1)}, f32[3,2,8,384]{3,2,1,0:T(8,128)S(1)}) custom-call(s32[1]{0:T(128)S(6)} %copy.5.start_ref, s32[3,8,128]{2,1,0:T(8,128)S(1)} %get-tuple-element.15.spread, bf16[2,2,192,128]{3,2,1,0:T(8,128)(2,1)S(1)} %get-tuple-element.16.refs_0_, bf16[2,2,192,128]{3,2,1,0:T(8,128)(2,1)S(1)} %collective-permute-done.refs_1_, ...), custom_call_target="tpu_custom_call" | custom-call | tf_op jit(solution)/shard_map/early/pallas_call | solution.py:435
  17.4 0.3 %collective-permute-done.2.refs_1_.refs_3_ = bf16[2,2,192,128]{3,2,1,0:T(8,128)(2,1)S(1)} collective-permute-done((bf16[2,2,192,128]{3,2,1,0:T(8,128)(2,1)S(1)}, bf16[2,2,192,128]{3,2,1,0:T(8,128)(2,1)S(1)}, u32[]{:S(2)}, u32[]{:S(2)}) %collective-permute-start.2) | collective-permute-done | bytes 196640 | tf_op jit(solution)/shard_map/ppermute | solution.py:402
  17.7 0.6 %early.3 = (f32[3,2,2,192,128]{4,3,2,1,0:T(8,128)S(1)}, f32[3,2,8,128]{3,2,1,0:T(8,128)S(1)}) custom-call(s32[1]{0:T(128)S(6)} %copy.5.start_ref, s32[3,8,128]{2,1,0:T(8,128)S(1)} %get-tuple-element.15.spread, f32[3,2,8,384]{3,2,1,0:T(8,128)S(1)} %get-tuple-element.22.refs_0_.refs_9_, bf16[2,2,192,128]{3,2,1,0:T(8,128)(2,1)S(1)} %collective-permute-done.2.refs_1_.refs_3_, ...), custom_call_target="tpu_custom_call" | custom-call | tf_op jit(solution)/shard_map/early/pallas_call | solution.py:435
  18.4 0.1 collective-permute-done.5.refs_7_
  18.5 8.8 %late.1 = f32[192,2,256]{2,1,0:T(2,128)} custom-call(s32[1]{0:T(128)S(6)} %copy.5.start_ref, s32[3]{0:T(128)} %first_hbm.3, s32[3,8,128]{2,1,0:T(8,128)S(1)} %get-tuple-element.15.spread, bf16[2,2,192,128]{3,2,1,0:T(8,128)(2,1)S(1)} %get-tuple-element.16.refs_0_, bf16[2,2,192,128]{3,2,1,0:T(8,128)(2,1)S(1)} %collective-permute-done.refs_1_, ...), custom_call_target="tpu_custom_call" | custom-call | tf_op jit(solution)/shard_map/late/pallas_call | solution.py:446
Async XLA Ops:
  2.5 10.5 %collective-permute-start.4 = (bf16[2,4,64,128]{3,2,1,0:T(8,128)(2,1)S(1)}, bf16[2,4,64,128]{3,2,1,0:T(8,128)(2,1)S(1)}, u32[]{:S(2)}, u32[]{:S(2)}) collective-permute-start(bf16[2,4,64,128]{3,2,1,0:T(8,128)(2,1)S(1)} %get-tuple-element.20.refs_3_.refs_2_.refs_4_), channel_id=1, source_target_pairs={{0,8},{4,12},{8,0},{12,4},{1,9},{5,13},{9,1},{13,5},{2,10},{6,14},... | collective-permute-start | bytes 393224 | tf_op jit(solution)/shard_map/ppermute | solution.py:402
  6.6 9.2 %collective-permute-start = (bf16[2,2,192,128]{3,2,1,0:T(8,128)(2,1)S(1)}, bf16[2,2,192,128]{3,2,1,0:T(8,128)(2,1)S(1)}, u32[]{:S(2)}, u32[]{:S(2)}) collective-permute-start(bf16[2,2,192,128]{3,2,1,0:T(8,128)(2,1)S(1)} %get-tuple-element.17), channel_id=1, source_target_pairs={{0,1},{1,0},{2,3},{3,2},{4,5},{5,4},{6,7},{7,6},{8,9},{9,8},{10,11... | collective-permute-start | bytes 589832 | tf_op jit(solution)/shard_map/ppermute | solution.py:402
  6.6 9.2 %collective-permute-start.1 = (bf16[2,2,192,128]{3,2,1,0:T(8,128)(2,1)S(1)}, bf16[2,2,192,128]{3,2,1,0:T(8,128)(2,1)S(1)}, u32[]{:S(2)}, u32[]{:S(2)}) collective-permute-start(bf16[2,2,192,128]{3,2,1,0:T(8,128)(2,1)S(1)} %get-tuple-element.18), channel_id=1, source_target_pairs={{0,2},{1,3},{2,0},{3,1},{4,6},{5,7},{6,4},{7,5},{8,10},{9,11},{10,... | collective-permute-start | bytes 589832 | tf_op jit(solution)/shard_map/ppermute | solution.py:402
  8.1 9.6 %collective-permute-start.2 = (bf16[2,2,192,128]{3,2,1,0:T(8,128)(2,1)S(1)}, bf16[2,2,192,128]{3,2,1,0:T(8,128)(2,1)S(1)}, u32[]{:S(2)}, u32[]{:S(2)}) collective-permute-start(bf16[2,2,192,128]{3,2,1,0:T(8,128)(2,1)S(1)} %get-tuple-element.19), channel_id=1, source_target_pairs={{0,3},{1,2},{2,1},{3,0},{4,7},{5,6},{6,5},{7,4},{8,11},{9,10},{10,... | collective-permute-start | bytes 589832 | tf_op jit(solution)/shard_map/ppermute | solution.py:402
  8.5 7.3 %collective-permute-start.3 = (bf16[2,4,64,128]{3,2,1,0:T(8,128)(2,1)S(1)}, bf16[2,4,64,128]{3,2,1,0:T(8,128)(2,1)S(1)}, u32[]{:S(2)}, u32[]{:S(2)}) collective-permute-start(bf16[2,4,64,128]{3,2,1,0:T(8,128)(2,1)S(1)} %get-tuple-element.20.refs_3_.refs_2_.refs_4_), channel_id=1, source_target_pairs={{0,4},{4,0},{8,12},{12,8},{1,5},{5,1},{9,13},{13,9},{2,6},{6,2},{1... | collective-permute-start | bytes 393224 | tf_op jit(solution)/shard_map/ppermute | solution.py:402
  13.0 5.5 %collective-permute-start.5 = (bf16[2,4,64,128]{3,2,1,0:T(8,128)(2,1)S(1)}, bf16[2,4,64,128]{3,2,1,0:T(8,128)(2,1)S(1)}, u32[]{:S(2)}, u32[]{:S(2)}) collective-permute-start(bf16[2,4,64,128]{3,2,1,0:T(8,128)(2,1)S(1)} %collective-permute-done.4.refs_5_.refs_4_.refs_6_), channel_id=1, source_target_pairs={{0,4},{4,0},{8,12},{12,8},{1,5},{5,1},{9,13},{13,9},{2,6},{6,2},{1... | collective-permute-start | bytes 393224 | tf_op jit(solution)/shard_map/ppermute | solution.py:402

commit v15 on v13

--- a/solution.py
+++ b/solution.py
@@ -30,12 +30,12 @@
     tokens = q_outs[0].shape[2]
     blocks = k_out.shape[2]
     q_rows = PACK * key_heads * heads
-    k_rows = PACK * 4
+    k_rows = PACK * 4 * key_heads
     k_copies, q_copies = [], []
     k_each, q_each = blocks // PACK // K_COPIES, tokens // PACK // Q_COPIES
     for n in range(K_COPIES):
         at = pl.ds(n * k_each * k_rows, k_each * k_rows)
-        k_copies.append(pltpu.make_async_copy(k_hbm.at[at, me], k_ref.at[at], k_sems.at[n]))
+        k_copies.append(pltpu.make_async_copy(k_hbm.at[at], k_ref.at[at], k_sems.at[n]))
     for n in range(Q_COPIES):
         at = pl.ds(n * q_each * q_rows, q_each * q_rows)
         q_copies.append(pltpu.make_async_copy(q_hbm.at[at], q_ref.at[at], q_sems.at[n]))
@@ -45,9 +45,9 @@
     def bits(value, low, count):
         return (value >> low.bit_length() - 1) & (count - 1)
 
-    out_row = lax.broadcasted_iota(jnp.int32, (own * k_rows, own * k_rows), 0)
-    in_row = lax.broadcasted_iota(jnp.int32, (own * k_rows, own * k_rows), 1)
-    source = (bits(out_row, 1, PACK) * 4 + bits(out_row, PACK, 4)) * own + bits(out_row, k_rows, own)
+    out_row = lax.broadcasted_iota(jnp.int32, (own * 4 * PACK, k_rows), 0)
+    in_row = lax.broadcasted_iota(jnp.int32, (own * 4 * PACK, k_rows), 1)
+    source = (bits(out_row, 1, PACK) * 4 + bits(out_row, PACK, 4)) * key_heads + me * own + bits(out_row, 4 * PACK, own)
     k_select = jnp.where(in_row == source, 1.0, 0.0).astype(jnp.bfloat16)
     out_row = lax.broadcasted_iota(jnp.int32, (n_head * width * PACK, q_rows), 0)
     in_row = lax.broadcasted_iota(jnp.int32, (n_head * width * PACK, q_rows), 1)
@@ -60,8 +60,9 @@
     for block in range(blocks // PACK):
         if block % k_each == 0:
             k_copies[block // k_each].wait()
-        rows = k_ref[block * k_rows:(block + 1) * k_rows].reshape(own * k_rows, k_ref.shape[2])
-        moved = jnp.dot(k_select, rows, preferred_element_type=jnp.float32).astype(jnp.bfloat16)
+        moved = jnp.dot(
+            k_select, k_ref[block * k_rows:(block + 1) * k_rows, :], preferred_element_type=jnp.float32
+        ).astype(jnp.bfloat16)
         for u in range(own * 4):
             k_out[u // 4, u % 4, block * PACK:(block + 1) * PACK, :] = moved[u * PACK:(u + 1) * PACK]
     for block in range(tokens // PACK):
@@ -387,7 +388,7 @@
         out_specs=[vmem] * (n_head + 2),
         scratch_shapes=[
             pltpu.VMEM((tokens * key_heads * heads, depth), queries.dtype),
-            pltpu.VMEM((blocks * 4, own, depth), keys.dtype),
+            pltpu.VMEM((blocks * 4 * key_heads, depth), keys.dtype),
             pltpu.SMEM(tile_first.shape, jnp.int32),
             pltpu.SemaphoreType.DMA((Q_COPIES,)),
             pltpu.SemaphoreType.DMA((K_COPIES,)),
@@ -395,7 +396,7 @@
         ],
         compiler_params=pltpu.CompilerParams(vmem_limit_bytes=16 * 2 ** 20),
         name="pack",
-    )(in_hbm(queries.reshape(-1, depth)), in_hbm(keys.reshape(-1, n_head, own, depth)), in_hbm(tile_first))
+    )(in_hbm(queries.reshape(-1, depth)), in_hbm(keys.reshape(-1, depth)), in_hbm(tile_first))
     q_parts, k_parts = list(packed[:n_head]), [packed[n_head]]
 
     def swap(array, axis, size, bit):

time: 27.2 us -> 27.3 us (level)
  no operation moved by 1% of the time
where the time goes in v15:
time: 27.3 us; the launch traced here: 27.1 us
  Pallas kernels  13.4 us (49%)
  starting transfers between devices  8.2 us (30%)
  waiting for transfers between devices  4.85 us (18%)
  between operations  0.68 us (2%)
    pallas_call x1, Pallas kernels, per_device(): pl.pallas_call(partial(late_kernel, n_head, n_ctx), out_shape=result, in_...  8.76 us
    ppermute x6, starting transfers between devices, swap(): return lax.ppermute(array, axis, [(i, i ^ bit) for i in range(size)])  8.2 us
    ppermute x6, waiting for transfers between devices, swap(): return lax.ppermute(array, axis, [(i, i ^ bit) for i in range(size)])  4.85 us
    pallas_call x1, Pallas kernels, per_device(): pl.pallas_call(partial(pack_kernel, n_head, key_heads, heads), out_shape=...  2.38 us
    pallas_call x2, Pallas kernels, per_device(): pl.pallas_call(partial(early_kernel, n_ctx, len(early[1:])), out_shape=[j...  2.26 us
  transfers between devices with their start and end apart: 6, of which 4 were waited for; matrix products, arithmetic and copies ran while one was open for 0% of the time, Pallas kernels for 8%

profile of v15, /device:TPU:0, one launch (start us, length us, event | category | flops | bytes accessed | tf_op | source)
XLA Modules:
  0.0 27.1 jit_solution(2025853156498432838)
XLA Ops:
  0.0 2.4 %pack.1 = (bf16[2,2,192,128]{3,2,1,0:T(8,128)(2,1)S(1)}, bf16[2,2,192,128]{3,2,1,0:T(8,128)(2,1)S(1)}, bf16[2,2,192,128]{3,2,1,0:T(8,128)(2,1)S(1)}, bf16[2,2,19...) custom-call(bf16[3072,128]{1,0:T(8,128)(2,1)} %bitcast.2, ...), custom_call_target="tpu_custom_call" | custom-call | tf_op jit(solution)/shard_map/pack/pallas_call | solution.py:384
  2.4 4.1 %collective-permute-start.4 = (bf16[2,4,64,128]{3,2,1,0:T(8,128)(2,1)S(1)}, bf16[2,4,64,128]{3,2,1,0:T(8,128)(2,1)S(1)}, u32[]{:S(2)}, u32[]{:S(2)}) collective-permute-start(bf16[2,4,64,128]{3,2,1,0:T(8,128)(2,1)S(1)} %get-tuple-element.20.refs_3_.refs_2_.refs_4_), channel_id=1, source_target_pairs={{0,8},{4,12},{8,0},{12,4},{1,9},{5,13},{9,1},{13,5},{2,10},{6,14},... | collective-permute-start | bytes 393224 | tf_op jit(solution)/shard_map/ppermute | solution.py:403
  6.5 0.0 collective-permute-start
  6.5 1.5 %collective-permute-start.1 = (bf16[2,2,192,128]{3,2,1,0:T(8,128)(2,1)S(1)}, bf16[2,2,192,128]{3,2,1,0:T(8,128)(2,1)S(1)}, u32[]{:S(2)}, u32[]{:S(2)}) collective-permute-start(bf16[2,2,192,128]{3,2,1,0:T(8,128)(2,1)S(1)} %get-tuple-element.18), channel_id=1, source_target_pairs={{0,2},{1,3},{2,0},{3,1},{4,6},{5,7},{6,4},{7,5},{8,10},{9,11},{10,... | collective-permute-start | bytes 589832 | tf_op jit(solution)/shard_map/ppermute | solution.py:403
  8.0 0.4 %collective-permute-start.2 = (bf16[2,2,192,128]{3,2,1,0:T(8,128)(2,1)S(1)}, bf16[2,2,192,128]{3,2,1,0:T(8,128)(2,1)S(1)}, u32[]{:S(2)}, u32[]{:S(2)}) collective-permute-start(bf16[2,2,192,128]{3,2,1,0:T(8,128)(2,1)S(1)} %get-tuple-element.19), channel_id=1, source_target_pairs={{0,3},{1,2},{2,1},{3,0},{4,7},{5,6},{6,5},{7,4},{8,11},{9,10},{10,... | collective-permute-start | bytes 589832 | tf_op jit(solution)/shard_map/ppermute | solution.py:403
  8.4 1.6 %collective-permute-start.3 = (bf16[2,4,64,128]{3,2,1,0:T(8,128)(2,1)S(1)}, bf16[2,4,64,128]{3,2,1,0:T(8,128)(2,1)S(1)}, u32[]{:S(2)}, u32[]{:S(2)}) collective-permute-start(bf16[2,4,64,128]{3,2,1,0:T(8,128)(2,1)S(1)} %get-tuple-element.20.refs_3_.refs_2_.refs_4_), channel_id=1, source_target_pairs={{0,4},{4,0},{8,12},{12,8},{1,5},{5,1},{9,13},{13,9},{2,6},{6,2},{1... | collective-permute-start | bytes 393224 | tf_op jit(solution)/shard_map/ppermute | solution.py:403
  9.9 3.0 %collective-permute-done.4.refs_5_.refs_4_.refs_6_ = bf16[2,4,64,128]{3,2,1,0:T(8,128)(2,1)S(1)} collective-permute-done((bf16[2,4,64,128]{3,2,1,0:T(8,128)(2,1)S(1)}, bf16[2,4,64,128]{3,2,1,0:T(8,128)(2,1)S(1)}, u32[]{:S(2)}, u32[]{:S(2)}) %collective-permute-start.4) | collective-permute-done | bytes 131104 | tf_op jit(solution)/shard_map/ppermute | solution.py:403
  12.9 0.7 %collective-permute-start.5 = (bf16[2,4,64,128]{3,2,1,0:T(8,128)(2,1)S(1)}, bf16[2,4,64,128]{3,2,1,0:T(8,128)(2,1)S(1)}, u32[]{:S(2)}, u32[]{:S(2)}) collective-permute-start(bf16[2,4,64,128]{3,2,1,0:T(8,128)(2,1)S(1)} %collective-permute-done.4.refs_5_.refs_4_.refs_6_), channel_id=1, source_target_pairs={{0,4},{4,0},{8,12},{12,8},{1,5},{5,1},{9,13},{13,9},{2,6},{6,2},{1... | collective-permute-start | bytes 393224 | tf_op jit(solution)/shard_map/ppermute | solution.py:403
  14.2 1.5 %collective-permute-done.3.refs_4_.refs_3_.refs_5_ = bf16[2,4,64,128]{3,2,1,0:T(8,128)(2,1)S(1)} collective-permute-done((bf16[2,4,64,128]{3,2,1,0:T(8,128)(2,1)S(1)}, bf16[2,4,64,128]{3,2,1,0:T(8,128)(2,1)S(1)}, u32[]{:S(2)}, u32[]{:S(2)}) %collective-permute-start.3) | collective-permute-done | bytes 131104 | tf_op jit(solution)/shard_map/ppermute | solution.py:403
  15.7 0.0 collective-permute-done.refs_1_
  15.7 0.0 collective-permute-done.1.refs_2_
  15.7 1.6 %early.2 = (f32[3,2,2,192,384]{4,3,2,1,0:T(8,128)S(1)}, f32[3,2,8,384]{3,2,1,0:T(8,128)S(1)}) custom-call(s32[1]{0:T(128)S(6)} %copy.5.start_ref, s32[3,8,128]{2,1,0:T(8,128)S(1)} %get-tuple-element.15.spread, bf16[2,2,192,128]{3,2,1,0:T(8,128)(2,1)S(1)} %get-tuple-element.16.refs_0_, bf16[2,2,192,128]{3,2,1,0:T(8,128)(2,1)S(1)} %collective-permute-done.refs_1_, ...), custom_call_target="tpu_custom_call" | custom-call | tf_op jit(solution)/shard_map/early/pallas_call | solution.py:436
  17.3 0.3 %collective-permute-done.2.refs_1_.refs_3_ = bf16[2,2,192,128]{3,2,1,0:T(8,128)(2,1)S(1)} collective-permute-done((bf16[2,2,192,128]{3,2,1,0:T(8,128)(2,1)S(1)}, bf16[2,2,192,128]{3,2,1,0:T(8,128)(2,1)S(1)}, u32[]{:S(2)}, u32[]{:S(2)}) %collective-permute-start.2) | collective-permute-done | bytes 196640 | tf_op jit(solution)/shard_map/ppermute | solution.py:403
  17.6 0.6 %early.3 = (f32[3,2,2,192,128]{4,3,2,1,0:T(8,128)S(1)}, f32[3,2,8,128]{3,2,1,0:T(8,128)S(1)}) custom-call(s32[1]{0:T(128)S(6)} %copy.5.start_ref, s32[3,8,128]{2,1,0:T(8,128)S(1)} %get-tuple-element.15.spread, f32[3,2,8,384]{3,2,1,0:T(8,128)S(1)} %get-tuple-element.22.refs_0_.refs_9_, bf16[2,2,192,128]{3,2,1,0:T(8,128)(2,1)S(1)} %collective-permute-done.2.refs_1_.refs_3_, ...), custom_call_target="tpu_custom_call" | custom-call | tf_op jit(solution)/shard_map/early/pallas_call | solution.py:436
  18.3 0.1 collective-permute-done.5.refs_7_
  18.4 8.8 %late.1 = f32[192,2,256]{2,1,0:T(2,128)} custom-call(s32[1]{0:T(128)S(6)} %copy.5.start_ref, s32[3]{0:T(128)} %first_hbm.3, s32[3,8,128]{2,1,0:T(8,128)S(1)} %get-tuple-element.15.spread, bf16[2,2,192,128]{3,2,1,0:T(8,128)(2,1)S(1)} %get-tuple-element.16.refs_0_, bf16[2,2,192,128]{3,2,1,0:T(8,128)(2,1)S(1)} %collective-permute-done.refs_1_, ...), custom_call_target="tpu_custom_call" | custom-call | tf_op jit(solution)/shard_map/late/pallas_call | solution.py:447
Async XLA Ops:
  2.4 10.5 %collective-permute-start.4 = (bf16[2,4,64,128]{3,2,1,0:T(8,128)(2,1)S(1)}, bf16[2,4,64,128]{3,2,1,0:T(8,128)(2,1)S(1)}, u32[]{:S(2)}, u32[]{:S(2)}) collective-permute-start(bf16[2,4,64,128]{3,2,1,0:T(8,128)(2,1)S(1)} %get-tuple-element.20.refs_3_.refs_2_.refs_4_), channel_id=1, source_target_pairs={{0,8},{4,12},{8,0},{12,4},{1,9},{5,13},{9,1},{13,5},{2,10},{6,14},... | collective-permute-start | bytes 393224 | tf_op jit(solution)/shard_map/ppermute | solution.py:403
  6.5 9.2 %collective-permute-start = (bf16[2,2,192,128]{3,2,1,0:T(8,128)(2,1)S(1)}, bf16[2,2,192,128]{3,2,1,0:T(8,128)(2,1)S(1)}, u32[]{:S(2)}, u32[]{:S(2)}) collective-permute-start(bf16[2,2,192,128]{3,2,1,0:T(8,128)(2,1)S(1)} %get-tuple-element.17), channel_id=1, source_target_pairs={{0,1},{1,0},{2,3},{3,2},{4,5},{5,4},{6,7},{7,6},{8,9},{9,8},{10,11... | collective-permute-start | bytes 589832 | tf_op jit(solution)/shard_map/ppermute | solution.py:403
  6.5 9.2 %collective-permute-start.1 = (bf16[2,2,192,128]{3,2,1,0:T(8,128)(2,1)S(1)}, bf16[2,2,192,128]{3,2,1,0:T(8,128)(2,1)S(1)}, u32[]{:S(2)}, u32[]{:S(2)}) collective-permute-start(bf16[2,2,192,128]{3,2,1,0:T(8,128)(2,1)S(1)} %get-tuple-element.18), channel_id=1, source_target_pairs={{0,2},{1,3},{2,0},{3,1},{4,6},{5,7},{6,4},{7,5},{8,10},{9,11},{10,... | collective-permute-start | bytes 589832 | tf_op jit(solution)/shard_map/ppermute | solution.py:403
  8.0 9.6 %collective-permute-start.2 = (bf16[2,2,192,128]{3,2,1,0:T(8,128)(2,1)S(1)}, bf16[2,2,192,128]{3,2,1,0:T(8,128)(2,1)S(1)}, u32[]{:S(2)}, u32[]{:S(2)}) collective-permute-start(bf16[2,2,192,128]{3,2,1,0:T(8,128)(2,1)S(1)} %get-tuple-element.19), channel_id=1, source_target_pairs={{0,3},{1,2},{2,1},{3,0},{4,7},{5,6},{6,5},{7,4},{8,11},{9,10},{10,... | collective-permute-start | bytes 589832 | tf_op jit(solution)/shard_map/ppermute | solution.py:403
  8.4 7.3 %collective-permute-start.3 = (bf16[2,4,64,128]{3,2,1,0:T(8,128)(2,1)S(1)}, bf16[2,4,64,128]{3,2,1,0:T(8,128)(2,1)S(1)}, u32[]{:S(2)}, u32[]{:S(2)}) collective-permute-start(bf16[2,4,64,128]{3,2,1,0:T(8,128)(2,1)S(1)} %get-tuple-element.20.refs_3_.refs_2_.refs_4_), channel_id=1, source_target_pairs={{0,4},{4,0},{8,12},{12,8},{1,5},{5,1},{9,13},{13,9},{2,6},{6,2},{1... | collective-permute-start | bytes 393224 | tf_op jit(solution)/shard_map/ppermute | solution.py:403
  12.9 5.5 %collective-permute-start.5 = (bf16[2,4,64,128]{3,2,1,0:T(8,128)(2,1)S(1)}, bf16[2,4,64,128]{3,2,1,0:T(8,128)(2,1)S(1)}, u32[]{:S(2)}, u32[]{:S(2)}) collective-permute-start(bf16[2,4,64,128]{3,2,1,0:T(8,128)(2,1)S(1)} %collective-permute-done.4.refs_5_.refs_4_.refs_6_), channel_id=1, source_target_pairs={{0,4},{4,0},{8,12},{12,8},{1,5},{5,1},{9,13},{13,9},{2,6},{6,2},{1... | collective-permute-start | bytes 393224 | tf_op jit(solution)/shard_map/ppermute | solution.py:403

commit v16 on v15

--- a/solution.py
+++ b/solution.py
@@ -11,7 +11,7 @@
 QTILE = 64
 PACK = 16
 K_COPIES = 2
-Q_COPIES = 3
+Q_COPIES = 6
 LANES = 128
 CHUNK = 512
 SPAN_ROWS = 256
@@ -404,6 +404,8 @@
 
     for d in range(1, n_head):
         q_parts[d] = swap(q_parts[d], "head", n_head, d)
+    if n_head > 2:
+        q_parts[1], q_parts[2] = q_parts[2], q_parts[1]
     bit = n_ctx // 2
     k_parts = {0: packed[n_head]}
     while bit:

time: 27.3 us -> 28 us (1.026)
  Pallas kernels: 13.4 us -> 14 us
  starting transfers between devices: 8.2 us -> 8.51 us
    pallas_call x1, Pallas kernels: 2.38 us -> 3 us  [per_device(): pl.pallas_call(partial(pack_kernel, n_head, key_heads, heads), out_shape=...]
    ppermute x6, starting transfers between devices: 8.2 us -> 8.51 us  [swap(): return lax.ppermute(array, axis, [(i, i ^ bit) for i in range(size)])]
    ppermute x6, waiting for transfers between devices: 4.85 us -> 4.57 us  [swap(): return lax.ppermute(array, axis, [(i, i ^ bit) for i in range(size)])]
  transfers between devices with their start and end apart: 6 -> 6, of which waited for: 4 -> 3; matrix products, arithmetic and copies ran while one was open for 0% -> 0% of each run, Pallas kernels for 8% -> 8%
where the time goes in v16:
time: 28 us; the launch traced here: 27.8 us
  Pallas kernels  14 us (50%)
  starting transfers between devices  8.51 us (30%)
  waiting for transfers between devices  4.57 us (16%)
  between operations  0.69 us (2%)
    pallas_call x1, Pallas kernels, per_device(): pl.pallas_call(partial(late_kernel, n_head, n_ctx), out_shape=result, in_...  8.78 us
    ppermute x6, starting transfers between devices, swap(): return lax.ppermute(array, axis, [(i, i ^ bit) for i in range(size)])  8.51 us
    ppermute x6, waiting for transfers between devices, swap(): return lax.ppermute(array, axis, [(i, i ^ bit) for i in range(size)])  4.57 us
    pallas_call x1, Pallas kernels, per_device(): pl.pallas_call(partial(pack_kernel, n_head, key_heads, heads), out_shape=...  3 us
    pallas_call x2, Pallas kernels, per_device(): pl.pallas_call(partial(early_kernel, n_ctx, len(early[1:])), out_shape=[j...  2.28 us
  transfers between devices with their start and end apart: 6, of which 3 were waited for; matrix products, arithmetic and copies ran while one was open for 0% of the time, Pallas kernels for 8%

profile of v16, /device:TPU:0, one launch (start us, length us, event | category | flops | bytes accessed | tf_op | source)
XLA Modules:
  0.0 27.8 jit_solution(4141622837321607709)
XLA Ops:
  0.0 3.0 %pack.1 = (bf16[2,2,192,128]{3,2,1,0:T(8,128)(2,1)S(1)}, bf16[2,2,192,128]{3,2,1,0:T(8,128)(2,1)S(1)}, bf16[2,2,192,128]{3,2,1,0:T(8,128)(2,1)S(1)}, bf16[2,2,19...) custom-call(bf16[3072,128]{1,0:T(8,128)(2,1)} %bitcast.2, ...), custom_call_target="tpu_custom_call" | custom-call | tf_op jit(solution)/shard_map/pack/pallas_call | solution.py:384
  3.0 4.1 %collective-permute-start.4 = (bf16[2,4,64,128]{3,2,1,0:T(8,128)(2,1)S(1)}, bf16[2,4,64,128]{3,2,1,0:T(8,128)(2,1)S(1)}, u32[]{:S(2)}, u32[]{:S(2)}) collective-permute-start(bf16[2,4,64,128]{3,2,1,0:T(8,128)(2,1)S(1)} %get-tuple-element.20.refs_3_.refs_2_.refs_4_), channel_id=1, source_target_pairs={{0,8},{4,12},{8,0},{12,4},{1,9},{5,13},{9,1},{13,5},{2,10},{6,14},... | collective-permute-start | bytes 393224 | tf_op jit(solution)/shard_map/ppermute | solution.py:403
  7.1 1.5 %collective-permute-start = (bf16[2,2,192,128]{3,2,1,0:T(8,128)(2,1)S(1)}, bf16[2,2,192,128]{3,2,1,0:T(8,128)(2,1)S(1)}, u32[]{:S(2)}, u32[]{:S(2)}) collective-permute-start(bf16[2,2,192,128]{3,2,1,0:T(8,128)(2,1)S(1)} %get-tuple-element.17), channel_id=1, source_target_pairs={{0,2},{1,3},{2,0},{3,1},{4,6},{5,7},{6,4},{7,5},{8,10},{9,11},{10,... | collective-permute-start | bytes 589832 | tf_op jit(solution)/shard_map/ppermute | solution.py:403
  8.6 0.0 collective-permute-start.1
  8.6 0.6 %collective-permute-start.2 = (bf16[2,2,192,128]{3,2,1,0:T(8,128)(2,1)S(1)}, bf16[2,2,192,128]{3,2,1,0:T(8,128)(2,1)S(1)}, u32[]{:S(2)}, u32[]{:S(2)}) collective-permute-start(bf16[2,2,192,128]{3,2,1,0:T(8,128)(2,1)S(1)} %get-tuple-element.19), channel_id=1, source_target_pairs={{0,3},{1,2},{2,1},{3,0},{4,7},{5,6},{6,5},{7,4},{8,11},{9,10},{10,... | collective-permute-start | bytes 589832 | tf_op jit(solution)/shard_map/ppermute | solution.py:403
  9.3 1.6 %collective-permute-start.3 = (bf16[2,4,64,128]{3,2,1,0:T(8,128)(2,1)S(1)}, bf16[2,4,64,128]{3,2,1,0:T(8,128)(2,1)S(1)}, u32[]{:S(2)}, u32[]{:S(2)}) collective-permute-start(bf16[2,4,64,128]{3,2,1,0:T(8,128)(2,1)S(1)} %get-tuple-element.20.refs_3_.refs_2_.refs_4_), channel_id=1, source_target_pairs={{0,4},{4,0},{8,12},{12,8},{1,5},{5,1},{9,13},{13,9},{2,6},{6,2},{1... | collective-permute-start | bytes 393224 | tf_op jit(solution)/shard_map/ppermute | solution.py:403
  10.9 2.7 %collective-permute-done.4.refs_5_.refs_4_.refs_6_ = bf16[2,4,64,128]{3,2,1,0:T(8,128)(2,1)S(1)} collective-permute-done((bf16[2,4,64,128]{3,2,1,0:T(8,128)(2,1)S(1)}, bf16[2,4,64,128]{3,2,1,0:T(8,128)(2,1)S(1)}, u32[]{:S(2)}, u32[]{:S(2)}) %collective-permute-start.4) | collective-permute-done | bytes 131104 | tf_op jit(solution)/shard_map/ppermute | solution.py:403
  13.5 0.7 %collective-permute-start.5 = (bf16[2,4,64,128]{3,2,1,0:T(8,128)(2,1)S(1)}, bf16[2,4,64,128]{3,2,1,0:T(8,128)(2,1)S(1)}, u32[]{:S(2)}, u32[]{:S(2)}) collective-permute-start(bf16[2,4,64,128]{3,2,1,0:T(8,128)(2,1)S(1)} %collective-permute-done.4.refs_5_.refs_4_.refs_6_), channel_id=1, source_target_pairs={{0,4},{4,0},{8,12},{12,8},{1,5},{5,1},{9,13},{13,9},{2,6},{6,2},{1... | collective-permute-start | bytes 393224 | tf_op jit(solution)/shard_map/ppermute | solution.py:403
  14.9 1.5 %collective-permute-done.3.refs_4_.refs_3_.refs_5_ = bf16[2,4,64,128]{3,2,1,0:T(8,128)(2,1)S(1)} collective-permute-done((bf16[2,4,64,128]{3,2,1,0:T(8,128)(2,1)S(1)}, bf16[2,4,64,128]{3,2,1,0:T(8,128)(2,1)S(1)}, u32[]{:S(2)}, u32[]{:S(2)}) %collective-permute-start.3) | collective-permute-done | bytes 131104 | tf_op jit(solution)/shard_map/ppermute | solution.py:403
  16.3 0.0 collective-permute-done.refs_1_
  16.4 0.0 collective-permute-done.1.refs_2_
  16.4 1.6 %early.2 = (f32[3,2,2,192,384]{4,3,2,1,0:T(8,128)S(1)}, f32[3,2,8,384]{3,2,1,0:T(8,128)S(1)}) custom-call(s32[1]{0:T(128)S(6)} %copy.5.start_ref, s32[3,8,128]{2,1,0:T(8,128)S(1)} %get-tuple-element.15.spread, bf16[2,2,192,128]{3,2,1,0:T(8,128)(2,1)S(1)} %get-tuple-element.16.refs_0_, bf16[2,2,192,128]{3,2,1,0:T(8,128)(2,1)S(1)} %collective-permute-done.refs_1_, ...), custom_call_target="tpu_custom_call" | custom-call | tf_op jit(solution)/shard_map/early/pallas_call | solution.py:438
  18.0 0.0 collective-permute-done.2.refs_1_.refs_3_
  18.0 0.6 %early.3 = (f32[3,2,2,192,128]{4,3,2,1,0:T(8,128)S(1)}, f32[3,2,8,128]{3,2,1,0:T(8,128)S(1)}) custom-call(s32[1]{0:T(128)S(6)} %copy.5.start_ref, s32[3,8,128]{2,1,0:T(8,128)S(1)} %get-tuple-element.15.spread, f32[3,2,8,384]{3,2,1,0:T(8,128)S(1)} %get-tuple-element.22.refs_0_.refs_9_, bf16[2,2,192,128]{3,2,1,0:T(8,128)(2,1)S(1)} %collective-permute-done.2.refs_1_.refs_3_, ...), custom_call_target="tpu_custom_call" | custom-call | tf_op jit(solution)/shard_map/early/pallas_call | solution.py:438
  18.7 0.4 %collective-permute-done.5.refs_7_ = bf16[2,4,64,128]{3,2,1,0:T(8,128)(2,1)S(1)} collective-permute-done((bf16[2,4,64,128]{3,2,1,0:T(8,128)(2,1)S(1)}, bf16[2,4,64,128]{3,2,1,0:T(8,128)(2,1)S(1)}, u32[]{:S(2)}, u32[]{:S(2)}) %collective-permute-start.5) | collective-permute-done | bytes 131104 | tf_op jit(solution)/shard_map/ppermute | solution.py:403
  19.0 8.8 %late.1 = f32[192,2,256]{2,1,0:T(2,128)} custom-call(s32[1]{0:T(128)S(6)} %copy.5.start_ref, s32[3]{0:T(128)} %first_hbm.3, s32[3,8,128]{2,1,0:T(8,128)S(1)} %get-tuple-element.15.spread, bf16[2,2,192,128]{3,2,1,0:T(8,128)(2,1)S(1)} %get-tuple-element.16.refs_0_, bf16[2,2,192,128]{3,2,1,0:T(8,128)(2,1)S(1)} %collective-permute-done.refs_1_, ...), custom_call_target="tpu_custom_call" | custom-call | tf_op jit(solution)/shard_map/late/pallas_call | solution.py:449
Async XLA Ops:
  3.0 10.5 %collective-permute-start.4 = (bf16[2,4,64,128]{3,2,1,0:T(8,128)(2,1)S(1)}, bf16[2,4,64,128]{3,2,1,0:T(8,128)(2,1)S(1)}, u32[]{:S(2)}, u32[]{:S(2)}) collective-permute-start(bf16[2,4,64,128]{3,2,1,0:T(8,128)(2,1)S(1)} %get-tuple-element.20.refs_3_.refs_2_.refs_4_), channel_id=1, source_target_pairs={{0,8},{4,12},{8,0},{12,4},{1,9},{5,13},{9,1},{13,5},{2,10},{6,14},... | collective-permute-start | bytes 393224 | tf_op jit(solution)/shard_map/ppermute | solution.py:403
  7.1 9.2 %collective-permute-start = (bf16[2,2,192,128]{3,2,1,0:T(8,128)(2,1)S(1)}, bf16[2,2,192,128]{3,2,1,0:T(8,128)(2,1)S(1)}, u32[]{:S(2)}, u32[]{:S(2)}) collective-permute-start(bf16[2,2,192,128]{3,2,1,0:T(8,128)(2,1)S(1)} %get-tuple-element.17), channel_id=1, source_target_pairs={{0,2},{1,3},{2,0},{3,1},{4,6},{5,7},{6,4},{7,5},{8,10},{9,11},{10,... | collective-permute-start | bytes 589832 | tf_op jit(solution)/shard_map/ppermute | solution.py:403
  8.6 7.7 %collective-permute-start.1 = (bf16[2,2,192,128]{3,2,1,0:T(8,128)(2,1)S(1)}, bf16[2,2,192,128]{3,2,1,0:T(8,128)(2,1)S(1)}, u32[]{:S(2)}, u32[]{:S(2)}) collective-permute-start(bf16[2,2,192,128]{3,2,1,0:T(8,128)(2,1)S(1)} %get-tuple-element.18), channel_id=1, source_target_pairs={{0,1},{1,0},{2,3},{3,2},{4,5},{5,4},{6,7},{7,6},{8,9},{9,8},{10,11... | collective-permute-start | bytes 589832 | tf_op jit(solution)/shard_map/ppermute | solution.py:403
  8.6 9.4 %collective-permute-start.2 = (bf16[2,2,192,128]{3,2,1,0:T(8,128)(2,1)S(1)}, bf16[2,2,192,128]{3,2,1,0:T(8,128)(2,1)S(1)}, u32[]{:S(2)}, u32[]{:S(2)}) collective-permute-start(bf16[2,2,192,128]{3,2,1,0:T(8,128)(2,1)S(1)} %get-tuple-element.19), channel_id=1, source_target_pairs={{0,3},{1,2},{2,1},{3,0},{4,7},{5,6},{6,5},{7,4},{8,11},{9,10},{10,... | collective-permute-start | bytes 589832 | tf_op jit(solution)/shard_map/ppermute | solution.py:403
  9.3 7.1 %collective-permute-start.3 = (bf16[2,4,64,128]{3,2,1,0:T(8,128)(2,1)S(1)}, bf16[2,4,64,128]{3,2,1,0:T(8,128)(2,1)S(1)}, u32[]{:S(2)}, u32[]{:S(2)}) collective-permute-start(bf16[2,4,64,128]{3,2,1,0:T(8,128)(2,1)S(1)} %get-tuple-element.20.refs_3_.refs_2_.refs_4_), channel_id=1, source_target_pairs={{0,4},{4,0},{8,12},{12,8},{1,5},{5,1},{9,13},{13,9},{2,6},{6,2},{1... | collective-permute-start | bytes 393224 | tf_op jit(solution)/shard_map/ppermute | solution.py:403
  13.5 5.5 %collective-permute-start.5 = (bf16[2,4,64,128]{3,2,1,0:T(8,128)(2,1)S(1)}, bf16[2,4,64,128]{3,2,1,0:T(8,128)(2,1)S(1)}, u32[]{:S(2)}, u32[]{:S(2)}) collective-permute-start(bf16[2,4,64,128]{3,2,1,0:T(8,128)(2,1)S(1)} %collective-permute-done.4.refs_5_.refs_4_.refs_6_), channel_id=1, source_target_pairs={{0,4},{4,0},{8,12},{12,8},{1,5},{5,1},{9,13},{13,9},{2,6},{6,2},{1... | collective-permute-start | bytes 393224 | tf_op jit(solution)/shard_map/ppermute | solution.py:403

commit v17 on v15

--- a/solution.py
+++ b/solution.py
@@ -10,8 +10,8 @@
 
 QTILE = 64
 PACK = 16
-K_COPIES = 2
-Q_COPIES = 3
+K_COPIES = 1
+Q_COPIES = 1
 LANES = 128
 CHUNK = 512
 SPAN_ROWS = 256

time: 27.3 us -> 26.9 us (0.985)
  Pallas kernels: 13.4 us -> 13 us
    pallas_call x1, Pallas kernels: 2.38 us -> 1.92 us  [per_device(): pl.pallas_call(partial(pack_kernel, n_head, key_heads, heads), out_shape=...]
where the time goes in v17:
time: 26.9 us; the launch traced here: 26.7 us
  Pallas kernels  13 us (48%)
  starting transfers between devices  8.2 us (30%)
  waiting for transfers between devices  4.85 us (18%)
  between operations  0.68 us (3%)
    pallas_call x1, Pallas kernels, per_device(): pl.pallas_call(partial(late_kernel, n_head, n_ctx), out_shape=result, in_...  8.77 us
    ppermute x6, starting transfers between devices, swap(): return lax.ppermute(array, axis, [(i, i ^ bit) for i in range(size)])  8.2 us
    ppermute x6, waiting for transfers between devices, swap(): return lax.ppermute(array, axis, [(i, i ^ bit) for i in range(size)])  4.85 us
    pallas_call x2, Pallas kernels, per_device(): pl.pallas_call(partial(early_kernel, n_ctx, len(early[1:])), out_shape=[j...  2.27 us
    pallas_call x1, Pallas kernels, per_device(): pl.pallas_call(partial(pack_kernel, n_head, key_heads, heads), out_shape=...  1.92 us
  transfers between devices with their start and end apart: 6, of which 4 were waited for; matrix products, arithmetic and copies ran while one was open for 0% of the time, Pallas kernels for 8%

profile of v17, /device:TPU:0, one launch (start us, length us, event | category | flops | bytes accessed | tf_op | source)
XLA Modules:
  0.0 26.7 jit_solution(13899282684784564379)
XLA Ops:
  0.0 1.9 %pack.1 = (bf16[2,2,192,128]{3,2,1,0:T(8,128)(2,1)S(1)}, bf16[2,2,192,128]{3,2,1,0:T(8,128)(2,1)S(1)}, bf16[2,2,192,128]{3,2,1,0:T(8,128)(2,1)S(1)}, bf16[2,2,19...) custom-call(bf16[3072,128]{1,0:T(8,128)(2,1)} %bitcast.2, ...), custom_call_target="tpu_custom_call" | custom-call | tf_op jit(solution)/shard_map/pack/pallas_call | solution.py:384
  1.9 4.1 %collective-permute-start.4 = (bf16[2,4,64,128]{3,2,1,0:T(8,128)(2,1)S(1)}, bf16[2,4,64,128]{3,2,1,0:T(8,128)(2,1)S(1)}, u32[]{:S(2)}, u32[]{:S(2)}) collective-permute-start(bf16[2,4,64,128]{3,2,1,0:T(8,128)(2,1)S(1)} %get-tuple-element.20.refs_3_.refs_2_.refs_4_), channel_id=1, source_target_pairs={{0,8},{4,12},{8,0},{12,4},{1,9},{5,13},{9,1},{13,5},{2,10},{6,14},... | collective-permute-start | bytes 393224 | tf_op jit(solution)/shard_map/ppermute | solution.py:403
  6.0 0.0 collective-permute-start
  6.0 1.5 %collective-permute-start.1 = (bf16[2,2,192,128]{3,2,1,0:T(8,128)(2,1)S(1)}, bf16[2,2,192,128]{3,2,1,0:T(8,128)(2,1)S(1)}, u32[]{:S(2)}, u32[]{:S(2)}) collective-permute-start(bf16[2,2,192,128]{3,2,1,0:T(8,128)(2,1)S(1)} %get-tuple-element.18), channel_id=1, source_target_pairs={{0,2},{1,3},{2,0},{3,1},{4,6},{5,7},{6,4},{7,5},{8,10},{9,11},{10,... | collective-permute-start | bytes 589832 | tf_op jit(solution)/shard_map/ppermute | solution.py:403
  7.5 0.4 %collective-permute-start.2 = (bf16[2,2,192,128]{3,2,1,0:T(8,128)(2,1)S(1)}, bf16[2,2,192,128]{3,2,1,0:T(8,128)(2,1)S(1)}, u32[]{:S(2)}, u32[]{:S(2)}) collective-permute-start(bf16[2,2,192,128]{3,2,1,0:T(8,128)(2,1)S(1)} %get-tuple-element.19), channel_id=1, source_target_pairs={{0,3},{1,2},{2,1},{3,0},{4,7},{5,6},{6,5},{7,4},{8,11},{9,10},{10,... | collective-permute-start | bytes 589832 | tf_op jit(solution)/shard_map/ppermute | solution.py:403
  7.9 1.6 %collective-permute-start.3 = (bf16[2,4,64,128]{3,2,1,0:T(8,128)(2,1)S(1)}, bf16[2,4,64,128]{3,2,1,0:T(8,128)(2,1)S(1)}, u32[]{:S(2)}, u32[]{:S(2)}) collective-permute-start(bf16[2,4,64,128]{3,2,1,0:T(8,128)(2,1)S(1)} %get-tuple-element.20.refs_3_.refs_2_.refs_4_), channel_id=1, source_target_pairs={{0,4},{4,0},{8,12},{12,8},{1,5},{5,1},{9,13},{13,9},{2,6},{6,2},{1... | collective-permute-start | bytes 393224 | tf_op jit(solution)/shard_map/ppermute | solution.py:403
  9.5 3.0 %collective-permute-done.4.refs_5_.refs_4_.refs_6_ = bf16[2,4,64,128]{3,2,1,0:T(8,128)(2,1)S(1)} collective-permute-done((bf16[2,4,64,128]{3,2,1,0:T(8,128)(2,1)S(1)}, bf16[2,4,64,128]{3,2,1,0:T(8,128)(2,1)S(1)}, u32[]{:S(2)}, u32[]{:S(2)}) %collective-permute-start.4) | collective-permute-done | bytes 131104 | tf_op jit(solution)/shard_map/ppermute | solution.py:403
  12.4 0.7 %collective-permute-start.5 = (bf16[2,4,64,128]{3,2,1,0:T(8,128)(2,1)S(1)}, bf16[2,4,64,128]{3,2,1,0:T(8,128)(2,1)S(1)}, u32[]{:S(2)}, u32[]{:S(2)}) collective-permute-start(bf16[2,4,64,128]{3,2,1,0:T(8,128)(2,1)S(1)} %collective-permute-done.4.refs_5_.refs_4_.refs_6_), channel_id=1, source_target_pairs={{0,4},{4,0},{8,12},{12,8},{1,5},{5,1},{9,13},{13,9},{2,6},{6,2},{1... | collective-permute-start | bytes 393224 | tf_op jit(solution)/shard_map/ppermute | solution.py:403
  13.8 1.5 %collective-permute-done.3.refs_4_.refs_3_.refs_5_ = bf16[2,4,64,128]{3,2,1,0:T(8,128)(2,1)S(1)} collective-permute-done((bf16[2,4,64,128]{3,2,1,0:T(8,128)(2,1)S(1)}, bf16[2,4,64,128]{3,2,1,0:T(8,128)(2,1)S(1)}, u32[]{:S(2)}, u32[]{:S(2)}) %collective-permute-start.3) | collective-permute-done | bytes 131104 | tf_op jit(solution)/shard_map/ppermute | solution.py:403
  15.2 0.0 collective-permute-done.refs_1_
  15.2 0.0 collective-permute-done.1.refs_2_
  15.2 1.6 %early.2 = (f32[3,2,2,192,384]{4,3,2,1,0:T(8,128)S(1)}, f32[3,2,8,384]{3,2,1,0:T(8,128)S(1)}) custom-call(s32[1]{0:T(128)S(6)} %copy.5.start_ref, s32[3,8,128]{2,1,0:T(8,128)S(1)} %get-tuple-element.15.spread, bf16[2,2,192,128]{3,2,1,0:T(8,128)(2,1)S(1)} %get-tuple-element.16.refs_0_, bf16[2,2,192,128]{3,2,1,0:T(8,128)(2,1)S(1)} %collective-permute-done.refs_1_, ...), custom_call_target="tpu_custom_call" | custom-call | tf_op jit(solution)/shard_map/early/pallas_call | solution.py:436
  16.9 0.3 %collective-permute-done.2.refs_1_.refs_3_ = bf16[2,2,192,128]{3,2,1,0:T(8,128)(2,1)S(1)} collective-permute-done((bf16[2,2,192,128]{3,2,1,0:T(8,128)(2,1)S(1)}, bf16[2,2,192,128]{3,2,1,0:T(8,128)(2,1)S(1)}, u32[]{:S(2)}, u32[]{:S(2)}) %collective-permute-start.2) | collective-permute-done | bytes 196640 | tf_op jit(solution)/shard_map/ppermute | solution.py:403
  17.2 0.6 %early.3 = (f32[3,2,2,192,128]{4,3,2,1,0:T(8,128)S(1)}, f32[3,2,8,128]{3,2,1,0:T(8,128)S(1)}) custom-call(s32[1]{0:T(128)S(6)} %copy.5.start_ref, s32[3,8,128]{2,1,0:T(8,128)S(1)} %get-tuple-element.15.spread, f32[3,2,8,384]{3,2,1,0:T(8,128)S(1)} %get-tuple-element.22.refs_0_.refs_9_, bf16[2,2,192,128]{3,2,1,0:T(8,128)(2,1)S(1)} %collective-permute-done.2.refs_1_.refs_3_, ...), custom_call_target="tpu_custom_call" | custom-call | tf_op jit(solution)/shard_map/early/pallas_call | solution.py:436
  17.8 0.1 collective-permute-done.5.refs_7_
  17.9 8.8 %late.1 = f32[192,2,256]{2,1,0:T(2,128)} custom-call(s32[1]{0:T(128)S(6)} %copy.5.start_ref, s32[3]{0:T(128)} %first_hbm.3, s32[3,8,128]{2,1,0:T(8,128)S(1)} %get-tuple-element.15.spread, bf16[2,2,192,128]{3,2,1,0:T(8,128)(2,1)S(1)} %get-tuple-element.16.refs_0_, bf16[2,2,192,128]{3,2,1,0:T(8,128)(2,1)S(1)} %collective-permute-done.refs_1_, ...), custom_call_target="tpu_custom_call" | custom-call | tf_op jit(solution)/shard_map/late/pallas_call | solution.py:447
Async XLA Ops:
  1.9 10.5 %collective-permute-start.4 = (bf16[2,4,64,128]{3,2,1,0:T(8,128)(2,1)S(1)}, bf16[2,4,64,128]{3,2,1,0:T(8,128)(2,1)S(1)}, u32[]{:S(2)}, u32[]{:S(2)}) collective-permute-start(bf16[2,4,64,128]{3,2,1,0:T(8,128)(2,1)S(1)} %get-tuple-element.20.refs_3_.refs_2_.refs_4_), channel_id=1, source_target_pairs={{0,8},{4,12},{8,0},{12,4},{1,9},{5,13},{9,1},{13,5},{2,10},{6,14},... | collective-permute-start | bytes 393224 | tf_op jit(solution)/shard_map/ppermute | solution.py:403
  6.0 9.2 %collective-permute-start = (bf16[2,2,192,128]{3,2,1,0:T(8,128)(2,1)S(1)}, bf16[2,2,192,128]{3,2,1,0:T(8,128)(2,1)S(1)}, u32[]{:S(2)}, u32[]{:S(2)}) collective-permute-start(bf16[2,2,192,128]{3,2,1,0:T(8,128)(2,1)S(1)} %get-tuple-element.17), channel_id=1, source_target_pairs={{0,1},{1,0},{2,3},{3,2},{4,5},{5,4},{6,7},{7,6},{8,9},{9,8},{10,11... | collective-permute-start | bytes 589832 | tf_op jit(solution)/shard_map/ppermute | solution.py:403
  6.0 9.2 %collective-permute-start.1 = (bf16[2,2,192,128]{3,2,1,0:T(8,128)(2,1)S(1)}, bf16[2,2,192,128]{3,2,1,0:T(8,128)(2,1)S(1)}, u32[]{:S(2)}, u32[]{:S(2)}) collective-permute-start(bf16[2,2,192,128]{3,2,1,0:T(8,128)(2,1)S(1)} %get-tuple-element.18), channel_id=1, source_target_pairs={{0,2},{1,3},{2,0},{3,1},{4,6},{5,7},{6,4},{7,5},{8,10},{9,11},{10,... | collective-permute-start | bytes 589832 | tf_op jit(solution)/shard_map/ppermute | solution.py:403
  7.5 9.6 %collective-permute-start.2 = (bf16[2,2,192,128]{3,2,1,0:T(8,128)(2,1)S(1)}, bf16[2,2,192,128]{3,2,1,0:T(8,128)(2,1)S(1)}, u32[]{:S(2)}, u32[]{:S(2)}) collective-permute-start(bf16[2,2,192,128]{3,2,1,0:T(8,128)(2,1)S(1)} %get-tuple-element.19), channel_id=1, source_target_pairs={{0,3},{1,2},{2,1},{3,0},{4,7},{5,6},{6,5},{7,4},{8,11},{9,10},{10,... | collective-permute-start | bytes 589832 | tf_op jit(solution)/shard_map/ppermute | solution.py:403
  7.9 7.3 %collective-permute-start.3 = (bf16[2,4,64,128]{3,2,1,0:T(8,128)(2,1)S(1)}, bf16[2,4,64,128]{3,2,1,0:T(8,128)(2,1)S(1)}, u32[]{:S(2)}, u32[]{:S(2)}) collective-permute-start(bf16[2,4,64,128]{3,2,1,0:T(8,128)(2,1)S(1)} %get-tuple-element.20.refs_3_.refs_2_.refs_4_), channel_id=1, source_target_pairs={{0,4},{4,0},{8,12},{12,8},{1,5},{5,1},{9,13},{13,9},{2,6},{6,2},{1... | collective-permute-start | bytes 393224 | tf_op jit(solution)/shard_map/ppermute | solution.py:403
  12.4 5.5 %collective-permute-start.5 = (bf16[2,4,64,128]{3,2,1,0:T(8,128)(2,1)S(1)}, bf16[2,4,64,128]{3,2,1,0:T(8,128)(2,1)S(1)}, u32[]{:S(2)}, u32[]{:S(2)}) collective-permute-start(bf16[2,4,64,128]{3,2,1,0:T(8,128)(2,1)S(1)} %collective-permute-done.4.refs_5_.refs_4_.refs_6_), channel_id=1, source_target_pairs={{0,4},{4,0},{8,12},{12,8},{1,5},{5,1},{9,13},{13,9},{2,6},{6,2},{1... | collective-permute-start | bytes 393224 | tf_op jit(solution)/shard_map/ppermute | solution.py:403
